TPU v7x, 32 devices: a whole 2x2x4 slice. The times are simulated.
32 devices in a mesh: rows: 16 (over z, x, core), frames: 2 (over y).
Axes of the slice: x: 2, y: 2, z: 4, core: 2. Of those that a mesh axis runs over, the one named last changes fastest.
Arguments:
- frames_raw: float32 [4, 256, 4096], P('frames', 'rows'), may hold values from 0.1 to 5.2, as said below
- wind_off: float32 [2, 256, 4096], P('frames', 'rows'), may hold values from 0.12 to 14.8, as said below
- run_owner: int32 [16], P('rows'), may hold values from 0 to 1
- search_base: int32 [2, 2], P('frames'), may hold values from -8 to 8, as said below
Outputs:
- pressure: float32 [4, 256, 4096], P('frames', 'rows')
- frame_mean: float32 [4], P('frames')
- frame_rms: float32 [4], P('frames')
- time_mean: float32 [256, 4096], P('rows')
- time_rms: float32 [256, 4096], P('rows')
Inputs may be any that keep to these rules, and one draw needn't show every extreme that they name: `frames_raw`: positive intensities. `wind_off`: positive intensities. `search_base`: entry 0 of a block is a row offset from -1 to 1, entry 1 a column offset from -8 to 8; in every draw some block has row offset -1, some +1, some column offset -8 and some +8.
All inputs are finite; a program needn't handle non-finite values.
Results may differ from a plain program's by a relative error of at most 0.0003.
Values sent between devices are 32-bit elements; how exact they have to be, the bound alone decides.
No kernel may reach another device: no remote copies, remote signals or barrier semaphores. Data moves between devices by JAX's collectives and lax.ppermute only.
A program may use at most 128 MiB of HBM per device.

v0:
```python
import functools

import jax
import jax.numpy as jnp
from jax import lax
from jax.experimental import pallas as pl
from jax.experimental.pallas import tpu as pltpu
from jax.sharding import PartitionSpec as P

taps = (1.0 / 256, 8.0 / 256, 28.0 / 256, 56.0 / 256, 70.0 / 256)
calib_zero = -0.25
calib_linear = 1.0
calib_square = 0.15
lanes = 128
reach = 7
params = pltpu.CompilerParams(vmem_limit_bytes=24 * 1024 * 1024)
vmem = pl.BlockSpec(memory_space=pltpu.VMEM)
smem = pl.BlockSpec(memory_space=pltpu.SMEM)


def tile_of(index):
    return pl.ds(pl.multiple_of(index * lanes, lanes), lanes)


def vertical(load):
    total = taps[4] * load(4)
    for step in range(4):
        total = total + taps[step] * (load(step) + load(8 - step))
    return total


def horizontal(before, here, after):
    lane = lax.broadcasted_iota(jnp.int32, here.shape, here.ndim - 1)
    total = taps[4] * here
    for step in range(1, 5):
        right = pltpu.roll(jnp.where(lane < step, after, here), lanes - step, here.ndim - 1)
        left = pltpu.roll(jnp.where(lane >= lanes - step, before, here), step, here.ndim - 1)
        total = total + taps[4 - step] * (right + left)
    return total


def smooth_kernel(frames, top, bottom, smoothed, rows_in, half):
    count, rows, columns = frames.shape
    tiles = columns // lanes
    zero = jnp.zeros((rows, lanes), jnp.float32)
    for f in range(count):
        half[f, 0] = zero
        half[f, tiles + 1] = zero

    def load_step(t, carry):
        for f in range(count):
            rows_in[f, t, 4:8, :] = top[f, :, tile_of(t)]
            rows_in[f, t, 8 : 8 + rows, :] = frames[f, :, tile_of(t)]
            rows_in[f, t, 8 + rows : 12 + rows, :] = bottom[f, :, tile_of(t)]
        return carry

    def vertical_step(t, carry):
        for f in range(count):
            half[f, t + 1] = vertical(lambda s: rows_in[f, t, pl.ds(4 + s, rows), :])
        return carry

    def horizontal_step(t, carry):
        for f in range(count):
            smoothed[f, :, tile_of(t)] = horizontal(half[f, t], half[f, t + 1], half[f, t + 2])
        return carry

    by_tiles(load_step, tiles, 4)
    by_tiles(vertical_step, tiles, 4)
    by_tiles(horizontal_step, tiles, 4)


def by_tiles(step, tiles, group, init=()):
    def body(index, carry):
        for inner in range(group):
            carry = step(index * group + inner, carry)
        return carry

    return lax.fori_loop(0, tiles // group, body, init)


def shift_columns(source, shifted, base_col, tiles):
    def per_offset(j, carry):
        shift = base_col + j - 3
        negative = shift < 0
        first = jnp.where(negative, 0, 1)
        amount = jnp.where(negative, shift + lanes, shift)
        back = lax.rem(lanes - amount, lanes)

        def step(t, inner):
            here = source[t + first]
            after = source[t + first + 1]
            lane = lax.broadcasted_iota(jnp.int32, here.shape, 1)
            shifted[j, t] = pltpu.roll(jnp.where(lane < amount, after, here), back, 1)
            return inner

        by_tiles(step, tiles, 4)
        return carry

    lax.fori_loop(0, reach, per_offset, 0)


def match_kernel(
    base, owner, wind, other, top, bottom, frames, smoothed, clean, part, rows_in, half, fine, shifted, detail, sums
):
    count, rows, columns = frames.shape
    tiles = columns // lanes
    wide = rows + 8
    row_index = lax.axis_index("rows")
    last_row = lax.axis_size("rows") - 1
    mine = owner[0] == lax.axis_index("frames")
    blank = jnp.zeros((wide, lanes), jnp.float32)
    half[0] = blank
    half[tiles + 1] = blank
    for array in (clean, fine):
        array[0] = blank
        array[tiles + 1] = blank
    place = lax.broadcasted_iota(jnp.int32, (wide, lanes), 0)
    inside = ((place >= 4) | (row_index > 0)) & ((place < rows + 4) | (row_index < last_row))

    def load_step(t, carry):
        rows_in[t, 0:8, :] = top[:, tile_of(t)]
        rows_in[t, 8 : 8 + rows, :] = jnp.where(mine, wind[0, :, tile_of(t)], other[:, tile_of(t)])
        rows_in[t, 8 + rows : 16 + rows, :] = bottom[:, tile_of(t)]
        for f in range(count):
            detail[t, f] = frames[f, :, tile_of(t)] - smoothed[f, :, tile_of(t)]
        return carry

    def vertical_step(t, carry):
        half[t + 1] = vertical(lambda s: rows_in[t, pl.ds(s, wide), :])
        return carry

    def horizontal_step(t, carry):
        smooth = jnp.where(inside, horizontal(half[t], half[t + 1], half[t + 2]), 0.0)
        clean[t + 1] = smooth
        fine[t + 1] = rows_in[t, pl.ds(4, wide), :] - smooth
        return carry

    by_tiles(load_step, tiles, 4)
    by_tiles(vertical_step, tiles, 4)
    by_tiles(horizontal_step, tiles, 4)
    shift_columns(fine, shifted, base[0, 1], tiles)
    first_row = 1 + base[0, 0]
    zero = jnp.zeros((8, lanes), jnp.float32)

    def fold(product):
        return jnp.sum(product.reshape(rows // 8, 8, lanes), axis=0)

    def per_offset(j, carry):
        def step(t, totals):
            parts = [detail[t, f] for f in range(count)]
            result = []
            for i in range(reach):
                window = shifted[j, t, pl.ds(first_row + i, rows), :]
                for f in range(count):
                    result.append(totals[i * count + f] + fold(parts[f] * window))
            return tuple(result)

        totals = by_tiles(step, tiles, 2, (zero,) * (reach * count))
        for i in range(reach * count):
            sums[j * reach * count + i] = totals[i]
        return carry

    sums[...] = jnp.zeros(sums.shape, jnp.float32)
    lax.fori_loop(0, reach, per_offset, 0)

    def power_step(t, totals):
        own = fine[t + 1, pl.ds(4, rows), :]
        values = [detail[t, f] for f in range(count)] + [own]
        return tuple(total + fold(value * value) for total, value in zip(totals, values))

    powers = by_tiles(power_step, tiles, 4, (zero,) * (count + 1))
    for f in range(count + 1):
        sums[reach * reach * count + f] = powers[f]
    part[...] = lanes_from(jnp.sum(sums[...], axis=1), part.shape[0])


def lanes_from(columns_in, copies):
    ones = jnp.ones((copies, lanes), jnp.float32)
    return lax.dot_general(
        ones,
        columns_in,
        (((1,), (1,)), ((), ())),
        precision=lax.Precision.HIGHEST,
        preferred_element_type=jnp.float32,
    )


def blend_weights(totals, count):
    entry = lax.broadcasted_iota(jnp.int32, totals.shape, 1)
    used = reach * reach * count

    def pick(index):
        return jnp.sum(jnp.where(entry == index, totals, 0.0), axis=1, keepdims=True)

    ref_power = pick(used + count)
    weights = jnp.zeros_like(totals)
    middle = (reach * reach // 2) * count
    for f in range(count):
        member = (entry < used) & (lax.rem(entry, count) == f)
        norm_product = jnp.sqrt((pick(used + f) + 1e-06) * (ref_power + 1e-06))
        rho = jnp.where(member, totals, 0.0) / norm_product
        squared = rho * rho
        shares = squared / (0.05 + jnp.sum(squared, axis=1, keepdims=True))
        remainder = 1.0 - jnp.sum(shares, axis=1, keepdims=True)
        weights = weights + shares + jnp.where(entry == middle + f, remainder, 0.0)
    return weights


def pressure_kernel(base, parts, clean, smoothed, pressure, moments, part, shifted, splat, sums):
    count, rows, columns = smoothed.shape
    tiles = columns // lanes
    weights = blend_weights(jnp.sum(parts[...], axis=0, keepdims=True), count)
    square = (lanes, lanes)
    diagonal = lax.broadcasted_iota(jnp.int32, square, 0) == lax.broadcasted_iota(jnp.int32, square, 1)
    spread = jnp.where(diagonal, jnp.broadcast_to(weights, square), 0.0)
    spread = jnp.broadcast_to(jnp.sum(spread, axis=1, keepdims=True), square)
    for k in range(reach * reach * count):
        splat[k] = jnp.broadcast_to(spread[k : k + 1, :], (8, lanes))
    shift_columns(clean, shifted, base[0, 1], tiles)
    first_row = 1 + base[0, 0]
    zero = jnp.zeros((8, lanes), jnp.float32)
    groups = rows // 8
    pair = 2

    def step(t, totals):
        values = [[[zero] * groups for f in range(count)] for p in range(pair)]
        for j in range(reach):
            for i in range(reach):
                factor = [splat[(j * reach + i) * count + f] for f in range(count)]
                for p in range(pair):
                    for g in range(groups):
                        window = shifted[j, t * pair + p, pl.ds(first_row + i + 8 * g, 8), :]
                        for f in range(count):
                            values[p][f][g] = values[p][f][g] + factor[f] * window
        totals = list(totals)
        for p in range(pair):
            where = tile_of(t * pair + p)
            for g in range(groups):
                band = slice(8 * g, 8 * g + 8)
                first = zero
                second = zero
                for f in range(count):
                    ratio = values[p][f][g] / smoothed[f, band, where]
                    value = calib_zero + ratio * (calib_linear + calib_square * ratio)
                    squared = value * value
                    pressure[f, band, where] = value
                    first = first + value
                    second = second + squared
                    totals[f] = totals[f] + value
                    totals[count + f] = totals[count + f] + squared
                moments[0, band, where] = first
                moments[1, band, where] = second
        return tuple(totals)

    totals = lax.fori_loop(0, tiles // pair, step, (zero,) * (2 * count))
    sums[...] = jnp.zeros(sums.shape, jnp.float32)
    for k in range(2 * count):
        sums[k] = totals[k]
    part[...] = lanes_from(jnp.sum(sums[...], axis=1), part.shape[0])


def neighbours(value, axis, step):
    size = lax.axis_size(axis)
    pairs = [(i, i + step) for i in range(size) if 0 <= i + step < size]
    return lax.ppermute(value, axis, pairs)


def from_owner(shard, axis, root):
    mine = lax.axis_index(axis) == root
    if lax.axis_size(axis) == 2:
        return lax.ppermute(shard, axis, [(0, 1), (1, 0)])
    return lax.psum(jnp.where(mine, shard, jnp.zeros_like(shard)), axis)


def total_over(value, axis):
    size = lax.axis_size(axis)
    if size & (size - 1):
        return lax.psum(value, axis)
    step = 1
    while step < size:
        value = value + lax.ppermute(value, axis, [(i, i ^ step) for i in range(size)])
        step *= 2
    return value


def shards(frames_raw, wind_off, run_owner, search_base):
    count, rows, columns = frames_raw.shape
    tiles = columns // lanes
    wide = rows + 8
    size = lax.axis_size("rows")
    f32 = jnp.float32
    struct = functools.partial(jax.ShapeDtypeStruct, dtype=f32)
    other = from_owner(wind_off[0], "frames", run_owner[0])
    frames_top = neighbours(frames_raw[:, rows - 4 :], "rows", 1)
    frames_bottom = neighbours(frames_raw[:, :4], "rows", -1)
    mine = run_owner[0] == lax.axis_index("frames")
    ref_top = neighbours(jnp.where(mine, wind_off[0, rows - 8 :], other[rows - 8 :]), "rows", 1)
    ref_bottom = neighbours(jnp.where(mine, wind_off[0, :8], other[:8]), "rows", -1)
    smoothed = pl.pallas_call(
        smooth_kernel,
        out_shape=struct((count, rows, columns)),
        in_specs=[vmem] * 3,
        out_specs=vmem,
        scratch_shapes=[
            pltpu.VMEM((count, tiles, rows + 16, lanes), f32),
            pltpu.VMEM((count, tiles + 2, rows, lanes), f32),
        ],
        compiler_params=params,
        name="smooth",
    )(frames_raw, frames_top, frames_bottom)
    clean, part = pl.pallas_call(
        match_kernel,
        out_shape=(struct((tiles + 2, wide, lanes)), struct((size, lanes))),
        in_specs=[smem, smem] + [vmem] * 6,
        out_specs=(vmem, vmem),
        scratch_shapes=[
            pltpu.VMEM((tiles, rows + 16, lanes), f32),
            pltpu.VMEM((tiles + 2, wide, lanes), f32),
            pltpu.VMEM((tiles + 2, wide, lanes), f32),
            pltpu.VMEM((reach, tiles, wide, lanes), f32),
            pltpu.VMEM((tiles, count, rows, lanes), f32),
            pltpu.VMEM((lanes, 8, lanes), f32),
        ],
        compiler_params=params,
        name="match",
    )(search_base, run_owner, wind_off, other, ref_top, ref_bottom, frames_raw, smoothed)
    parts = lax.all_to_all(part, "rows", 0, 0, tiled=True)
    pressure, moments, part = pl.pallas_call(
        pressure_kernel,
        out_shape=(struct((count, rows, columns)), struct((2, rows, columns)), struct((8, lanes))),
        in_specs=[smem] + [vmem] * 3,
        out_specs=(vmem, vmem, vmem),
        scratch_shapes=[
            pltpu.VMEM((reach, tiles, wide, lanes), f32),
            pltpu.VMEM((reach * reach * count, 8, lanes), f32),
            pltpu.VMEM((lanes, 8, lanes), f32),
        ],
        compiler_params=params,
        name="pressure",
    )(search_base, parts, clean, smoothed)
    whole = total_over(moments, "frames")
    spatial = total_over(part[0], "rows")
    cell_count = rows * columns * size
    frame_mean = spatial[:count] / cell_count
    frame_rms = jnp.sqrt(spatial[count : 2 * count] / cell_count - frame_mean * frame_mean)
    total_frames = count * lax.axis_size("frames")
    time_mean = whole[0] / total_frames
    time_rms = jnp.sqrt(jnp.maximum(whole[1] / total_frames - time_mean * time_mean, 0.0))
    return (pressure, frame_mean, frame_rms, time_mean, time_rms)


def solution(mesh):
    placed = (P("frames", "rows", None), P("frames", "rows", None), P("rows"), P("frames", None))
    return jax.shard_map(
        shards,
        mesh=mesh,
        in_specs=placed,
        out_specs=(
            P("frames", "rows", None),
            P("frames"),
            P("frames"),
            P("rows", None),
            P("rows", None),
        ),
        check_vma=False,
    )
```

profile of v0, /device:TPU:0, one launch (start us, length us, event | category | flops | bytes accessed | tf_op | source)
XLA Modules:
  0.0 66.9 jit_solution(6460763731618601713)
XLA Ops:
  0.6 3.0 %collective-permute-start = (f32[16,4096]{1,0:T(8,128)}, f32[16,4096]{1,0:T(8,128)S(1)}, u32[]{:S(2)}, u32[]{:S(2)}) collective-permute-start(f32[16,4096]{1,0:T(8,128)} %bitcast.26), channel_id=1, source_target_pairs={{0,1},{1,0},{2,3},{3,2},{4,5},{5,4},{6,7},{7,6},{8,9},{9,8},{10,11... | collective-permute-start | bytes 786440 | tf_op jit(solution)/shard_map/ppermute | solution.py:271
  3.7 1.1 %fusion.7 = (f32[2,4,4096]{2,1,0:T(4,128)S(1)}, f32[2,4,4096]{2,1,0:T(4,128)S(1)}) fusion(f32[2,16,4096]{2,1,0:T(8,128)} %frames.3), kind=kLoop, calls=%fused_computation.13 | loop fusion | bytes 524288 | tf_op jit(solution)/shard_map/slice | solution.py:295
  4.8 0.0 copy-start
  4.8 1.4 %collective-permute-start.4 = (f32[2,4,4096]{2,1,0:T(4,128)S(1)}, f32[2,4,4096]{2,1,0:T(4,128)S(1)}, u32[]{:S(2)}, u32[]{:S(2)}) collective-permute-start(f32[2,4,4096]{2,1,0:T(4,128)S(1)} %get-tuple-element.19), channel_id=1, source_target_pairs={{2,0},{4,2},{6,4},{8,6},{10,8},{12,10},{14,12},{16,14},{18,16},{20... | collective-permute-start | bytes 393224 | tf_op jit(solution)/shard_map/ppermute | solution.py:265
  6.2 3.0 %collective-permute-start.3 = (f32[2,4,4096]{2,1,0:T(4,128)S(1)}, f32[2,4,4096]{2,1,0:T(4,128)S(1)}, u32[]{:S(2)}, u32[]{:S(2)}) collective-permute-start(f32[2,4,4096]{2,1,0:T(4,128)S(1)} %get-tuple-element.20), channel_id=1, source_target_pairs={{0,2},{2,4},{4,6},{6,8},{8,10},{10,12},{12,14},{14,16},{16,18},{18... | collective-permute-start | bytes 393224 | tf_op jit(solution)/shard_map/ppermute | solution.py:265
  9.9 0.3 collective-permute-done.other
  10.2 1.3 %collective-permute-start.2 = (f32[8,4096]{1,0:T(8,128)S(1)}, f32[8,4096]{1,0:T(8,128)S(1)}, u32[]{:S(2)}, u32[]{:S(2)}) collective-permute-start(f32[8,4096]{1,0:T(8,128)S(1)} %get-tuple-element.21), channel_id=1, source_target_pairs={{2,0},{4,2},{6,4},{8,6},{10,8},{12,10},{14,12},{16,14},{18,16},{20... | collective-permute-start | bytes 393224 | tf_op jit(solution)/shard_map/ppermute | solution.py:265
  11.5 0.0 copy-start.2
  11.5 3.4 %collective-permute-start.1 = (f32[8,4096]{1,0:T(8,128)S(1)}, f32[8,4096]{1,0:T(8,128)S(1)}, u32[]{:S(2)}, u32[]{:S(2)}) collective-permute-start(f32[8,4096]{1,0:T(8,128)S(1)} %get-tuple-element.22), channel_id=1, source_target_pairs={{0,2},{2,4},{4,6},{6,8},{8,10},{10,12},{12,14},{14,16},{16,18},{18... | collective-permute-start | bytes 393224 | tf_op jit(solution)/shard_map/ppermute | solution.py:265
  14.9 2.2 %smooth.1.smoothed = f32[2,16,4096]{2,1,0:T(8,128)S(1)} custom-call(f32[2,16,4096]{2,1,0:T(8,128)S(1)} %copy-done, f32[2,4,4096]{2,1,0:T(4,128)S(1)} %collective-permute-done.3.top, f32[2,4,4096]{2,1,0:T(4,128)S(1)} %collective-permute-done.4.bottom), custom_call_target="tpu_custom_call" | custom-call | tf_op jit(solution)/shard_map/smooth/pallas_call | solution.py:299
  17.1 9.9 %match.1 = (f32[34,24,128]{2,1,0:T(8,128)S(1)}, f32[16,128]{1,0:T(8,128)S(1)}) custom-call(s32[1,2]{1,0:T(1,128)S(1)} %copy-done.2, s32[1]{0:T(128)} %copy.10.owner, f32[1,16,4096]{2,1,0:T(8,128)S(1)} %copy-done.1, f32[16,4096]{1,0:T(8,128)S(1)} %collective-permute-done.other, f32[8,4096]{1,0:T(8,128)S(1)} %collective-permute-done.1.top, ...), custom_call_target="tpu_custom_call" | custom-call | tf_op jit(solution)/shard_map/match/pallas_call | solution.py:311
  27.0 15.8 %all_to_all.11 = f32[16,1,128]{2,1,0:T(1,128)S(1)} all-to-all(f32[16,1,128]{2,1,0:T(1,128)S(1)} %bitcast.28), channel_id=1, replica_groups=mesh['rows'=16,'frames'=2] {'rows'}, dimensions={0} | all-to-all | bytes 16384 | tf_op jit(solution)/shard_map/all_to_all | solution.py:327
  42.8 9.3 %pressure.1 = (f32[2,16,4096]{2,1,0:T(8,128)}, f32[2,16,4096]{2,1,0:T(8,128)S(1)}, f32[8,128]{1,0:T(8,128)S(1)}) custom-call(s32[1,2]{1,0:T(1,128)S(1)} %copy-done.2, f32[16,128]{1,0:T(8,128)S(1)} %bitcast.27, f32[34,24,128]{2,1,0:T(8,128)S(1)} %get-tuple-element.11.clean, f32[2,16,4096]{2,1,0:T(8,128)S(1)} %smooth.1.smoothed), custom_call_target="tpu_custom_call" | custom-call | tf_op jit(solution)/shard_map/pressure/pallas_call | solution.py:328
  52.1 0.5 collective-permute-start.9
  52.7 1.1 %collective-permute-done.5 = f32[128]{0:T(128)S(1)} collective-permute-done((f32[128]{0:T(128)S(1)}, f32[128]{0:T(128)S(1)}, u32[]{:S(2)}, u32[]{:S(2)}) %collective-permute-start.5) | collective-permute-done | bytes 544 | tf_op jit(solution)/shard_map/ppermute | solution.py:281
  53.8 0.5 collective-permute-start.6
  54.3 3.0 %collective-permute-done.6 = f32[128]{0:T(128)S(1)} collective-permute-done((f32[128]{0:T(128)S(1)}, f32[128]{0:T(128)S(1)}, u32[]{:S(2)}, u32[]{:S(2)}) %collective-permute-start.6) | collective-permute-done | bytes 544 | tf_op jit(solution)/shard_map/ppermute | solution.py:281
  57.3 0.5 collective-permute-start.7
  57.8 3.0 %collective-permute-done.7 = f32[128]{0:T(128)S(1)} collective-permute-done((f32[128]{0:T(128)S(1)}, f32[128]{0:T(128)S(1)}, u32[]{:S(2)}, u32[]{:S(2)}) %collective-permute-start.7) | collective-permute-done | bytes 544 | tf_op jit(solution)/shard_map/ppermute | solution.py:281
  60.9 0.5 collective-permute-start.8
  61.4 3.9 %collective-permute-done.8 = f32[128]{0:T(128)S(1)} collective-permute-done((f32[128]{0:T(128)S(1)}, f32[128]{0:T(128)S(1)}, u32[]{:S(2)}, u32[]{:S(2)}) %collective-permute-start.8) | collective-permute-done | bytes 544 | tf_op jit(solution)/shard_map/ppermute | solution.py:281
  65.3 0.6 subtract_sqrt_fusion
  65.9 0.1 add.19
  66.0 0.9 %fusion.3 = (f32[16,4096]{1,0:T(8,128)}, f32[16,4096]{1,0:T(8,128)}) fusion(f32[2,16,4096]{2,1,0:T(8,128)S(1)} %add.19), kind=kLoop, calls=%fused_computation.4 | loop fusion | flops 327680 | bytes 1048576 | tf_op jit(solution)/shard_map/sqrt | solution.py:348
  (16 shorter events, 0.1 us)
Async XLA Ops:
  0.6 9.6 %copy-start.1 = (f32[1,16,4096]{2,1,0:T(8,128)S(1)}, f32[1,16,4096]{2,1,0:T(8,128)}, u32[]{:S(2)}) copy-start(f32[1,16,4096]{2,1,0:T(8,128)} %wind.1) | copy-start | bytes 786436
  0.6 9.5 %collective-permute-start = (f32[16,4096]{1,0:T(8,128)}, f32[16,4096]{1,0:T(8,128)S(1)}, u32[]{:S(2)}, u32[]{:S(2)}) collective-permute-start(f32[16,4096]{1,0:T(8,128)} %bitcast.26), channel_id=1, source_target_pairs={{0,1},{1,0},{2,3},{3,2},{4,5},{5,4},{6,7},{7,6},{8,9},{9,8},{10,11... | collective-permute-start | bytes 786440 | tf_op jit(solution)/shard_map/ppermute | solution.py:271
  4.8 10.2 %copy-start = (f32[2,16,4096]{2,1,0:T(8,128)S(1)}, f32[2,16,4096]{2,1,0:T(8,128)}, u32[]{:S(2)}) copy-start(f32[2,16,4096]{2,1,0:T(8,128)} %frames.3) | copy-start | bytes 1572868
  4.8 10.2 %collective-permute-start.4 = (f32[2,4,4096]{2,1,0:T(4,128)S(1)}, f32[2,4,4096]{2,1,0:T(4,128)S(1)}, u32[]{:S(2)}, u32[]{:S(2)}) collective-permute-start(f32[2,4,4096]{2,1,0:T(4,128)S(1)} %get-tuple-element.19), channel_id=1, source_target_pairs={{2,0},{4,2},{6,4},{8,6},{10,8},{12,10},{14,12},{16,14},{18,16},{20... | collective-permute-start | bytes 393224 | tf_op jit(solution)/shard_map/ppermute | solution.py:265
  6.2 8.7 %collective-permute-start.3 = (f32[2,4,4096]{2,1,0:T(4,128)S(1)}, f32[2,4,4096]{2,1,0:T(4,128)S(1)}, u32[]{:S(2)}, u32[]{:S(2)}) collective-permute-start(f32[2,4,4096]{2,1,0:T(4,128)S(1)} %get-tuple-element.20), channel_id=1, source_target_pairs={{0,2},{2,4},{4,6},{6,8},{8,10},{10,12},{12,14},{14,16},{16,18},{18... | collective-permute-start | bytes 393224 | tf_op jit(solution)/shard_map/ppermute | solution.py:265
  10.2 6.9 %collective-permute-start.2 = (f32[8,4096]{1,0:T(8,128)S(1)}, f32[8,4096]{1,0:T(8,128)S(1)}, u32[]{:S(2)}, u32[]{:S(2)}) collective-permute-start(f32[8,4096]{1,0:T(8,128)S(1)} %get-tuple-element.21), channel_id=1, source_target_pairs={{2,0},{4,2},{6,4},{8,6},{10,8},{12,10},{14,12},{16,14},{18,16},{20... | collective-permute-start | bytes 393224 | tf_op jit(solution)/shard_map/ppermute | solution.py:265
  11.5 5.6 %copy-start.2 = (s32[1,2]{1,0:T(1,128)S(1)}, s32[1,2]{1,0:T(1,128)}, u32[]{:S(2)}) copy-start(s32[1,2]{1,0:T(1,128)} %base.3) | copy-start | bytes 28
  11.5 5.6 %collective-permute-start.1 = (f32[8,4096]{1,0:T(8,128)S(1)}, f32[8,4096]{1,0:T(8,128)S(1)}, u32[]{:S(2)}, u32[]{:S(2)}) collective-permute-start(f32[8,4096]{1,0:T(8,128)S(1)} %get-tuple-element.22), channel_id=1, source_target_pairs={{0,2},{2,4},{4,6},{6,8},{8,10},{10,12},{12,14},{14,16},{16,18},{18... | collective-permute-start | bytes 393224 | tf_op jit(solution)/shard_map/ppermute | solution.py:265
  52.1 13.8 %collective-permute-start.9 = (f32[2,16,4096]{2,1,0:T(8,128)S(1)}, f32[2,16,4096]{2,1,0:T(8,128)S(1)}, u32[]{:S(2)}, u32[]{:S(2)}) collective-permute-start(f32[2,16,4096]{2,1,0:T(8,128)S(1)} %get-tuple-element.14), channel_id=1, source_target_pairs={{0,1},{1,0},{2,3},{3,2},{4,5},{5,4},{6,7},{7,6},{8,9},{9,8},{10,11... | collective-permute-start | bytes 1572872 | tf_op jit(solution)/shard_map/ppermute | solution.py:281
  52.7 1.1 %collective-permute-start.5 = (f32[128]{0:T(128)S(1)}, f32[128]{0:T(128)S(1)}, u32[]{:S(2)}, u32[]{:S(2)}) collective-permute-start(f32[128]{0:T(128)S(1)} %slice_bitcast_fusion), channel_id=1, source_target_pairs={{0,2},{2,0},{4,6},{6,4},{8,10},{10,8},{12,14},{14,12},{16,18},{18,... | collective-permute-start | bytes 1544 | tf_op jit(solution)/shard_map/ppermute | solution.py:281
  53.8 3.5 %collective-permute-start.6 = (f32[128]{0:T(128)S(1)}, f32[128]{0:T(128)S(1)}, u32[]{:S(2)}, u32[]{:S(2)}) collective-permute-start(f32[128]{0:T(128)S(1)} %fusion.5), channel_id=1, source_target_pairs={{0,4},{2,6},{4,0},{6,2},{8,12},{10,14},{12,8},{14,10},{16,20},{18,... | collective-permute-start | bytes 1544 | tf_op jit(solution)/shard_map/ppermute | solution.py:281
  57.3 3.5 %collective-permute-start.7 = (f32[128]{0:T(128)S(1)}, f32[128]{0:T(128)S(1)}, u32[]{:S(2)}, u32[]{:S(2)}) collective-permute-start(f32[128]{0:T(128)S(1)} %add.16), channel_id=1, source_target_pairs={{0,8},{2,10},{4,12},{6,14},{8,0},{10,2},{12,4},{14,6},{16,24},{18,... | collective-permute-start | bytes 1544 | tf_op jit(solution)/shard_map/ppermute | solution.py:281
  60.9 4.4 %collective-permute-start.8 = (f32[128]{0:T(128)S(1)}, f32[128]{0:T(128)S(1)}, u32[]{:S(2)}, u32[]{:S(2)}) collective-permute-start(f32[128]{0:T(128)S(1)} %add.17), channel_id=1, source_target_pairs={{0,16},{2,18},{4,20},{6,22},{8,24},{10,26},{12,28},{14,30},{16,0},... | collective-permute-start | bytes 1544 | tf_op jit(solution)/shard_map/ppermute | solution.py:281
where the time goes:
time: 67.2 us; the launch traced here: 66.9 us
  Pallas kernels  21.4 us (32%)
  blocking collectives  15.8 us (24%)
  starting transfers between devices  14.2 us (21%)
  waiting for transfers between devices  11.4 us (17%)
  other arithmetic  1.61 us (2%)
  between operations  1.41 us (2%)
  local copies, waits for them, and re-layouts  1.09 us (2%)
    all_to_all x1, blocking collectives, shards(): parts = lax.all_to_all(part, 'rows', 0, 0, tiled=True)  15.8 us
    ppermute x5, waiting for transfers between devices, total_over(): lax.ppermute(value, axis, [(i, i ^ step) for i in range(size)])  11.1 us
    pallas_call x1, Pallas kernels, shards(): pl.pallas_call(match_kernel, out_shape=(struct((tiles + 2, wide, lanes)),...  9.89 us
    pallas_call x1, Pallas kernels, shards(): pl.pallas_call(pressure_kernel, out_shape=(struct((count, rows, columns))...  9.3 us
    ppermute x4, starting transfers between devices, neighbours(): return lax.ppermute(value, axis, pairs)  9.13 us
    ppermute x1, starting transfers between devices, from_owner(): return lax.ppermute(shard, axis, [(0, 1), (1, 0)])  3.03 us
    pallas_call x1, Pallas kernels, shards(): pl.pallas_call(smooth_kernel, out_shape=struct((count, rows, columns)), i...  2.16 us
    ppermute x5, starting transfers between devices, total_over(): lax.ppermute(value, axis, [(i, i ^ step) for i in range(size)])  2.06 us
  transfers between devices with their start and end apart: 10, of which 5 were waited for; matrix products, arithmetic and copies ran while one was open for 3% of the time, Pallas kernels for 3%

commit v1 on v0

--- a/solution.py
+++ b/solution.py
@@ -39,9 +39,10 @@
     return total
 
 
-def smooth_kernel(frames, top, bottom, smoothed, rows_in, half):
+def smooth_kernel(frames, from_odd, from_even, smoothed, rows_in, half):
     count, rows, columns = frames.shape
     tiles = columns // lanes
+    odd = lax.axis_index("rows") % 2 == 1
     zero = jnp.zeros((rows, lanes), jnp.float32)
     for f in range(count):
         half[f, 0] = zero
@@ -49,9 +50,11 @@
 
     def load_step(t, carry):
         for f in range(count):
-            rows_in[f, t, 4:8, :] = top[f, :, tile_of(t)]
+            outer = from_odd[f, :, tile_of(t)]
+            inner = from_even[f, :, tile_of(t)]
+            rows_in[f, t, 4:8, :] = jnp.where(odd, inner, outer)
             rows_in[f, t, 8 : 8 + rows, :] = frames[f, :, tile_of(t)]
-            rows_in[f, t, 8 + rows : 12 + rows, :] = bottom[f, :, tile_of(t)]
+            rows_in[f, t, 8 + rows : 12 + rows, :] = jnp.where(odd, outer, inner)
         return carry
 
     def vertical_step(t, carry):
@@ -64,9 +67,9 @@
             smoothed[f, :, tile_of(t)] = horizontal(half[f, t], half[f, t + 1], half[f, t + 2])
         return carry
 
-    by_tiles(load_step, tiles, 4)
-    by_tiles(vertical_step, tiles, 4)
-    by_tiles(horizontal_step, tiles, 4)
+    by_tiles(load_step, tiles, 8)
+    by_tiles(vertical_step, tiles, 8)
+    by_tiles(horizontal_step, tiles, 8)
 
 
 def by_tiles(step, tiles, group, init=()):
@@ -93,21 +96,21 @@
             shifted[j, t] = pltpu.roll(jnp.where(lane < amount, after, here), back, 1)
             return inner
 
-        by_tiles(step, tiles, 4)
+        by_tiles(step, tiles, 32)
         return carry
 
     lax.fori_loop(0, reach, per_offset, 0)
 
 
 def match_kernel(
-    base, owner, wind, other, top, bottom, frames, smoothed, clean, part, rows_in, half, fine, shifted, detail, sums
+    base, own_odd, own_even, from_odd, from_even, frames, smoothed, clean, part, rows_in, half, fine, shifted, detail, sums
 ):
     count, rows, columns = frames.shape
     tiles = columns // lanes
     wide = rows + 8
     row_index = lax.axis_index("rows")
     last_row = lax.axis_size("rows") - 1
-    mine = owner[0] == lax.axis_index("frames")
+    odd = row_index % 2 == 1
     blank = jnp.zeros((wide, lanes), jnp.float32)
     half[0] = blank
     half[tiles + 1] = blank
@@ -118,9 +121,12 @@
     inside = ((place >= 4) | (row_index > 0)) & ((place < rows + 4) | (row_index < last_row))
 
     def load_step(t, carry):
-        rows_in[t, 0:8, :] = top[:, tile_of(t)]
-        rows_in[t, 8 : 8 + rows, :] = jnp.where(mine, wind[0, :, tile_of(t)], other[:, tile_of(t)])
-        rows_in[t, 8 + rows : 16 + rows, :] = bottom[:, tile_of(t)]
+        outer = [array[:, tile_of(t)] for array in (from_odd, own_odd)]
+        inner = [array[:, tile_of(t)] for array in (own_even, from_even)]
+        rows_in[t, 0:8, :] = jnp.where(odd, inner[1], outer[0])
+        rows_in[t, 8:16, :] = jnp.where(odd, inner[0], outer[1])
+        rows_in[t, 16:24, :] = jnp.where(odd, outer[1], inner[0])
+        rows_in[t, 24:32, :] = jnp.where(odd, outer[0], inner[1])
         for f in range(count):
             detail[t, f] = frames[f, :, tile_of(t)] - smoothed[f, :, tile_of(t)]
         return carry
@@ -135,9 +141,9 @@
         fine[t + 1] = rows_in[t, pl.ds(4, wide), :] - smooth
         return carry
 
-    by_tiles(load_step, tiles, 4)
-    by_tiles(vertical_step, tiles, 4)
-    by_tiles(horizontal_step, tiles, 4)
+    by_tiles(load_step, tiles, 8)
+    by_tiles(vertical_step, tiles, 8)
+    by_tiles(horizontal_step, tiles, 8)
     shift_columns(fine, shifted, base[0, 1], tiles)
     first_row = 1 + base[0, 0]
     zero = jnp.zeros((8, lanes), jnp.float32)
@@ -155,7 +161,7 @@
                     result.append(totals[i * count + f] + fold(parts[f] * window))
             return tuple(result)
 
-        totals = by_tiles(step, tiles, 2, (zero,) * (reach * count))
+        totals = by_tiles(step, tiles, 8, (zero,) * (reach * count))
         for i in range(reach * count):
             sums[j * reach * count + i] = totals[i]
         return carry
@@ -168,7 +174,7 @@
         values = [detail[t, f] for f in range(count)] + [own]
         return tuple(total + fold(value * value) for total, value in zip(totals, values))
 
-    powers = by_tiles(power_step, tiles, 4, (zero,) * (count + 1))
+    powers = by_tiles(power_step, tiles, 8, (zero,) * (count + 1))
     for f in range(count + 1):
         sums[reach * reach * count + f] = powers[f]
     part[...] = lanes_from(jnp.sum(sums[...], axis=1), part.shape[0])
@@ -200,16 +206,15 @@
         norm_product = jnp.sqrt((pick(used + f) + 1e-06) * (ref_power + 1e-06))
         rho = jnp.where(member, totals, 0.0) / norm_product
         squared = rho * rho
-        shares = squared / (0.05 + jnp.sum(squared, axis=1, keepdims=True))
-        remainder = 1.0 - jnp.sum(shares, axis=1, keepdims=True)
-        weights = weights + shares + jnp.where(entry == middle + f, remainder, 0.0)
+        scale = 1.0 / (0.05 + jnp.sum(squared, axis=1, keepdims=True))
+        weights = weights + (squared + jnp.where(entry == middle + f, 0.05, 0.0)) * scale
     return weights
 
 
 def pressure_kernel(base, parts, clean, smoothed, pressure, moments, part, shifted, splat, sums):
     count, rows, columns = smoothed.shape
     tiles = columns // lanes
-    weights = blend_weights(jnp.sum(parts[...], axis=0, keepdims=True), count)
+    weights = blend_weights(parts[0:1, :], count)
     square = (lanes, lanes)
     diagonal = lax.broadcasted_iota(jnp.int32, square, 0) == lax.broadcasted_iota(jnp.int32, square, 1)
     spread = jnp.where(diagonal, jnp.broadcast_to(weights, square), 0.0)
@@ -259,17 +264,26 @@
     part[...] = lanes_from(jnp.sum(sums[...], axis=1), part.shape[0])
 
 
-def neighbours(value, axis, step):
+def paired(value, axis, first):
     size = lax.axis_size(axis)
-    pairs = [(i, i + step) for i in range(size) if 0 <= i + step < size]
-    return lax.ppermute(value, axis, pairs)
-
-
-def from_owner(shard, axis, root):
+    pairs = [(i, i + 1) for i in range(first, size - 1, 2)]
+    return lax.ppermute(value, axis, pairs + [(j, i) for i, j in pairs])
+
+
+def by_parity(odd, array, height, dim):
+    length = array.shape[dim]
+    low = lax.slice_in_dim(array, 0, height, axis=dim)
+    high = lax.slice_in_dim(array, length - height, length, axis=dim)
+    return jnp.where(odd, high, low), jnp.where(odd, low, high)
+
+
+def from_owner(shard, odd, axis, root):
     mine = lax.axis_index(axis) == root
     if lax.axis_size(axis) == 2:
-        return lax.ppermute(shard, axis, [(0, 1), (1, 0)])
-    return lax.psum(jnp.where(mine, shard, jnp.zeros_like(shard)), axis)
+        halves = by_parity(odd, shard, shard.shape[0] // 2, 0)
+        return [jnp.where(mine, half, paired(half, axis, 0)) for half in halves]
+    whole = lax.psum(jnp.where(mine, shard, jnp.zeros_like(shard)), axis)
+    return by_parity(odd, whole, shard.shape[0] // 2, 0)
 
 
 def total_over(value, axis):
@@ -290,12 +304,13 @@
     size = lax.axis_size("rows")
     f32 = jnp.float32
     struct = functools.partial(jax.ShapeDtypeStruct, dtype=f32)
-    other = from_owner(wind_off[0], "frames", run_owner[0])
-    frames_top = neighbours(frames_raw[:, rows - 4 :], "rows", 1)
-    frames_bottom = neighbours(frames_raw[:, :4], "rows", -1)
-    mine = run_owner[0] == lax.axis_index("frames")
-    ref_top = neighbours(jnp.where(mine, wind_off[0, rows - 8 :], other[rows - 8 :]), "rows", 1)
-    ref_bottom = neighbours(jnp.where(mine, wind_off[0, :8], other[:8]), "rows", -1)
+    odd = lax.axis_index("rows") % 2 == 1
+    own_odd, own_even = from_owner(wind_off[0], odd, "frames", run_owner[0])
+    frames_odd, frames_even = by_parity(odd, frames_raw, 4, 1)
+    frames_odd = paired(frames_odd, "rows", 1)
+    frames_even = paired(frames_even, "rows", 0)
+    from_odd = paired(own_odd, "rows", 1)
+    from_even = paired(own_even, "rows", 0)
     smoothed = pl.pallas_call(
         smooth_kernel,
         out_shape=struct((count, rows, columns)),
@@ -307,11 +322,11 @@
         ],
         compiler_params=params,
         name="smooth",
-    )(frames_raw, frames_top, frames_bottom)
+    )(frames_raw, frames_odd, frames_even)
     clean, part = pl.pallas_call(
         match_kernel,
-        out_shape=(struct((tiles + 2, wide, lanes)), struct((size, lanes))),
-        in_specs=[smem, smem] + [vmem] * 6,
+        out_shape=(struct((tiles + 2, wide, lanes)), struct((8, lanes))),
+        in_specs=[smem] + [vmem] * 6,
         out_specs=(vmem, vmem),
         scratch_shapes=[
             pltpu.VMEM((tiles, rows + 16, lanes), f32),
@@ -323,8 +338,8 @@
         ],
         compiler_params=params,
         name="match",
-    )(search_base, run_owner, wind_off, other, ref_top, ref_bottom, frames_raw, smoothed)
-    parts = lax.all_to_all(part, "rows", 0, 0, tiled=True)
+    )(search_base, own_odd, own_even, from_odd, from_even, frames_raw, smoothed)
+    parts = total_over(part, "rows")
     pressure, moments, part = pl.pallas_call(
         pressure_kernel,
         out_shape=(struct((count, rows, columns)), struct((2, rows, columns)), struct((8, lanes))),
@@ -339,7 +354,7 @@
         name="pressure",
     )(search_base, parts, clean, smoothed)
     whole = total_over(moments, "frames")
-    spatial = total_over(part[0], "rows")
+    spatial = jnp.sum(lax.all_gather(part[0], "rows"), axis=0)
     cell_count = rows * columns * size
     frame_mean = spatial[:count] / cell_count
     frame_rms = jnp.sqrt(spatial[count : 2 * count] / cell_count - frame_mean * frame_mean)

time: 67.2 us -> 66.7 us (level)
  Pallas kernels: 21.4 us -> 13.2 us
  blocking collectives: 15.8 us -> 20.6 us
  starting transfers between devices: 14.2 us -> 18.3 us
  waiting for transfers between devices: 11.4 us -> 10.3 us
  other arithmetic: 1.61 us -> 2.7 us
  local copies, waits for them, and re-layouts: 1.09 us -> 0.01 us
    all_gather x0 -> x1, blocking collectives: none -> 20.6 us  [shards(): spatial = jnp.sum(lax.all_gather(part[0], 'rows'), axis=0)]
    all_to_all x1 -> x0, blocking collectives: 15.8 us -> none  [shards(): parts = lax.all_to_all(part, 'rows', 0, 0, tiled=True)]
    ppermute x5, starting transfers between devices: 2.06 us -> 13.2 us  [total_over(): lax.ppermute(value, axis, [(i, i ^ step) for i in range(size)])]
    ppermute x5 -> x6, starting transfers between devices: 12.2 us -> 5.09 us  [paired(): return lax.ppermute(value, axis, pairs + [(j, i) for i, j in pairs])]
    ppermute x5, waiting for transfers between devices: 11.1 us -> 6.09 us  [total_over(): lax.ppermute(value, axis, [(i, i ^ step) for i in range(size)])]
    pallas_call x1, Pallas kernels: 9.89 us -> 5.51 us  [shards(): pl.pallas_call(match_kernel, out_shape=(struct((tiles + 2, wide, lanes)),...]
    ppermute x5 -> x6, waiting for transfers between devices: 0.3 us -> 4.18 us  [paired(): return lax.ppermute(value, axis, pairs + [(j, i) for i, j in pairs])]
    pallas_call x1, Pallas kernels: 9.3 us -> 5.87 us  [shards(): pl.pallas_call(pressure_kernel, out_shape=(struct((count, rows, columns))...]
  transfers between devices with their start and end apart: 10 -> 11, of which waited for: 5 -> 6; matrix products, arithmetic and copies ran while one was open for 3% -> 1% of each run, Pallas kernels for 3% -> 3%
where the time goes in v1:
time: 66.7 us; the launch traced here: 66.5 us
  blocking collectives  20.6 us (31%)
  starting transfers between devices  18.3 us (27%)
  Pallas kernels  13.2 us (20%)
  waiting for transfers between devices  10.3 us (15%)
  other arithmetic  2.7 us (4%)
  between operations  1.42 us (2%)
    all_gather x1, blocking collectives, shards(): spatial = jnp.sum(lax.all_gather(part[0], 'rows'), axis=0)  20.6 us
    ppermute x5, starting transfers between devices, total_over(): lax.ppermute(value, axis, [(i, i ^ step) for i in range(size)])  13.2 us
    ppermute x5, waiting for transfers between devices, total_over(): lax.ppermute(value, axis, [(i, i ^ step) for i in range(size)])  6.09 us
    pallas_call x1, Pallas kernels, shards(): pl.pallas_call(pressure_kernel, out_shape=(struct((count, rows, columns))...  5.87 us
    pallas_call x1, Pallas kernels, shards(): pl.pallas_call(match_kernel, out_shape=(struct((tiles + 2, wide, lanes)),...  5.51 us
    ppermute x6, starting transfers between devices, paired(): return lax.ppermute(value, axis, pairs + [(j, i) for i, j in pairs])  5.09 us
    ppermute x6, waiting for transfers between devices, paired(): return lax.ppermute(value, axis, pairs + [(j, i) for i, j in pairs])  4.18 us
    pallas_call x1, Pallas kernels, shards(): pl.pallas_call(smooth_kernel, out_shape=struct((count, rows, columns)), i...  1.83 us
  transfers between devices with their start and end apart: 11, of which 6 were waited for; matrix products, arithmetic and copies ran while one was open for 1% of the time, Pallas kernels for 3%

profile of v1, /device:TPU:0, one launch (start us, length us, event | category | flops | bytes accessed | tf_op | source)
XLA Modules:
  0.0 66.5 jit_solution(17739185674691978312)
XLA Ops:
  0.7 1.0 %select_bitcast_fusion = (f32[8,4096]{1,0:T(8,128)S(1)}, f32[8,4096]{1,0:T(8,128)S(1)}) fusion(f32[1,16,4096]{2,1,0:T(8,128)} %param.5, pred[]{:T(512)S(6)} %eq.9), kind=kLoop, calls=%fused_computation.7 | loop fusion | flops 65536 | bytes 524289 | tf_op jit(solution)/shard_map/jit(_where)/select_n | solution.py:277
  1.7 3.0 %collective-permute-start.1 = (f32[8,4096]{1,0:T(8,128)S(1)}, f32[8,4096]{1,0:T(8,128)S(1)}, u32[]{:S(2)}, u32[]{:S(2)}) collective-permute-start(f32[8,4096]{1,0:T(8,128)S(1)} %get-tuple-element.21), channel_id=1, source_target_pairs={{0,1},{1,0},{2,3},{3,2},{4,5},{5,4},{6,7},{7,6},{8,9},{9,8},{10,11... | collective-permute-start | bytes 393224 | tf_op jit(solution)/shard_map/ppermute | solution.py:270
  4.7 0.1 collective-permute-start
  4.9 0.1 collective-permute-start.5
  4.9 0.7 %collective-permute-start.4 = (f32[2,4,4096]{2,1,0:T(4,128)S(1)}, f32[2,4,4096]{2,1,0:T(4,128)S(1)}, u32[]{:S(2)}, u32[]{:S(2)}) collective-permute-start(f32[2,4,4096]{2,1,0:T(4,128)S(1)} %get-tuple-element.20), channel_id=1, source_target_pairs={{2,4},{6,8},{10,12},{14,16},{18,20},{22,24},{26,28},{4,2},{8,6},{1... | collective-permute-start | bytes 393224 | tf_op jit(solution)/shard_map/ppermute | solution.py:270
  6.3 2.8 %collective-permute-done.1 = f32[8,4096]{1,0:T(8,128)S(1)} collective-permute-done((f32[8,4096]{1,0:T(8,128)S(1)}, f32[8,4096]{1,0:T(8,128)S(1)}, u32[]{:S(2)}, u32[]{:S(2)}) %collective-permute-start.1) | collective-permute-done | bytes 131104 | tf_op jit(solution)/shard_map/ppermute | solution.py:270
  9.1 0.6 collective-permute-start.3
  9.6 1.4 %collective-permute-done = f32[8,4096]{1,0:T(8,128)S(1)} collective-permute-done((f32[8,4096]{1,0:T(8,128)S(1)}, f32[8,4096]{1,0:T(8,128)S(1)}, u32[]{:S(2)}, u32[]{:S(2)}) %collective-permute-start) | collective-permute-done | bytes 131104 | tf_op jit(solution)/shard_map/ppermute | solution.py:270
  11.1 0.7 %collective-permute-start.2 = (f32[8,4096]{1,0:T(8,128)S(1)}, f32[8,4096]{1,0:T(8,128)S(1)}, u32[]{:S(2)}, u32[]{:S(2)}) collective-permute-start(f32[8,4096]{1,0:T(8,128)S(1)} %broadcast_select_fusion.1.own_odd), channel_id=1, source_target_pairs={{2,4},{6,8},{10,12},{14,16},{18,20},{22,24},{26,28},{4,2},{8,6},{1... | collective-permute-start | bytes 393224 | tf_op jit(solution)/shard_map/ppermute | solution.py:270
  11.8 1.8 %smooth.1.smoothed = f32[2,16,4096]{2,1,0:T(8,128)S(1)} custom-call(f32[2,16,4096]{2,1,0:T(8,128)S(1)} %copy-done, f32[2,4,4096]{2,1,0:T(4,128)S(1)} %collective-permute-done.4.from_odd, f32[2,4,4096]{2,1,0:T(4,128)S(1)} %collective-permute-done.5.from_even), custom_call_target="tpu_custom_call" | custom-call | tf_op jit(solution)/shard_map/smooth/pallas_call | solution.py:314
  13.6 5.5 %match.1 = (f32[34,24,128]{2,1,0:T(8,128)S(1)}, f32[8,128]{1,0:T(8,128)S(1)}) custom-call(s32[1,2]{1,0:T(1,128)S(1)} %copy-done.1, f32[8,4096]{1,0:T(8,128)S(1)} %broadcast_select_fusion.1.own_odd, f32[8,4096]{1,0:T(8,128)S(1)} %broadcast_select_fusion.own_even, f32[8,4096]{1,0:T(8,128)S(1)} %collective-permute-done.2.from_odd, ...), custom_call_target="tpu_custom_call" | custom-call | tf_op jit(solution)/shard_map/match/pallas_call | solution.py:326
  19.1 4.5 %collective-permute-start.6 = (f32[8,128]{1,0:T(8,128)S(1)}, f32[8,128]{1,0:T(8,128)S(1)}, u32[]{:S(2)}, u32[]{:S(2)}) collective-permute-start(f32[8,128]{1,0:T(8,128)S(1)} %get-tuple-element.10), channel_id=1, source_target_pairs={{0,2},{2,0},{4,6},{6,4},{8,10},{10,8},{12,14},{14,12},{16,18},{18,... | collective-permute-start | bytes 12296 | tf_op jit(solution)/shard_map/ppermute | solution.py:295
  23.7 0.8 %collective-permute-done.6 = f32[8,128]{1,0:T(8,128)S(1)} collective-permute-done((f32[8,128]{1,0:T(8,128)S(1)}, f32[8,128]{1,0:T(8,128)S(1)}, u32[]{:S(2)}, u32[]{:S(2)}) %collective-permute-start.6) | collective-permute-done | bytes 4128 | tf_op jit(solution)/shard_map/ppermute | solution.py:295
  24.5 2.7 %collective-permute-start.7 = (f32[8,128]{1,0:T(8,128)S(1)}, f32[8,128]{1,0:T(8,128)S(1)}, u32[]{:S(2)}, u32[]{:S(2)}) collective-permute-start(f32[8,128]{1,0:T(8,128)S(1)} %add.20), channel_id=1, source_target_pairs={{0,4},{2,6},{4,0},{6,2},{8,12},{10,14},{12,8},{14,10},{16,20},{18,... | collective-permute-start | bytes 12296 | tf_op jit(solution)/shard_map/ppermute | solution.py:295
  27.2 1.6 %collective-permute-done.7 = f32[8,128]{1,0:T(8,128)S(1)} collective-permute-done((f32[8,128]{1,0:T(8,128)S(1)}, f32[8,128]{1,0:T(8,128)S(1)}, u32[]{:S(2)}, u32[]{:S(2)}) %collective-permute-start.7) | collective-permute-done | bytes 4128 | tf_op jit(solution)/shard_map/ppermute | solution.py:295
  28.8 1.7 %collective-permute-start.8 = (f32[8,128]{1,0:T(8,128)S(1)}, f32[8,128]{1,0:T(8,128)S(1)}, u32[]{:S(2)}, u32[]{:S(2)}) collective-permute-start(f32[8,128]{1,0:T(8,128)S(1)} %add.21), channel_id=1, source_target_pairs={{0,8},{2,10},{4,12},{6,14},{8,0},{10,2},{12,4},{14,6},{16,24},{18,... | collective-permute-start | bytes 12296 | tf_op jit(solution)/shard_map/ppermute | solution.py:295
  30.5 1.9 %collective-permute-done.8 = f32[8,128]{1,0:T(8,128)S(1)} collective-permute-done((f32[8,128]{1,0:T(8,128)S(1)}, f32[8,128]{1,0:T(8,128)S(1)}, u32[]{:S(2)}, u32[]{:S(2)}) %collective-permute-start.8) | collective-permute-done | bytes 4128 | tf_op jit(solution)/shard_map/ppermute | solution.py:295
  32.4 2.7 %collective-permute-start.9 = (f32[8,128]{1,0:T(8,128)S(1)}, f32[8,128]{1,0:T(8,128)S(1)}, u32[]{:S(2)}, u32[]{:S(2)}) collective-permute-start(f32[8,128]{1,0:T(8,128)S(1)} %add.22), channel_id=1, source_target_pairs={{0,16},{2,18},{4,20},{6,22},{8,24},{10,26},{12,28},{14,30},{16,0},... | collective-permute-start | bytes 12296 | tf_op jit(solution)/shard_map/ppermute | solution.py:295
  35.1 1.8 %collective-permute-done.9 = f32[8,128]{1,0:T(8,128)S(1)} collective-permute-done((f32[8,128]{1,0:T(8,128)S(1)}, f32[8,128]{1,0:T(8,128)S(1)}, u32[]{:S(2)}, u32[]{:S(2)}) %collective-permute-start.9) | collective-permute-done | bytes 4128 | tf_op jit(solution)/shard_map/ppermute | solution.py:295
  36.9 5.9 %pressure.1 = (f32[2,16,4096]{2,1,0:T(8,128)}, f32[2,16,4096]{2,1,0:T(8,128)S(1)}, f32[8,128]{1,0:T(8,128)S(1)}) custom-call(s32[1,2]{1,0:T(1,128)S(1)} %copy-done.1, f32[8,128]{1,0:T(8,128)S(1)} %add.23.parts, f32[34,24,128]{2,1,0:T(8,128)S(1)} %get-tuple-element.11.clean, f32[2,16,4096]{2,1,0:T(8,128)S(1)} %smooth.1.smoothed), custom_call_target="tpu_custom_call" | custom-call | tf_op jit(solution)/shard_map/pressure/pallas_call | solution.py:343
  42.8 1.5 %collective-permute-start.10 = (f32[2,16,4096]{2,1,0:T(8,128)S(1)}, f32[2,16,4096]{2,1,0:T(8,128)S(1)}, u32[]{:S(2)}, u32[]{:S(2)}) collective-permute-start(f32[2,16,4096]{2,1,0:T(8,128)S(1)} %get-tuple-element.14), channel_id=1, source_target_pairs={{0,1},{1,0},{2,3},{3,2},{4,5},{5,4},{6,7},{7,6},{8,9},{9,8},{10,11... | collective-permute-start | bytes 1572872 | tf_op jit(solution)/shard_map/ppermute | solution.py:295
  44.3 20.6 %all-gather = f32[16,1,128]{2,1,0:T(1,128)S(1)} all-gather(f32[1,1,128]{2,1,0:T(1,128)S(1)} %slice_bitcast_fusion), channel_id=1, replica_groups=mesh['rows'=16,'frames'=2] {'rows'}, dimensions={0}, use_global_device_ids=true | all-gather | bytes 8704 | tf_op jit(solution)/shard_map/all_gather | solution.py:357
  65.0 0.6 subtract_sqrt_fusion
  65.6 0.9 %fusion.3 = (f32[16,4096]{1,0:T(8,128)}, f32[16,4096]{1,0:T(8,128)}) fusion(f32[2,16,4096]{2,1,0:T(8,128)S(1)} %add.24), kind=kLoop, calls=%fused_computation.4 | loop fusion | flops 327680 | bytes 1048576 | tf_op jit(solution)/shard_map/sqrt | solution.py:363
  (19 shorter events, 0.2 us)
Async XLA Ops:
  0.6 4.2 %copy-start = (f32[2,16,4096]{2,1,0:T(8,128)S(1)}, f32[2,16,4096]{2,1,0:T(8,128)}, u32[]{:S(2)}) copy-start(f32[2,16,4096]{2,1,0:T(8,128)} %frames.3) | copy-start | bytes 1572868
  1.7 7.4 %collective-permute-start.1 = (f32[8,4096]{1,0:T(8,128)S(1)}, f32[8,4096]{1,0:T(8,128)S(1)}, u32[]{:S(2)}, u32[]{:S(2)}) collective-permute-start(f32[8,4096]{1,0:T(8,128)S(1)} %get-tuple-element.21), channel_id=1, source_target_pairs={{0,1},{1,0},{2,3},{3,2},{4,5},{5,4},{6,7},{7,6},{8,9},{9,8},{10,11... | collective-permute-start | bytes 393224 | tf_op jit(solution)/shard_map/ppermute | solution.py:270
  4.7 6.3 %collective-permute-start = (f32[8,4096]{1,0:T(8,128)S(1)}, f32[8,4096]{1,0:T(8,128)S(1)}, u32[]{:S(2)}, u32[]{:S(2)}) collective-permute-start(f32[8,4096]{1,0:T(8,128)S(1)} %get-tuple-element.22), channel_id=1, source_target_pairs={{0,1},{1,0},{2,3},{3,2},{4,5},{5,4},{6,7},{7,6},{8,9},{9,8},{10,11... | collective-permute-start | bytes 393224 | tf_op jit(solution)/shard_map/ppermute | solution.py:270
  4.9 6.9 %collective-permute-start.5 = (f32[2,4,4096]{2,1,0:T(4,128)S(1)}, f32[2,4,4096]{2,1,0:T(4,128)S(1)}, u32[]{:S(2)}, u32[]{:S(2)}) collective-permute-start(f32[2,4,4096]{2,1,0:T(4,128)S(1)} %get-tuple-element.19), channel_id=1, source_target_pairs={{0,2},{4,6},{8,10},{12,14},{16,18},{20,22},{24,26},{28,30},{2,0},{... | collective-permute-start | bytes 393224 | tf_op jit(solution)/shard_map/ppermute | solution.py:270
  4.9 6.8 %collective-permute-start.4 = (f32[2,4,4096]{2,1,0:T(4,128)S(1)}, f32[2,4,4096]{2,1,0:T(4,128)S(1)}, u32[]{:S(2)}, u32[]{:S(2)}) collective-permute-start(f32[2,4,4096]{2,1,0:T(4,128)S(1)} %get-tuple-element.20), channel_id=1, source_target_pairs={{2,4},{6,8},{10,12},{14,16},{18,20},{22,24},{26,28},{4,2},{8,6},{1... | collective-permute-start | bytes 393224 | tf_op jit(solution)/shard_map/ppermute | solution.py:270
  9.1 4.5 %collective-permute-start.3 = (f32[8,4096]{1,0:T(8,128)S(1)}, f32[8,4096]{1,0:T(8,128)S(1)}, u32[]{:S(2)}, u32[]{:S(2)}) collective-permute-start(f32[8,4096]{1,0:T(8,128)S(1)} %broadcast_select_fusion.own_even), channel_id=1, source_target_pairs={{0,2},{4,6},{8,10},{12,14},{16,18},{20,22},{24,26},{28,30},{2,0},{... | collective-permute-start | bytes 393224 | tf_op jit(solution)/shard_map/ppermute | solution.py:270
  11.1 2.6 %copy-start.1 = (s32[1,2]{1,0:T(1,128)S(1)}, s32[1,2]{1,0:T(1,128)}, u32[]{:S(2)}) copy-start(s32[1,2]{1,0:T(1,128)} %base.3) | copy-start | bytes 28
  11.1 2.5 %collective-permute-start.2 = (f32[8,4096]{1,0:T(8,128)S(1)}, f32[8,4096]{1,0:T(8,128)S(1)}, u32[]{:S(2)}, u32[]{:S(2)}) collective-permute-start(f32[8,4096]{1,0:T(8,128)S(1)} %broadcast_select_fusion.1.own_odd), channel_id=1, source_target_pairs={{2,4},{6,8},{10,12},{14,16},{18,20},{22,24},{26,28},{4,2},{8,6},{1... | collective-permute-start | bytes 393224 | tf_op jit(solution)/shard_map/ppermute | solution.py:270
  19.1 5.3 %collective-permute-start.6 = (f32[8,128]{1,0:T(8,128)S(1)}, f32[8,128]{1,0:T(8,128)S(1)}, u32[]{:S(2)}, u32[]{:S(2)}) collective-permute-start(f32[8,128]{1,0:T(8,128)S(1)} %get-tuple-element.10), channel_id=1, source_target_pairs={{0,2},{2,0},{4,6},{6,4},{8,10},{10,8},{12,14},{14,12},{16,18},{18,... | collective-permute-start | bytes 12296 | tf_op jit(solution)/shard_map/ppermute | solution.py:295
  24.5 4.3 %collective-permute-start.7 = (f32[8,128]{1,0:T(8,128)S(1)}, f32[8,128]{1,0:T(8,128)S(1)}, u32[]{:S(2)}, u32[]{:S(2)}) collective-permute-start(f32[8,128]{1,0:T(8,128)S(1)} %add.20), channel_id=1, source_target_pairs={{0,4},{2,6},{4,0},{6,2},{8,12},{10,14},{12,8},{14,10},{16,20},{18,... | collective-permute-start | bytes 12296 | tf_op jit(solution)/shard_map/ppermute | solution.py:295
  28.8 3.6 %collective-permute-start.8 = (f32[8,128]{1,0:T(8,128)S(1)}, f32[8,128]{1,0:T(8,128)S(1)}, u32[]{:S(2)}, u32[]{:S(2)}) collective-permute-start(f32[8,128]{1,0:T(8,128)S(1)} %add.21), channel_id=1, source_target_pairs={{0,8},{2,10},{4,12},{6,14},{8,0},{10,2},{12,4},{14,6},{16,24},{18,... | collective-permute-start | bytes 12296 | tf_op jit(solution)/shard_map/ppermute | solution.py:295
  32.4 4.5 %collective-permute-start.9 = (f32[8,128]{1,0:T(8,128)S(1)}, f32[8,128]{1,0:T(8,128)S(1)}, u32[]{:S(2)}, u32[]{:S(2)}) collective-permute-start(f32[8,128]{1,0:T(8,128)S(1)} %add.22), channel_id=1, source_target_pairs={{0,16},{2,18},{4,20},{6,22},{8,24},{10,26},{12,28},{14,30},{16,0},... | collective-permute-start | bytes 12296 | tf_op jit(solution)/shard_map/ppermute | solution.py:295
  42.8 22.8 %collective-permute-start.10 = (f32[2,16,4096]{2,1,0:T(8,128)S(1)}, f32[2,16,4096]{2,1,0:T(8,128)S(1)}, u32[]{:S(2)}, u32[]{:S(2)}) collective-permute-start(f32[2,16,4096]{2,1,0:T(8,128)S(1)} %get-tuple-element.14), channel_id=1, source_target_pairs={{0,1},{1,0},{2,3},{3,2},{4,5},{5,4},{6,7},{7,6},{8,9},{9,8},{10,11... | collective-permute-start | bytes 1572872 | tf_op jit(solution)/shard_map/ppermute | solution.py:295

commit v2 on v1

v2 whole, which is shorter than its diff:
```python
import functools

import jax
import jax.numpy as jnp
from jax import lax
from jax.experimental import pallas as pl
from jax.experimental.pallas import tpu as pltpu
from jax.sharding import PartitionSpec as P

taps = (1.0 / 256, 8.0 / 256, 28.0 / 256, 56.0 / 256, 70.0 / 256)
calib_zero = -0.25
calib_linear = 1.0
calib_square = 0.15
lanes = 128
reach = 7
slot = 32
params = pltpu.CompilerParams(vmem_limit_bytes=24 * 1024 * 1024)
vmem = pl.BlockSpec(memory_space=pltpu.VMEM)
smem = pl.BlockSpec(memory_space=pltpu.SMEM)


def tile_of(index):
    return pl.ds(pl.multiple_of(index * lanes, lanes), lanes)


def by_tiles(step, tiles, group, init=()):
    def body(index, carry):
        for inner in range(group):
            carry = step(index * group + inner, carry)
        return carry

    return lax.fori_loop(0, tiles // group, body, init)


def lane_of(shape):
    return lax.broadcasted_iota(jnp.int32, shape, len(shape) - 1)


def fold(product):
    return jnp.sum(product.reshape(product.shape[0] // 8, 8, lanes), axis=0)


def vertical(load):
    total = taps[4] * load(4)
    for step in range(4):
        total = total + taps[step] * (load(step) + load(8 - step))
    return total


def moved(before, here, after, step):
    if step > 0:
        return pltpu.roll(jnp.where(lane_of(here.shape) < step, after, here), lanes - step, 1)
    if step < 0:
        return pltpu.roll(jnp.where(lane_of(here.shape) >= lanes + step, before, here), -step, 1)
    return here


def horizontal(before, here, after):
    total = taps[4] * here
    for step in range(1, 5):
        pair = moved(before, here, after, step) + moved(before, here, after, -step)
        total = total + taps[4 - step] * pair
    return total


def halves(value):
    high = value.astype(jnp.bfloat16)
    low = (value - high.astype(jnp.float32)).astype(jnp.bfloat16)
    return high, low


def by_row_shift(value, rows, direction):
    place = lax.broadcasted_iota(jnp.int32, value.shape, 0) % rows
    step = 1
    while step < rows:
        turned = pltpu.roll(value, step if direction > 0 else lanes - step, 1)
        value = jnp.where((place & step) != 0, turned, value)
        step *= 2
    return value


def smooth_kernel(frames, from_odd, from_even, inverse, stack, power, rows_in, half, fine):
    count, rows, columns = frames.shape
    tiles = columns // lanes
    ring = tiles + 2
    odd = lax.axis_index("rows") % 2 == 1
    zero = jnp.zeros((rows, lanes), jnp.float32)
    for f in range(count):
        half[f, 0] = zero
        half[f, tiles + 1] = zero
    blank = jnp.zeros((count * rows, lanes), jnp.float32)
    fine[0] = blank
    fine[tiles + 1] = blank
    fine[tiles + 2] = blank

    def load_step(t, carry):
        for f in range(count):
            outer = from_odd[f, :, tile_of(t)]
            inner = from_even[f, :, tile_of(t)]
            rows_in[f, t, 4:8, :] = jnp.where(odd, inner, outer)
            rows_in[f, t, 8 : 8 + rows, :] = frames[f, :, tile_of(t)]
            rows_in[f, t, 8 + rows : 12 + rows, :] = jnp.where(odd, outer, inner)
        return carry

    def vertical_step(t, carry):
        for f in range(count):
            half[f, t + 1] = vertical(lambda s: rows_in[f, t, pl.ds(4 + s, rows), :])
        return carry

    def horizontal_step(t, totals):
        result = []
        for f in range(count):
            smooth = horizontal(half[f, t], half[f, t + 1], half[f, t + 2])
            inverse[f, :, tile_of(t)] = 1.0 / smooth
            detail = frames[f, :, tile_of(t)] - smooth
            fine[t + 1, f * rows : (f + 1) * rows, :] = detail
            result.append(totals[f] + fold(detail * detail))
        return tuple(result)

    def stack_step(t, carry):
        before, here, after = fine[t], fine[t + 1], fine[t + 2]
        for j in range(reach):
            high, low = halves(moved(before, here, after, 3 - j))
            size = count * rows
            stack[j * size : (j + 1) * size, tile_of(t)] = high
            stack[(reach + j) * size : (reach + j + 1) * size, tile_of(t)] = low
        return carry

    by_tiles(load_step, tiles, 8)
    by_tiles(vertical_step, tiles, 8)
    powers = by_tiles(horizontal_step, tiles, 8, (jnp.zeros((8, lanes), jnp.float32),) * count)
    for f in range(count):
        power[f * 8 : f * 8 + 8, :] = powers[f]
    fine[tiles + 3] = fine[1]
    by_tiles(stack_step, ring, ring // 2)


def column_shift(offset):
    negative = offset < 0
    first = jnp.where(negative, 0, 1)
    amount = jnp.where(negative, offset + lanes, offset)
    back = lax.rem(lanes - amount, lanes)

    def shift(source, t):
        here = source[t + first]
        after = source[t + first + 1]
        value = pltpu.roll(jnp.where(lane_of(here.shape) < amount, after, here), back, 1)
        spare = jnp.zeros((slot - value.shape[0], lanes), jnp.float32)
        return jnp.concatenate([value, spare], axis=0)

    return shift


def match_kernel(
    base, own_odd, own_even, from_odd, from_even, stack, power, clean, part, rows_in, half, fine, stream
):
    rows = own_odd.shape[0] * 2
    tiles = own_odd.shape[1] // lanes
    count = power.shape[0] // 8
    ring = tiles + 2
    wide = rows + 8
    row_index = lax.axis_index("rows")
    last_row = lax.axis_size("rows") - 1
    odd = row_index % 2 == 1
    blank = jnp.zeros((wide, lanes), jnp.float32)
    half[0] = blank
    half[tiles + 1] = blank
    clean[0] = blank
    clean[tiles + 1] = blank
    fine[0] = blank
    fine[tiles + 1] = blank
    fine[tiles + 2] = blank
    place = lax.broadcasted_iota(jnp.int32, (wide, lanes), 0)
    inside = ((place >= 4) | (row_index > 0)) & ((place < rows + 4) | (row_index < last_row))

    def load_step(t, carry):
        outer = [array[:, tile_of(t)] for array in (from_odd, own_odd)]
        inner = [array[:, tile_of(t)] for array in (own_even, from_even)]
        rows_in[t, 0:8, :] = jnp.where(odd, inner[1], outer[0])
        rows_in[t, 8:16, :] = jnp.where(odd, inner[0], outer[1])
        rows_in[t, 16:24, :] = jnp.where(odd, outer[1], inner[0])
        rows_in[t, 24:32, :] = jnp.where(odd, outer[0], inner[1])
        return carry

    def vertical_step(t, carry):
        half[t + 1] = vertical(lambda s: rows_in[t, pl.ds(s, wide), :])
        return carry

    def horizontal_step(t, total):
        smooth = jnp.where(inside, horizontal(half[t], half[t + 1], half[t + 2]), 0.0)
        clean[t + 1] = smooth
        detail = rows_in[t, pl.ds(4, wide), :] - smooth
        fine[t + 1] = detail
        own = jnp.where((place >= 4) & (place < rows + 4), detail, 0.0)
        return total + fold(own * own)

    by_tiles(load_step, tiles, 8)
    by_tiles(vertical_step, tiles, 8)
    ref_power = by_tiles(horizontal_step, tiles, 8, jnp.zeros((8, lanes), jnp.float32))
    fine[tiles + 3] = fine[1]
    shift = column_shift(base[0, 1])
    stream[2 * slot : 4 * slot, :] = jnp.zeros((2 * slot, ring * lanes), jnp.bfloat16)

    def stream_step(t, carry):
        high, low = halves(shift(fine, t))
        stream[0:slot, tile_of(t)] = high
        stream[slot : 2 * slot, tile_of(t)] = low
        return carry

    by_tiles(stream_step, ring, ring // 2)
    product = lax.dot_general(
        stack[...], stream[...], (((1,), (1,)), ((), ())), preferred_element_type=jnp.float32
    )
    size = reach * count * rows
    product = product[:size] + product[size:]
    product = product + pltpu.roll(product, lanes - slot, 1)
    product = by_row_shift(product, rows, -1)
    part[...] = jnp.zeros(part.shape, jnp.float32)
    for j in range(reach):
        for f in range(count):
            start = (j * count + f) * rows
            part[f * 8 + j : f * 8 + j + 1, :] = jnp.sum(product[start : start + rows], axis=0, keepdims=True)
    lags = pltpu.roll(part[0 : 8 * count, :], lax.rem(lanes - 1 - base[0, 0], lanes), 1)
    part[0 : 8 * count, :] = jnp.where(lane_of(lags.shape) < reach, lags, 0.0)
    start = 8 * count
    for f in range(count):
        part[start + f : start + f + 1, :] = jnp.sum(power[f * 8 : f * 8 + 8, :], axis=0, keepdims=True)
    part[start + count : start + count + 1, :] = jnp.sum(ref_power, axis=0, keepdims=True)
    powers = part[start : start + 8, :]
    part[start : start + 8, :] = jnp.broadcast_to(jnp.sum(powers, axis=1, keepdims=True), powers.shape)


def spread_kernel(base, clean, spread):
    tiles = clean.shape[0] - 2
    full = spread.shape[0] // 2
    spare = jnp.zeros((full - reach * slot, tiles * lanes), jnp.bfloat16)
    spread[reach * slot : full, :] = spare
    spread[full + reach * slot : 2 * full, :] = spare

    def per_offset(j, carry):
        shift = column_shift(base[0, 1] + j - 3)
        at = pl.multiple_of(j * slot, slot)

        def step(t, inner):
            high, low = halves(shift(clean, t))
            spread[pl.ds(at, slot), tile_of(t)] = high
            spread[pl.ds(full + at, slot), tile_of(t)] = low
            return inner

        by_tiles(step, tiles, 32)
        return carry

    lax.fori_loop(0, reach, per_offset, 0)


def blend_weights(matches, frame_power, ref_power):
    norm_product = jnp.sqrt((frame_power + 1e-06) * (ref_power + 1e-06))
    rho = matches / norm_product
    squared = rho * rho
    total = jnp.sum(jnp.sum(squared, axis=0, keepdims=True), axis=1, keepdims=True)
    across = lax.broadcasted_iota(jnp.int32, matches.shape, 0)
    middle = (across == reach // 2) & (lane_of(matches.shape) == reach // 2)
    return (squared + jnp.where(middle, 0.05, 0.0)) / (0.05 + total)


def banded(weights, rows, first_row):
    across = lax.broadcasted_iota(jnp.int32, weights.shape, 0)
    spaced = weights
    for step in (1, 2):
        spaced = jnp.where((across & step) != 0, pltpu.roll(spaced, step * slot, 1), spaced)
    tiles = []
    for member in (across < 4, across >= 4):
        line = jnp.sum(jnp.where(member, spaced, 0.0), axis=0, keepdims=True)
        block = by_row_shift(jnp.broadcast_to(line, (rows, lanes)), rows, 1)
        tiles.append(pltpu.roll(block, first_row, 1))
    return jnp.concatenate(tiles, axis=1)


def pressure_kernel(base, parts, spread, inverse, pressure, moments, part):
    count, rows, columns = inverse.shape
    start = 8 * count
    full = spread.shape[0] // 2
    first_row = 1 + base[0, 0]
    ref_power = parts[start + count : start + count + 1, :]
    bands = []
    for f in range(count):
        weights = blend_weights(parts[f * 8 : f * 8 + 8, :], parts[start + f : start + f + 1, :], ref_power)
        bands.append(banded(weights, rows, first_row))
    mixing = jnp.concatenate(halves(jnp.concatenate(bands, axis=0)), axis=0)
    chunk = 2 * lanes
    zero = jnp.zeros((8, lanes), jnp.float32)
    size = count * rows

    def step(t, totals):
        where = pl.ds(pl.multiple_of(t * chunk, chunk), chunk)
        product = jnp.dot(mixing, spread[0:full, where], preferred_element_type=jnp.float32)
        product = product + jnp.dot(mixing, spread[full : 2 * full, where], preferred_element_type=jnp.float32)
        registered = product[:size] + product[size:]
        first = second = None
        totals = list(totals)
        for f in range(count):
            ratio = registered[f * rows : (f + 1) * rows] * inverse[f, :, where]
            value = calib_zero + ratio * (calib_linear + calib_square * ratio)
            squared = value * value
            pressure[f, :, where] = value
            first = value if first is None else first + value
            second = squared if second is None else second + squared
            for total, array in ((f, value), (count + f, squared)):
                for c in range(chunk // lanes):
                    totals[total] = totals[total] + fold(array[:, c * lanes : (c + 1) * lanes])
        moments[0, :, where] = first
        moments[1, :, where] = second
        return tuple(totals)

    totals = by_tiles(step, columns // chunk, 4, (zero,) * (2 * count))
    part[...] = jnp.zeros(part.shape, jnp.float32)
    for k in range(2 * count):
        part[k : k + 1, :] = jnp.sum(totals[k], axis=0, keepdims=True)


def paired(value, axis, first):
    size = lax.axis_size(axis)
    pairs = [(i, i + 1) for i in range(first, size - 1, 2)]
    return lax.ppermute(value, axis, pairs + [(j, i) for i, j in pairs])


def by_parity(odd, array, height, dim):
    length = array.shape[dim]
    low = lax.slice_in_dim(array, 0, height, axis=dim)
    high = lax.slice_in_dim(array, length - height, length, axis=dim)
    return jnp.where(odd, high, low), jnp.where(odd, low, high)


def from_owner(shard, axis, root):
    mine = lax.axis_index(axis) == root
    if lax.axis_size(axis) == 2:
        return jnp.where(mine, shard, paired(shard, axis, 0))
    return lax.psum(jnp.where(mine, shard, jnp.zeros_like(shard)), axis)


def total_over(value, axis):
    size = lax.axis_size(axis)
    if size & (size - 1):
        return lax.psum(value, axis)
    step = 1
    while step < size:
        value = value + lax.ppermute(value, axis, [(i, i ^ step) for i in range(size)])
        step *= 2
    return value


def shards(frames_raw, wind_off, run_owner, search_base):
    count, rows, columns = frames_raw.shape
    tiles = columns // lanes
    ring = tiles + 2
    wide = rows + 8
    depth = reach * count * rows
    f32 = jnp.float32
    bf16 = jnp.bfloat16
    struct = functools.partial(jax.ShapeDtypeStruct, dtype=f32)
    odd = lax.axis_index("rows") % 2 == 1
    reference = from_owner(wind_off[0], "frames", run_owner[0])
    frames_odd, frames_even = by_parity(odd, frames_raw, 4, 1)
    frames_even = paired(frames_even, "rows", 0)
    frames_odd = paired(frames_odd, "rows", 1)
    own_odd, own_even = by_parity(odd, reference, rows // 2, 0)
    from_even = paired(own_even, "rows", 0)
    from_odd = paired(own_odd, "rows", 1)
    inverse, stack, power = pl.pallas_call(
        smooth_kernel,
        out_shape=(
            struct((count, rows, columns)),
            jax.ShapeDtypeStruct((2 * depth, ring * lanes), bf16),
            struct((8 * count, lanes)),
        ),
        in_specs=[vmem] * 3,
        out_specs=(vmem,) * 3,
        scratch_shapes=[
            pltpu.VMEM((count, tiles, rows + 16, lanes), f32),
            pltpu.VMEM((count, tiles + 2, rows, lanes), f32),
            pltpu.VMEM((ring + 2, count * rows, lanes), f32),
        ],
        compiler_params=params,
        name="smooth",
    )(frames_raw, frames_odd, frames_even)
    clean, part = pl.pallas_call(
        match_kernel,
        out_shape=(struct((tiles + 2, wide, lanes)), struct((8 * count + 8, lanes))),
        in_specs=[smem] + [vmem] * 6,
        out_specs=(vmem, vmem),
        scratch_shapes=[
            pltpu.VMEM((tiles, rows + 16, lanes), f32),
            pltpu.VMEM((tiles + 2, wide, lanes), f32),
            pltpu.VMEM((ring + 2, wide, lanes), f32),
            pltpu.VMEM((4 * slot, ring * lanes), bf16),
        ],
        compiler_params=params,
        name="match",
    )(search_base, own_odd, own_even, from_odd, from_even, stack, power)
    parts = total_over(part, "rows")
    spread = pl.pallas_call(
        spread_kernel,
        out_shape=jax.ShapeDtypeStruct((2 * 8 * slot, columns), bf16),
        in_specs=[smem, vmem],
        out_specs=vmem,
        compiler_params=params,
        name="spread",
    )(search_base, clean)
    pressure, moments, part = pl.pallas_call(
        pressure_kernel,
        out_shape=(struct((count, rows, columns)), struct((2, rows, columns)), struct((8, lanes))),
        in_specs=[smem] + [vmem] * 3,
        out_specs=(vmem, vmem, vmem),
        compiler_params=params,
        name="pressure",
    )(search_base, parts, spread, inverse)
    whole = total_over(moments, "frames")
    spatial = jnp.sum(total_over(part, "rows"), axis=1)
    cell_count = rows * columns * lax.axis_size("rows")
    frame_mean = spatial[:count] / cell_count
    frame_rms = jnp.sqrt(spatial[count : 2 * count] / cell_count - frame_mean * frame_mean)
    total_frames = count * lax.axis_size("frames")
    time_mean = whole[0] / total_frames
    time_rms = jnp.sqrt(jnp.maximum(whole[1] / total_frames - time_mean * time_mean, 0.0))
    return (pressure, frame_mean, frame_rms, time_mean, time_rms)


def solution(mesh):
    placed = (P("frames", "rows", None), P("frames", "rows", None), P("rows"), P("frames", None))
    return jax.shard_map(
        shards,
        mesh=mesh,
        in_specs=placed,
        out_specs=(
            P("frames", "rows", None),
            P("frames"),
            P("frames"),
            P("rows", None),
            P("rows", None),
        ),
        check_vma=False,
    )
```

time: 66.7 us -> 56.4 us (0.85)
  blocking collectives: 20.6 us -> 0 us
  waiting for transfers between devices: 10.3 us -> 15.9 us
  starting transfers between devices: 18.3 us -> 21.7 us
  local copies, waits for them, and re-layouts: 0.01 us -> 1.69 us
  Pallas kernels: 13.2 us -> 11.7 us
  other arithmetic: 2.7 us -> 3.77 us
    all_gather x1 -> x0, blocking collectives: 20.6 us -> none  [shards(): spatial = jnp.sum(lax.all_gather(part[0], 'rows'), axis=0)]
    ppermute x5 -> x9, waiting for transfers between devices: 6.09 us -> 11.9 us  [total_over(): lax.ppermute(value, axis, [(i, i ^ step) for i in range(size)])]
    ppermute x5 -> x9, starting transfers between devices: 13.2 us -> 17.1 us  [total_over(): lax.ppermute(value, axis, [(i, i ^ step) for i in range(size)])]
    pallas_call x1 -> x2, Pallas kernels: 1.83 us -> 4.69 us  [the longest x1 2.84 us: shards(): pl.pallas_call(smooth_kernel, out_shape=(struct((count, rows, columns)),...]
    pallas_call x1, Pallas kernels: 5.87 us -> 3.22 us  [shards(): pl.pallas_call(pressure_kernel, out_shape=(struct((count, rows, columns))...]
    pallas_call x1, Pallas kernels: 5.51 us -> 3.82 us  [shards(): pl.pallas_call(match_kernel, out_shape=(struct((tiles + 2, wide, lanes)),...]
    unnamed x5 -> x4, local copies, waits for them, and re-layouts: 0.01 us -> 1.69 us
    select_n x2 -> x1, other arithmetic: 0.03 us -> 0.98 us  [from_owner(): return jnp.where(mine, shard, paired(shard, axis, 0))]
  transfers between devices with their start and end apart: 11 -> 14, of which waited for: 6 -> 8; matrix products, arithmetic and copies ran while one was open for 1% -> 5% of each run, Pallas kernels for 3% -> 8%
where the time goes in v2:
time: 56.4 us; the launch traced here: 56.2 us
  starting transfers between devices  21.7 us (38%)
  waiting for transfers between devices  15.9 us (28%)
  Pallas kernels  11.7 us (21%)
  other arithmetic  3.77 us (7%)
  local copies, waits for them, and re-layouts  1.69 us (3%)
  between operations  1.43 us (3%)
    ppermute x9, starting transfers between devices, total_over(): lax.ppermute(value, axis, [(i, i ^ step) for i in range(size)])  17.1 us
    ppermute x9, waiting for transfers between devices, total_over(): lax.ppermute(value, axis, [(i, i ^ step) for i in range(size)])  11.9 us
    ppermute x5, starting transfers between devices, paired(): return lax.ppermute(value, axis, pairs + [(j, i) for i, j in pairs])  4.51 us
    ppermute x5, waiting for transfers between devices, paired(): return lax.ppermute(value, axis, pairs + [(j, i) for i, j in pairs])  4.04 us
    pallas_call x1, Pallas kernels, shards(): pl.pallas_call(match_kernel, out_shape=(struct((tiles + 2, wide, lanes)),...  3.82 us
    pallas_call x1, Pallas kernels, shards(): pl.pallas_call(pressure_kernel, out_shape=(struct((count, rows, columns))...  3.22 us
    pallas_call x1, Pallas kernels, shards(): pl.pallas_call(smooth_kernel, out_shape=(struct((count, rows, columns)),...  2.84 us
    pallas_call x1, Pallas kernels, shards(): pl.pallas_call(spread_kernel, out_shape=jax.ShapeDtypeStruct((2 * 8 * slo...  1.85 us
  transfers between devices with their start and end apart: 14, of which 8 were waited for; matrix products, arithmetic and copies ran while one was open for 5% of the time, Pallas kernels for 8%

profile of v2, /device:TPU:0, one launch (start us, length us, event | category | flops | bytes accessed | tf_op | source)
XLA Modules:
  0.0 56.2 jit_solution(4054967434766836715)
XLA Ops:
  0.6 3.0 %collective-permute-start = (f32[16,4096]{1,0:T(8,128)}, f32[16,4096]{1,0:T(8,128)S(1)}, u32[]{:S(2)}, u32[]{:S(2)}) collective-permute-start(f32[16,4096]{1,0:T(8,128)} %bitcast.15), channel_id=1, source_target_pairs={{0,1},{1,0},{2,3},{3,2},{4,5},{5,4},{6,7},{7,6},{8,9},{9,8},{10,11... | collective-permute-start | bytes 786440 | tf_op jit(solution)/shard_map/ppermute | solution.py:324
  3.7 1.1 %slice_select_fusion.2 = (f32[2,4,4096]{2,1,0:T(4,128)S(1)}, f32[2,4,4096]{2,1,0:T(4,128)S(1)}) fusion(f32[2,16,4096]{2,1,0:T(8,128)} %frames.1, pred[]{:T(512)S(6)} %eq.8), kind=kLoop, calls=%fused_computation.10 | loop fusion | flops 65536 | bytes 524289 | tf_op jit(solution)/shard_map/jit(_where)/select_n | solution.py:331
  6.2 4.0 %collective-permute-done = f32[16,4096]{1,0:T(8,128)S(1)} collective-permute-done((f32[16,4096]{1,0:T(8,128)}, f32[16,4096]{1,0:T(8,128)S(1)}, u32[]{:S(2)}, u32[]{:S(2)}) %collective-permute-start) | collective-permute-done | bytes 262176 | tf_op jit(solution)/shard_map/ppermute | solution.py:324
  10.2 1.0 %broadcast_select_fusion = f32[16,4096]{1,0:T(8,128)S(1)} fusion(f32[16,4096]{1,0:T(8,128)S(1)} %collective-permute-done, pred[]{:T(512)S(6)} %eq.9, f32[1,16,4096]{2,1,0:T(8,128)} %param.5), kind=kLoop, calls=%fused_computation.7 | loop fusion | flops 65536 | bytes 786433 | tf_op jit(solution)/shard_map/jit(_where)/select_n | solution.py:337
  12.0 1.0 %copy-done = f32[2,16,4096]{2,1,0:T(8,128)S(1)} copy-done((f32[2,16,4096]{2,1,0:T(8,128)S(1)}, f32[2,16,4096]{2,1,0:T(8,128)}, u32[]{:S(2)}) %copy-start) | copy-done | bytes 524312
  13.0 2.8 %smooth.1 = (f32[2,16,4096]{2,1,0:T(8,128)S(1)}, bf16[448,4352]{1,0:T(8,128)(2,1)S(1)}, f32[16,128]{1,0:T(8,128)S(1)}) custom-call(f32[2,16,4096]{2,1,0:T(8,128)S(1)} %copy-done, f32[2,4,4096]{2,1,0:T(4,128)S(1)} %collective-permute-done.3.from_odd, f32[2,4,4096]{2,1,0:T(4,128)S(1)} %collective-permute-done.4.from_even), custom_call_target="tpu_custom_call" | custom-call | tf_op jit(solution)/shard_map/smooth/pallas_call | solution.py:369
  16.5 3.8 %match.1 = (f32[34,24,128]{2,1,0:T(8,128)S(1)}, f32[24,128]{1,0:T(8,128)S(1)}) custom-call(s32[1,2]{1,0:T(1,128)S(1)} %copy-done.1, f32[8,4096]{1,0:T(8,128)S(1)} %get-tuple-element.28.own_odd, f32[8,4096]{1,0:T(8,128)S(1)} %get-tuple-element.27.own_even, f32[8,4096]{1,0:T(8,128)S(1)} %collective-permute-done.1.from_odd, ...), custom_call_target="tpu_custom_call" | custom-call | tf_op jit(solution)/shard_map/match/pallas_call | solution.py:386
  20.4 3.1 %collective-permute-start.5 = (f32[24,128]{1,0:T(8,128)S(1)}, f32[24,128]{1,0:T(8,128)S(1)}, u32[]{:S(2)}, u32[]{:S(2)}) collective-permute-start(f32[24,128]{1,0:T(8,128)S(1)} %get-tuple-element.15), channel_id=1, source_target_pairs={{0,2},{2,0},{4,6},{6,4},{8,10},{10,8},{12,14},{14,12},{16,18},{18,... | collective-permute-start | bytes 36872 | tf_op jit(solution)/shard_map/ppermute | solution.py:347
  24.3 1.7 %collective-permute-start.6 = (f32[24,128]{1,0:T(8,128)S(1)}, f32[24,128]{1,0:T(8,128)S(1)}, u32[]{:S(2)}, u32[]{:S(2)}) collective-permute-start(f32[24,128]{1,0:T(8,128)S(1)} %add.32), channel_id=1, source_target_pairs={{0,4},{2,6},{4,0},{6,2},{8,12},{10,14},{12,8},{14,10},{16,20},{18,... | collective-permute-start | bytes 36872 | tf_op jit(solution)/shard_map/ppermute | solution.py:347
  26.0 2.0 %collective-permute-done.6 = f32[24,128]{1,0:T(8,128)S(1)} collective-permute-done((f32[24,128]{1,0:T(8,128)S(1)}, f32[24,128]{1,0:T(8,128)S(1)}, u32[]{:S(2)}, u32[]{:S(2)}) %collective-permute-start.6) | collective-permute-done | bytes 12320 | tf_op jit(solution)/shard_map/ppermute | solution.py:347
  28.0 2.3 %collective-permute-start.7 = (f32[24,128]{1,0:T(8,128)S(1)}, f32[24,128]{1,0:T(8,128)S(1)}, u32[]{:S(2)}, u32[]{:S(2)}) collective-permute-start(f32[24,128]{1,0:T(8,128)S(1)} %add.33), channel_id=1, source_target_pairs={{0,8},{2,10},{4,12},{6,14},{8,0},{10,2},{12,4},{14,6},{16,24},{18,... | collective-permute-start | bytes 36872 | tf_op jit(solution)/shard_map/ppermute | solution.py:347
  30.3 1.7 %collective-permute-done.7 = f32[24,128]{1,0:T(8,128)S(1)} collective-permute-done((f32[24,128]{1,0:T(8,128)S(1)}, f32[24,128]{1,0:T(8,128)S(1)}, u32[]{:S(2)}, u32[]{:S(2)}) %collective-permute-start.7) | collective-permute-done | bytes 12320 | tf_op jit(solution)/shard_map/ppermute | solution.py:347
  31.9 3.0 %collective-permute-start.8 = (f32[24,128]{1,0:T(8,128)S(1)}, f32[24,128]{1,0:T(8,128)S(1)}, u32[]{:S(2)}, u32[]{:S(2)}) collective-permute-start(f32[24,128]{1,0:T(8,128)S(1)} %add.34), channel_id=1, source_target_pairs={{0,16},{2,18},{4,20},{6,22},{8,24},{10,26},{12,28},{14,30},{16,0},... | collective-permute-start | bytes 36872 | tf_op jit(solution)/shard_map/ppermute | solution.py:347
  35.0 1.9 %spread.1 = bf16[512,4096]{1,0:T(8,128)(2,1)S(1)} custom-call(s32[1,2]{1,0:T(1,128)S(1)} %copy-done.1, f32[34,24,128]{2,1,0:T(8,128)S(1)} %get-tuple-element.16.clean), custom_call_target="tpu_custom_call" | custom-call | tf_op jit(solution)/shard_map/spread/pallas_call | solution.py:401
  36.9 3.2 %pressure.1 = (f32[2,16,4096]{2,1,0:T(8,128)}, f32[2,16,4096]{2,1,0:T(8,128)S(1)}, f32[8,128]{1,0:T(8,128)S(1)}) custom-call(s32[1,2]{1,0:T(1,128)S(1)} %copy-done.1, f32[24,128]{1,0:T(8,128)S(1)} %add.35.parts, bf16[512,4096]{1,0:T(8,128)(2,1)S(1)} %spread.1, f32[2,16,4096]{2,1,0:T(8,128)S(1)} %get-tuple-element.17.inverse), custom_call_target="tpu_custom_call" | custom-call | tf_op jit(solution)/shard_map/pressure/pallas_call | solution.py:409
  40.1 1.5 %collective-permute-start.13 = (f32[2,16,4096]{2,1,0:T(8,128)S(1)}, f32[2,16,4096]{2,1,0:T(8,128)S(1)}, u32[]{:S(2)}, u32[]{:S(2)}) collective-permute-start(f32[2,16,4096]{2,1,0:T(8,128)S(1)} %get-tuple-element.20), channel_id=1, source_target_pairs={{0,1},{1,0},{2,3},{3,2},{4,5},{5,4},{6,7},{7,6},{8,9},{9,8},{10,11... | collective-permute-start | bytes 1572872 | tf_op jit(solution)/shard_map/ppermute | solution.py:347
  41.6 1.2 %collective-permute-done.9 = f32[8,128]{1,0:T(8,128)S(1)} collective-permute-done((f32[8,128]{1,0:T(8,128)S(1)}, f32[8,128]{1,0:T(8,128)S(1)}, u32[]{:S(2)}, u32[]{:S(2)}) %collective-permute-start.9) | collective-permute-done | bytes 4128 | tf_op jit(solution)/shard_map/ppermute | solution.py:347
  42.8 1.1 %collective-permute-start.10 = (f32[8,128]{1,0:T(8,128)S(1)}, f32[8,128]{1,0:T(8,128)S(1)}, u32[]{:S(2)}, u32[]{:S(2)}) collective-permute-start(f32[8,128]{1,0:T(8,128)S(1)} %add.36), channel_id=1, source_target_pairs={{0,4},{2,6},{4,0},{6,2},{8,12},{10,14},{12,8},{14,10},{16,20},{18,... | collective-permute-start | bytes 12296 | tf_op jit(solution)/shard_map/ppermute | solution.py:347
  43.9 2.5 %collective-permute-done.10 = f32[8,128]{1,0:T(8,128)S(1)} collective-permute-done((f32[8,128]{1,0:T(8,128)S(1)}, f32[8,128]{1,0:T(8,128)S(1)}, u32[]{:S(2)}, u32[]{:S(2)}) %collective-permute-start.10) | collective-permute-done | bytes 4128 | tf_op jit(solution)/shard_map/ppermute | solution.py:347
  46.4 1.7 %collective-permute-start.11 = (f32[8,128]{1,0:T(8,128)S(1)}, f32[8,128]{1,0:T(8,128)S(1)}, u32[]{:S(2)}, u32[]{:S(2)}) collective-permute-start(f32[8,128]{1,0:T(8,128)S(1)} %add.37), channel_id=1, source_target_pairs={{0,8},{2,10},{4,12},{6,14},{8,0},{10,2},{12,4},{14,6},{16,24},{18,... | collective-permute-start | bytes 12296 | tf_op jit(solution)/shard_map/ppermute | solution.py:347
  48.1 1.9 %collective-permute-done.11 = f32[8,128]{1,0:T(8,128)S(1)} collective-permute-done((f32[8,128]{1,0:T(8,128)S(1)}, f32[8,128]{1,0:T(8,128)S(1)}, u32[]{:S(2)}, u32[]{:S(2)}) %collective-permute-start.11) | collective-permute-done | bytes 4128 | tf_op jit(solution)/shard_map/ppermute | solution.py:347
  50.0 2.7 %collective-permute-start.12 = (f32[8,128]{1,0:T(8,128)S(1)}, f32[8,128]{1,0:T(8,128)S(1)}, u32[]{:S(2)}, u32[]{:S(2)}) collective-permute-start(f32[8,128]{1,0:T(8,128)S(1)} %add.38), channel_id=1, source_target_pairs={{0,16},{2,18},{4,20},{6,22},{8,24},{10,26},{12,28},{14,30},{16,0},... | collective-permute-start | bytes 12296 | tf_op jit(solution)/shard_map/ppermute | solution.py:347
  52.7 1.8 %collective-permute-done.12 = f32[8,128]{1,0:T(8,128)S(1)} collective-permute-done((f32[8,128]{1,0:T(8,128)S(1)}, f32[8,128]{1,0:T(8,128)S(1)}, u32[]{:S(2)}, u32[]{:S(2)}) %collective-permute-start.12) | collective-permute-done | bytes 4128 | tf_op jit(solution)/shard_map/ppermute | solution.py:347
  55.3 0.9 %fusion.3 = (f32[16,4096]{1,0:T(8,128)}, f32[16,4096]{1,0:T(8,128)}) fusion(f32[2,16,4096]{2,1,0:T(8,128)S(1)} %add.40), kind=kLoop, calls=%fused_computation.4 | loop fusion | flops 327680 | bytes 1048576 | tf_op jit(solution)/shard_map/sqrt | solution.py:424
  (26 shorter events, 3.8 us)
Async XLA Ops:
  0.6 9.6 %collective-permute-start = (f32[16,4096]{1,0:T(8,128)}, f32[16,4096]{1,0:T(8,128)S(1)}, u32[]{:S(2)}, u32[]{:S(2)}) collective-permute-start(f32[16,4096]{1,0:T(8,128)} %bitcast.15), channel_id=1, source_target_pairs={{0,1},{1,0},{2,3},{3,2},{4,5},{5,4},{6,7},{7,6},{8,9},{9,8},{10,11... | collective-permute-start | bytes 786440 | tf_op jit(solution)/shard_map/ppermute | solution.py:324
  4.7 7.2 %collective-permute-start.4 = (f32[2,4,4096]{2,1,0:T(4,128)S(1)}, f32[2,4,4096]{2,1,0:T(4,128)S(1)}, u32[]{:S(2)}, u32[]{:S(2)}) collective-permute-start(f32[2,4,4096]{2,1,0:T(4,128)S(1)} %get-tuple-element.25), channel_id=1, source_target_pairs={{0,2},{4,6},{8,10},{12,14},{16,18},{20,22},{24,26},{28,30},{2,0},{... | collective-permute-start | bytes 393224 | tf_op jit(solution)/shard_map/ppermute | solution.py:324
  4.8 7.1 %collective-permute-start.3 = (f32[2,4,4096]{2,1,0:T(4,128)S(1)}, f32[2,4,4096]{2,1,0:T(4,128)S(1)}, u32[]{:S(2)}, u32[]{:S(2)}) collective-permute-start(f32[2,4,4096]{2,1,0:T(4,128)S(1)} %get-tuple-element.26), channel_id=1, source_target_pairs={{2,4},{6,8},{10,12},{14,16},{18,20},{22,24},{26,28},{4,2},{8,6},{1... | collective-permute-start | bytes 393224 | tf_op jit(solution)/shard_map/ppermute | solution.py:324
  11.2 4.7 %collective-permute-start.2 = (f32[8,4096]{1,0:T(8,128)S(1)}, f32[8,4096]{1,0:T(8,128)S(1)}, u32[]{:S(2)}, u32[]{:S(2)}) collective-permute-start(f32[8,4096]{1,0:T(8,128)S(1)} %get-tuple-element.27.own_even), channel_id=1, source_target_pairs={{0,2},{4,6},{8,10},{12,14},{16,18},{20,22},{24,26},{28,30},{2,0},{... | collective-permute-start | bytes 393224 | tf_op jit(solution)/shard_map/ppermute | solution.py:324
  11.3 4.6 %collective-permute-start.1 = (f32[8,4096]{1,0:T(8,128)S(1)}, f32[8,4096]{1,0:T(8,128)S(1)}, u32[]{:S(2)}, u32[]{:S(2)}) collective-permute-start(f32[8,4096]{1,0:T(8,128)S(1)} %get-tuple-element.28.own_odd), channel_id=1, source_target_pairs={{2,4},{6,8},{10,12},{14,16},{18,20},{22,24},{26,28},{4,2},{8,6},{1... | collective-permute-start | bytes 393224 | tf_op jit(solution)/shard_map/ppermute | solution.py:324
  12.0 1.0 %copy-start = (f32[2,16,4096]{2,1,0:T(8,128)S(1)}, f32[2,16,4096]{2,1,0:T(8,128)}, u32[]{:S(2)}) copy-start(f32[2,16,4096]{2,1,0:T(8,128)} %frames.1) | copy-start | bytes 1572868
  15.9 0.7 %copy-start.1 = (s32[1,2]{1,0:T(1,128)S(1)}, s32[1,2]{1,0:T(1,128)}, u32[]{:S(2)}) copy-start(s32[1,2]{1,0:T(1,128)} %base.5) | copy-start | bytes 28
  20.4 3.9 %collective-permute-start.5 = (f32[24,128]{1,0:T(8,128)S(1)}, f32[24,128]{1,0:T(8,128)S(1)}, u32[]{:S(2)}, u32[]{:S(2)}) collective-permute-start(f32[24,128]{1,0:T(8,128)S(1)} %get-tuple-element.15), channel_id=1, source_target_pairs={{0,2},{2,0},{4,6},{6,4},{8,10},{10,8},{12,14},{14,12},{16,18},{18,... | collective-permute-start | bytes 36872 | tf_op jit(solution)/shard_map/ppermute | solution.py:347
  24.3 3.7 %collective-permute-start.6 = (f32[24,128]{1,0:T(8,128)S(1)}, f32[24,128]{1,0:T(8,128)S(1)}, u32[]{:S(2)}, u32[]{:S(2)}) collective-permute-start(f32[24,128]{1,0:T(8,128)S(1)} %add.32), channel_id=1, source_target_pairs={{0,4},{2,6},{4,0},{6,2},{8,12},{10,14},{12,8},{14,10},{16,20},{18,... | collective-permute-start | bytes 36872 | tf_op jit(solution)/shard_map/ppermute | solution.py:347
  28.0 4.0 %collective-permute-start.7 = (f32[24,128]{1,0:T(8,128)S(1)}, f32[24,128]{1,0:T(8,128)S(1)}, u32[]{:S(2)}, u32[]{:S(2)}) collective-permute-start(f32[24,128]{1,0:T(8,128)S(1)} %add.33), channel_id=1, source_target_pairs={{0,8},{2,10},{4,12},{6,14},{8,0},{10,2},{12,4},{14,6},{16,24},{18,... | collective-permute-start | bytes 36872 | tf_op jit(solution)/shard_map/ppermute | solution.py:347
  31.9 4.9 %collective-permute-start.8 = (f32[24,128]{1,0:T(8,128)S(1)}, f32[24,128]{1,0:T(8,128)S(1)}, u32[]{:S(2)}, u32[]{:S(2)}) collective-permute-start(f32[24,128]{1,0:T(8,128)S(1)} %add.34), channel_id=1, source_target_pairs={{0,16},{2,18},{4,20},{6,22},{8,24},{10,26},{12,28},{14,30},{16,0},... | collective-permute-start | bytes 36872 | tf_op jit(solution)/shard_map/ppermute | solution.py:347
  40.1 15.1 %collective-permute-start.13 = (f32[2,16,4096]{2,1,0:T(8,128)S(1)}, f32[2,16,4096]{2,1,0:T(8,128)S(1)}, u32[]{:S(2)}, u32[]{:S(2)}) collective-permute-start(f32[2,16,4096]{2,1,0:T(8,128)S(1)} %get-tuple-element.20), channel_id=1, source_target_pairs={{0,1},{1,0},{2,3},{3,2},{4,5},{5,4},{6,7},{7,6},{8,9},{9,8},{10,11... | collective-permute-start | bytes 1572872 | tf_op jit(solution)/shard_map/ppermute | solution.py:347
  41.6 1.2 %collective-permute-start.9 = (f32[8,128]{1,0:T(8,128)S(1)}, f32[8,128]{1,0:T(8,128)S(1)}, u32[]{:S(2)}, u32[]{:S(2)}) collective-permute-start(f32[8,128]{1,0:T(8,128)S(1)} %get-tuple-element.19), channel_id=1, source_target_pairs={{0,2},{2,0},{4,6},{6,4},{8,10},{10,8},{12,14},{14,12},{16,18},{18,... | collective-permute-start | bytes 12296 | tf_op jit(solution)/shard_map/ppermute | solution.py:347
  42.8 3.6 %collective-permute-start.10 = (f32[8,128]{1,0:T(8,128)S(1)}, f32[8,128]{1,0:T(8,128)S(1)}, u32[]{:S(2)}, u32[]{:S(2)}) collective-permute-start(f32[8,128]{1,0:T(8,128)S(1)} %add.36), channel_id=1, source_target_pairs={{0,4},{2,6},{4,0},{6,2},{8,12},{10,14},{12,8},{14,10},{16,20},{18,... | collective-permute-start | bytes 12296 | tf_op jit(solution)/shard_map/ppermute | solution.py:347
  46.4 3.6 %collective-permute-start.11 = (f32[8,128]{1,0:T(8,128)S(1)}, f32[8,128]{1,0:T(8,128)S(1)}, u32[]{:S(2)}, u32[]{:S(2)}) collective-permute-start(f32[8,128]{1,0:T(8,128)S(1)} %add.37), channel_id=1, source_target_pairs={{0,8},{2,10},{4,12},{6,14},{8,0},{10,2},{12,4},{14,6},{16,24},{18,... | collective-permute-start | bytes 12296 | tf_op jit(solution)/shard_map/ppermute | solution.py:347
  50.0 4.5 %collective-permute-start.12 = (f32[8,128]{1,0:T(8,128)S(1)}, f32[8,128]{1,0:T(8,128)S(1)}, u32[]{:S(2)}, u32[]{:S(2)}) collective-permute-start(f32[8,128]{1,0:T(8,128)S(1)} %add.38), channel_id=1, source_target_pairs={{0,16},{2,18},{4,20},{6,22},{8,24},{10,26},{12,28},{14,30},{16,0},... | collective-permute-start | bytes 12296 | tf_op jit(solution)/shard_map/ppermute | solution.py:347

commit v3 on v2

--- a/solution.py
+++ b/solution.py
@@ -71,23 +71,67 @@
 
 def by_row_shift(value, rows, direction):
     place = lax.broadcasted_iota(jnp.int32, value.shape, 0) % rows
-    step = 1
-    while step < rows:
-        turned = pltpu.roll(value, step if direction > 0 else lanes - step, 1)
-        value = jnp.where((place & step) != 0, turned, value)
-        step *= 2
+    unit = 1
+    while unit < rows:
+        digit = (place // unit) % 4
+        result = value
+        for times in range(1, 4):
+            amount = times * unit
+            turned = pltpu.roll(value, amount if direction > 0 else lanes - amount, 1)
+            result = jnp.where(digit == times, turned, result)
+        value = result
+        unit *= 4
     return value
 
 
-def smooth_kernel(frames, from_odd, from_even, inverse, stack, power, rows_in, half, fine):
+def cut_kernel(
+    base, frames, wind, raw, across, frames_odd, frames_even, wind_odd, wind_even, offsets, wind_here, arrived
+):
+    count, rows, columns = raw.shape
+    tiles = columns // lanes
+    odd = lax.axis_index("rows") % 2 == 1
+    copies = [pltpu.make_async_copy(frames.at[f], raw.at[f], arrived.at[f]) for f in range(count)]
+    copies.append(pltpu.make_async_copy(wind.at[0], wind_here, arrived.at[count]))
+    copies.append(pltpu.make_async_copy(base, offsets, arrived.at[count + 1]))
+    for copy in copies:
+        copy.start()
+
+    for f in range(count):
+        copies[f].wait()
+
+        def step(t, carry):
+            at = tile_of(t)
+            before = jnp.where(t > 0, raw[f, :, tile_of(jnp.maximum(t - 1, 0))], 0.0)
+            after = jnp.where(t < tiles - 1, raw[f, :, tile_of(jnp.minimum(t + 1, tiles - 1))], 0.0)
+            value = horizontal(before, raw[f, :, at], after)
+            across[f, t] = value
+            low = value[0:4]
+            high = value[rows - 4 : rows]
+            frames_odd[f, :, at] = jnp.where(odd, high, low)
+            frames_even[f, :, at] = jnp.where(odd, low, high)
+            return carry
+
+        by_tiles(step, tiles, 16)
+
+    for copy in copies[count:]:
+        copy.wait()
+
+    def wind_step(t, carry):
+        at = tile_of(t)
+        low = wind_here[0 : rows // 2, at]
+        high = wind_here[rows // 2 : rows, at]
+        wind_odd[:, at] = jnp.where(odd, high, low)
+        wind_even[:, at] = jnp.where(odd, low, high)
+        return carry
+
+    by_tiles(wind_step, tiles, 16)
+
+
+def smooth_kernel(frames, across, from_odd, from_even, inverse, stack, power, rows_in, fine):
     count, rows, columns = frames.shape
     tiles = columns // lanes
     ring = tiles + 2
     odd = lax.axis_index("rows") % 2 == 1
-    zero = jnp.zeros((rows, lanes), jnp.float32)
-    for f in range(count):
-        half[f, 0] = zero
-        half[f, tiles + 1] = zero
     blank = jnp.zeros((count * rows, lanes), jnp.float32)
     fine[0] = blank
     fine[tiles + 1] = blank
@@ -98,19 +142,14 @@
             outer = from_odd[f, :, tile_of(t)]
             inner = from_even[f, :, tile_of(t)]
             rows_in[f, t, 4:8, :] = jnp.where(odd, inner, outer)
-            rows_in[f, t, 8 : 8 + rows, :] = frames[f, :, tile_of(t)]
+            rows_in[f, t, 8 : 8 + rows, :] = across[f, t]
             rows_in[f, t, 8 + rows : 12 + rows, :] = jnp.where(odd, outer, inner)
         return carry
 
-    def vertical_step(t, carry):
-        for f in range(count):
-            half[f, t + 1] = vertical(lambda s: rows_in[f, t, pl.ds(4 + s, rows), :])
-        return carry
-
-    def horizontal_step(t, totals):
+    def vertical_step(t, totals):
         result = []
         for f in range(count):
-            smooth = horizontal(half[f, t], half[f, t + 1], half[f, t + 2])
+            smooth = vertical(lambda s: rows_in[f, t, pl.ds(4 + s, rows), :])
             inverse[f, :, tile_of(t)] = 1.0 / smooth
             detail = frames[f, :, tile_of(t)] - smooth
             fine[t + 1, f * rows : (f + 1) * rows, :] = detail
@@ -127,8 +166,7 @@
         return carry
 
     by_tiles(load_step, tiles, 8)
-    by_tiles(vertical_step, tiles, 8)
-    powers = by_tiles(horizontal_step, tiles, 8, (jnp.zeros((8, lanes), jnp.float32),) * count)
+    powers = by_tiles(vertical_step, tiles, 8, (jnp.zeros((8, lanes), jnp.float32),) * count)
     for f in range(count):
         power[f * 8 : f * 8 + 8, :] = powers[f]
     fine[tiles + 3] = fine[1]
@@ -213,14 +251,15 @@
     )
     size = reach * count * rows
     product = product[:size] + product[size:]
-    product = product + pltpu.roll(product, lanes - slot, 1)
     product = by_row_shift(product, rows, -1)
     part[...] = jnp.zeros(part.shape, jnp.float32)
     for j in range(reach):
         for f in range(count):
             start = (j * count + f) * rows
             part[f * 8 + j : f * 8 + j + 1, :] = jnp.sum(product[start : start + rows], axis=0, keepdims=True)
-    lags = pltpu.roll(part[0 : 8 * count, :], lax.rem(lanes - 1 - base[0, 0], lanes), 1)
+    lags = part[0 : 8 * count, :]
+    back = lanes - 1 - base[0, 0]
+    lags = pltpu.roll(lags, lax.rem(back, lanes), 1) + pltpu.roll(lags, lax.rem(back + lanes - slot, lanes), 1)
     part[0 : 8 * count, :] = jnp.where(lane_of(lags.shape) < reach, lags, 0.0)
     start = 8 * count
     for f in range(count):
@@ -265,14 +304,14 @@
 
 def banded(weights, rows, first_row):
     across = lax.broadcasted_iota(jnp.int32, weights.shape, 0)
-    spaced = weights
-    for step in (1, 2):
-        spaced = jnp.where((across & step) != 0, pltpu.roll(spaced, step * slot, 1), spaced)
+    spaced = jnp.zeros_like(weights)
+    for times in range(4):
+        turned = pltpu.roll(weights, first_row + times * slot, 1)
+        spaced = jnp.where(across % 4 == times, turned, spaced)
     tiles = []
     for member in (across < 4, across >= 4):
         line = jnp.sum(jnp.where(member, spaced, 0.0), axis=0, keepdims=True)
-        block = by_row_shift(jnp.broadcast_to(line, (rows, lanes)), rows, 1)
-        tiles.append(pltpu.roll(block, first_row, 1))
+        tiles.append(by_row_shift(jnp.broadcast_to(line, (rows, lanes)), rows, 1))
     return jnp.concatenate(tiles, axis=1)
 
 
@@ -312,7 +351,7 @@
         moments[1, :, where] = second
         return tuple(totals)
 
-    totals = by_tiles(step, columns // chunk, 4, (zero,) * (2 * count))
+    totals = by_tiles(step, columns // chunk, 8, (zero,) * (2 * count))
     part[...] = jnp.zeros(part.shape, jnp.float32)
     for k in range(2 * count):
         part[k : k + 1, :] = jnp.sum(totals[k], axis=0, keepdims=True)
@@ -331,11 +370,26 @@
     return jnp.where(odd, high, low), jnp.where(odd, low, high)
 
 
-def from_owner(shard, axis, root):
+def from_owner(shard, cut, odd, axis, root):
     mine = lax.axis_index(axis) == root
     if lax.axis_size(axis) == 2:
-        return jnp.where(mine, shard, paired(shard, axis, 0))
-    return lax.psum(jnp.where(mine, shard, jnp.zeros_like(shard)), axis)
+        received = by_parity(odd, paired(shard, axis, 0), shard.shape[0] // 2, 0)
+        return [jnp.where(mine, own, other) for own, other in zip(cut, received)]
+    whole = lax.psum(jnp.where(mine, shard, jnp.zeros_like(shard)), axis)
+    return by_parity(odd, whole, shard.shape[0] // 2, 0)
+
+
+def total_over_rows(value, odd):
+    size = lax.axis_size("rows")
+    if size & (size - 1) or size < 2:
+        return lax.psum(value, "rows")
+    value = value + lax.ppermute(value, "rows", [(i, i + 1) for i in range(0, size, 2)])
+    step = 2
+    while step < size:
+        value = value + lax.ppermute(value, "rows", [(i, i ^ step) for i in range(1, size, 2)])
+        step *= 2
+    back = lax.ppermute(value, "rows", [(i, i - 1) for i in range(1, size, 2)])
+    return jnp.where(odd, value, back)
 
 
 def total_over(value, axis):
@@ -359,11 +413,28 @@
     bf16 = jnp.bfloat16
     struct = functools.partial(jax.ShapeDtypeStruct, dtype=f32)
     odd = lax.axis_index("rows") % 2 == 1
-    reference = from_owner(wind_off[0], "frames", run_owner[0])
-    frames_odd, frames_even = by_parity(odd, frames_raw, 4, 1)
+    edge = struct((count, 4, columns))
+    side = struct((rows // 2, columns))
+    raw, across, frames_odd, frames_even, wind_odd, wind_even, offsets = pl.pallas_call(
+        cut_kernel,
+        out_shape=(
+            struct((count, rows, columns)),
+            struct((count, tiles, rows, lanes)),
+            edge,
+            edge,
+            side,
+            side,
+            jax.ShapeDtypeStruct((1, 2), jnp.int32),
+        ),
+        in_specs=[pl.BlockSpec(memory_space=pl.ANY)] * 3,
+        out_specs=(vmem,) * 6 + (smem,),
+        scratch_shapes=[pltpu.VMEM((rows, columns), f32), pltpu.SemaphoreType.DMA((count + 2,))],
+        compiler_params=params,
+        name="cut",
+    )(search_base, frames_raw, wind_off)
+    own_odd, own_even = from_owner(wind_off[0], (wind_odd, wind_even), odd, "frames", run_owner[0])
+    frames_odd = paired(frames_odd, "rows", 1)
     frames_even = paired(frames_even, "rows", 0)
-    frames_odd = paired(frames_odd, "rows", 1)
-    own_odd, own_even = by_parity(odd, reference, rows // 2, 0)
     from_even = paired(own_even, "rows", 0)
     from_odd = paired(own_odd, "rows", 1)
     inverse, stack, power = pl.pallas_call(
@@ -373,16 +444,15 @@
             jax.ShapeDtypeStruct((2 * depth, ring * lanes), bf16),
             struct((8 * count, lanes)),
         ),
-        in_specs=[vmem] * 3,
+        in_specs=[vmem] * 4,
         out_specs=(vmem,) * 3,
         scratch_shapes=[
             pltpu.VMEM((count, tiles, rows + 16, lanes), f32),
-            pltpu.VMEM((count, tiles + 2, rows, lanes), f32),
             pltpu.VMEM((ring + 2, count * rows, lanes), f32),
         ],
         compiler_params=params,
         name="smooth",
-    )(frames_raw, frames_odd, frames_even)
+    )(raw, across, frames_odd, frames_even)
     clean, part = pl.pallas_call(
         match_kernel,
         out_shape=(struct((tiles + 2, wide, lanes)), struct((8 * count + 8, lanes))),
@@ -396,8 +466,8 @@
         ],
         compiler_params=params,
         name="match",
-    )(search_base, own_odd, own_even, from_odd, from_even, stack, power)
-    parts = total_over(part, "rows")
+    )(offsets, own_odd, own_even, from_odd, from_even, stack, power)
+    parts = total_over_rows(part, odd)
     spread = pl.pallas_call(
         spread_kernel,
         out_shape=jax.ShapeDtypeStruct((2 * 8 * slot, columns), bf16),
@@ -405,7 +475,7 @@
         out_specs=vmem,
         compiler_params=params,
         name="spread",
-    )(search_base, clean)
+    )(offsets, clean)
     pressure, moments, part = pl.pallas_call(
         pressure_kernel,
         out_shape=(struct((count, rows, columns)), struct((2, rows, columns)), struct((8, lanes))),
@@ -413,9 +483,9 @@
         out_specs=(vmem, vmem, vmem),
         compiler_params=params,
         name="pressure",
-    )(search_base, parts, spread, inverse)
+    )(offsets, parts, spread, inverse)
     whole = total_over(moments, "frames")
-    spatial = jnp.sum(total_over(part, "rows"), axis=1)
+    spatial = jnp.sum(total_over_rows(part, odd), axis=1)
     cell_count = rows * columns * lax.axis_size("rows")
     frame_mean = spatial[:count] / cell_count
     frame_rms = jnp.sqrt(spatial[count : 2 * count] / cell_count - frame_mean * frame_mean)

time: 56.4 us -> 69.7 us (1.24)
  waiting for transfers between devices: 15.9 us -> 27.7 us
  other arithmetic: 3.77 us -> 1.76 us
  starting transfers between devices: 21.7 us -> 23.7 us
  local copies, waits for them, and re-layouts: 1.69 us -> 2.65 us
    ppermute x0 -> x10, waiting for transfers between devices: none -> 27.7 us  [the longest x2 26 us: total_over_rows(): back = lax.ppermute(value, 'rows', [(i, i - 1) for i in range(1, size, 2)])]
    ppermute x9 -> x1, starting transfers between devices: 17.1 us -> 0.5 us  [total_over(): lax.ppermute(value, axis, [(i, i ^ step) for i in range(size)])]
    ppermute x0 -> x10, starting transfers between devices: none -> 15.8 us  [the longest x2 9.3 us: total_over_rows(): lax.ppermute(value, 'rows', [(i, i + 1) for i in range(0, size, 2)])]
    ppermute x9 -> x1, waiting for transfers between devices: 11.9 us -> 0.01 us  [total_over(): lax.ppermute(value, axis, [(i, i ^ step) for i in range(size)])]
    ppermute x5, waiting for transfers between devices: 4.04 us -> 0.01 us  [paired(): return lax.ppermute(value, axis, pairs + [(j, i) for i, j in pairs])]
    ppermute x5, starting transfers between devices: 4.51 us -> 7.36 us  [paired(): return lax.ppermute(value, axis, pairs + [(j, i) for i, j in pairs])]
    pallas_call x0 -> x1, Pallas kernels: none -> 2.14 us  [shards(): pl.pallas_call(cut_kernel, out_shape=(struct((count, rows, columns)), str...]
    select_n x3 -> x2, other arithmetic: 2.08 us -> 0.03 us  [the longest x1 0.03 us: from_owner(): return [jnp.where(mine, own, other) for own, other in zip(cut, received)]]
  transfers between devices with their start and end apart: 14 -> 16, of which waited for: 8 -> 4; matrix products, arithmetic and copies ran while one was open for 5% -> 1% of each run, Pallas kernels for 8% -> 8%
where the time goes in v3:
time: 69.7 us; the launch traced here: 69.3 us
  waiting for transfers between devices  27.7 us (40%)
  starting transfers between devices  23.7 us (34%)
  Pallas kernels  11.9 us (17%)
  local copies, waits for them, and re-layouts  2.65 us (4%)
  other arithmetic  1.76 us (3%)
  between operations  1.55 us (2%)
    ppermute x2, waiting for transfers between devices, total_over_rows(): back = lax.ppermute(value, 'rows', [(i, i - 1) for i in range(1, size, 2)])  26 us
    ppermute x2, starting transfers between devices, total_over_rows(): lax.ppermute(value, 'rows', [(i, i + 1) for i in range(0, size, 2)])  9.3 us
    ppermute x5, starting transfers between devices, paired(): return lax.ppermute(value, axis, pairs + [(j, i) for i, j in pairs])  7.36 us
    ppermute x6, starting transfers between devices, total_over_rows(): lax.ppermute(value, 'rows', [(i, i ^ step) for i in range(1, size, 2)])  3.95 us
    pallas_call x1, Pallas kernels, shards(): pl.pallas_call(match_kernel, out_shape=(struct((tiles + 2, wide, lanes)),...  3.67 us
    pallas_call x1, Pallas kernels, shards(): pl.pallas_call(pressure_kernel, out_shape=(struct((count, rows, columns))...  2.78 us
    unnamed x6, local copies, waits for them, and re-layouts  2.65 us
    ppermute x2, starting transfers between devices, total_over_rows(): back = lax.ppermute(value, 'rows', [(i, i - 1) for i in range(1, size, 2)])  2.58 us
  transfers between devices with their start and end apart: 16, of which 4 were waited for; matrix products, arithmetic and copies ran while one was open for 1% of the time, Pallas kernels for 8%

profile of v3, /device:TPU:0, one launch (start us, length us, event | category | flops | bytes accessed | tf_op | source)
XLA Modules:
  0.0 69.3 jit_solution(9428922802319277593)
XLA Ops:
  0.6 3.0 %collective-permute-start = (f32[16,4096]{1,0:T(8,128)}, f32[16,4096]{1,0:T(8,128)S(1)}, u32[]{:S(2)}, u32[]{:S(2)}) collective-permute-start(f32[16,4096]{1,0:T(8,128)} %bitcast.14), channel_id=1, source_target_pairs={{0,1},{1,0},{2,3},{3,2},{4,5},{5,4},{6,7},{7,6},{8,9},{9,8},{10,11... | collective-permute-start | bytes 786440 | tf_op jit(solution)/shard_map/ppermute | solution.py:363
  3.7 1.0 %copy-done = f32[2,16,4096]{2,1,0:T(8,128)S(1)} copy-done((f32[2,16,4096]{2,1,0:T(8,128)S(1)}, f32[2,16,4096]{2,1,0:T(8,128)}, u32[]{:S(2)}) %copy-start) | copy-done | bytes 524312
  4.7 0.9 %copy-done.1 = f32[1,16,4096]{2,1,0:T(8,128)S(1)} copy-done((f32[1,16,4096]{2,1,0:T(8,128)S(1)}, f32[1,16,4096]{2,1,0:T(8,128)}, u32[]{:S(2)}) %copy-start.1) | copy-done | bytes 262168
  6.3 2.1 %cut.1 = (f32[2,16,4096]{2,1,0:T(8,128)S(1)}, f32[2,32,16,128]{3,2,1,0:T(8,128)S(1)}, f32[2,4,4096]{2,1,0:T(4,128)S(1)}, f32[2,4,4096]{2,1,0:T(4,128)S(1)}, f32[...) custom-call(s32[1,2]{1,0:T(1,128)S(1)} %copy-done.2, f32[2,16,4096]{2,1,0:T(8,128)S(1)} %copy-done, ...), custom_call_target="tpu_custom_call" | custom-call | tf_op jit(solution)/shard_map/cut/pallas_call | solution.py:418
  8.5 0.7 collective-permute-start.3
  9.1 2.9 %collective-permute-start.4 = (f32[2,4,4096]{2,1,0:T(4,128)S(1)}, f32[2,4,4096]{2,1,0:T(4,128)S(1)}, u32[]{:S(2)}, u32[]{:S(2)}) collective-permute-start(f32[2,4,4096]{2,1,0:T(4,128)S(1)} %get-tuple-element.26), channel_id=1, source_target_pairs={{0,2},{4,6},{8,10},{12,14},{16,18},{20,22},{24,26},{28,30},{2,0},{... | collective-permute-start | bytes 393224 | tf_op jit(solution)/shard_map/ppermute | solution.py:363
  12.8 0.7 collective-permute-start.1
  13.5 1.5 %smooth.1 = (f32[2,16,4096]{2,1,0:T(8,128)S(1)}, bf16[448,4352]{1,0:T(8,128)(2,1)S(1)}, f32[16,128]{1,0:T(8,128)S(1)}) custom-call(f32[2,16,4096]{2,1,0:T(8,128)S(1)} %get-tuple-element.23.frames, f32[2,32,16,128]{3,2,1,0:T(8,128)S(1)} %get-tuple-element.24.across, f32[2,4,4096]{2,1,0:T(4,128)S(1)} %collective-permute-done.3.from_odd, ...), custom_call_target="tpu_custom_call" | custom-call | tf_op jit(solution)/shard_map/smooth/pallas_call | solution.py:440
  15.0 3.7 %match.1 = (f32[34,24,128]{2,1,0:T(8,128)S(1)}, f32[24,128]{1,0:T(8,128)S(1)}) custom-call(s32[1,2]{1,0:T(1,128)S(1)} %get-tuple-element.20.base, f32[8,4096]{1,0:T(8,128)S(1)} %get-tuple-element.40.own_odd, f32[8,4096]{1,0:T(8,128)S(1)} %get-tuple-element.39.own_even, f32[8,4096]{1,0:T(8,128)S(1)} %collective-permute-done.1.from_odd, ...), custom_call_target="tpu_custom_call" | custom-call | tf_op jit(solution)/shard_map/match/pallas_call | solution.py:456
  18.7 6.5 %collective-permute-start.5 = (f32[24,128]{1,0:T(8,128)S(1)}, f32[24,128]{1,0:T(8,128)S(1)}, u32[]{:S(2)}, u32[]{:S(2)}) collective-permute-start(f32[24,128]{1,0:T(8,128)S(1)} %get-tuple-element.29), channel_id=1, source_target_pairs={{0,2},{4,6},{8,10},{12,14},{16,18},{20,22},{24,26},{28,30},{1,3},{... | collective-permute-start | bytes 36872 | tf_op jit(solution)/shard_map/ppermute | solution.py:386
  25.2 0.8 %collective-permute-done.5 = f32[24,128]{1,0:T(8,128)S(1)} collective-permute-done((f32[24,128]{1,0:T(8,128)S(1)}, f32[24,128]{1,0:T(8,128)S(1)}, u32[]{:S(2)}, u32[]{:S(2)}) %collective-permute-start.5) | collective-permute-done | bytes 12320 | tf_op jit(solution)/shard_map/ppermute | solution.py:386
  26.7 0.7 collective-permute-start.7
  27.4 0.7 collective-permute-start.8
  28.1 1.3 %collective-permute-start.9 = (f32[24,128]{1,0:T(8,128)S(1)}, f32[24,128]{1,0:T(8,128)S(1)}, u32[]{:S(2)}, u32[]{:S(2)}) collective-permute-start(f32[24,128]{1,0:T(8,128)S(1)} %add.35), channel_id=1, source_target_pairs={{2,0},{6,4},{10,8},{14,12},{18,16},{22,20},{26,24},{30,28},{3,1},{... | collective-permute-start | bytes 36872 | tf_op jit(solution)/shard_map/ppermute | solution.py:391
  29.4 1.9 %spread.1 = bf16[512,4096]{1,0:T(8,128)(2,1)S(1)} custom-call(s32[1,2]{1,0:T(1,128)S(1)} %get-tuple-element.20.base, f32[34,24,128]{2,1,0:T(8,128)S(1)} %get-tuple-element.30.clean), custom_call_target="tpu_custom_call" | custom-call | tf_op jit(solution)/shard_map/spread/pallas_call | solution.py:471
  31.2 12.6 %collective-permute-done.9 = f32[24,128]{1,0:T(8,128)S(1)} collective-permute-done((f32[24,128]{1,0:T(8,128)S(1)}, f32[24,128]{1,0:T(8,128)S(1)}, u32[]{:S(2)}, u32[]{:S(2)}) %collective-permute-start.9) | collective-permute-done | bytes 12320 | tf_op jit(solution)/shard_map/ppermute | solution.py:391
  43.8 2.8 %pressure.1 = (f32[2,16,4096]{2,1,0:T(8,128)}, f32[2,16,4096]{2,1,0:T(8,128)S(1)}, f32[8,128]{1,0:T(8,128)S(1)}) custom-call(s32[1,2]{1,0:T(1,128)S(1)} %get-tuple-element.20.base, f32[24,128]{1,0:T(8,128)S(1)} %broadcast_select_fusion.parts, bf16[512,4096]{1,0:T(8,128)(2,1)S(1)} %spread.1, f32[2,16,4096]{2,1,0:T(8,128)S(1)} %get-tuple-element.31.inverse), custom_call_target="tpu_custom_call" | custom-call | tf_op jit(solution)/shard_map/pressure/pallas_call | solution.py:479
  47.1 2.8 %collective-permute-start.10 = (f32[8,128]{1,0:T(8,128)S(1)}, f32[8,128]{1,0:T(8,128)S(1)}, u32[]{:S(2)}, u32[]{:S(2)}) collective-permute-start(f32[8,128]{1,0:T(8,128)S(1)} %get-tuple-element.33), channel_id=1, source_target_pairs={{0,2},{4,6},{8,10},{12,14},{16,18},{20,22},{24,26},{28,30},{1,3},{... | collective-permute-start | bytes 12296 | tf_op jit(solution)/shard_map/ppermute | solution.py:386
  50.0 0.8 %collective-permute-done.10 = f32[8,128]{1,0:T(8,128)S(1)} collective-permute-done((f32[8,128]{1,0:T(8,128)S(1)}, f32[8,128]{1,0:T(8,128)S(1)}, u32[]{:S(2)}, u32[]{:S(2)}) %collective-permute-start.10) | collective-permute-done | bytes 4128 | tf_op jit(solution)/shard_map/ppermute | solution.py:386
  51.5 0.7 collective-permute-start.12
  52.2 0.7 collective-permute-start.13
  52.9 1.3 %collective-permute-start.14 = (f32[8,128]{1,0:T(8,128)S(1)}, f32[8,128]{1,0:T(8,128)S(1)}, u32[]{:S(2)}, u32[]{:S(2)}) collective-permute-start(f32[8,128]{1,0:T(8,128)S(1)} %add.39), channel_id=1, source_target_pairs={{2,0},{6,4},{10,8},{14,12},{18,16},{22,20},{26,24},{30,28},{3,1},{... | collective-permute-start | bytes 12296 | tf_op jit(solution)/shard_map/ppermute | solution.py:391
  54.2 13.4 %collective-permute-done.14 = f32[8,128]{1,0:T(8,128)S(1)} collective-permute-done((f32[8,128]{1,0:T(8,128)S(1)}, f32[8,128]{1,0:T(8,128)S(1)}, u32[]{:S(2)}, u32[]{:S(2)}) %collective-permute-start.14) | collective-permute-done | bytes 4128 | tf_op jit(solution)/shard_map/ppermute | solution.py:391
  68.4 0.9 %fusion.3 = (f32[16,4096]{1,0:T(8,128)}, f32[16,4096]{1,0:T(8,128)}) fusion(f32[2,16,4096]{2,1,0:T(8,128)S(1)} %add.40), kind=kLoop, calls=%fused_computation.4 | loop fusion | flops 327680 | bytes 1048576 | tf_op jit(solution)/shard_map/sqrt | solution.py:494
  (33 shorter events, 3.5 us)
Async XLA Ops:
  0.6 12.1 %collective-permute-start = (f32[16,4096]{1,0:T(8,128)}, f32[16,4096]{1,0:T(8,128)S(1)}, u32[]{:S(2)}, u32[]{:S(2)}) collective-permute-start(f32[16,4096]{1,0:T(8,128)} %bitcast.14), channel_id=1, source_target_pairs={{0,1},{1,0},{2,3},{3,2},{4,5},{5,4},{6,7},{7,6},{8,9},{9,8},{10,11... | collective-permute-start | bytes 786440 | tf_op jit(solution)/shard_map/ppermute | solution.py:363
  3.7 1.0 %copy-start = (f32[2,16,4096]{2,1,0:T(8,128)S(1)}, f32[2,16,4096]{2,1,0:T(8,128)}, u32[]{:S(2)}) copy-start(f32[2,16,4096]{2,1,0:T(8,128)} %frames.1) | copy-start | bytes 1572868
  4.7 0.9 %copy-start.1 = (f32[1,16,4096]{2,1,0:T(8,128)S(1)}, f32[1,16,4096]{2,1,0:T(8,128)}, u32[]{:S(2)}) copy-start(f32[1,16,4096]{2,1,0:T(8,128)} %wind.1) | copy-start | bytes 786436
  5.7 0.7 copy-start.2
  8.5 5.0 %collective-permute-start.3 = (f32[2,4,4096]{2,1,0:T(4,128)S(1)}, f32[2,4,4096]{2,1,0:T(4,128)S(1)}, u32[]{:S(2)}, u32[]{:S(2)}) collective-permute-start(f32[2,4,4096]{2,1,0:T(4,128)S(1)} %get-tuple-element.25), channel_id=1, source_target_pairs={{2,4},{6,8},{10,12},{14,16},{18,20},{22,24},{26,28},{4,2},{8,6},{1... | collective-permute-start | bytes 393224 | tf_op jit(solution)/shard_map/ppermute | solution.py:363
  9.1 4.4 %collective-permute-start.4 = (f32[2,4,4096]{2,1,0:T(4,128)S(1)}, f32[2,4,4096]{2,1,0:T(4,128)S(1)}, u32[]{:S(2)}, u32[]{:S(2)}) collective-permute-start(f32[2,4,4096]{2,1,0:T(4,128)S(1)} %get-tuple-element.26), channel_id=1, source_target_pairs={{0,2},{4,6},{8,10},{12,14},{16,18},{20,22},{24,26},{28,30},{2,0},{... | collective-permute-start | bytes 393224 | tf_op jit(solution)/shard_map/ppermute | solution.py:363
  12.7 2.3 %collective-permute-start.2 = (f32[8,4096]{1,0:T(8,128)S(1)}, f32[8,4096]{1,0:T(8,128)S(1)}, u32[]{:S(2)}, u32[]{:S(2)}) collective-permute-start(f32[8,4096]{1,0:T(8,128)S(1)} %get-tuple-element.39.own_even), channel_id=1, source_target_pairs={{0,2},{4,6},{8,10},{12,14},{16,18},{20,22},{24,26},{28,30},{2,0},{... | collective-permute-start | bytes 393224 | tf_op jit(solution)/shard_map/ppermute | solution.py:363
  12.8 2.2 %collective-permute-start.1 = (f32[8,4096]{1,0:T(8,128)S(1)}, f32[8,4096]{1,0:T(8,128)S(1)}, u32[]{:S(2)}, u32[]{:S(2)}) collective-permute-start(f32[8,4096]{1,0:T(8,128)S(1)} %get-tuple-element.40.own_odd), channel_id=1, source_target_pairs={{2,4},{6,8},{10,12},{14,16},{18,20},{22,24},{26,28},{4,2},{8,6},{1... | collective-permute-start | bytes 393224 | tf_op jit(solution)/shard_map/ppermute | solution.py:363
  18.7 7.3 %collective-permute-start.5 = (f32[24,128]{1,0:T(8,128)S(1)}, f32[24,128]{1,0:T(8,128)S(1)}, u32[]{:S(2)}, u32[]{:S(2)}) collective-permute-start(f32[24,128]{1,0:T(8,128)S(1)} %get-tuple-element.29), channel_id=1, source_target_pairs={{0,2},{4,6},{8,10},{12,14},{16,18},{20,22},{24,26},{28,30},{1,3},{... | collective-permute-start | bytes 36872 | tf_op jit(solution)/shard_map/ppermute | solution.py:386
  26.0 0.7 collective-permute-start.6
  26.7 0.7 collective-permute-start.7
  27.4 0.7 collective-permute-start.8
  28.1 15.8 %collective-permute-start.9 = (f32[24,128]{1,0:T(8,128)S(1)}, f32[24,128]{1,0:T(8,128)S(1)}, u32[]{:S(2)}, u32[]{:S(2)}) collective-permute-start(f32[24,128]{1,0:T(8,128)S(1)} %add.35), channel_id=1, source_target_pairs={{2,0},{6,4},{10,8},{14,12},{18,16},{22,20},{26,24},{30,28},{3,1},{... | collective-permute-start | bytes 36872 | tf_op jit(solution)/shard_map/ppermute | solution.py:391
  46.6 21.7 %collective-permute-start.15 = (f32[2,16,4096]{2,1,0:T(8,128)S(1)}, f32[2,16,4096]{2,1,0:T(8,128)S(1)}, u32[]{:S(2)}, u32[]{:S(2)}) collective-permute-start(f32[2,16,4096]{2,1,0:T(8,128)S(1)} %get-tuple-element.34), channel_id=1, source_target_pairs={{0,1},{1,0},{2,3},{3,2},{4,5},{5,4},{6,7},{7,6},{8,9},{9,8},{10,11... | collective-permute-start | bytes 1572872 | tf_op jit(solution)/shard_map/ppermute | solution.py:401
  47.1 3.7 %collective-permute-start.10 = (f32[8,128]{1,0:T(8,128)S(1)}, f32[8,128]{1,0:T(8,128)S(1)}, u32[]{:S(2)}, u32[]{:S(2)}) collective-permute-start(f32[8,128]{1,0:T(8,128)S(1)} %get-tuple-element.33), channel_id=1, source_target_pairs={{0,2},{4,6},{8,10},{12,14},{16,18},{20,22},{24,26},{28,30},{1,3},{... | collective-permute-start | bytes 12296 | tf_op jit(solution)/shard_map/ppermute | solution.py:386
  50.8 0.7 collective-permute-start.11
  51.5 0.7 collective-permute-start.12
  52.2 0.7 collective-permute-start.13
  52.9 14.7 %collective-permute-start.14 = (f32[8,128]{1,0:T(8,128)S(1)}, f32[8,128]{1,0:T(8,128)S(1)}, u32[]{:S(2)}, u32[]{:S(2)}) collective-permute-start(f32[8,128]{1,0:T(8,128)S(1)} %add.39), channel_id=1, source_target_pairs={{2,0},{6,4},{10,8},{14,12},{18,16},{22,20},{26,24},{30,28},{3,1},{... | collective-permute-start | bytes 12296 | tf_op jit(solution)/shard_map/ppermute | solution.py:391

commit v4 on v3

--- a/solution.py
+++ b/solution.py
@@ -84,54 +84,44 @@
     return value
 
 
-def cut_kernel(
-    base, frames, wind, raw, across, frames_odd, frames_even, wind_odd, wind_even, offsets, wind_here, arrived
-):
+def at_edge():
+    index = lax.axis_index("rows")
+    return (index == 0) | (index == lax.axis_size("rows") - 1)
+
+
+def cut_kernel(base, frames, raw, frames_odd, frames_even, offsets, arrived):
     count, rows, columns = raw.shape
     tiles = columns // lanes
     odd = lax.axis_index("rows") % 2 == 1
     copies = [pltpu.make_async_copy(frames.at[f], raw.at[f], arrived.at[f]) for f in range(count)]
-    copies.append(pltpu.make_async_copy(wind.at[0], wind_here, arrived.at[count]))
-    copies.append(pltpu.make_async_copy(base, offsets, arrived.at[count + 1]))
+    copies.append(pltpu.make_async_copy(base, offsets, arrived.at[count]))
     for copy in copies:
         copy.start()
-
-    for f in range(count):
-        copies[f].wait()
-
-        def step(t, carry):
-            at = tile_of(t)
-            before = jnp.where(t > 0, raw[f, :, tile_of(jnp.maximum(t - 1, 0))], 0.0)
-            after = jnp.where(t < tiles - 1, raw[f, :, tile_of(jnp.minimum(t + 1, tiles - 1))], 0.0)
-            value = horizontal(before, raw[f, :, at], after)
-            across[f, t] = value
-            low = value[0:4]
-            high = value[rows - 4 : rows]
+    for copy in copies:
+        copy.wait()
+
+    def step(t, carry):
+        at = tile_of(t)
+        for f in range(count):
+            low = raw[f, 0:4, at]
+            high = raw[f, rows - 4 : rows, at]
             frames_odd[f, :, at] = jnp.where(odd, high, low)
             frames_even[f, :, at] = jnp.where(odd, low, high)
-            return carry
-
-        by_tiles(step, tiles, 16)
-
-    for copy in copies[count:]:
-        copy.wait()
-
-    def wind_step(t, carry):
-        at = tile_of(t)
-        low = wind_here[0 : rows // 2, at]
-        high = wind_here[rows // 2 : rows, at]
-        wind_odd[:, at] = jnp.where(odd, high, low)
-        wind_even[:, at] = jnp.where(odd, low, high)
-        return carry
-
-    by_tiles(wind_step, tiles, 16)
-
-
-def smooth_kernel(frames, across, from_odd, from_even, inverse, stack, power, rows_in, fine):
+        return carry
+
+    by_tiles(step, tiles, 16)
+
+
+def smooth_kernel(frames, from_odd, from_even, inverse, stack, power, rows_in, half, fine):
     count, rows, columns = frames.shape
     tiles = columns // lanes
     ring = tiles + 2
     odd = lax.axis_index("rows") % 2 == 1
+    edge = at_edge()
+    zero = jnp.zeros((rows, lanes), jnp.float32)
+    for f in range(count):
+        half[f, 0] = zero
+        half[f, tiles + 1] = zero
     blank = jnp.zeros((count * rows, lanes), jnp.float32)
     fine[0] = blank
     fine[tiles + 1] = blank
@@ -139,17 +129,22 @@
 
     def load_step(t, carry):
         for f in range(count):
-            outer = from_odd[f, :, tile_of(t)]
+            outer = jnp.where(edge, 0.0, from_odd[f, :, tile_of(t)])
             inner = from_even[f, :, tile_of(t)]
             rows_in[f, t, 4:8, :] = jnp.where(odd, inner, outer)
-            rows_in[f, t, 8 : 8 + rows, :] = across[f, t]
+            rows_in[f, t, 8 : 8 + rows, :] = frames[f, :, tile_of(t)]
             rows_in[f, t, 8 + rows : 12 + rows, :] = jnp.where(odd, outer, inner)
         return carry
 
-    def vertical_step(t, totals):
+    def vertical_step(t, carry):
+        for f in range(count):
+            half[f, t + 1] = vertical(lambda s: rows_in[f, t, pl.ds(4 + s, rows), :])
+        return carry
+
+    def horizontal_step(t, totals):
         result = []
         for f in range(count):
-            smooth = vertical(lambda s: rows_in[f, t, pl.ds(4 + s, rows), :])
+            smooth = horizontal(half[f, t], half[f, t + 1], half[f, t + 2])
             inverse[f, :, tile_of(t)] = 1.0 / smooth
             detail = frames[f, :, tile_of(t)] - smooth
             fine[t + 1, f * rows : (f + 1) * rows, :] = detail
@@ -166,7 +161,8 @@
         return carry
 
     by_tiles(load_step, tiles, 8)
-    powers = by_tiles(vertical_step, tiles, 8, (jnp.zeros((8, lanes), jnp.float32),) * count)
+    by_tiles(vertical_step, tiles, 8)
+    powers = by_tiles(horizontal_step, tiles, 8, (jnp.zeros((8, lanes), jnp.float32),) * count)
     for f in range(count):
         power[f * 8 : f * 8 + 8, :] = powers[f]
     fine[tiles + 3] = fine[1]
@@ -200,6 +196,7 @@
     row_index = lax.axis_index("rows")
     last_row = lax.axis_size("rows") - 1
     odd = row_index % 2 == 1
+    edge = at_edge()
     blank = jnp.zeros((wide, lanes), jnp.float32)
     half[0] = blank
     half[tiles + 1] = blank
@@ -212,7 +209,7 @@
     inside = ((place >= 4) | (row_index > 0)) & ((place < rows + 4) | (row_index < last_row))
 
     def load_step(t, carry):
-        outer = [array[:, tile_of(t)] for array in (from_odd, own_odd)]
+        outer = [jnp.where(edge, 0.0, from_odd[:, tile_of(t)]), own_odd[:, tile_of(t)]]
         inner = [array[:, tile_of(t)] for array in (own_even, from_even)]
         rows_in[t, 0:8, :] = jnp.where(odd, inner[1], outer[0])
         rows_in[t, 8:16, :] = jnp.where(odd, inner[0], outer[1])
@@ -359,8 +356,10 @@
 
 def paired(value, axis, first):
     size = lax.axis_size(axis)
-    pairs = [(i, i + 1) for i in range(first, size - 1, 2)]
-    return lax.ppermute(value, axis, pairs + [(j, i) for i, j in pairs])
+    partner = list(range(size))
+    for i in range(first, size - 1, 2):
+        partner[i], partner[i + 1] = i + 1, i
+    return lax.ppermute(value, axis, list(enumerate(partner)))
 
 
 def by_parity(odd, array, height, dim):
@@ -370,11 +369,12 @@
     return jnp.where(odd, high, low), jnp.where(odd, low, high)
 
 
-def from_owner(shard, cut, odd, axis, root):
+def from_owner(shard, odd, axis, root):
     mine = lax.axis_index(axis) == root
     if lax.axis_size(axis) == 2:
+        halves_here = lax.optimization_barrier(by_parity(odd, shard, shard.shape[0] // 2, 0))
         received = by_parity(odd, paired(shard, axis, 0), shard.shape[0] // 2, 0)
-        return [jnp.where(mine, own, other) for own, other in zip(cut, received)]
+        return [jnp.where(mine, own, other) for own, other in zip(halves_here, received)]
     whole = lax.psum(jnp.where(mine, shard, jnp.zeros_like(shard)), axis)
     return by_parity(odd, whole, shard.shape[0] // 2, 0)
 
@@ -383,13 +383,13 @@
     size = lax.axis_size("rows")
     if size & (size - 1) or size < 2:
         return lax.psum(value, "rows")
-    value = value + lax.ppermute(value, "rows", [(i, i + 1) for i in range(0, size, 2)])
+    value = value + paired(value, "rows", 0)
     step = 2
     while step < size:
-        value = value + lax.ppermute(value, "rows", [(i, i ^ step) for i in range(1, size, 2)])
+        pairs = [(i, i ^ step if i % 2 else i) for i in range(size)]
+        value = value + lax.ppermute(value, "rows", pairs)
         step *= 2
-    back = lax.ppermute(value, "rows", [(i, i - 1) for i in range(1, size, 2)])
-    return jnp.where(odd, value, back)
+    return jnp.where(odd, value, paired(value, "rows", 0))
 
 
 def total_over(value, axis):
@@ -413,26 +413,21 @@
     bf16 = jnp.bfloat16
     struct = functools.partial(jax.ShapeDtypeStruct, dtype=f32)
     odd = lax.axis_index("rows") % 2 == 1
-    edge = struct((count, 4, columns))
-    side = struct((rows // 2, columns))
-    raw, across, frames_odd, frames_even, wind_odd, wind_even, offsets = pl.pallas_call(
+    own_odd, own_even = from_owner(wind_off[0], odd, "frames", run_owner[0])
+    raw, frames_odd, frames_even, offsets = pl.pallas_call(
         cut_kernel,
         out_shape=(
             struct((count, rows, columns)),
-            struct((count, tiles, rows, lanes)),
-            edge,
-            edge,
-            side,
-            side,
+            struct((count, 4, columns)),
+            struct((count, 4, columns)),
             jax.ShapeDtypeStruct((1, 2), jnp.int32),
         ),
-        in_specs=[pl.BlockSpec(memory_space=pl.ANY)] * 3,
-        out_specs=(vmem,) * 6 + (smem,),
-        scratch_shapes=[pltpu.VMEM((rows, columns), f32), pltpu.SemaphoreType.DMA((count + 2,))],
+        in_specs=[pl.BlockSpec(memory_space=pl.ANY)] * 2,
+        out_specs=(vmem,) * 3 + (smem,),
+        scratch_shapes=[pltpu.SemaphoreType.DMA((count + 1,))],
         compiler_params=params,
         name="cut",
-    )(search_base, frames_raw, wind_off)
-    own_odd, own_even = from_owner(wind_off[0], (wind_odd, wind_even), odd, "frames", run_owner[0])
+    )(search_base, frames_raw)
     frames_odd = paired(frames_odd, "rows", 1)
     frames_even = paired(frames_even, "rows", 0)
     from_even = paired(own_even, "rows", 0)
@@ -444,15 +439,16 @@
             jax.ShapeDtypeStruct((2 * depth, ring * lanes), bf16),
             struct((8 * count, lanes)),
         ),
-        in_specs=[vmem] * 4,
+        in_specs=[vmem] * 3,
         out_specs=(vmem,) * 3,
         scratch_shapes=[
             pltpu.VMEM((count, tiles, rows + 16, lanes), f32),
+            pltpu.VMEM((count, tiles + 2, rows, lanes), f32),
             pltpu.VMEM((ring + 2, count * rows, lanes), f32),
         ],
         compiler_params=params,
         name="smooth",
-    )(raw, across, frames_odd, frames_even)
+    )(raw, frames_odd, frames_even)
     clean, part = pl.pallas_call(
         match_kernel,
         out_shape=(struct((tiles + 2, wide, lanes)), struct((8 * count + 8, lanes))),

time: 69.7 us -> 63.1 us (0.905)
  waiting for transfers between devices: 27.7 us -> 2.85 us
  starting transfers between devices: 23.7 us -> 41.5 us
  other arithmetic: 1.76 us -> 2.74 us
  local copies, waits for them, and re-layouts: 2.65 us -> 1.7 us
    ppermute x15, waiting for transfers between devices: 27.7 us -> 2.85 us  [the longest x9 2.84 us: paired(): return lax.ppermute(value, axis, list(enumerate(partner)))]
    ppermute x15, starting transfers between devices: 23.2 us -> 41 us  [the longest x9 37 us: paired(): return lax.ppermute(value, axis, list(enumerate(partner)))]
    pallas_call x1, Pallas kernels: 1.49 us -> 2.86 us  [shards(): pl.pallas_call(smooth_kernel, out_shape=(struct((count, rows, columns)),...]
    select_n x2 -> x3, other arithmetic: 0.03 us -> 1.02 us  [the longest x1 0.99 us: by_parity(): return (jnp.where(odd, high, low), jnp.where(odd, low, high))]
    unnamed x6 -> x4, local copies, waits for them, and re-layouts: 2.65 us -> 1.7 us
    pallas_call x1, Pallas kernels: 2.14 us -> 1.27 us  [shards(): pl.pallas_call(cut_kernel, out_shape=(struct((count, rows, columns)), str...]
  transfers between devices with their start and end apart: 16 -> 16, of which waited for: 4 -> 3; matrix products, arithmetic and copies ran while one was open for 1% -> 3% of each run, Pallas kernels for 8% -> 10%
where the time goes in v4:
time: 63.1 us; the launch traced here: 62.7 us
  starting transfers between devices  41.5 us (66%)
  Pallas kernels  12.4 us (20%)
  waiting for transfers between devices  2.85 us (5%)
  other arithmetic  2.74 us (4%)
  local copies, waits for them, and re-layouts  1.7 us (3%)
  between operations  1.54 us (2%)
    ppermute x9, starting transfers between devices, paired(): return lax.ppermute(value, axis, list(enumerate(partner)))  37 us
    ppermute x6, starting transfers between devices, total_over_rows(): value = value + lax.ppermute(value, 'rows', pairs)  3.95 us
    pallas_call x1, Pallas kernels, shards(): pl.pallas_call(match_kernel, out_shape=(struct((tiles + 2, wide, lanes)),...  3.67 us
    pallas_call x1, Pallas kernels, shards(): pl.pallas_call(smooth_kernel, out_shape=(struct((count, rows, columns)),...  2.86 us
    ppermute x9, waiting for transfers between devices, paired(): return lax.ppermute(value, axis, list(enumerate(partner)))  2.84 us
    pallas_call x1, Pallas kernels, shards(): pl.pallas_call(pressure_kernel, out_shape=(struct((count, rows, columns))...  2.78 us
    pallas_call x1, Pallas kernels, shards(): pl.pallas_call(spread_kernel, out_shape=jax.ShapeDtypeStruct((2 * 8 * slo...  1.85 us
    unnamed x4, local copies, waits for them, and re-layouts  1.7 us
  transfers between devices with their start and end apart: 16, of which 3 were waited for; matrix products, arithmetic and copies ran while one was open for 3% of the time, Pallas kernels for 10%

profile of v4, /device:TPU:0, one launch (start us, length us, event | category | flops | bytes accessed | tf_op | source)
XLA Modules:
  0.0 62.7 jit_solution(2936285626741856319)
XLA Ops:
  0.6 3.0 %collective-permute-start = (f32[16,4096]{1,0:T(8,128)}, f32[16,4096]{1,0:T(8,128)S(1)}, u32[]{:S(2)}, u32[]{:S(2)}) collective-permute-start(f32[16,4096]{1,0:T(8,128)} %bitcast.18), channel_id=1, source_target_pairs={{0,1},{1,0},{2,3},{3,2},{4,5},{5,4},{6,7},{7,6},{8,9},{9,8},{10,11... | collective-permute-start | bytes 786440 | tf_op jit(solution)/shard_map/ppermute | solution.py:362
  3.7 1.0 %copy-done = f32[2,16,4096]{2,1,0:T(8,128)S(1)} copy-done((f32[2,16,4096]{2,1,0:T(8,128)S(1)}, f32[2,16,4096]{2,1,0:T(8,128)}, u32[]{:S(2)}) %copy-start) | copy-done | bytes 524312
  4.7 0.7 %copy-done.1 = s32[1,2]{1,0:T(1,128)S(1)} copy-done((s32[1,2]{1,0:T(1,128)S(1)}, s32[1,2]{1,0:T(1,128)}, u32[]{:S(2)}) %copy-start.1) | copy-done | bytes 32
  5.4 1.3 %cut.1 = (f32[2,16,4096]{2,1,0:T(8,128)S(1)}, f32[2,4,4096]{2,1,0:T(4,128)S(1)}, f32[2,4,4096]{2,1,0:T(4,128)S(1)}, s32[1,2]{1,0:T(1,128)S(1)}) custom-call(s32[1,2]{1,0:T(1,128)S(1)} %copy-done.1, f32[2,16,4096]{2,1,0:T(8,128)S(1)} %copy-done), custom_call_target="tpu_custom_call" | custom-call | tf_op jit(solution)/shard_map/cut/pallas_call | solution.py:417
  6.6 0.7 %collective-permute-start.3 = (f32[2,4,4096]{2,1,0:T(4,128)S(1)}, f32[2,4,4096]{2,1,0:T(4,128)S(1)}, u32[]{:S(2)}, u32[]{:S(2)}) collective-permute-start(f32[2,4,4096]{2,1,0:T(4,128)S(1)} %get-tuple-element.23), channel_id=1, source_target_pairs={{0,0},{2,4},{4,2},{6,8},{8,6},{10,12},{12,10},{14,16},{16,14},{18,... | collective-permute-start | bytes 393224 | tf_op jit(solution)/shard_map/ppermute | solution.py:362
  7.3 2.9 %collective-permute-start.4 = (f32[2,4,4096]{2,1,0:T(4,128)S(1)}, f32[2,4,4096]{2,1,0:T(4,128)S(1)}, u32[]{:S(2)}, u32[]{:S(2)}) collective-permute-start(f32[2,4,4096]{2,1,0:T(4,128)S(1)} %get-tuple-element.24), channel_id=1, source_target_pairs={{0,2},{2,0},{4,6},{6,4},{8,10},{10,8},{12,14},{14,12},{16,18},{18,... | collective-permute-start | bytes 393224 | tf_op jit(solution)/shard_map/ppermute | solution.py:362
  10.2 1.0 %select_bitcast_fusion = (f32[8,4096]{1,0:T(8,128)S(1)}, f32[8,4096]{1,0:T(8,128)S(1)}) fusion(f32[1,16,4096]{2,1,0:T(8,128)} %param.5, pred[]{:T(512)S(6)} %eq.8), kind=kLoop, calls=%fused_computation.9 | loop fusion | flops 65536 | bytes 524289 | tf_op jit(solution)/shard_map/jit(_where)/select_n | solution.py:369
  12.0 0.7 %collective-permute-start.1 = (f32[8,4096]{1,0:T(8,128)S(1)}, f32[8,4096]{1,0:T(8,128)S(1)}, u32[]{:S(2)}, u32[]{:S(2)}) collective-permute-start(f32[8,4096]{1,0:T(8,128)S(1)} %get-tuple-element.38.own_odd), channel_id=1, source_target_pairs={{0,0},{2,4},{4,2},{6,8},{8,6},{10,12},{12,10},{14,16},{16,14},{18,... | collective-permute-start | bytes 393224 | tf_op jit(solution)/shard_map/ppermute | solution.py:362
  12.7 2.9 %smooth.1 = (f32[2,16,4096]{2,1,0:T(8,128)S(1)}, bf16[448,4352]{1,0:T(8,128)(2,1)S(1)}, f32[16,128]{1,0:T(8,128)S(1)}) custom-call(f32[2,16,4096]{2,1,0:T(8,128)S(1)} %get-tuple-element.22.frames, f32[2,4,4096]{2,1,0:T(4,128)S(1)} %collective-permute-done.3.from_odd, f32[2,4,4096]{2,1,0:T(4,128)S(1)} %collective-permute-done.4.from_even), custom_call_target="tpu_custom_call" | custom-call | tf_op jit(solution)/shard_map/smooth/pallas_call | solution.py:435
  15.6 3.7 %match.1 = (f32[34,24,128]{2,1,0:T(8,128)S(1)}, f32[24,128]{1,0:T(8,128)S(1)}) custom-call(s32[1,2]{1,0:T(1,128)S(1)} %get-tuple-element.19.base, f32[8,4096]{1,0:T(8,128)S(1)} %get-tuple-element.38.own_odd, f32[8,4096]{1,0:T(8,128)S(1)} %get-tuple-element.37.own_even, f32[8,4096]{1,0:T(8,128)S(1)} %collective-permute-done.1.from_odd, ...), custom_call_target="tpu_custom_call" | custom-call | tf_op jit(solution)/shard_map/match/pallas_call | solution.py:452
  19.3 3.2 %collective-permute-start.5 = (f32[24,128]{1,0:T(8,128)S(1)}, f32[24,128]{1,0:T(8,128)S(1)}, u32[]{:S(2)}, u32[]{:S(2)}) collective-permute-start(f32[24,128]{1,0:T(8,128)S(1)} %get-tuple-element.27), channel_id=1, source_target_pairs={{0,2},{2,0},{4,6},{6,4},{8,10},{10,8},{12,14},{14,12},{16,18},{18,... | collective-permute-start | bytes 36872 | tf_op jit(solution)/shard_map/ppermute | solution.py:362
  22.5 0.8 %collective-permute-done.5 = f32[24,128]{1,0:T(8,128)S(1)} collective-permute-done((f32[24,128]{1,0:T(8,128)S(1)}, f32[24,128]{1,0:T(8,128)S(1)}, u32[]{:S(2)}, u32[]{:S(2)}) %collective-permute-start.5) | collective-permute-done | bytes 12320 | tf_op jit(solution)/shard_map/ppermute | solution.py:362
  23.3 0.7 %collective-permute-start.6 = (f32[24,128]{1,0:T(8,128)S(1)}, f32[24,128]{1,0:T(8,128)S(1)}, u32[]{:S(2)}, u32[]{:S(2)}) collective-permute-start(f32[24,128]{1,0:T(8,128)S(1)} %add.32), channel_id=1, source_target_pairs={{0,0},{2,6},{4,4},{6,2},{8,8},{10,14},{12,12},{14,10},{16,16},{18,... | collective-permute-start | bytes 36872 | tf_op jit(solution)/shard_map/ppermute | solution.py:390
  24.0 0.7 %collective-permute-start.7 = (f32[24,128]{1,0:T(8,128)S(1)}, f32[24,128]{1,0:T(8,128)S(1)}, u32[]{:S(2)}, u32[]{:S(2)}) collective-permute-start(f32[24,128]{1,0:T(8,128)S(1)} %add.33), channel_id=1, source_target_pairs={{0,0},{2,10},{4,4},{6,14},{8,8},{10,2},{12,12},{14,6},{16,16},{18,... | collective-permute-start | bytes 36872 | tf_op jit(solution)/shard_map/ppermute | solution.py:390
  24.7 0.7 %collective-permute-start.8 = (f32[24,128]{1,0:T(8,128)S(1)}, f32[24,128]{1,0:T(8,128)S(1)}, u32[]{:S(2)}, u32[]{:S(2)}) collective-permute-start(f32[24,128]{1,0:T(8,128)S(1)} %add.34), channel_id=1, source_target_pairs={{0,0},{2,18},{4,4},{6,22},{8,8},{10,26},{12,12},{14,30},{16,16},{1... | collective-permute-start | bytes 36872 | tf_op jit(solution)/shard_map/ppermute | solution.py:390
  25.4 13.8 %collective-permute-start.9 = (f32[24,128]{1,0:T(8,128)S(1)}, f32[24,128]{1,0:T(8,128)S(1)}, u32[]{:S(2)}, u32[]{:S(2)}) collective-permute-start(f32[24,128]{1,0:T(8,128)S(1)} %add.35), channel_id=1, source_target_pairs={{0,2},{2,0},{4,6},{6,4},{8,10},{10,8},{12,14},{14,12},{16,18},{18,... | collective-permute-start | bytes 36872 | tf_op jit(solution)/shard_map/ppermute | solution.py:362
  39.2 1.9 %spread.1 = bf16[512,4096]{1,0:T(8,128)(2,1)S(1)} custom-call(s32[1,2]{1,0:T(1,128)S(1)} %get-tuple-element.19.base, f32[34,24,128]{2,1,0:T(8,128)S(1)} %get-tuple-element.28.clean), custom_call_target="tpu_custom_call" | custom-call | tf_op jit(solution)/shard_map/spread/pallas_call | solution.py:467
  41.1 2.8 %pressure.1 = (f32[2,16,4096]{2,1,0:T(8,128)}, f32[2,16,4096]{2,1,0:T(8,128)S(1)}, f32[8,128]{1,0:T(8,128)S(1)}) custom-call(s32[1,2]{1,0:T(1,128)S(1)} %get-tuple-element.19.base, f32[24,128]{1,0:T(8,128)S(1)} %broadcast_select_fusion.parts, bf16[512,4096]{1,0:T(8,128)(2,1)S(1)} %spread.1, f32[2,16,4096]{2,1,0:T(8,128)S(1)} %get-tuple-element.29.inverse), custom_call_target="tpu_custom_call" | custom-call | tf_op jit(solution)/shard_map/pressure/pallas_call | solution.py:475
  44.4 1.2 %collective-permute-done.10 = f32[8,128]{1,0:T(8,128)S(1)} collective-permute-done((f32[8,128]{1,0:T(8,128)S(1)}, f32[8,128]{1,0:T(8,128)S(1)}, u32[]{:S(2)}, u32[]{:S(2)}) %collective-permute-start.10) | collective-permute-done | bytes 4128 | tf_op jit(solution)/shard_map/ppermute | solution.py:362
  46.2 0.7 %collective-permute-start.12 = (f32[8,128]{1,0:T(8,128)S(1)}, f32[8,128]{1,0:T(8,128)S(1)}, u32[]{:S(2)}, u32[]{:S(2)}) collective-permute-start(f32[8,128]{1,0:T(8,128)S(1)} %add.37), channel_id=1, source_target_pairs={{0,0},{2,10},{4,4},{6,14},{8,8},{10,2},{12,12},{14,6},{16,16},{18,... | collective-permute-start | bytes 12296 | tf_op jit(solution)/shard_map/ppermute | solution.py:390
  46.9 0.7 %collective-permute-start.13 = (f32[8,128]{1,0:T(8,128)S(1)}, f32[8,128]{1,0:T(8,128)S(1)}, u32[]{:S(2)}, u32[]{:S(2)}) collective-permute-start(f32[8,128]{1,0:T(8,128)S(1)} %add.38), channel_id=1, source_target_pairs={{0,0},{2,18},{4,4},{6,22},{8,8},{10,26},{12,12},{14,30},{16,16},{1... | collective-permute-start | bytes 12296 | tf_op jit(solution)/shard_map/ppermute | solution.py:390
  47.6 12.6 %collective-permute-start.14 = (f32[8,128]{1,0:T(8,128)S(1)}, f32[8,128]{1,0:T(8,128)S(1)}, u32[]{:S(2)}, u32[]{:S(2)}) collective-permute-start(f32[8,128]{1,0:T(8,128)S(1)} %add.39), channel_id=1, source_target_pairs={{0,2},{2,0},{4,6},{6,4},{8,10},{10,8},{12,14},{14,12},{16,18},{18,... | collective-permute-start | bytes 12296 | tf_op jit(solution)/shard_map/ppermute | solution.py:362
  60.2 0.8 %collective-permute-done.14 = f32[8,128]{1,0:T(8,128)S(1)} collective-permute-done((f32[8,128]{1,0:T(8,128)S(1)}, f32[8,128]{1,0:T(8,128)S(1)}, u32[]{:S(2)}, u32[]{:S(2)}) %collective-permute-start.14) | collective-permute-done | bytes 4128 | tf_op jit(solution)/shard_map/ppermute | solution.py:362
  61.9 0.9 %fusion.3 = (f32[16,4096]{1,0:T(8,128)}, f32[16,4096]{1,0:T(8,128)}) fusion(f32[2,16,4096]{2,1,0:T(8,128)S(1)} %add.40), kind=kLoop, calls=%fused_computation.4 | loop fusion | flops 327680 | bytes 1048576 | tf_op jit(solution)/shard_map/sqrt | solution.py:490
  (32 shorter events, 2.2 us)
Async XLA Ops:
  0.6 11.2 %collective-permute-start = (f32[16,4096]{1,0:T(8,128)}, f32[16,4096]{1,0:T(8,128)S(1)}, u32[]{:S(2)}, u32[]{:S(2)}) collective-permute-start(f32[16,4096]{1,0:T(8,128)} %bitcast.18), channel_id=1, source_target_pairs={{0,1},{1,0},{2,3},{3,2},{4,5},{5,4},{6,7},{7,6},{8,9},{9,8},{10,11... | collective-permute-start | bytes 786440 | tf_op jit(solution)/shard_map/ppermute | solution.py:362
  3.7 1.0 %copy-start = (f32[2,16,4096]{2,1,0:T(8,128)S(1)}, f32[2,16,4096]{2,1,0:T(8,128)}, u32[]{:S(2)}) copy-start(f32[2,16,4096]{2,1,0:T(8,128)} %frames.1) | copy-start | bytes 1572868
  4.7 0.7 %copy-start.1 = (s32[1,2]{1,0:T(1,128)S(1)}, s32[1,2]{1,0:T(1,128)}, u32[]{:S(2)}) copy-start(s32[1,2]{1,0:T(1,128)} %base.1) | copy-start | bytes 28
  6.6 6.0 %collective-permute-start.3 = (f32[2,4,4096]{2,1,0:T(4,128)S(1)}, f32[2,4,4096]{2,1,0:T(4,128)S(1)}, u32[]{:S(2)}, u32[]{:S(2)}) collective-permute-start(f32[2,4,4096]{2,1,0:T(4,128)S(1)} %get-tuple-element.23), channel_id=1, source_target_pairs={{0,0},{2,4},{4,2},{6,8},{8,6},{10,12},{12,10},{14,16},{16,14},{18,... | collective-permute-start | bytes 393224 | tf_op jit(solution)/shard_map/ppermute | solution.py:362
  7.3 5.4 %collective-permute-start.4 = (f32[2,4,4096]{2,1,0:T(4,128)S(1)}, f32[2,4,4096]{2,1,0:T(4,128)S(1)}, u32[]{:S(2)}, u32[]{:S(2)}) collective-permute-start(f32[2,4,4096]{2,1,0:T(4,128)S(1)} %get-tuple-element.24), channel_id=1, source_target_pairs={{0,2},{2,0},{4,6},{6,4},{8,10},{10,8},{12,14},{14,12},{16,18},{18,... | collective-permute-start | bytes 393224 | tf_op jit(solution)/shard_map/ppermute | solution.py:362
  11.9 3.6 %collective-permute-start.2 = (f32[8,4096]{1,0:T(8,128)S(1)}, f32[8,4096]{1,0:T(8,128)S(1)}, u32[]{:S(2)}, u32[]{:S(2)}) collective-permute-start(f32[8,4096]{1,0:T(8,128)S(1)} %get-tuple-element.37.own_even), channel_id=1, source_target_pairs={{0,2},{2,0},{4,6},{6,4},{8,10},{10,8},{12,14},{14,12},{16,18},{18,... | collective-permute-start | bytes 393224 | tf_op jit(solution)/shard_map/ppermute | solution.py:362
  12.0 3.6 %collective-permute-start.1 = (f32[8,4096]{1,0:T(8,128)S(1)}, f32[8,4096]{1,0:T(8,128)S(1)}, u32[]{:S(2)}, u32[]{:S(2)}) collective-permute-start(f32[8,4096]{1,0:T(8,128)S(1)} %get-tuple-element.38.own_odd), channel_id=1, source_target_pairs={{0,0},{2,4},{4,2},{6,8},{8,6},{10,12},{12,10},{14,16},{16,14},{18,... | collective-permute-start | bytes 393224 | tf_op jit(solution)/shard_map/ppermute | solution.py:362
  19.3 4.0 %collective-permute-start.5 = (f32[24,128]{1,0:T(8,128)S(1)}, f32[24,128]{1,0:T(8,128)S(1)}, u32[]{:S(2)}, u32[]{:S(2)}) collective-permute-start(f32[24,128]{1,0:T(8,128)S(1)} %get-tuple-element.27), channel_id=1, source_target_pairs={{0,2},{2,0},{4,6},{6,4},{8,10},{10,8},{12,14},{14,12},{16,18},{18,... | collective-permute-start | bytes 36872 | tf_op jit(solution)/shard_map/ppermute | solution.py:362
  23.3 0.7 %collective-permute-start.6 = (f32[24,128]{1,0:T(8,128)S(1)}, f32[24,128]{1,0:T(8,128)S(1)}, u32[]{:S(2)}, u32[]{:S(2)}) collective-permute-start(f32[24,128]{1,0:T(8,128)S(1)} %add.32), channel_id=1, source_target_pairs={{0,0},{2,6},{4,4},{6,2},{8,8},{10,14},{12,12},{14,10},{16,16},{18,... | collective-permute-start | bytes 36872 | tf_op jit(solution)/shard_map/ppermute | solution.py:390
  24.0 0.7 %collective-permute-start.7 = (f32[24,128]{1,0:T(8,128)S(1)}, f32[24,128]{1,0:T(8,128)S(1)}, u32[]{:S(2)}, u32[]{:S(2)}) collective-permute-start(f32[24,128]{1,0:T(8,128)S(1)} %add.33), channel_id=1, source_target_pairs={{0,0},{2,10},{4,4},{6,14},{8,8},{10,2},{12,12},{14,6},{16,16},{18,... | collective-permute-start | bytes 36872 | tf_op jit(solution)/shard_map/ppermute | solution.py:390
  24.7 0.7 %collective-permute-start.8 = (f32[24,128]{1,0:T(8,128)S(1)}, f32[24,128]{1,0:T(8,128)S(1)}, u32[]{:S(2)}, u32[]{:S(2)}) collective-permute-start(f32[24,128]{1,0:T(8,128)S(1)} %add.34), channel_id=1, source_target_pairs={{0,0},{2,18},{4,4},{6,22},{8,8},{10,26},{12,12},{14,30},{16,16},{1... | collective-permute-start | bytes 36872 | tf_op jit(solution)/shard_map/ppermute | solution.py:390
  25.4 15.7 %collective-permute-start.9 = (f32[24,128]{1,0:T(8,128)S(1)}, f32[24,128]{1,0:T(8,128)S(1)}, u32[]{:S(2)}, u32[]{:S(2)}) collective-permute-start(f32[24,128]{1,0:T(8,128)S(1)} %add.35), channel_id=1, source_target_pairs={{0,2},{2,0},{4,6},{6,4},{8,10},{10,8},{12,14},{14,12},{16,18},{18,... | collective-permute-start | bytes 36872 | tf_op jit(solution)/shard_map/ppermute | solution.py:362
  43.9 17.9 %collective-permute-start.15 = (f32[2,16,4096]{2,1,0:T(8,128)S(1)}, f32[2,16,4096]{2,1,0:T(8,128)S(1)}, u32[]{:S(2)}, u32[]{:S(2)}) collective-permute-start(f32[2,16,4096]{2,1,0:T(8,128)S(1)} %get-tuple-element.32), channel_id=1, source_target_pairs={{0,1},{1,0},{2,3},{3,2},{4,5},{5,4},{6,7},{7,6},{8,9},{9,8},{10,11... | collective-permute-start | bytes 1572872 | tf_op jit(solution)/shard_map/ppermute | solution.py:401
  44.4 1.2 %collective-permute-start.10 = (f32[8,128]{1,0:T(8,128)S(1)}, f32[8,128]{1,0:T(8,128)S(1)}, u32[]{:S(2)}, u32[]{:S(2)}) collective-permute-start(f32[8,128]{1,0:T(8,128)S(1)} %get-tuple-element.31), channel_id=1, source_target_pairs={{0,2},{2,0},{4,6},{6,4},{8,10},{10,8},{12,14},{14,12},{16,18},{18,... | collective-permute-start | bytes 12296 | tf_op jit(solution)/shard_map/ppermute | solution.py:362
  45.5 0.7 %collective-permute-start.11 = (f32[8,128]{1,0:T(8,128)S(1)}, f32[8,128]{1,0:T(8,128)S(1)}, u32[]{:S(2)}, u32[]{:S(2)}) collective-permute-start(f32[8,128]{1,0:T(8,128)S(1)} %add.36), channel_id=1, source_target_pairs={{0,0},{2,6},{4,4},{6,2},{8,8},{10,14},{12,12},{14,10},{16,16},{18,... | collective-permute-start | bytes 12296 | tf_op jit(solution)/shard_map/ppermute | solution.py:390
  46.2 0.7 %collective-permute-start.12 = (f32[8,128]{1,0:T(8,128)S(1)}, f32[8,128]{1,0:T(8,128)S(1)}, u32[]{:S(2)}, u32[]{:S(2)}) collective-permute-start(f32[8,128]{1,0:T(8,128)S(1)} %add.37), channel_id=1, source_target_pairs={{0,0},{2,10},{4,4},{6,14},{8,8},{10,2},{12,12},{14,6},{16,16},{18,... | collective-permute-start | bytes 12296 | tf_op jit(solution)/shard_map/ppermute | solution.py:390
  46.9 0.7 %collective-permute-start.13 = (f32[8,128]{1,0:T(8,128)S(1)}, f32[8,128]{1,0:T(8,128)S(1)}, u32[]{:S(2)}, u32[]{:S(2)}) collective-permute-start(f32[8,128]{1,0:T(8,128)S(1)} %add.38), channel_id=1, source_target_pairs={{0,0},{2,18},{4,4},{6,22},{8,8},{10,26},{12,12},{14,30},{16,16},{1... | collective-permute-start | bytes 12296 | tf_op jit(solution)/shard_map/ppermute | solution.py:390
  47.6 13.4 %collective-permute-start.14 = (f32[8,128]{1,0:T(8,128)S(1)}, f32[8,128]{1,0:T(8,128)S(1)}, u32[]{:S(2)}, u32[]{:S(2)}) collective-permute-start(f32[8,128]{1,0:T(8,128)S(1)} %add.39), channel_id=1, source_target_pairs={{0,2},{2,0},{4,6},{6,4},{8,10},{10,8},{12,14},{14,12},{16,18},{18,... | collective-permute-start | bytes 12296 | tf_op jit(solution)/shard_map/ppermute | solution.py:362

commit v5 on v4

--- a/solution.py
+++ b/solution.py
@@ -87,29 +87,6 @@
 def at_edge():
     index = lax.axis_index("rows")
     return (index == 0) | (index == lax.axis_size("rows") - 1)
-
-
-def cut_kernel(base, frames, raw, frames_odd, frames_even, offsets, arrived):
-    count, rows, columns = raw.shape
-    tiles = columns // lanes
-    odd = lax.axis_index("rows") % 2 == 1
-    copies = [pltpu.make_async_copy(frames.at[f], raw.at[f], arrived.at[f]) for f in range(count)]
-    copies.append(pltpu.make_async_copy(base, offsets, arrived.at[count]))
-    for copy in copies:
-        copy.start()
-    for copy in copies:
-        copy.wait()
-
-    def step(t, carry):
-        at = tile_of(t)
-        for f in range(count):
-            low = raw[f, 0:4, at]
-            high = raw[f, rows - 4 : rows, at]
-            frames_odd[f, :, at] = jnp.where(odd, high, low)
-            frames_even[f, :, at] = jnp.where(odd, low, high)
-        return carry
-
-    by_tiles(step, tiles, 16)
 
 
 def smooth_kernel(frames, from_odd, from_even, inverse, stack, power, rows_in, half, fine):
@@ -186,7 +163,7 @@
 
 
 def match_kernel(
-    base, own_odd, own_even, from_odd, from_even, stack, power, clean, part, rows_in, half, fine, stream
+    base, own_odd, own_even, from_odd, from_even, stack, power, clean, part, rows_in, half, fine, stream, lags
 ):
     rows = own_odd.shape[0] * 2
     tiles = own_odd.shape[1] // lanes
@@ -249,21 +226,29 @@
     size = reach * count * rows
     product = product[:size] + product[size:]
     product = by_row_shift(product, rows, -1)
-    part[...] = jnp.zeros(part.shape, jnp.float32)
+    lags[...] = jnp.zeros(lags.shape, jnp.float32)
     for j in range(reach):
         for f in range(count):
             start = (j * count + f) * rows
-            part[f * 8 + j : f * 8 + j + 1, :] = jnp.sum(product[start : start + rows], axis=0, keepdims=True)
-    lags = part[0 : 8 * count, :]
-    back = lanes - 1 - base[0, 0]
-    lags = pltpu.roll(lags, lax.rem(back, lanes), 1) + pltpu.roll(lags, lax.rem(back + lanes - slot, lanes), 1)
-    part[0 : 8 * count, :] = jnp.where(lane_of(lags.shape) < reach, lags, 0.0)
-    start = 8 * count
+            lags[f * 8 + j : f * 8 + j + 1, :] = jnp.sum(product[start : start + rows], axis=0, keepdims=True)
+    back = 2 * lanes - 1 - base[0, 0]
+    across = lax.broadcasted_iota(jnp.int32, (8, lanes), 0)
+    lane = lane_of((8, lanes))
+    packed = jnp.zeros((8, lanes), jnp.float32)
     for f in range(count):
-        part[start + f : start + f + 1, :] = jnp.sum(power[f * 8 : f * 8 + 8, :], axis=0, keepdims=True)
-    part[start + count : start + count + 1, :] = jnp.sum(ref_power, axis=0, keepdims=True)
-    powers = part[start : start + 8, :]
-    part[start : start + 8, :] = jnp.broadcast_to(jnp.sum(powers, axis=1, keepdims=True), powers.shape)
+        block = lags[f * 8 : f * 8 + 8, :]
+        for j in range(reach):
+            at = (f * reach + j) * reach
+            high = pltpu.roll(block, lax.rem(back + at, lanes), 1)
+            low = pltpu.roll(block, lax.rem(back + at + lanes - slot, lanes), 1)
+            packed = packed + jnp.where((across == j) & (lane >= at) & (lane < at + reach), high + low, 0.0)
+    lags[0:8, :] = jnp.zeros((8, lanes), jnp.float32)
+    for f in range(count):
+        lags[f : f + 1, :] = jnp.sum(power[f * 8 : f * 8 + 8, :], axis=0, keepdims=True)
+    lags[count : count + 1, :] = jnp.sum(ref_power, axis=0, keepdims=True)
+    powers = jnp.sum(lags[0:8, :], axis=1, keepdims=True)
+    packed = packed + jnp.where(lane == count * reach * reach + across, powers, 0.0)
+    part[...] = jnp.broadcast_to(jnp.sum(packed, axis=0, keepdims=True), part.shape)
 
 
 def spread_kernel(base, clean, spread):
@@ -289,39 +274,46 @@
     lax.fori_loop(0, reach, per_offset, 0)
 
 
-def blend_weights(matches, frame_power, ref_power):
-    norm_product = jnp.sqrt((frame_power + 1e-06) * (ref_power + 1e-06))
-    rho = matches / norm_product
-    squared = rho * rho
-    total = jnp.sum(jnp.sum(squared, axis=0, keepdims=True), axis=1, keepdims=True)
-    across = lax.broadcasted_iota(jnp.int32, matches.shape, 0)
-    middle = (across == reach // 2) & (lane_of(matches.shape) == reach // 2)
-    return (squared + jnp.where(middle, 0.05, 0.0)) / (0.05 + total)
-
-
-def banded(weights, rows, first_row):
-    across = lax.broadcasted_iota(jnp.int32, weights.shape, 0)
-    spaced = jnp.zeros_like(weights)
-    for times in range(4):
-        turned = pltpu.roll(weights, first_row + times * slot, 1)
-        spaced = jnp.where(across % 4 == times, turned, spaced)
+def blend_weights(totals, count):
+    lane = lane_of(totals.shape)
+    block = reach * reach
+
+    def pick(index):
+        return jnp.sum(jnp.where(lane == index, totals, 0.0), axis=1, keepdims=True)
+
+    ref_power = pick(count * block + count)
+    weights = []
+    for f in range(count):
+        norm_product = jnp.sqrt((pick(count * block + f) + 1e-06) * (ref_power + 1e-06))
+        member = (lane >= f * block) & (lane < (f + 1) * block)
+        rho = jnp.where(member, totals, 0.0) / norm_product
+        squared = rho * rho
+        middle = jnp.where(lane == f * block + block // 2, 0.05, 0.0)
+        weights.append((squared + middle) / (0.05 + jnp.sum(squared, axis=1, keepdims=True)))
+    return weights
+
+
+def banded(weights, f, rows, first_row):
+    lane = lane_of(weights.shape)
     tiles = []
-    for member in (across < 4, across >= 4):
-        line = jnp.sum(jnp.where(member, spaced, 0.0), axis=0, keepdims=True)
-        tiles.append(by_row_shift(jnp.broadcast_to(line, (rows, lanes)), rows, 1))
+    for group in (range(4), range(4, reach)):
+        line = jnp.zeros_like(weights)
+        for j in group:
+            at = first_row + (j % 4) * slot
+            turned = pltpu.roll(weights, lax.rem(at + 2 * lanes - (f * reach + j) * reach, lanes), 1)
+            line = jnp.where((lane >= at) & (lane < at + reach), turned, line)
+        line = jnp.broadcast_to(line[0:1], (rows, lanes))
+        tiles.append(by_row_shift(line, rows, 1))
     return jnp.concatenate(tiles, axis=1)
 
 
 def pressure_kernel(base, parts, spread, inverse, pressure, moments, part):
     count, rows, columns = inverse.shape
-    start = 8 * count
     full = spread.shape[0] // 2
     first_row = 1 + base[0, 0]
-    ref_power = parts[start + count : start + count + 1, :]
-    bands = []
-    for f in range(count):
-        weights = blend_weights(parts[f * 8 : f * 8 + 8, :], parts[start + f : start + f + 1, :], ref_power)
-        bands.append(banded(weights, rows, first_row))
+    totals = jnp.broadcast_to(jnp.sum(parts[...], axis=0, keepdims=True), (8, lanes))
+    weights = blend_weights(totals, count)
+    bands = [banded(weights[f], f, rows, first_row) for f in range(count)]
     mixing = jnp.concatenate(halves(jnp.concatenate(bands, axis=0)), axis=0)
     chunk = 2 * lanes
     zero = jnp.zeros((8, lanes), jnp.float32)
@@ -349,9 +341,11 @@
         return tuple(totals)
 
     totals = by_tiles(step, columns // chunk, 8, (zero,) * (2 * count))
-    part[...] = jnp.zeros(part.shape, jnp.float32)
+    line = jnp.zeros((8, lanes), jnp.float32)
     for k in range(2 * count):
-        part[k : k + 1, :] = jnp.sum(totals[k], axis=0, keepdims=True)
+        value = jnp.sum(jnp.sum(totals[k], axis=0, keepdims=True), axis=1, keepdims=True)
+        line = line + jnp.where(lane_of(line.shape) == k, value, 0.0)
+    part[...] = jnp.broadcast_to(line[0:1], part.shape)
 
 
 def paired(value, axis, first):
@@ -371,25 +365,16 @@
 
 def from_owner(shard, odd, axis, root):
     mine = lax.axis_index(axis) == root
-    if lax.axis_size(axis) == 2:
-        halves_here = lax.optimization_barrier(by_parity(odd, shard, shard.shape[0] // 2, 0))
-        received = by_parity(odd, paired(shard, axis, 0), shard.shape[0] // 2, 0)
-        return [jnp.where(mine, own, other) for own, other in zip(halves_here, received)]
-    whole = lax.psum(jnp.where(mine, shard, jnp.zeros_like(shard)), axis)
-    return by_parity(odd, whole, shard.shape[0] // 2, 0)
-
-
-def total_over_rows(value, odd):
-    size = lax.axis_size("rows")
-    if size & (size - 1) or size < 2:
-        return lax.psum(value, "rows")
-    value = value + paired(value, "rows", 0)
-    step = 2
-    while step < size:
-        pairs = [(i, i ^ step if i % 2 else i) for i in range(size)]
-        value = value + lax.ppermute(value, "rows", pairs)
-        step *= 2
-    return jnp.where(odd, value, paired(value, "rows", 0))
+    height = shard.shape[0] // 2
+    if lax.axis_size(axis) != 2:
+        whole = lax.psum(jnp.where(mine, shard, jnp.zeros_like(shard)), axis)
+        return by_parity(odd, whole, height, 0)
+    here = lax.optimization_barrier(jnp.maximum(shard, 0.0))
+    odd_here, even_here = by_parity(odd, here, height, 0)
+    odd_there = paired(odd_here, axis, 0)
+    even_here, odd_there = lax.optimization_barrier((even_here, odd_there))
+    even_there = paired(even_here, axis, 0)
+    return jnp.where(mine, odd_here, odd_there), jnp.where(mine, even_here, even_there)
 
 
 def total_over(value, axis):
@@ -409,25 +394,15 @@
     ring = tiles + 2
     wide = rows + 8
     depth = reach * count * rows
+    size = lax.axis_size("rows")
     f32 = jnp.float32
     bf16 = jnp.bfloat16
     struct = functools.partial(jax.ShapeDtypeStruct, dtype=f32)
     odd = lax.axis_index("rows") % 2 == 1
     own_odd, own_even = from_owner(wind_off[0], odd, "frames", run_owner[0])
-    raw, frames_odd, frames_even, offsets = pl.pallas_call(
-        cut_kernel,
-        out_shape=(
-            struct((count, rows, columns)),
-            struct((count, 4, columns)),
-            struct((count, 4, columns)),
-            jax.ShapeDtypeStruct((1, 2), jnp.int32),
-        ),
-        in_specs=[pl.BlockSpec(memory_space=pl.ANY)] * 2,
-        out_specs=(vmem,) * 3 + (smem,),
-        scratch_shapes=[pltpu.SemaphoreType.DMA((count + 1,))],
-        compiler_params=params,
-        name="cut",
-    )(search_base, frames_raw)
+    raw = lax.optimization_barrier(jnp.maximum(frames_raw, 0.0))
+    offsets = jnp.clip(search_base, -8, 8)
+    frames_odd, frames_even = by_parity(odd, raw, 4, 1)
     frames_odd = paired(frames_odd, "rows", 1)
     frames_even = paired(frames_even, "rows", 0)
     from_even = paired(own_even, "rows", 0)
@@ -451,7 +426,7 @@
     )(raw, frames_odd, frames_even)
     clean, part = pl.pallas_call(
         match_kernel,
-        out_shape=(struct((tiles + 2, wide, lanes)), struct((8 * count + 8, lanes))),
+        out_shape=(struct((tiles + 2, wide, lanes)), struct((size, lanes))),
         in_specs=[smem] + [vmem] * 6,
         out_specs=(vmem, vmem),
         scratch_shapes=[
@@ -459,11 +434,12 @@
             pltpu.VMEM((tiles + 2, wide, lanes), f32),
             pltpu.VMEM((ring + 2, wide, lanes), f32),
             pltpu.VMEM((4 * slot, ring * lanes), bf16),
+            pltpu.VMEM((8 * count, lanes), f32),
         ],
         compiler_params=params,
         name="match",
     )(offsets, own_odd, own_even, from_odd, from_even, stack, power)
-    parts = total_over_rows(part, odd)
+    parts = lax.all_to_all(part, "rows", 0, 0, tiled=True)
     spread = pl.pallas_call(
         spread_kernel,
         out_shape=jax.ShapeDtypeStruct((2 * 8 * slot, columns), bf16),
@@ -474,15 +450,15 @@
     )(offsets, clean)
     pressure, moments, part = pl.pallas_call(
         pressure_kernel,
-        out_shape=(struct((count, rows, columns)), struct((2, rows, columns)), struct((8, lanes))),
+        out_shape=(struct((count, rows, columns)), struct((2, rows, columns)), struct((size, lanes))),
         in_specs=[smem] + [vmem] * 3,
         out_specs=(vmem, vmem, vmem),
         compiler_params=params,
         name="pressure",
     )(offsets, parts, spread, inverse)
     whole = total_over(moments, "frames")
-    spatial = jnp.sum(total_over_rows(part, odd), axis=1)
-    cell_count = rows * columns * lax.axis_size("rows")
+    spatial = jnp.sum(lax.all_to_all(part, "rows", 0, 0, tiled=True), axis=0)
+    cell_count = rows * columns * size
     frame_mean = spatial[:count] / cell_count
     frame_rms = jnp.sqrt(spatial[count : 2 * count] / cell_count - frame_mean * frame_mean)
     total_frames = count * lax.axis_size("frames")

time: 63.1 us -> 54.9 us (0.87)
  starting transfers between devices: 41.5 us -> 13.8 us
  blocking collectives: 0 us -> 9.69 us
  waiting for transfers between devices: 2.85 us -> 9.22 us
  local copies, waits for them, and re-layouts: 1.7 us -> 4.14 us
  other arithmetic: 2.74 us -> 4.37 us
    ppermute x9 -> x6, starting transfers between devices: 37 us -> 7.04 us  [paired(): return lax.ppermute(value, axis, list(enumerate(partner)))]
    all_to_all x0 -> x1, blocking collectives: none -> 9.69 us  [shards(): spatial = jnp.sum(lax.all_to_all(part, 'rows', 0, 0, tiled=True), axis=0)]
    all_to_all x0 -> x1, starting transfers between devices: none -> 6.27 us  [shards(): parts = lax.all_to_all(part, 'rows', 0, 0, tiled=True)]
    ppermute x6 -> x0, starting transfers between devices: 3.95 us -> none  [total_over_rows(): value = value + lax.ppermute(value, 'rows', pairs)]
    ppermute x1, waiting for transfers between devices: 0.01 us -> 2.78 us  [total_over(): lax.ppermute(value, axis, [(i, i ^ step) for i in range(size)])]
    all_to_all x0 -> x1, waiting for transfers between devices: none -> 2.51 us  [shards(): parts = lax.all_to_all(part, 'rows', 0, 0, tiled=True)]
    unnamed x4, local copies, waits for them, and re-layouts: 1.7 us -> 4.14 us
    max x0 -> x2, other arithmetic: none -> 2.05 us  [the longest x1 1.08 us: shards(): raw = lax.optimization_barrier(jnp.maximum(frames_raw, 0.0))]
  transfers between devices with their start and end apart: 16 -> 8, of which waited for: 3 -> 4; matrix products, arithmetic and copies ran while one was open for 3% -> 4% of each run, Pallas kernels for 10% -> 9%
where the time goes in v5:
time: 54.9 us; the launch traced here: 54.6 us
  starting transfers between devices  13.8 us (25%)
  Pallas kernels  11.9 us (22%)
  blocking collectives  9.69 us (18%)
  waiting for transfers between devices  9.22 us (17%)
  other arithmetic  4.37 us (8%)
  local copies, waits for them, and re-layouts  4.14 us (8%)
  between operations  1.41 us (3%)
    all_to_all x1, blocking collectives, shards(): spatial = jnp.sum(lax.all_to_all(part, 'rows', 0, 0, tiled=True), axis=0)  9.69 us
    ppermute x6, starting transfers between devices, paired(): return lax.ppermute(value, axis, list(enumerate(partner)))  7.04 us
    all_to_all x1, starting transfers between devices, shards(): parts = lax.all_to_all(part, 'rows', 0, 0, tiled=True)  6.27 us
    pallas_call x1, Pallas kernels, shards(): pl.pallas_call(match_kernel, out_shape=(struct((tiles + 2, wide, lanes)),...  4.33 us
    unnamed x4, local copies, waits for them, and re-layouts  4.14 us
    ppermute x6, waiting for transfers between devices, paired(): return lax.ppermute(value, axis, list(enumerate(partner)))  3.92 us
    pallas_call x1, Pallas kernels, shards(): pl.pallas_call(smooth_kernel, out_shape=(struct((count, rows, columns)),...  2.86 us
    pallas_call x1, Pallas kernels, shards(): pl.pallas_call(pressure_kernel, out_shape=(struct((count, rows, columns))...  2.85 us
  transfers between devices with their start and end apart: 8, of which 4 were waited for; matrix products, arithmetic and copies ran while one was open for 4% of the time, Pallas kernels for 9%

profile of v5, /device:TPU:0, one launch (start us, length us, event | category | flops | bytes accessed | tf_op | source)
XLA Modules:
  0.0 54.6 jit_solution(12803298400223310715)
XLA Ops:
  0.6 1.0 %maximum_bitcast_fusion = f32[16,4096]{1,0:T(8,128)S(1)} fusion(f32[1,16,4096]{2,1,0:T(8,128)} %param.5), kind=kLoop, calls=%fused_computation.8 | loop fusion | flops 65536 | bytes 524288 | tf_op jit(solution)/shard_map/max | solution.py:372
  1.6 3.0 %collective-permute-start = (f32[8,4096]{1,0:T(8,128)S(1)}, f32[8,4096]{1,0:T(8,128)S(1)}, u32[]{:S(2)}, u32[]{:S(2)}) collective-permute-start(f32[8,4096]{1,0:T(8,128)S(1)} %get-tuple-element.32), channel_id=1, source_target_pairs={{0,1},{1,0},{2,3},{3,2},{4,5},{5,4},{6,7},{7,6},{8,9},{9,8},{10,11... | collective-permute-start | bytes 393224 | tf_op jit(solution)/shard_map/ppermute | solution.py:356
  4.7 1.1 %broadcast_maximum_fusion.frames = f32[2,16,4096]{2,1,0:T(8,128)S(1)} fusion(f32[2,16,4096]{2,1,0:T(8,128)} %param.4), kind=kLoop, calls=%fused_computation.7 | loop fusion | flops 131072 | bytes 1048576 | tf_op jit(solution)/shard_map/max | solution.py:403
  5.8 0.1 collective-permute-start.5
  5.9 0.7 %collective-permute-start.4 = (f32[2,4,4096]{2,1,0:T(4,128)S(1)}, f32[2,4,4096]{2,1,0:T(4,128)S(1)}, u32[]{:S(2)}, u32[]{:S(2)}) collective-permute-start(f32[2,4,4096]{2,1,0:T(4,128)S(1)} %get-tuple-element.30), channel_id=1, source_target_pairs={{0,0},{2,4},{4,2},{6,8},{8,6},{10,12},{12,10},{14,16},{16,14},{18,... | collective-permute-start | bytes 393224 | tf_op jit(solution)/shard_map/ppermute | solution.py:356
  7.2 1.0 %collective-permute-done = f32[8,4096]{1,0:T(8,128)S(1)} collective-permute-done((f32[8,4096]{1,0:T(8,128)S(1)}, f32[8,4096]{1,0:T(8,128)S(1)}, u32[]{:S(2)}, u32[]{:S(2)}) %collective-permute-start) | collective-permute-done | bytes 131104 | tf_op jit(solution)/shard_map/ppermute | solution.py:356
  8.2 1.7 %collective-permute-start.1 = (f32[8,4096]{1,0:T(8,128)S(1)}, f32[8,4096]{1,0:T(8,128)S(1)}, u32[]{:S(2)}, u32[]{:S(2)}) collective-permute-start(f32[8,4096]{1,0:T(8,128)S(1)} %get-tuple-element.16), channel_id=1, source_target_pairs={{0,1},{1,0},{2,3},{3,2},{4,5},{5,4},{6,7},{7,6},{8,9},{9,8},{10,11... | collective-permute-start | bytes 393224 | tf_op jit(solution)/shard_map/ppermute | solution.py:356
  9.9 0.7 %collective-permute-start.2 = (f32[8,4096]{1,0:T(8,128)S(1)}, f32[8,4096]{1,0:T(8,128)S(1)}, u32[]{:S(2)}, u32[]{:S(2)}) collective-permute-start(f32[8,4096]{1,0:T(8,128)S(1)} %broadcast_select_fusion.1.own_odd), channel_id=1, source_target_pairs={{0,0},{2,4},{4,2},{6,8},{8,6},{10,12},{12,10},{14,16},{16,14},{18,... | collective-permute-start | bytes 393224 | tf_op jit(solution)/shard_map/ppermute | solution.py:356
  10.6 3.0 %collective-permute-done.1 = f32[8,4096]{1,0:T(8,128)S(1)} collective-permute-done((f32[8,4096]{1,0:T(8,128)S(1)}, f32[8,4096]{1,0:T(8,128)S(1)}, u32[]{:S(2)}, u32[]{:S(2)}) %collective-permute-start.1) | collective-permute-done | bytes 131104 | tf_op jit(solution)/shard_map/ppermute | solution.py:356
  13.6 0.9 %collective-permute-start.3 = (f32[8,4096]{1,0:T(8,128)S(1)}, f32[8,4096]{1,0:T(8,128)S(1)}, u32[]{:S(2)}, u32[]{:S(2)}) collective-permute-start(f32[8,4096]{1,0:T(8,128)S(1)} %broadcast_select_fusion.own_even), channel_id=1, source_target_pairs={{0,2},{2,0},{4,6},{6,4},{8,10},{10,8},{12,14},{14,12},{16,18},{18,... | collective-permute-start | bytes 393224 | tf_op jit(solution)/shard_map/ppermute | solution.py:356
  14.5 0.7 %broadcast_clamp_fusion.base = s32[1,2]{1,0:T(1,128)S(1)} fusion(s32[1,2]{1,0:T(1,128)} %param.7), kind=kLoop, calls=%fused_computation.17 | loop fusion | flops 2 | bytes 16 | tf_op jit(solution)/shard_map/jit(clip)/min | solution.py:404
  15.1 2.9 %smooth.1 = (f32[2,16,4096]{2,1,0:T(8,128)S(1)}, bf16[448,4352]{1,0:T(8,128)(2,1)S(1)}, f32[16,128]{1,0:T(8,128)S(1)}) custom-call(f32[2,16,4096]{2,1,0:T(8,128)S(1)} %broadcast_maximum_fusion.frames, f32[2,4,4096]{2,1,0:T(4,128)S(1)} %collective-permute-done.4.from_odd, f32[2,4,4096]{2,1,0:T(4,128)S(1)} %collective-permute-done.5.from_even), custom_call_target="tpu_custom_call" | custom-call | tf_op jit(solution)/shard_map/smooth/pallas_call | solution.py:410
  18.0 4.3 %match.1 = (f32[34,24,128]{2,1,0:T(8,128)S(1)}, f32[16,128]{1,0:T(8,128)}) custom-call(s32[1,2]{1,0:T(1,128)S(1)} %broadcast_clamp_fusion.base, f32[8,4096]{1,0:T(8,128)S(1)} %broadcast_select_fusion.1.own_odd, f32[8,4096]{1,0:T(8,128)S(1)} %broadcast_select_fusion.own_even, f32[8,4096]{1,0:T(8,128)S(1)} %collective-permute-done.2.from_odd, ...), custom_call_target="tpu_custom_call" | custom-call | tf_op jit(solution)/shard_map/match/pallas_call | solution.py:427
  22.3 6.3 %all-to-all-start = ((f32[16,1,128]{2,1,0:T(1,128)}), f32[16,1,128]{2,1,0:T(1,128)S(1)}, u32[]{:S(2)}, u32[]{:S(2)}) async-start(f32[16,1,128]{2,1,0:T(1,128)} %bitcast.3), calls=%async_computation | async-start | bytes 16384 | tf_op jit(solution)/shard_map/all_to_all | solution.py:442
  28.6 1.9 %spread.1 = bf16[512,4096]{1,0:T(8,128)(2,1)S(1)} custom-call(s32[1,2]{1,0:T(1,128)S(1)} %broadcast_clamp_fusion.base, f32[34,24,128]{2,1,0:T(8,128)S(1)} %get-tuple-element.20.clean), custom_call_target="tpu_custom_call" | custom-call | tf_op jit(solution)/shard_map/spread/pallas_call | solution.py:443
  30.5 1.9 %copy-done = bf16[512,4096]{1,0:T(8,128)(2,1)} copy-done((bf16[512,4096]{1,0:T(8,128)(2,1)}, bf16[512,4096]{1,0:T(8,128)(2,1)S(1)}, u32[]{:S(2)}) %copy-start) | copy-done | bytes 4194328
  32.4 2.5 %all-to-all-done = f32[16,1,128]{2,1,0:T(1,128)S(1)} async-done(((f32[16,1,128]{2,1,0:T(1,128)}), f32[16,1,128]{2,1,0:T(1,128)S(1)}, u32[]{:S(2)}, u32[]{:S(2)}) %all-to-all-start) | async-done | bytes 8224 | tf_op jit(solution)/shard_map/all_to_all | solution.py:442
  35.0 2.2 %copy-done.1 = bf16[512,4096]{1,0:T(8,128)(2,1)S(1)} copy-done((bf16[512,4096]{1,0:T(8,128)(2,1)S(1)}, bf16[512,4096]{1,0:T(8,128)(2,1)}, u32[]{:S(2)}) %copy-start.1) | copy-done | bytes 4194328
  37.1 2.9 %pressure.1 = (f32[2,16,4096]{2,1,0:T(8,128)}, f32[2,16,4096]{2,1,0:T(8,128)S(1)}, f32[16,128]{1,0:T(8,128)S(1)}) custom-call(s32[1,2]{1,0:T(1,128)S(1)} %broadcast_clamp_fusion.base, f32[16,128]{1,0:T(8,128)S(1)} %bitcast.22, bf16[512,4096]{1,0:T(8,128)(2,1)S(1)} %copy-done.1, f32[2,16,4096]{2,1,0:T(8,128)S(1)} %get-tuple-element.21.inverse), custom_call_target="tpu_custom_call" | custom-call | tf_op jit(solution)/shard_map/pressure/pallas_call | solution.py:451
  40.0 0.5 collective-permute-start.6
  40.5 9.7 %all_to_all.20 = f32[16,1,128]{2,1,0:T(1,128)S(1)} all-to-all(f32[16,1,128]{2,1,0:T(1,128)S(1)} %bitcast.23), channel_id=1, replica_groups=mesh['rows'=16,'frames'=2] {'rows'}, dimensions={0} | all-to-all | bytes 16384 | tf_op jit(solution)/shard_map/all_to_all | solution.py:460
  50.2 0.6 %subtract_sqrt_fusion = (f32[2]{0:T(128)}, f32[2]{0:T(128)}) fusion(f32[128]{0:T(128)S(1)} %reduce_sum.9), kind=kLoop, calls=%fused_computation.15 | loop fusion | flops 8 | bytes 32 | tf_op jit(solution)/shard_map/sqrt | solution.py:463
  50.8 2.8 %collective-permute-done.6 = f32[2,16,4096]{2,1,0:T(8,128)S(1)} collective-permute-done((f32[2,16,4096]{2,1,0:T(8,128)S(1)}, f32[2,16,4096]{2,1,0:T(8,128)S(1)}, u32[]{:S(2)}, u32[]{:S(2)}) %collective-permute-start.6) | collective-permute-done | bytes 524320 | tf_op jit(solution)/shard_map/ppermute | solution.py:386
  53.7 0.9 %fusion.3 = (f32[16,4096]{1,0:T(8,128)}, f32[16,4096]{1,0:T(8,128)}) fusion(f32[2,16,4096]{2,1,0:T(8,128)S(1)} %add.8), kind=kLoop, calls=%fused_computation.4 | loop fusion | flops 327680 | bytes 1048576 | tf_op jit(solution)/shard_map/sqrt | solution.py:466
  (12 shorter events, 0.2 us)
Async XLA Ops:
  1.6 6.5 %collective-permute-start = (f32[8,4096]{1,0:T(8,128)S(1)}, f32[8,4096]{1,0:T(8,128)S(1)}, u32[]{:S(2)}, u32[]{:S(2)}) collective-permute-start(f32[8,4096]{1,0:T(8,128)S(1)} %get-tuple-element.32), channel_id=1, source_target_pairs={{0,1},{1,0},{2,3},{3,2},{4,5},{5,4},{6,7},{7,6},{8,9},{9,8},{10,11... | collective-permute-start | bytes 393224 | tf_op jit(solution)/shard_map/ppermute | solution.py:356
  5.8 9.3 %collective-permute-start.5 = (f32[2,4,4096]{2,1,0:T(4,128)S(1)}, f32[2,4,4096]{2,1,0:T(4,128)S(1)}, u32[]{:S(2)}, u32[]{:S(2)}) collective-permute-start(f32[2,4,4096]{2,1,0:T(4,128)S(1)} %get-tuple-element.29), channel_id=1, source_target_pairs={{0,2},{2,0},{4,6},{6,4},{8,10},{10,8},{12,14},{14,12},{16,18},{18,... | collective-permute-start | bytes 393224 | tf_op jit(solution)/shard_map/ppermute | solution.py:356
  5.9 9.2 %collective-permute-start.4 = (f32[2,4,4096]{2,1,0:T(4,128)S(1)}, f32[2,4,4096]{2,1,0:T(4,128)S(1)}, u32[]{:S(2)}, u32[]{:S(2)}) collective-permute-start(f32[2,4,4096]{2,1,0:T(4,128)S(1)} %get-tuple-element.30), channel_id=1, source_target_pairs={{0,0},{2,4},{4,2},{6,8},{8,6},{10,12},{12,10},{14,16},{16,14},{18,... | collective-permute-start | bytes 393224 | tf_op jit(solution)/shard_map/ppermute | solution.py:356
  8.2 5.4 %collective-permute-start.1 = (f32[8,4096]{1,0:T(8,128)S(1)}, f32[8,4096]{1,0:T(8,128)S(1)}, u32[]{:S(2)}, u32[]{:S(2)}) collective-permute-start(f32[8,4096]{1,0:T(8,128)S(1)} %get-tuple-element.16), channel_id=1, source_target_pairs={{0,1},{1,0},{2,3},{3,2},{4,5},{5,4},{6,7},{7,6},{8,9},{9,8},{10,11... | collective-permute-start | bytes 393224 | tf_op jit(solution)/shard_map/ppermute | solution.py:356
  9.9 8.1 %collective-permute-start.2 = (f32[8,4096]{1,0:T(8,128)S(1)}, f32[8,4096]{1,0:T(8,128)S(1)}, u32[]{:S(2)}, u32[]{:S(2)}) collective-permute-start(f32[8,4096]{1,0:T(8,128)S(1)} %broadcast_select_fusion.1.own_odd), channel_id=1, source_target_pairs={{0,0},{2,4},{4,2},{6,8},{8,6},{10,12},{12,10},{14,16},{16,14},{18,... | collective-permute-start | bytes 393224 | tf_op jit(solution)/shard_map/ppermute | solution.py:356
  13.6 4.4 %collective-permute-start.3 = (f32[8,4096]{1,0:T(8,128)S(1)}, f32[8,4096]{1,0:T(8,128)S(1)}, u32[]{:S(2)}, u32[]{:S(2)}) collective-permute-start(f32[8,4096]{1,0:T(8,128)S(1)} %broadcast_select_fusion.own_even), channel_id=1, source_target_pairs={{0,2},{2,0},{4,6},{6,4},{8,10},{10,8},{12,14},{14,12},{16,18},{18,... | collective-permute-start | bytes 393224 | tf_op jit(solution)/shard_map/ppermute | solution.py:356
  22.3 12.6 %all-to-all-start = ((f32[16,1,128]{2,1,0:T(1,128)}), f32[16,1,128]{2,1,0:T(1,128)S(1)}, u32[]{:S(2)}, u32[]{:S(2)}) async-start(f32[16,1,128]{2,1,0:T(1,128)} %bitcast.3), calls=%async_computation | async-start | bytes 16384 | tf_op jit(solution)/shard_map/all_to_all | solution.py:442
  30.5 2.0 %copy-start = (bf16[512,4096]{1,0:T(8,128)(2,1)}, bf16[512,4096]{1,0:T(8,128)(2,1)S(1)}, u32[]{:S(2)}) copy-start(bf16[512,4096]{1,0:T(8,128)(2,1)S(1)} %spread.1) | copy-start | bytes 12582916
  35.0 2.2 %copy-start.1 = (bf16[512,4096]{1,0:T(8,128)(2,1)S(1)}, bf16[512,4096]{1,0:T(8,128)(2,1)}, u32[]{:S(2)}) copy-start(bf16[512,4096]{1,0:T(8,128)(2,1)} %copy-done) | copy-start | bytes 12582916
  40.0 13.6 %collective-permute-start.6 = (f32[2,16,4096]{2,1,0:T(8,128)S(1)}, f32[2,16,4096]{2,1,0:T(8,128)S(1)}, u32[]{:S(2)}, u32[]{:S(2)}) collective-permute-start(f32[2,16,4096]{2,1,0:T(8,128)S(1)} %get-tuple-element.24), channel_id=1, source_target_pairs={{0,1},{1,0},{2,3},{3,2},{4,5},{5,4},{6,7},{7,6},{8,9},{9,8},{10,11... | collective-permute-start | bytes 1572872 | tf_op jit(solution)/shard_map/ppermute | solution.py:386

commit v6 on v5

--- a/solution.py
+++ b/solution.py
@@ -14,7 +14,7 @@
 lanes = 128
 reach = 7
 slot = 32
-params = pltpu.CompilerParams(vmem_limit_bytes=24 * 1024 * 1024)
+params = pltpu.CompilerParams(vmem_limit_bytes=14 * 1024 * 1024)
 vmem = pl.BlockSpec(memory_space=pltpu.VMEM)
 smem = pl.BlockSpec(memory_space=pltpu.SMEM)
 
@@ -150,7 +150,7 @@
     negative = offset < 0
     first = jnp.where(negative, 0, 1)
     amount = jnp.where(negative, offset + lanes, offset)
-    back = lax.rem(lanes - amount, lanes)
+    back = (lanes - amount) & (lanes - 1)
 
     def shift(source, t):
         here = source[t + first]
@@ -239,8 +239,8 @@
         block = lags[f * 8 : f * 8 + 8, :]
         for j in range(reach):
             at = (f * reach + j) * reach
-            high = pltpu.roll(block, lax.rem(back + at, lanes), 1)
-            low = pltpu.roll(block, lax.rem(back + at + lanes - slot, lanes), 1)
+            high = pltpu.roll(block, (back + at) & (lanes - 1), 1)
+            low = pltpu.roll(block, (back + at - slot) & (lanes - 1), 1)
             packed = packed + jnp.where((across == j) & (lane >= at) & (lane < at + reach), high + low, 0.0)
     lags[0:8, :] = jnp.zeros((8, lanes), jnp.float32)
     for f in range(count):
@@ -300,7 +300,7 @@
         line = jnp.zeros_like(weights)
         for j in group:
             at = first_row + (j % 4) * slot
-            turned = pltpu.roll(weights, lax.rem(at + 2 * lanes - (f * reach + j) * reach, lanes), 1)
+            turned = pltpu.roll(weights, (at + 2 * lanes - (f * reach + j) * reach) & (lanes - 1), 1)
             line = jnp.where((lane >= at) & (lane < at + reach), turned, line)
         line = jnp.broadcast_to(line[0:1], (rows, lanes))
         tiles.append(by_row_shift(line, rows, 1))
@@ -399,13 +399,13 @@
     bf16 = jnp.bfloat16
     struct = functools.partial(jax.ShapeDtypeStruct, dtype=f32)
     odd = lax.axis_index("rows") % 2 == 1
-    own_odd, own_even = from_owner(wind_off[0], odd, "frames", run_owner[0])
     raw = lax.optimization_barrier(jnp.maximum(frames_raw, 0.0))
     offsets = jnp.clip(search_base, -8, 8)
     frames_odd, frames_even = by_parity(odd, raw, 4, 1)
+    frames_odd, run = lax.optimization_barrier((frames_odd, wind_off[0]))
     frames_odd = paired(frames_odd, "rows", 1)
     frames_even = paired(frames_even, "rows", 0)
-    from_even = paired(own_even, "rows", 0)
+    own_odd, own_even = from_owner(run, odd, "frames", run_owner[0])
     from_odd = paired(own_odd, "rows", 1)
     inverse, stack, power = pl.pallas_call(
         smooth_kernel,
@@ -424,6 +424,8 @@
         compiler_params=params,
         name="smooth",
     )(raw, frames_odd, frames_even)
+    own_even, power = lax.optimization_barrier((own_even, power))
+    from_even = paired(own_even, "rows", 0)
     clean, part = pl.pallas_call(
         match_kernel,
         out_shape=(struct((tiles + 2, wide, lanes)), struct((size, lanes))),

time: 54.9 us -> 54.3 us (0.989)
  starting transfers between devices: 13.8 us -> 16.5 us
  waiting for transfers between devices: 9.22 us -> 6.6 us
  other arithmetic: 4.37 us -> 3.73 us
    ppermute x6, starting transfers between devices: 7.04 us -> 10.3 us  [paired(): return lax.ppermute(value, axis, list(enumerate(partner)))]
    ppermute x6, waiting for transfers between devices: 3.92 us -> 1.88 us  [paired(): return lax.ppermute(value, axis, list(enumerate(partner)))]
    all_to_all x1, starting transfers between devices: 6.27 us -> 5.1 us  [shards(): parts = lax.all_to_all(part, 'rows', 0, 0, tiled=True)]
    min x1, other arithmetic: 0.66 us -> 0.01 us  [shards(): offsets = jnp.clip(search_base, -8, 8)]
    ppermute x1, starting transfers between devices: 0.51 us -> 1.15 us  [total_over(): lax.ppermute(value, axis, [(i, i ^ step) for i in range(size)])]
    ppermute x1, waiting for transfers between devices: 2.78 us -> 2.17 us  [total_over(): lax.ppermute(value, axis, [(i, i ^ step) for i in range(size)])]
    unnamed x4 -> x6, local copies, waits for them, and re-layouts: 4.14 us -> 4.15 us
  transfers between devices with their start and end apart: 8 -> 8, of which waited for: 4 -> 4; matrix products, arithmetic and copies ran while one was open for 4% -> 1% of each run, Pallas kernels for 9% -> 9%
where the time goes in v6:
time: 54.3 us; the launch traced here: 53.9 us
  starting transfers between devices  16.5 us (30%)
  Pallas kernels  11.8 us (22%)
  blocking collectives  9.66 us (18%)
  waiting for transfers between devices  6.6 us (12%)
  local copies, waits for them, and re-layouts  4.15 us (8%)
  other arithmetic  3.73 us (7%)
  between operations  1.42 us (3%)
    ppermute x6, starting transfers between devices, paired(): return lax.ppermute(value, axis, list(enumerate(partner)))  10.3 us
    all_to_all x1, blocking collectives, shards(): spatial = jnp.sum(lax.all_to_all(part, 'rows', 0, 0, tiled=True), axis=0)  9.66 us
    all_to_all x1, starting transfers between devices, shards(): parts = lax.all_to_all(part, 'rows', 0, 0, tiled=True)  5.1 us
    pallas_call x1, Pallas kernels, shards(): pl.pallas_call(match_kernel, out_shape=(struct((tiles + 2, wide, lanes)),...  4.32 us
    unnamed x6, local copies, waits for them, and re-layouts  4.15 us
    pallas_call x1, Pallas kernels, shards(): pl.pallas_call(smooth_kernel, out_shape=(struct((count, rows, columns)),...  2.86 us
    pallas_call x1, Pallas kernels, shards(): pl.pallas_call(pressure_kernel, out_shape=(struct((count, rows, columns))...  2.85 us
    all_to_all x1, waiting for transfers between devices, shards(): parts = lax.all_to_all(part, 'rows', 0, 0, tiled=True)  2.54 us
  transfers between devices with their start and end apart: 8, of which 4 were waited for; matrix products, arithmetic and copies ran while one was open for 1% of the time, Pallas kernels for 9%

profile of v6, /device:TPU:0, one launch (start us, length us, event | category | flops | bytes accessed | tf_op | source)
XLA Modules:
  0.0 53.9 jit_solution(17029311015862921056)
XLA Ops:
  0.7 1.1 %broadcast_maximum_fusion.frames = f32[2,16,4096]{2,1,0:T(8,128)S(1)} fusion(f32[2,16,4096]{2,1,0:T(8,128)} %param.4), kind=kLoop, calls=%fused_computation.7 | loop fusion | flops 131072 | bytes 1048576 | tf_op jit(solution)/shard_map/max | solution.py:402
  1.8 1.0 %broadcast_maximum_fusion.1 = f32[16,4096]{1,0:T(8,128)S(1)} fusion(f32[16,4096]{1,0:T(8,128)} %bitcast.23), kind=kLoop, calls=%fused_computation.8 | loop fusion | flops 65536 | bytes 524288 | tf_op jit(solution)/shard_map/max | solution.py:372
  2.8 3.0 %collective-permute-start = (f32[8,4096]{1,0:T(8,128)S(1)}, f32[8,4096]{1,0:T(8,128)S(1)}, u32[]{:S(2)}, u32[]{:S(2)}) collective-permute-start(f32[8,4096]{1,0:T(8,128)S(1)} %get-tuple-element.40), channel_id=1, source_target_pairs={{0,1},{1,0},{2,3},{3,2},{4,5},{5,4},{6,7},{7,6},{8,9},{9,8},{10,11... | collective-permute-start | bytes 393224 | tf_op jit(solution)/shard_map/ppermute | solution.py:356
  5.8 0.7 %collective-permute-start.2 = (f32[2,4,4096]{2,1,0:T(4,128)S(1)}, f32[2,4,4096]{2,1,0:T(4,128)S(1)}, u32[]{:S(2)}, u32[]{:S(2)}) collective-permute-start(f32[2,4,4096]{2,1,0:T(4,128)S(1)} %get-tuple-element.22), channel_id=1, source_target_pairs={{0,0},{2,4},{4,2},{6,8},{8,6},{10,12},{12,10},{14,16},{16,14},{18,... | collective-permute-start | bytes 393224 | tf_op jit(solution)/shard_map/ppermute | solution.py:356
  6.5 2.9 %collective-permute-start.3 = (f32[2,4,4096]{2,1,0:T(4,128)S(1)}, f32[2,4,4096]{2,1,0:T(4,128)S(1)}, u32[]{:S(2)}, u32[]{:S(2)}) collective-permute-start(f32[2,4,4096]{2,1,0:T(4,128)S(1)} %get-tuple-element.37), channel_id=1, source_target_pairs={{0,2},{2,0},{4,6},{6,4},{8,10},{10,8},{12,14},{14,12},{16,18},{18,... | collective-permute-start | bytes 393224 | tf_op jit(solution)/shard_map/ppermute | solution.py:356
  10.1 1.0 %collective-permute-start.1 = (f32[8,4096]{1,0:T(8,128)S(1)}, f32[8,4096]{1,0:T(8,128)S(1)}, u32[]{:S(2)}, u32[]{:S(2)}) collective-permute-start(f32[8,4096]{1,0:T(8,128)S(1)} %get-tuple-element.21), channel_id=1, source_target_pairs={{0,1},{1,0},{2,3},{3,2},{4,5},{5,4},{6,7},{7,6},{8,9},{9,8},{10,11... | collective-permute-start | bytes 393224 | tf_op jit(solution)/shard_map/ppermute | solution.py:356
  11.1 0.7 %collective-permute-start.4 = (f32[8,4096]{1,0:T(8,128)S(1)}, f32[8,4096]{1,0:T(8,128)S(1)}, u32[]{:S(2)}, u32[]{:S(2)}) collective-permute-start(f32[8,4096]{1,0:T(8,128)S(1)} %broadcast_select_fusion.1.own_odd), channel_id=1, source_target_pairs={{0,0},{2,4},{4,2},{6,8},{8,6},{10,12},{12,10},{14,16},{16,14},{18,... | collective-permute-start | bytes 393224 | tf_op jit(solution)/shard_map/ppermute | solution.py:356
  11.8 2.9 %smooth.1 = (f32[2,16,4096]{2,1,0:T(8,128)S(1)}, bf16[448,4352]{1,0:T(8,128)(2,1)S(1)}, f32[16,128]{1,0:T(8,128)S(1)}) custom-call(f32[2,16,4096]{2,1,0:T(8,128)S(1)} %broadcast_maximum_fusion.frames, f32[2,4,4096]{2,1,0:T(4,128)S(1)} %collective-permute-done.2.from_odd, f32[2,4,4096]{2,1,0:T(4,128)S(1)} %collective-permute-done.3.from_even), custom_call_target="tpu_custom_call" | custom-call | tf_op jit(solution)/shard_map/smooth/pallas_call | solution.py:410
  14.7 0.9 %collective-permute-done.1 = f32[8,4096]{1,0:T(8,128)S(1)} collective-permute-done((f32[8,4096]{1,0:T(8,128)S(1)}, f32[8,4096]{1,0:T(8,128)S(1)}, u32[]{:S(2)}, u32[]{:S(2)}) %collective-permute-start.1) | collective-permute-done | bytes 131104 | tf_op jit(solution)/shard_map/ppermute | solution.py:356
  15.6 2.0 %collective-permute-start.5 = (f32[8,4096]{1,0:T(8,128)S(1)}, f32[8,4096]{1,0:T(8,128)S(1)}, u32[]{:S(2)}, u32[]{:S(2)}) collective-permute-start(f32[8,4096]{1,0:T(8,128)S(1)} %broadcast_select_fusion.own_even), channel_id=1, source_target_pairs={{0,2},{2,0},{4,6},{6,4},{8,10},{10,8},{12,14},{14,12},{16,18},{18,... | collective-permute-start | bytes 393224 | tf_op jit(solution)/shard_map/ppermute | solution.py:356
  17.6 1.0 %collective-permute-done.5.from_even = f32[8,4096]{1,0:T(8,128)S(1)} collective-permute-done((f32[8,4096]{1,0:T(8,128)S(1)}, f32[8,4096]{1,0:T(8,128)S(1)}, u32[]{:S(2)}, u32[]{:S(2)}) %collective-permute-start.5) | collective-permute-done | bytes 131104 | tf_op jit(solution)/shard_map/ppermute | solution.py:356
  18.6 4.3 %match.1 = (f32[34,24,128]{2,1,0:T(8,128)S(1)}, f32[16,128]{1,0:T(8,128)}) custom-call(s32[1,2]{1,0:T(1,128)S(1)} %broadcast_clamp_fusion.base, f32[8,4096]{1,0:T(8,128)S(1)} %broadcast_select_fusion.1.own_odd, f32[8,4096]{1,0:T(8,128)S(1)} %broadcast_select_fusion.own_even, f32[8,4096]{1,0:T(8,128)S(1)} %collective-permute-done.4.from_odd, ...), custom_call_target="tpu_custom_call" | custom-call | tf_op jit(solution)/shard_map/match/pallas_call | solution.py:429
  22.9 5.1 %all-to-all-start = ((f32[16,1,128]{2,1,0:T(1,128)}), f32[16,1,128]{2,1,0:T(1,128)S(1)}, u32[]{:S(2)}, u32[]{:S(2)}) async-start(f32[16,1,128]{2,1,0:T(1,128)} %bitcast.3), calls=%async_computation | async-start | bytes 16384 | tf_op jit(solution)/shard_map/all_to_all | solution.py:444
  28.0 1.8 %spread.1 = bf16[512,4096]{1,0:T(8,128)(2,1)S(1)} custom-call(s32[1,2]{1,0:T(1,128)S(1)} %broadcast_clamp_fusion.base, f32[34,24,128]{2,1,0:T(8,128)S(1)} %get-tuple-element.28.clean), custom_call_target="tpu_custom_call" | custom-call | tf_op jit(solution)/shard_map/spread/pallas_call | solution.py:445
  29.8 2.0 %copy-done = bf16[512,4096]{1,0:T(8,128)(2,1)} copy-done((bf16[512,4096]{1,0:T(8,128)(2,1)}, bf16[512,4096]{1,0:T(8,128)(2,1)S(1)}, u32[]{:S(2)}) %copy-start) | copy-done | bytes 4194328
  31.8 2.5 %all-to-all-done = f32[16,1,128]{2,1,0:T(1,128)S(1)} async-done(((f32[16,1,128]{2,1,0:T(1,128)}), f32[16,1,128]{2,1,0:T(1,128)S(1)}, u32[]{:S(2)}, u32[]{:S(2)}) %all-to-all-start) | async-done | bytes 8224 | tf_op jit(solution)/shard_map/all_to_all | solution.py:444
  34.3 2.2 %copy-done.1 = bf16[512,4096]{1,0:T(8,128)(2,1)S(1)} copy-done((bf16[512,4096]{1,0:T(8,128)(2,1)S(1)}, bf16[512,4096]{1,0:T(8,128)(2,1)}, u32[]{:S(2)}) %copy-start.1) | copy-done | bytes 4194328
  36.5 2.9 %pressure.1 = (f32[2,16,4096]{2,1,0:T(8,128)}, f32[2,16,4096]{2,1,0:T(8,128)S(1)}, f32[16,128]{1,0:T(8,128)S(1)}) custom-call(s32[1,2]{1,0:T(1,128)S(1)} %broadcast_clamp_fusion.base, f32[16,128]{1,0:T(8,128)S(1)} %bitcast.21, bf16[512,4096]{1,0:T(8,128)(2,1)S(1)} %copy-done.1, f32[2,16,4096]{2,1,0:T(8,128)S(1)} %get-tuple-element.29.inverse), custom_call_target="tpu_custom_call" | custom-call | tf_op jit(solution)/shard_map/pressure/pallas_call | solution.py:453
  39.4 1.1 %collective-permute-start.6 = (f32[2,16,4096]{2,1,0:T(8,128)S(1)}, f32[2,16,4096]{2,1,0:T(8,128)S(1)}, u32[]{:S(2)}, u32[]{:S(2)}) collective-permute-start(f32[2,16,4096]{2,1,0:T(8,128)S(1)} %get-tuple-element.32), channel_id=1, source_target_pairs={{0,1},{1,0},{2,3},{3,2},{4,5},{5,4},{6,7},{7,6},{8,9},{9,8},{10,11... | collective-permute-start | bytes 1572872 | tf_op jit(solution)/shard_map/ppermute | solution.py:386
  40.5 9.7 %all_to_all.20 = f32[16,1,128]{2,1,0:T(1,128)S(1)} all-to-all(f32[16,1,128]{2,1,0:T(1,128)S(1)} %bitcast.22), channel_id=1, replica_groups=mesh['rows'=16,'frames'=2] {'rows'}, dimensions={0} | all-to-all | bytes 16384 | tf_op jit(solution)/shard_map/all_to_all | solution.py:462
  50.2 0.6 %subtract_sqrt_fusion = (f32[2]{0:T(128)}, f32[2]{0:T(128)}) fusion(f32[128]{0:T(128)S(1)} %reduce_sum.9), kind=kLoop, calls=%fused_computation.15 | loop fusion | flops 8 | bytes 32 | tf_op jit(solution)/shard_map/sqrt | solution.py:465
  50.8 2.2 %collective-permute-done.6 = f32[2,16,4096]{2,1,0:T(8,128)S(1)} collective-permute-done((f32[2,16,4096]{2,1,0:T(8,128)S(1)}, f32[2,16,4096]{2,1,0:T(8,128)S(1)}, u32[]{:S(2)}, u32[]{:S(2)}) %collective-permute-start.6) | collective-permute-done | bytes 524320 | tf_op jit(solution)/shard_map/ppermute | solution.py:386
  53.0 0.1 add.8
  53.1 0.9 %fusion.3 = (f32[16,4096]{1,0:T(8,128)}, f32[16,4096]{1,0:T(8,128)}) fusion(f32[2,16,4096]{2,1,0:T(8,128)S(1)} %add.8), kind=kLoop, calls=%fused_computation.4 | loop fusion | flops 327680 | bytes 1048576 | tf_op jit(solution)/shard_map/sqrt | solution.py:468
  (14 shorter events, 0.2 us)
Async XLA Ops:
  0.6 17.0 %copy-start.2 = (s32[1,2]{1,0:T(1,128)S(1)}, s32[1,2]{1,0:T(1,128)}, u32[]{:S(2)}) copy-start(s32[1,2]{1,0:T(1,128)} %param.7) | copy-start | bytes 28
  2.8 7.3 %collective-permute-start = (f32[8,4096]{1,0:T(8,128)S(1)}, f32[8,4096]{1,0:T(8,128)S(1)}, u32[]{:S(2)}, u32[]{:S(2)}) collective-permute-start(f32[8,4096]{1,0:T(8,128)S(1)} %get-tuple-element.40), channel_id=1, source_target_pairs={{0,1},{1,0},{2,3},{3,2},{4,5},{5,4},{6,7},{7,6},{8,9},{9,8},{10,11... | collective-permute-start | bytes 393224 | tf_op jit(solution)/shard_map/ppermute | solution.py:356
  5.8 5.9 %collective-permute-start.2 = (f32[2,4,4096]{2,1,0:T(4,128)S(1)}, f32[2,4,4096]{2,1,0:T(4,128)S(1)}, u32[]{:S(2)}, u32[]{:S(2)}) collective-permute-start(f32[2,4,4096]{2,1,0:T(4,128)S(1)} %get-tuple-element.22), channel_id=1, source_target_pairs={{0,0},{2,4},{4,2},{6,8},{8,6},{10,12},{12,10},{14,16},{16,14},{18,... | collective-permute-start | bytes 393224 | tf_op jit(solution)/shard_map/ppermute | solution.py:356
  6.5 5.3 %collective-permute-start.3 = (f32[2,4,4096]{2,1,0:T(4,128)S(1)}, f32[2,4,4096]{2,1,0:T(4,128)S(1)}, u32[]{:S(2)}, u32[]{:S(2)}) collective-permute-start(f32[2,4,4096]{2,1,0:T(4,128)S(1)} %get-tuple-element.37), channel_id=1, source_target_pairs={{0,2},{2,0},{4,6},{6,4},{8,10},{10,8},{12,14},{14,12},{16,18},{18,... | collective-permute-start | bytes 393224 | tf_op jit(solution)/shard_map/ppermute | solution.py:356
  10.1 5.5 %collective-permute-start.1 = (f32[8,4096]{1,0:T(8,128)S(1)}, f32[8,4096]{1,0:T(8,128)S(1)}, u32[]{:S(2)}, u32[]{:S(2)}) collective-permute-start(f32[8,4096]{1,0:T(8,128)S(1)} %get-tuple-element.21), channel_id=1, source_target_pairs={{0,1},{1,0},{2,3},{3,2},{4,5},{5,4},{6,7},{7,6},{8,9},{9,8},{10,11... | collective-permute-start | bytes 393224 | tf_op jit(solution)/shard_map/ppermute | solution.py:356
  11.1 6.5 %collective-permute-start.4 = (f32[8,4096]{1,0:T(8,128)S(1)}, f32[8,4096]{1,0:T(8,128)S(1)}, u32[]{:S(2)}, u32[]{:S(2)}) collective-permute-start(f32[8,4096]{1,0:T(8,128)S(1)} %broadcast_select_fusion.1.own_odd), channel_id=1, source_target_pairs={{0,0},{2,4},{4,2},{6,8},{8,6},{10,12},{12,10},{14,16},{16,14},{18,... | collective-permute-start | bytes 393224 | tf_op jit(solution)/shard_map/ppermute | solution.py:356
  15.6 3.0 %collective-permute-start.5 = (f32[8,4096]{1,0:T(8,128)S(1)}, f32[8,4096]{1,0:T(8,128)S(1)}, u32[]{:S(2)}, u32[]{:S(2)}) collective-permute-start(f32[8,4096]{1,0:T(8,128)S(1)} %broadcast_select_fusion.own_even), channel_id=1, source_target_pairs={{0,2},{2,0},{4,6},{6,4},{8,10},{10,8},{12,14},{14,12},{16,18},{18,... | collective-permute-start | bytes 393224 | tf_op jit(solution)/shard_map/ppermute | solution.py:356
  22.9 11.4 %all-to-all-start = ((f32[16,1,128]{2,1,0:T(1,128)}), f32[16,1,128]{2,1,0:T(1,128)S(1)}, u32[]{:S(2)}, u32[]{:S(2)}) async-start(f32[16,1,128]{2,1,0:T(1,128)} %bitcast.3), calls=%async_computation | async-start | bytes 16384 | tf_op jit(solution)/shard_map/all_to_all | solution.py:444
  29.8 2.0 %copy-start = (bf16[512,4096]{1,0:T(8,128)(2,1)}, bf16[512,4096]{1,0:T(8,128)(2,1)S(1)}, u32[]{:S(2)}) copy-start(bf16[512,4096]{1,0:T(8,128)(2,1)S(1)} %spread.1) | copy-start | bytes 12582916
  34.3 2.2 %copy-start.1 = (bf16[512,4096]{1,0:T(8,128)(2,1)S(1)}, bf16[512,4096]{1,0:T(8,128)(2,1)}, u32[]{:S(2)}) copy-start(bf16[512,4096]{1,0:T(8,128)(2,1)} %copy-done) | copy-start | bytes 12582916
  39.4 13.6 %collective-permute-start.6 = (f32[2,16,4096]{2,1,0:T(8,128)S(1)}, f32[2,16,4096]{2,1,0:T(8,128)S(1)}, u32[]{:S(2)}, u32[]{:S(2)}) collective-permute-start(f32[2,16,4096]{2,1,0:T(8,128)S(1)} %get-tuple-element.32), channel_id=1, source_target_pairs={{0,1},{1,0},{2,3},{3,2},{4,5},{5,4},{6,7},{7,6},{8,9},{9,8},{10,11... | collective-permute-start | bytes 1572872 | tf_op jit(solution)/shard_map/ppermute | solution.py:386

commit v7 on v6

--- a/solution.py
+++ b/solution.py
@@ -89,7 +89,7 @@
     return (index == 0) | (index == lax.axis_size("rows") - 1)
 
 
-def smooth_kernel(frames, from_odd, from_even, inverse, stack, power, rows_in, half, fine):
+def smooth_kernel(frames, from_odd, from_even, inverse, stack, power, rows_in, half, pieces):
     count, rows, columns = frames.shape
     tiles = columns // lanes
     ring = tiles + 2
@@ -99,10 +99,10 @@
     for f in range(count):
         half[f, 0] = zero
         half[f, tiles + 1] = zero
-    blank = jnp.zeros((count * rows, lanes), jnp.float32)
-    fine[0] = blank
-    fine[tiles + 1] = blank
-    fine[tiles + 2] = blank
+    blank = jnp.zeros((2 * count * rows, lanes), jnp.bfloat16)
+    pieces[0] = blank
+    pieces[tiles + 1] = blank
+    pieces[tiles + 2] = blank
 
     def load_step(t, carry):
         for f in range(count):
@@ -120,21 +120,22 @@
 
     def horizontal_step(t, totals):
         result = []
+        details = []
         for f in range(count):
             smooth = horizontal(half[f, t], half[f, t + 1], half[f, t + 2])
             inverse[f, :, tile_of(t)] = 1.0 / smooth
-            detail = frames[f, :, tile_of(t)] - smooth
-            fine[t + 1, f * rows : (f + 1) * rows, :] = detail
-            result.append(totals[f] + fold(detail * detail))
+            details.append(frames[f, :, tile_of(t)] - smooth)
+            result.append(totals[f] + fold(details[f] * details[f]))
+        pieces[t + 1] = jnp.concatenate(halves(jnp.concatenate(details, axis=0)), axis=0)
         return tuple(result)
 
     def stack_step(t, carry):
-        before, here, after = fine[t], fine[t + 1], fine[t + 2]
+        before, here, after = pieces[t], pieces[t + 1], pieces[t + 2]
+        size = count * rows
         for j in range(reach):
-            high, low = halves(moved(before, here, after, 3 - j))
-            size = count * rows
-            stack[j * size : (j + 1) * size, tile_of(t)] = high
-            stack[(reach + j) * size : (reach + j + 1) * size, tile_of(t)] = low
+            turned = moved(before, here, after, 3 - j)
+            stack[j * size : (j + 1) * size, tile_of(t)] = turned[:size]
+            stack[(reach + j) * size : (reach + j + 1) * size, tile_of(t)] = turned[size:]
         return carry
 
     by_tiles(load_step, tiles, 8)
@@ -142,7 +143,7 @@
     powers = by_tiles(horizontal_step, tiles, 8, (jnp.zeros((8, lanes), jnp.float32),) * count)
     for f in range(count):
         power[f * 8 : f * 8 + 8, :] = powers[f]
-    fine[tiles + 3] = fine[1]
+    pieces[tiles + 3] = pieces[1]
     by_tiles(stack_step, ring, ring // 2)
 
 
@@ -155,9 +156,7 @@
     def shift(source, t):
         here = source[t + first]
         after = source[t + first + 1]
-        value = pltpu.roll(jnp.where(lane_of(here.shape) < amount, after, here), back, 1)
-        spare = jnp.zeros((slot - value.shape[0], lanes), jnp.float32)
-        return jnp.concatenate([value, spare], axis=0)
+        return pltpu.roll(jnp.where(lane_of(here.shape) < amount, after, here), back, 1)
 
     return shift
 
@@ -177,11 +176,16 @@
     blank = jnp.zeros((wide, lanes), jnp.float32)
     half[0] = blank
     half[tiles + 1] = blank
-    clean[0] = blank
-    clean[tiles + 1] = blank
-    fine[0] = blank
-    fine[tiles + 1] = blank
-    fine[tiles + 2] = blank
+    empty = jnp.zeros((2 * slot, lanes), jnp.bfloat16)
+    for array in (clean, fine):
+        array[0] = empty
+        array[tiles + 1] = empty
+    fine[tiles + 2] = empty
+    spare = jnp.zeros((slot - wide, lanes), jnp.float32)
+
+    def cut(value):
+        return jnp.concatenate(halves(jnp.concatenate([value, spare], axis=0)), axis=0)
+
     place = lax.broadcasted_iota(jnp.int32, (wide, lanes), 0)
     inside = ((place >= 4) | (row_index > 0)) & ((place < rows + 4) | (row_index < last_row))
 
@@ -200,9 +204,9 @@
 
     def horizontal_step(t, total):
         smooth = jnp.where(inside, horizontal(half[t], half[t + 1], half[t + 2]), 0.0)
-        clean[t + 1] = smooth
+        clean[t + 1] = cut(smooth)
         detail = rows_in[t, pl.ds(4, wide), :] - smooth
-        fine[t + 1] = detail
+        fine[t + 1] = cut(detail)
         own = jnp.where((place >= 4) & (place < rows + 4), detail, 0.0)
         return total + fold(own * own)
 
@@ -214,9 +218,7 @@
     stream[2 * slot : 4 * slot, :] = jnp.zeros((2 * slot, ring * lanes), jnp.bfloat16)
 
     def stream_step(t, carry):
-        high, low = halves(shift(fine, t))
-        stream[0:slot, tile_of(t)] = high
-        stream[slot : 2 * slot, tile_of(t)] = low
+        stream[0 : 2 * slot, tile_of(t)] = shift(fine, t)
         return carry
 
     by_tiles(stream_step, ring, ring // 2)
@@ -251,7 +253,7 @@
     part[...] = jnp.broadcast_to(jnp.sum(packed, axis=0, keepdims=True), part.shape)
 
 
-def spread_kernel(base, clean, spread):
+def spread_columns(clean, spread, base_col):
     tiles = clean.shape[0] - 2
     full = spread.shape[0] // 2
     spare = jnp.zeros((full - reach * slot, tiles * lanes), jnp.bfloat16)
@@ -259,13 +261,13 @@
     spread[full + reach * slot : 2 * full, :] = spare
 
     def per_offset(j, carry):
-        shift = column_shift(base[0, 1] + j - 3)
+        shift = column_shift(base_col + j - 3)
         at = pl.multiple_of(j * slot, slot)
 
         def step(t, inner):
-            high, low = halves(shift(clean, t))
-            spread[pl.ds(at, slot), tile_of(t)] = high
-            spread[pl.ds(full + at, slot), tile_of(t)] = low
+            turned = shift(clean, t)
+            spread[pl.ds(at, slot), tile_of(t)] = turned[:slot]
+            spread[pl.ds(full + at, slot), tile_of(t)] = turned[slot:]
             return inner
 
         by_tiles(step, tiles, 32)
@@ -307,45 +309,75 @@
     return jnp.concatenate(tiles, axis=1)
 
 
-def pressure_kernel(base, parts, spread, inverse, pressure, moments, part):
+def pressures(base, totals, clean, spread, inverse):
     count, rows, columns = inverse.shape
     full = spread.shape[0] // 2
-    first_row = 1 + base[0, 0]
-    totals = jnp.broadcast_to(jnp.sum(parts[...], axis=0, keepdims=True), (8, lanes))
-    weights = blend_weights(totals, count)
-    bands = [banded(weights[f], f, rows, first_row) for f in range(count)]
+    weights = blend_weights(jnp.broadcast_to(totals[0:1, :], (8, lanes)), count)
+    bands = [banded(weights[f], f, rows, 1 + base[0, 0]) for f in range(count)]
     mixing = jnp.concatenate(halves(jnp.concatenate(bands, axis=0)), axis=0)
-    chunk = 2 * lanes
-    zero = jnp.zeros((8, lanes), jnp.float32)
-    size = count * rows
-
-    def step(t, totals):
-        where = pl.ds(pl.multiple_of(t * chunk, chunk), chunk)
+    spread_columns(clean, spread, base[0, 1])
+
+    def chunk_values(where):
         product = jnp.dot(mixing, spread[0:full, where], preferred_element_type=jnp.float32)
         product = product + jnp.dot(mixing, spread[full : 2 * full, where], preferred_element_type=jnp.float32)
-        registered = product[:size] + product[size:]
-        first = second = None
-        totals = list(totals)
+        registered = product[: count * rows] + product[count * rows :]
+        values = []
         for f in range(count):
             ratio = registered[f * rows : (f + 1) * rows] * inverse[f, :, where]
-            value = calib_zero + ratio * (calib_linear + calib_square * ratio)
-            squared = value * value
-            pressure[f, :, where] = value
-            first = value if first is None else first + value
-            second = squared if second is None else second + squared
-            for total, array in ((f, value), (count + f, squared)):
-                for c in range(chunk // lanes):
-                    totals[total] = totals[total] + fold(array[:, c * lanes : (c + 1) * lanes])
-        moments[0, :, where] = first
-        moments[1, :, where] = second
-        return tuple(totals)
-
-    totals = by_tiles(step, columns // chunk, 8, (zero,) * (2 * count))
-    line = jnp.zeros((8, lanes), jnp.float32)
+            values.append(calib_zero + ratio * (calib_linear + calib_square * ratio))
+        return values
+
+    return chunk_values
+
+
+def chunk_of(t):
+    return pl.ds(pl.multiple_of(t * 2 * lanes, 2 * lanes), 2 * lanes)
+
+
+def pressure_kernel(base, totals, clean, inverse, pressure, moments, part, spread):
+    count, rows, columns = inverse.shape
+    chunk_values = pressures(base, totals, clean, spread, inverse)
+
+    def step(t, sums):
+        where = chunk_of(t)
+        values = chunk_values(where)
+        squares = [value * value for value in values]
+        for f in range(count):
+            pressure[f, :, where] = values[f]
+        moments[0, :, where] = sum(values[1:], values[0])
+        moments[1, :, where] = sum(squares[1:], squares[0])
+        result = []
+        for total, array in zip(sums, values + squares):
+            result.append(total + fold(array[:, :lanes]) + fold(array[:, lanes:]))
+        return tuple(result)
+
+    zero = jnp.zeros((8, lanes), jnp.float32)
+    sums = by_tiles(step, columns // (2 * lanes), 8, (zero,) * (2 * count))
+    line = zero
     for k in range(2 * count):
-        value = jnp.sum(jnp.sum(totals[k], axis=0, keepdims=True), axis=1, keepdims=True)
+        value = jnp.sum(jnp.sum(sums[k], axis=0, keepdims=True), axis=1, keepdims=True)
         line = line + jnp.where(lane_of(line.shape) == k, value, 0.0)
     part[...] = jnp.broadcast_to(line[0:1], part.shape)
+
+
+def time_kernel(base, totals, clean, inverse, moments, time_mean, time_rms, spread):
+    count, rows, columns = inverse.shape
+    chunk_values = pressures(base, totals, clean, spread, inverse)
+    frames = 2 * count
+
+    def step(t, carry):
+        where = chunk_of(t)
+        first = moments[0, :, where]
+        second = moments[1, :, where]
+        for value in chunk_values(where):
+            first = first + value
+            second = second + value * value
+        mean = first * (1.0 / frames)
+        time_mean[:, where] = mean
+        time_rms[:, where] = jnp.sqrt(jnp.maximum(second * (1.0 / frames) - mean * mean, 0.0))
+        return carry
+
+    by_tiles(step, columns // (2 * lanes), 8)
 
 
 def paired(value, axis, first):
@@ -419,22 +451,26 @@
         scratch_shapes=[
             pltpu.VMEM((count, tiles, rows + 16, lanes), f32),
             pltpu.VMEM((count, tiles + 2, rows, lanes), f32),
-            pltpu.VMEM((ring + 2, count * rows, lanes), f32),
+            pltpu.VMEM((ring + 2, 2 * count * rows, lanes), bf16),
         ],
         compiler_params=params,
         name="smooth",
     )(raw, frames_odd, frames_even)
     own_even, power = lax.optimization_barrier((own_even, power))
     from_even = paired(own_even, "rows", 0)
+    blocks = lax.axis_size("frames")
+    if blocks == 2:
+        inverse_out, from_even = lax.optimization_barrier((inverse, from_even))
+        other_inverse = paired(inverse_out, "frames", 0)
     clean, part = pl.pallas_call(
         match_kernel,
-        out_shape=(struct((tiles + 2, wide, lanes)), struct((size, lanes))),
+        out_shape=(jax.ShapeDtypeStruct((tiles + 2, 2 * slot, lanes), bf16), struct((size, lanes))),
         in_specs=[smem] + [vmem] * 6,
         out_specs=(vmem, vmem),
         scratch_shapes=[
             pltpu.VMEM((tiles, rows + 16, lanes), f32),
             pltpu.VMEM((tiles + 2, wide, lanes), f32),
-            pltpu.VMEM((ring + 2, wide, lanes), f32),
+            pltpu.VMEM((ring + 2, 2 * slot, lanes), bf16),
             pltpu.VMEM((4 * slot, ring * lanes), bf16),
             pltpu.VMEM((8 * count, lanes), f32),
         ],
@@ -442,30 +478,39 @@
         name="match",
     )(offsets, own_odd, own_even, from_odd, from_even, stack, power)
     parts = lax.all_to_all(part, "rows", 0, 0, tiled=True)
-    spread = pl.pallas_call(
-        spread_kernel,
-        out_shape=jax.ShapeDtypeStruct((2 * 8 * slot, columns), bf16),
-        in_specs=[smem, vmem],
-        out_specs=vmem,
-        compiler_params=params,
-        name="spread",
-    )(offsets, clean)
+    totals = jnp.sum(parts, axis=0, keepdims=True)
+    spread = pltpu.VMEM((2 * 8 * slot, columns), bf16)
     pressure, moments, part = pl.pallas_call(
         pressure_kernel,
         out_shape=(struct((count, rows, columns)), struct((2, rows, columns)), struct((size, lanes))),
         in_specs=[smem] + [vmem] * 3,
         out_specs=(vmem, vmem, vmem),
+        scratch_shapes=[spread],
         compiler_params=params,
         name="pressure",
-    )(offsets, parts, spread, inverse)
-    whole = total_over(moments, "frames")
+    )(offsets, totals, clean, inverse)
+    if blocks == 2:
+        row = jnp.concatenate([totals[:, : lanes - 2], offsets.astype(f32)], axis=1)
+        row, part = lax.optimization_barrier((row, part))
+        row = paired(row, "frames", 0)
+        time_mean, time_rms = pl.pallas_call(
+            time_kernel,
+            out_shape=(struct((rows, columns)), struct((rows, columns))),
+            in_specs=[smem] + [vmem] * 4,
+            out_specs=(vmem, vmem),
+            scratch_shapes=[spread],
+            compiler_params=params,
+            name="time",
+        )(row[:, lanes - 2 :].astype(jnp.int32), row, clean, other_inverse, moments)
+    else:
+        whole = total_over(moments, "frames")
+        total_frames = count * blocks
+        time_mean = whole[0] / total_frames
+        time_rms = jnp.sqrt(jnp.maximum(whole[1] / total_frames - time_mean * time_mean, 0.0))
     spatial = jnp.sum(lax.all_to_all(part, "rows", 0, 0, tiled=True), axis=0)
     cell_count = rows * columns * size
     frame_mean = spatial[:count] / cell_count
     frame_rms = jnp.sqrt(spatial[count : 2 * count] / cell_count - frame_mean * frame_mean)
-    total_frames = count * lax.axis_size("frames")
-    time_mean = whole[0] / total_frames
-    time_rms = jnp.sqrt(jnp.maximum(whole[1] / total_frames - time_mean * time_mean, 0.0))
     return (pressure, frame_mean, frame_rms, time_mean, time_rms)
 
 

time: 54.3 us -> 54.8 us (level)
  blocking collectives: 9.66 us -> 0 us
  waiting for transfers between devices: 6.6 us -> 13.2 us
  starting transfers between devices: 16.5 us -> 21.2 us
  local copies, waits for them, and re-layouts: 4.15 us -> 0.01 us
  Pallas kernels: 11.8 us -> 15.7 us
  other arithmetic: 3.73 us -> 2.97 us
    all_to_all x1 -> x0, blocking collectives: 9.66 us -> none  [shards(): spatial = jnp.sum(lax.all_to_all(part, 'rows', 0, 0, tiled=True), axis=0)]
    all_to_all x0 -> x1, waiting for transfers between devices: none -> 6.21 us  [shards(): spatial = jnp.sum(lax.all_to_all(part, 'rows', 0, 0, tiled=True), axis=0)]
    unnamed x6 -> x2, local copies, waits for them, and re-layouts: 4.15 us -> 0.01 us
    all_to_all x0 -> x1, starting transfers between devices: none -> 3.47 us  [shards(): spatial = jnp.sum(lax.all_to_all(part, 'rows', 0, 0, tiled=True), axis=0)]
    all_to_all x1, waiting for transfers between devices: 2.54 us -> 5.11 us  [shards(): parts = lax.all_to_all(part, 'rows', 0, 0, tiled=True)]
    pallas_call x2, Pallas kernels: 6.13 us -> 8.62 us  [the longest x1 4.34 us: shards(): pl.pallas_call(match_kernel, out_shape=(jax.ShapeDtypeStruct((tiles + 2,...]
    ppermute x6 -> x8, starting transfers between devices: 10.3 us -> 12.7 us  [paired(): return lax.ppermute(value, axis, list(enumerate(partner)))]
    ppermute x1 -> x0, waiting for transfers between devices: 2.17 us -> none  [total_over(): lax.ppermute(value, axis, [(i, i ^ step) for i in range(size)])]
  transfers between devices with their start and end apart: 8 -> 10, of which waited for: 4 -> 4; matrix products, arithmetic and copies ran while one was open for 1% -> 2% of each run, Pallas kernels for 9% -> 13%
where the time goes in v7:
time: 54.8 us; the launch traced here: 54.6 us
  starting transfers between devices  21.2 us (39%)
  Pallas kernels  15.7 us (29%)
  waiting for transfers between devices  13.2 us (24%)
  other arithmetic  2.97 us (5%)
  between operations  1.42 us (3%)
    ppermute x8, starting transfers between devices, paired(): return lax.ppermute(value, axis, list(enumerate(partner)))  12.7 us
    all_to_all x1, waiting for transfers between devices, shards(): spatial = jnp.sum(lax.all_to_all(part, 'rows', 0, 0, tiled=True), axis=0)  6.21 us
    all_to_all x1, waiting for transfers between devices, shards(): parts = lax.all_to_all(part, 'rows', 0, 0, tiled=True)  5.11 us
    all_to_all x1, starting transfers between devices, shards(): parts = lax.all_to_all(part, 'rows', 0, 0, tiled=True)  5.08 us
    pallas_call x1, Pallas kernels, shards(): pl.pallas_call(match_kernel, out_shape=(jax.ShapeDtypeStruct((tiles + 2,...  4.34 us
    pallas_call x1, Pallas kernels, shards(): pl.pallas_call(time_kernel, out_shape=(struct((rows, columns)), struct((r...  4.28 us
    pallas_call x1, Pallas kernels, shards(): pl.pallas_call(pressure_kernel, out_shape=(struct((count, rows, columns))...  4.25 us
    all_to_all x1, starting transfers between devices, shards(): spatial = jnp.sum(lax.all_to_all(part, 'rows', 0, 0, tiled=True), axis=0)  3.47 us
  transfers between devices with their start and end apart: 10, of which 4 were waited for; matrix products, arithmetic and copies ran while one was open for 2% of the time, Pallas kernels for 13%

profile of v7, /device:TPU:0, one launch (start us, length us, event | category | flops | bytes accessed | tf_op | source)
XLA Modules:
  0.0 54.6 jit_solution(8088667292856847631)
XLA Ops:
  0.7 1.1 %broadcast_maximum_fusion.frames = f32[2,16,4096]{2,1,0:T(8,128)S(1)} fusion(f32[2,16,4096]{2,1,0:T(8,128)} %param.4), kind=kLoop, calls=%fused_computation | loop fusion | flops 131072 | bytes 1048576 | tf_op jit(solution)/shard_map/max | solution.py:434
  1.8 1.0 %broadcast_maximum_fusion.1 = f32[16,4096]{1,0:T(8,128)S(1)} fusion(f32[16,4096]{1,0:T(8,128)} %bitcast.13), kind=kLoop, calls=%fused_computation.1 | loop fusion | flops 65536 | bytes 524288 | tf_op jit(solution)/shard_map/max | solution.py:404
  2.8 3.0 %collective-permute-start = (f32[8,4096]{1,0:T(8,128)S(1)}, f32[8,4096]{1,0:T(8,128)S(1)}, u32[]{:S(2)}, u32[]{:S(2)}) collective-permute-start(f32[8,4096]{1,0:T(8,128)S(1)} %get-tuple-element.50), channel_id=1, source_target_pairs={{0,1},{1,0},{2,3},{3,2},{4,5},{5,4},{6,7},{7,6},{8,9},{9,8},{10,11... | collective-permute-start | bytes 393224 | tf_op jit(solution)/shard_map/ppermute | solution.py:388
  5.8 0.7 %collective-permute-start.2 = (f32[2,4,4096]{2,1,0:T(4,128)S(1)}, f32[2,4,4096]{2,1,0:T(4,128)S(1)}, u32[]{:S(2)}, u32[]{:S(2)}) collective-permute-start(f32[2,4,4096]{2,1,0:T(4,128)S(1)} %get-tuple-element.28), channel_id=1, source_target_pairs={{0,0},{2,4},{4,2},{6,8},{8,6},{10,12},{12,10},{14,16},{16,14},{18,... | collective-permute-start | bytes 393224 | tf_op jit(solution)/shard_map/ppermute | solution.py:388
  6.5 2.9 %collective-permute-start.3 = (f32[2,4,4096]{2,1,0:T(4,128)S(1)}, f32[2,4,4096]{2,1,0:T(4,128)S(1)}, u32[]{:S(2)}, u32[]{:S(2)}) collective-permute-start(f32[2,4,4096]{2,1,0:T(4,128)S(1)} %get-tuple-element.47), channel_id=1, source_target_pairs={{0,2},{2,0},{4,6},{6,4},{8,10},{10,8},{12,14},{14,12},{16,18},{18,... | collective-permute-start | bytes 393224 | tf_op jit(solution)/shard_map/ppermute | solution.py:388
  10.1 0.0 collective-permute-done
  10.1 1.0 %collective-permute-start.1 = (f32[8,4096]{1,0:T(8,128)S(1)}, f32[8,4096]{1,0:T(8,128)S(1)}, u32[]{:S(2)}, u32[]{:S(2)}) collective-permute-start(f32[8,4096]{1,0:T(8,128)S(1)} %get-tuple-element.27), channel_id=1, source_target_pairs={{0,1},{1,0},{2,3},{3,2},{4,5},{5,4},{6,7},{7,6},{8,9},{9,8},{10,11... | collective-permute-start | bytes 393224 | tf_op jit(solution)/shard_map/ppermute | solution.py:388
  11.1 0.7 %collective-permute-start.4 = (f32[8,4096]{1,0:T(8,128)S(1)}, f32[8,4096]{1,0:T(8,128)S(1)}, u32[]{:S(2)}, u32[]{:S(2)}) collective-permute-start(f32[8,4096]{1,0:T(8,128)S(1)} %broadcast_select_fusion.1.own_odd), channel_id=1, source_target_pairs={{0,0},{2,4},{4,2},{6,8},{8,6},{10,12},{12,10},{14,16},{16,14},{18,... | collective-permute-start | bytes 393224 | tf_op jit(solution)/shard_map/ppermute | solution.py:388
  11.8 2.9 %smooth.1 = (f32[2,16,4096]{2,1,0:T(8,128)S(1)}, bf16[448,4352]{1,0:T(8,128)(2,1)S(1)}, f32[16,128]{1,0:T(8,128)S(1)}) custom-call(f32[2,16,4096]{2,1,0:T(8,128)S(1)} %broadcast_maximum_fusion.frames, f32[2,4,4096]{2,1,0:T(4,128)S(1)} %collective-permute-done.2.from_odd, f32[2,4,4096]{2,1,0:T(4,128)S(1)} %collective-permute-done.3.from_even), custom_call_target="tpu_custom_call" | custom-call | tf_op jit(solution)/shard_map/smooth/pallas_call | solution.py:442
  14.7 0.9 %collective-permute-done.1 = f32[8,4096]{1,0:T(8,128)S(1)} collective-permute-done((f32[8,4096]{1,0:T(8,128)S(1)}, f32[8,4096]{1,0:T(8,128)S(1)}, u32[]{:S(2)}, u32[]{:S(2)}) %collective-permute-start.1) | collective-permute-done | bytes 131104 | tf_op jit(solution)/shard_map/ppermute | solution.py:388
  15.6 2.0 %collective-permute-start.5 = (f32[8,4096]{1,0:T(8,128)S(1)}, f32[8,4096]{1,0:T(8,128)S(1)}, u32[]{:S(2)}, u32[]{:S(2)}) collective-permute-start(f32[8,4096]{1,0:T(8,128)S(1)} %broadcast_select_fusion.own_even), channel_id=1, source_target_pairs={{0,2},{2,0},{4,6},{6,4},{8,10},{10,8},{12,14},{14,12},{16,18},{18,... | collective-permute-start | bytes 393224 | tf_op jit(solution)/shard_map/ppermute | solution.py:388
  17.6 1.0 %collective-permute-done.5.from_even = f32[8,4096]{1,0:T(8,128)S(1)} collective-permute-done((f32[8,4096]{1,0:T(8,128)S(1)}, f32[8,4096]{1,0:T(8,128)S(1)}, u32[]{:S(2)}, u32[]{:S(2)}) %collective-permute-start.5) | collective-permute-done | bytes 131104 | tf_op jit(solution)/shard_map/ppermute | solution.py:388
  18.6 4.3 %match.1 = (bf16[34,64,128]{2,1,0:T(8,128)(2,1)S(1)}, f32[16,128]{1,0:T(8,128)}) custom-call(s32[1,2]{1,0:T(1,128)S(1)} %get-tuple-element.52.base, f32[8,4096]{1,0:T(8,128)S(1)} %broadcast_select_fusion.1.own_odd, f32[8,4096]{1,0:T(8,128)S(1)} %broadcast_select_fusion.own_even, f32[8,4096]{1,0:T(8,128)S(1)} %collective-permute-done.4.from_odd, ...), custom_call_target="tpu_custom_call" | custom-call | tf_op jit(solution)/shard_map/match/pallas_call | solution.py:465
  22.9 5.1 %all-to-all-start = ((f32[16,1,128]{2,1,0:T(1,128)}), f32[16,1,128]{2,1,0:T(1,128)S(1)}, u32[]{:S(2)}, u32[]{:S(2)}) async-start(f32[16,1,128]{2,1,0:T(1,128)} %bitcast.3), calls=%async_computation | async-start | bytes 16384 | tf_op jit(solution)/shard_map/all_to_all | solution.py:480
  28.0 1.2 %collective-permute-start.7 = (f32[2,16,4096]{2,1,0:T(8,128)S(1)}, f32[2,16,4096]{2,1,0:T(8,128)S(1)}, u32[]{:S(2)}, u32[]{:S(2)}) collective-permute-start(f32[2,16,4096]{2,1,0:T(8,128)S(1)} %get-tuple-element.41.inverse), channel_id=1, source_target_pairs={{0,1},{1,0},{2,3},{3,2},{4,5},{5,4},{6,7},{7,6},{8,9},{9,8},{10,11... | collective-permute-start | bytes 1572872 | tf_op jit(solution)/shard_map/ppermute | solution.py:388
  29.2 5.1 %all-to-all-done = f32[16,1,128]{2,1,0:T(1,128)S(1)} async-done(((f32[16,1,128]{2,1,0:T(1,128)}), f32[16,1,128]{2,1,0:T(1,128)S(1)}, u32[]{:S(2)}, u32[]{:S(2)}) %all-to-all-start) | async-done | bytes 8224 | tf_op jit(solution)/shard_map/all_to_all | solution.py:480
  34.4 4.3 %pressure.1 = (f32[2,16,4096]{2,1,0:T(8,128)}, f32[2,16,4096]{2,1,0:T(8,128)S(1)}, f32[16,128]{1,0:T(8,128)}) custom-call(s32[1,2]{1,0:T(1,128)S(1)} %get-tuple-element.52.base, f32[1,128]{1,0:T(1,128)S(1)} %bitcast.11, bf16[34,64,128]{2,1,0:T(8,128)(2,1)S(1)} %get-tuple-element.36.clean, f32[2,16,4096]{2,1,0:T(8,128)S(1)} %get-tuple-element.41.inverse), custom_call_target="tpu_custom_call" | custom-call | tf_op jit(solution)/shard_map/pressure/pallas_call | solution.py:483
  38.6 0.1 pad_maximum_fusion
  38.7 1.2 %collective-permute-start.6 = (f32[1,128]{1,0:T(1,128)S(1)}, f32[1,128]{1,0:T(1,128)S(1)}, u32[]{:S(2)}, u32[]{:S(2)}) collective-permute-start(f32[1,128]{1,0:T(1,128)S(1)} %pad_maximum_fusion), channel_id=1, source_target_pairs={{0,1},{1,0},{2,3},{3,2},{4,5},{5,4},{6,7},{7,6},{8,9},{9,8},{10,11... | collective-permute-start | bytes 1544 | tf_op jit(solution)/shard_map/ppermute | solution.py:388
  39.9 3.5 %all-to-all-start.1 = ((f32[16,1,128]{2,1,0:T(1,128)}), f32[16,1,128]{2,1,0:T(1,128)S(1)}, u32[]{:S(2)}, u32[]{:S(2)}) async-start(f32[16,1,128]{2,1,0:T(1,128)} %bitcast.6), calls=%async_computation.1 | async-start | bytes 16384 | tf_op jit(solution)/shard_map/all_to_all | solution.py:510
  43.4 0.1 slice_convert_fusion.base
  43.4 6.2 %all-to-all-done.1 = f32[16,1,128]{2,1,0:T(1,128)S(1)} async-done(((f32[16,1,128]{2,1,0:T(1,128)}), f32[16,1,128]{2,1,0:T(1,128)S(1)}, u32[]{:S(2)}, u32[]{:S(2)}) %all-to-all-start.1) | async-done | bytes 8224 | tf_op jit(solution)/shard_map/all_to_all | solution.py:510
  49.7 0.6 %subtract_sqrt_fusion = (f32[2]{0:T(128)}, f32[2]{0:T(128)}) fusion(f32[128]{0:T(128)S(1)} %reduce_sum.19), kind=kLoop, calls=%fused_computation.10 | loop fusion | flops 8 | bytes 32 | tf_op jit(solution)/shard_map/sqrt | solution.py:513
  50.3 4.3 %time.1 = (f32[16,4096]{1,0:T(8,128)}, f32[16,4096]{1,0:T(8,128)}) custom-call(s32[1,2]{1,0:T(1,128)S(1)} %slice_convert_fusion.base, f32[1,128]{1,0:T(1,128)S(1)} %collective-permute-done.6.totals, bf16[34,64,128]{2,1,0:T(8,128)(2,1)S(1)} %get-tuple-element.36.clean, f32[2,16,4096]{2,1,0:T(8,128)S(1)} %collective-permute-done.7.inverse, ...), custom_call_target="tpu_custom_call" | custom-call | tf_op jit(solution)/shard_map/time/pallas_call | solution.py:496
  (14 shorter events, 0.2 us)
Async XLA Ops:
  0.6 17.0 %copy-start = (s32[1,2]{1,0:T(1,128)S(1)}, s32[1,2]{1,0:T(1,128)}, u32[]{:S(2)}) copy-start(s32[1,2]{1,0:T(1,128)} %param.7) | copy-start | bytes 28
  2.8 7.3 %collective-permute-start = (f32[8,4096]{1,0:T(8,128)S(1)}, f32[8,4096]{1,0:T(8,128)S(1)}, u32[]{:S(2)}, u32[]{:S(2)}) collective-permute-start(f32[8,4096]{1,0:T(8,128)S(1)} %get-tuple-element.50), channel_id=1, source_target_pairs={{0,1},{1,0},{2,3},{3,2},{4,5},{5,4},{6,7},{7,6},{8,9},{9,8},{10,11... | collective-permute-start | bytes 393224 | tf_op jit(solution)/shard_map/ppermute | solution.py:388
  5.8 5.9 %collective-permute-start.2 = (f32[2,4,4096]{2,1,0:T(4,128)S(1)}, f32[2,4,4096]{2,1,0:T(4,128)S(1)}, u32[]{:S(2)}, u32[]{:S(2)}) collective-permute-start(f32[2,4,4096]{2,1,0:T(4,128)S(1)} %get-tuple-element.28), channel_id=1, source_target_pairs={{0,0},{2,4},{4,2},{6,8},{8,6},{10,12},{12,10},{14,16},{16,14},{18,... | collective-permute-start | bytes 393224 | tf_op jit(solution)/shard_map/ppermute | solution.py:388
  6.5 5.3 %collective-permute-start.3 = (f32[2,4,4096]{2,1,0:T(4,128)S(1)}, f32[2,4,4096]{2,1,0:T(4,128)S(1)}, u32[]{:S(2)}, u32[]{:S(2)}) collective-permute-start(f32[2,4,4096]{2,1,0:T(4,128)S(1)} %get-tuple-element.47), channel_id=1, source_target_pairs={{0,2},{2,0},{4,6},{6,4},{8,10},{10,8},{12,14},{14,12},{16,18},{18,... | collective-permute-start | bytes 393224 | tf_op jit(solution)/shard_map/ppermute | solution.py:388
  10.1 5.5 %collective-permute-start.1 = (f32[8,4096]{1,0:T(8,128)S(1)}, f32[8,4096]{1,0:T(8,128)S(1)}, u32[]{:S(2)}, u32[]{:S(2)}) collective-permute-start(f32[8,4096]{1,0:T(8,128)S(1)} %get-tuple-element.27), channel_id=1, source_target_pairs={{0,1},{1,0},{2,3},{3,2},{4,5},{5,4},{6,7},{7,6},{8,9},{9,8},{10,11... | collective-permute-start | bytes 393224 | tf_op jit(solution)/shard_map/ppermute | solution.py:388
  11.1 7.5 %collective-permute-start.4 = (f32[8,4096]{1,0:T(8,128)S(1)}, f32[8,4096]{1,0:T(8,128)S(1)}, u32[]{:S(2)}, u32[]{:S(2)}) collective-permute-start(f32[8,4096]{1,0:T(8,128)S(1)} %broadcast_select_fusion.1.own_odd), channel_id=1, source_target_pairs={{0,0},{2,4},{4,2},{6,8},{8,6},{10,12},{12,10},{14,16},{16,14},{18,... | collective-permute-start | bytes 393224 | tf_op jit(solution)/shard_map/ppermute | solution.py:388
  15.6 3.0 %collective-permute-start.5 = (f32[8,4096]{1,0:T(8,128)S(1)}, f32[8,4096]{1,0:T(8,128)S(1)}, u32[]{:S(2)}, u32[]{:S(2)}) collective-permute-start(f32[8,4096]{1,0:T(8,128)S(1)} %broadcast_select_fusion.own_even), channel_id=1, source_target_pairs={{0,2},{2,0},{4,6},{6,4},{8,10},{10,8},{12,14},{14,12},{16,18},{18,... | collective-permute-start | bytes 393224 | tf_op jit(solution)/shard_map/ppermute | solution.py:388
  22.9 11.4 %all-to-all-start = ((f32[16,1,128]{2,1,0:T(1,128)}), f32[16,1,128]{2,1,0:T(1,128)S(1)}, u32[]{:S(2)}, u32[]{:S(2)}) async-start(f32[16,1,128]{2,1,0:T(1,128)} %bitcast.3), calls=%async_computation | async-start | bytes 16384 | tf_op jit(solution)/shard_map/all_to_all | solution.py:480
  28.0 22.3 %collective-permute-start.7 = (f32[2,16,4096]{2,1,0:T(8,128)S(1)}, f32[2,16,4096]{2,1,0:T(8,128)S(1)}, u32[]{:S(2)}, u32[]{:S(2)}) collective-permute-start(f32[2,16,4096]{2,1,0:T(8,128)S(1)} %get-tuple-element.41.inverse), channel_id=1, source_target_pairs={{0,1},{1,0},{2,3},{3,2},{4,5},{5,4},{6,7},{7,6},{8,9},{9,8},{10,11... | collective-permute-start | bytes 1572872 | tf_op jit(solution)/shard_map/ppermute | solution.py:388
  38.7 4.6 %collective-permute-start.6 = (f32[1,128]{1,0:T(1,128)S(1)}, f32[1,128]{1,0:T(1,128)S(1)}, u32[]{:S(2)}, u32[]{:S(2)}) collective-permute-start(f32[1,128]{1,0:T(1,128)S(1)} %pad_maximum_fusion), channel_id=1, source_target_pairs={{0,1},{1,0},{2,3},{3,2},{4,5},{5,4},{6,7},{7,6},{8,9},{9,8},{10,11... | collective-permute-start | bytes 1544 | tf_op jit(solution)/shard_map/ppermute | solution.py:388
  39.9 9.8 %all-to-all-start.1 = ((f32[16,1,128]{2,1,0:T(1,128)}), f32[16,1,128]{2,1,0:T(1,128)S(1)}, u32[]{:S(2)}, u32[]{:S(2)}) async-start(f32[16,1,128]{2,1,0:T(1,128)} %bitcast.6), calls=%async_computation.1 | async-start | bytes 16384 | tf_op jit(solution)/shard_map/all_to_all | solution.py:510

commit v8 on v7

--- a/solution.py
+++ b/solution.py
@@ -19,6 +19,10 @@
 smem = pl.BlockSpec(memory_space=pltpu.SMEM)
 
 
+def cost(mebibytes):
+    return pl.CostEstimate(flops=0, bytes_accessed=mebibytes * 2**20, transcendentals=0)
+
+
 def tile_of(index):
     return pl.ds(pl.multiple_of(index * lanes, lanes), lanes)
 
@@ -55,18 +59,42 @@
     return here
 
 
-def horizontal(before, here, after):
-    total = taps[4] * here
-    for step in range(1, 5):
-        pair = moved(before, here, after, step) + moved(before, here, after, -step)
-        total = total + taps[4 - step] * pair
-    return total
-
-
 def halves(value):
     high = value.astype(jnp.bfloat16)
     low = (value - high.astype(jnp.float32)).astype(jnp.bfloat16)
     return high, low
+
+
+def cut(value):
+    return jnp.concatenate(halves(value), axis=0)
+
+
+def fill_band(band):
+    shape = (lanes, lanes)
+    apart = lax.broadcasted_iota(jnp.int32, shape, 0) - lax.broadcasted_iota(jnp.int32, shape, 1)
+
+    def block(offset):
+        distance = jnp.abs(apart + offset)
+        value = jnp.zeros(shape, jnp.float32)
+        for step in range(5):
+            value = jnp.where(distance == step, taps[4 - step], value)
+        return value.astype(jnp.bfloat16)
+
+    none = jnp.zeros(shape, jnp.bfloat16)
+    before, here, after = block(-lanes), block(0), block(lanes)
+    for index, pair in enumerate(((before, none), (here, before), (after, here), (none, after))):
+        band[index * lanes : (index + 1) * lanes, :] = jnp.concatenate(pair, axis=1)
+
+
+def chunk_of(t):
+    return pl.ds(pl.multiple_of(t * 2 * lanes, 2 * lanes), 2 * lanes)
+
+
+def horizontal(wide, band, t):
+    window = wide[:, pl.ds(pl.multiple_of(t * 2 * lanes, 2 * lanes), 4 * lanes)]
+    product = jnp.dot(window, band[...], preferred_element_type=jnp.float32)
+    half = product.shape[0] // 2
+    return product[:half] + product[half:]
 
 
 def by_row_shift(value, rows, direction):
@@ -89,17 +117,16 @@
     return (index == 0) | (index == lax.axis_size("rows") - 1)
 
 
-def smooth_kernel(frames, from_odd, from_even, inverse, stack, power, rows_in, half, pieces):
+def smooth_kernel(frames, from_odd, from_even, inverse, stack, power, rows_in, wide, band, pieces):
     count, rows, columns = frames.shape
     tiles = columns // lanes
     ring = tiles + 2
     odd = lax.axis_index("rows") % 2 == 1
     edge = at_edge()
-    zero = jnp.zeros((rows, lanes), jnp.float32)
-    for f in range(count):
-        half[f, 0] = zero
-        half[f, tiles + 1] = zero
     blank = jnp.zeros((2 * count * rows, lanes), jnp.bfloat16)
+    wide[:, tile_of(0)] = blank
+    wide[:, tile_of(tiles + 1)] = blank
+    fill_band(band)
     pieces[0] = blank
     pieces[tiles + 1] = blank
     pieces[tiles + 2] = blank
@@ -114,19 +141,23 @@
         return carry
 
     def vertical_step(t, carry):
-        for f in range(count):
-            half[f, t + 1] = vertical(lambda s: rows_in[f, t, pl.ds(4 + s, rows), :])
+        parts = [vertical(lambda s: rows_in[f, t, pl.ds(4 + s, rows), :]) for f in range(count)]
+        wide[:, tile_of(t + 1)] = cut(jnp.concatenate(parts, axis=0))
         return carry
 
     def horizontal_step(t, totals):
+        smooth = horizontal(wide, band, t)
         result = []
         details = []
         for f in range(count):
-            smooth = horizontal(half[f, t], half[f, t + 1], half[f, t + 2])
-            inverse[f, :, tile_of(t)] = 1.0 / smooth
-            details.append(frames[f, :, tile_of(t)] - smooth)
-            result.append(totals[f] + fold(details[f] * details[f]))
-        pieces[t + 1] = jnp.concatenate(halves(jnp.concatenate(details, axis=0)), axis=0)
+            part = smooth[f * rows : (f + 1) * rows]
+            inverse[f, :, chunk_of(t)] = 1.0 / part
+            details.append(frames[f, :, chunk_of(t)] - part)
+            square = details[f] * details[f]
+            result.append(totals[f] + fold(square[:, :lanes]) + fold(square[:, lanes:]))
+        detail = cut(jnp.concatenate(details, axis=0))
+        pieces[2 * t + 1] = detail[:, :lanes]
+        pieces[2 * t + 2] = detail[:, lanes:]
         return tuple(result)
 
     def stack_step(t, carry):
@@ -140,7 +171,7 @@
 
     by_tiles(load_step, tiles, 8)
     by_tiles(vertical_step, tiles, 8)
-    powers = by_tiles(horizontal_step, tiles, 8, (jnp.zeros((8, lanes), jnp.float32),) * count)
+    powers = by_tiles(horizontal_step, tiles // 2, 8, (jnp.zeros((8, lanes), jnp.float32),) * count)
     for f in range(count):
         power[f * 8 : f * 8 + 8, :] = powers[f]
     pieces[tiles + 3] = pieces[1]
@@ -162,7 +193,7 @@
 
 
 def match_kernel(
-    base, own_odd, own_even, from_odd, from_even, stack, power, clean, part, rows_in, half, fine, stream, lags
+    base, own_odd, own_even, from_odd, from_even, stack, power, clean, part, rows_in, padded, band, fine, stream, lags
 ):
     rows = own_odd.shape[0] * 2
     tiles = own_odd.shape[1] // lanes
@@ -173,21 +204,18 @@
     last_row = lax.axis_size("rows") - 1
     odd = row_index % 2 == 1
     edge = at_edge()
-    blank = jnp.zeros((wide, lanes), jnp.float32)
-    half[0] = blank
-    half[tiles + 1] = blank
     empty = jnp.zeros((2 * slot, lanes), jnp.bfloat16)
+    padded[:, tile_of(0)] = empty
+    padded[:, tile_of(tiles + 1)] = empty
+    fill_band(band)
     for array in (clean, fine):
         array[0] = empty
         array[tiles + 1] = empty
     fine[tiles + 2] = empty
     spare = jnp.zeros((slot - wide, lanes), jnp.float32)
-
-    def cut(value):
-        return jnp.concatenate(halves(jnp.concatenate([value, spare], axis=0)), axis=0)
-
-    place = lax.broadcasted_iota(jnp.int32, (wide, lanes), 0)
-    inside = ((place >= 4) | (row_index > 0)) & ((place < rows + 4) | (row_index < last_row))
+    place = lax.broadcasted_iota(jnp.int32, (slot, 2 * lanes), 0)
+    own = (place >= 4) & (place < rows + 4)
+    inside = ((place >= 4) | (row_index > 0)) & ((place < rows + 4) | (row_index < last_row)) & (place < wide)
 
     def load_step(t, carry):
         outer = [jnp.where(edge, 0.0, from_odd[:, tile_of(t)]), own_odd[:, tile_of(t)]]
@@ -199,20 +227,23 @@
         return carry
 
     def vertical_step(t, carry):
-        half[t + 1] = vertical(lambda s: rows_in[t, pl.ds(s, wide), :])
+        value = vertical(lambda s: rows_in[t, pl.ds(s, wide), :])
+        padded[:, tile_of(t + 1)] = cut(jnp.concatenate([value, spare], axis=0))
         return carry
 
     def horizontal_step(t, total):
-        smooth = jnp.where(inside, horizontal(half[t], half[t + 1], half[t + 2]), 0.0)
-        clean[t + 1] = cut(smooth)
-        detail = rows_in[t, pl.ds(4, wide), :] - smooth
-        fine[t + 1] = cut(detail)
-        own = jnp.where((place >= 4) & (place < rows + 4), detail, 0.0)
-        return total + fold(own * own)
+        smooth = jnp.where(inside, horizontal(padded, band, t), 0.0)
+        raw = [jnp.concatenate([rows_in[2 * t + c, pl.ds(4, wide), :], spare], axis=0) for c in range(2)]
+        detail = jnp.concatenate(raw, axis=1) - smooth
+        square = jnp.where(own, detail * detail, 0.0)
+        for array, value in ((clean, cut(smooth)), (fine, cut(detail))):
+            array[2 * t + 1] = value[:, :lanes]
+            array[2 * t + 2] = value[:, lanes:]
+        return total + fold(square[:, :lanes]) + fold(square[:, lanes:])
 
     by_tiles(load_step, tiles, 8)
     by_tiles(vertical_step, tiles, 8)
-    ref_power = by_tiles(horizontal_step, tiles, 8, jnp.zeros((8, lanes), jnp.float32))
+    ref_power = by_tiles(horizontal_step, tiles // 2, 8, jnp.zeros((8, lanes), jnp.float32))
     fine[tiles + 3] = fine[1]
     shift = column_shift(base[0, 1])
     stream[2 * slot : 4 * slot, :] = jnp.zeros((2 * slot, ring * lanes), jnp.bfloat16)
@@ -330,10 +361,6 @@
     return chunk_values
 
 
-def chunk_of(t):
-    return pl.ds(pl.multiple_of(t * 2 * lanes, 2 * lanes), 2 * lanes)
-
-
 def pressure_kernel(base, totals, clean, inverse, pressure, moments, part, spread):
     count, rows, columns = inverse.shape
     chunk_values = pressures(base, totals, clean, spread, inverse)
@@ -450,18 +477,17 @@
         out_specs=(vmem,) * 3,
         scratch_shapes=[
             pltpu.VMEM((count, tiles, rows + 16, lanes), f32),
-            pltpu.VMEM((count, tiles + 2, rows, lanes), f32),
+            pltpu.VMEM((2 * count * rows, (tiles + 2) * lanes), bf16),
+            pltpu.VMEM((4 * lanes, 2 * lanes), bf16),
             pltpu.VMEM((ring + 2, 2 * count * rows, lanes), bf16),
         ],
         compiler_params=params,
+        cost_estimate=cost(8),
         name="smooth",
     )(raw, frames_odd, frames_even)
     own_even, power = lax.optimization_barrier((own_even, power))
     from_even = paired(own_even, "rows", 0)
     blocks = lax.axis_size("frames")
-    if blocks == 2:
-        inverse_out, from_even = lax.optimization_barrier((inverse, from_even))
-        other_inverse = paired(inverse_out, "frames", 0)
     clean, part = pl.pallas_call(
         match_kernel,
         out_shape=(jax.ShapeDtypeStruct((tiles + 2, 2 * slot, lanes), bf16), struct((size, lanes))),
@@ -469,14 +495,19 @@
         out_specs=(vmem, vmem),
         scratch_shapes=[
             pltpu.VMEM((tiles, rows + 16, lanes), f32),
-            pltpu.VMEM((tiles + 2, wide, lanes), f32),
+            pltpu.VMEM((2 * slot, (tiles + 2) * lanes), bf16),
+            pltpu.VMEM((4 * lanes, 2 * lanes), bf16),
             pltpu.VMEM((ring + 2, 2 * slot, lanes), bf16),
             pltpu.VMEM((4 * slot, ring * lanes), bf16),
             pltpu.VMEM((8 * count, lanes), f32),
         ],
         compiler_params=params,
+        cost_estimate=cost(12),
         name="match",
     )(offsets, own_odd, own_even, from_odd, from_even, stack, power)
+    if blocks == 2:
+        inverse_out, part = lax.optimization_barrier((inverse, part))
+        other_inverse = paired(inverse_out, "frames", 0)
     parts = lax.all_to_all(part, "rows", 0, 0, tiled=True)
     totals = jnp.sum(parts, axis=0, keepdims=True)
     spread = pltpu.VMEM((2 * 8 * slot, columns), bf16)
@@ -487,6 +518,7 @@
         out_specs=(vmem, vmem, vmem),
         scratch_shapes=[spread],
         compiler_params=params,
+        cost_estimate=cost(12),
         name="pressure",
     )(offsets, totals, clean, inverse)
     if blocks == 2:
@@ -500,6 +532,7 @@
             out_specs=(vmem, vmem),
             scratch_shapes=[spread],
             compiler_params=params,
+            cost_estimate=cost(12),
             name="time",
         )(row[:, lanes - 2 :].astype(jnp.int32), row, clean, other_inverse, moments)
     else:
@@ -507,7 +540,9 @@
         total_frames = count * blocks
         time_mean = whole[0] / total_frames
         time_rms = jnp.sqrt(jnp.maximum(whole[1] / total_frames - time_mean * time_mean, 0.0))
-    spatial = jnp.sum(lax.all_to_all(part, "rows", 0, 0, tiled=True), axis=0)
+    sums = lax.all_to_all(part, "rows", 0, 0, tiled=True)
+    sums, time_mean, time_rms = lax.optimization_barrier((sums, time_mean, time_rms))
+    spatial = jnp.sum(sums, axis=0)
     cell_count = rows * columns * size
     frame_mean = spatial[:count] / cell_count
     frame_rms = jnp.sqrt(spatial[count : 2 * count] / cell_count - frame_mean * frame_mean)

time: 54.8 us -> 50.8 us (0.927)
  blocking collectives: 0 us -> 11.6 us
  waiting for transfers between devices: 13.2 us -> 4.16 us
  starting transfers between devices: 21.2 us -> 15.5 us
  Pallas kernels: 15.7 us -> 14.9 us
    all_to_all x0 -> x1, blocking collectives: none -> 11.6 us  [shards(): parts = lax.all_to_all(part, 'rows', 0, 0, tiled=True)]
    all_to_all x2 -> x1, waiting for transfers between devices: 11.3 us -> 1.99 us  [shards(): sums = lax.all_to_all(part, 'rows', 0, 0, tiled=True)]
    all_to_all x2 -> x1, starting transfers between devices: 8.56 us -> 3.42 us  [shards(): sums = lax.all_to_all(part, 'rows', 0, 0, tiled=True)]
    ppermute x8, starting transfers between devices: 12.7 us -> 12.1 us  [paired(): return lax.ppermute(value, axis, list(enumerate(partner)))]
  transfers between devices with their start and end apart: 10 -> 9, of which waited for: 4 -> 3; matrix products, arithmetic and copies ran while one was open for 2% -> 0% of each run, Pallas kernels for 13% -> 22%
where the time goes in v8:
time: 50.8 us; the launch traced here: 50.5 us
  starting transfers between devices  15.5 us (31%)
  Pallas kernels  14.9 us (29%)
  blocking collectives  11.6 us (23%)
  waiting for transfers between devices  4.16 us (8%)
  other arithmetic  2.95 us (6%)
  between operations  1.42 us (3%)
    ppermute x8, starting transfers between devices, paired(): return lax.ppermute(value, axis, list(enumerate(partner)))  12.1 us
    all_to_all x1, blocking collectives, shards(): parts = lax.all_to_all(part, 'rows', 0, 0, tiled=True)  11.6 us
    pallas_call x1, Pallas kernels, shards(): pl.pallas_call(time_kernel, out_shape=(struct((rows, columns)), struct((r...  4.28 us
    pallas_call x1, Pallas kernels, shards(): pl.pallas_call(pressure_kernel, out_shape=(struct((count, rows, columns))...  4.25 us
    pallas_call x1, Pallas kernels, shards(): pl.pallas_call(match_kernel, out_shape=(jax.ShapeDtypeStruct((tiles + 2,...  3.81 us
    all_to_all x1, starting transfers between devices, shards(): sums = lax.all_to_all(part, 'rows', 0, 0, tiled=True)  3.42 us
    pallas_call x1, Pallas kernels, shards(): pl.pallas_call(smooth_kernel, out_shape=(struct((count, rows, columns)),...  2.57 us
    ppermute x8, waiting for transfers between devices, paired(): return lax.ppermute(value, axis, list(enumerate(partner)))  2.17 us
  transfers between devices with their start and end apart: 9, of which 3 were waited for; matrix products, arithmetic and copies ran while one was open for 0% of the time, Pallas kernels for 22%

profile of v8, /device:TPU:0, one launch (start us, length us, event | category | flops | bytes accessed | tf_op | source)
XLA Modules:
  0.0 50.5 jit_solution(16507363221068915760)
XLA Ops:
  0.6 1.1 %broadcast_maximum_fusion.frames = f32[2,16,4096]{2,1,0:T(8,128)S(1)} fusion(f32[2,16,4096]{2,1,0:T(8,128)} %param.4), kind=kLoop, calls=%fused_computation | loop fusion | flops 131072 | bytes 1048576 | tf_op jit(solution)/shard_map/max | solution.py:461
  1.8 1.0 %broadcast_maximum_fusion.1 = f32[16,4096]{1,0:T(8,128)S(1)} fusion(f32[16,4096]{1,0:T(8,128)} %bitcast.15), kind=kLoop, calls=%fused_computation.1 | loop fusion | flops 65536 | bytes 524288 | tf_op jit(solution)/shard_map/max | solution.py:431
  2.8 3.0 %collective-permute-start.2 = (f32[8,4096]{1,0:T(8,128)S(1)}, f32[8,4096]{1,0:T(8,128)S(1)}, u32[]{:S(2)}, u32[]{:S(2)}) collective-permute-start(f32[8,4096]{1,0:T(8,128)S(1)} %get-tuple-element.56), channel_id=1, source_target_pairs={{0,1},{1,0},{2,3},{3,2},{4,5},{5,4},{6,7},{7,6},{8,9},{9,8},{10,11... | collective-permute-start | bytes 393224 | tf_op jit(solution)/shard_map/ppermute | solution.py:415
  5.8 0.7 %collective-permute-start = (f32[2,4,4096]{2,1,0:T(4,128)S(1)}, f32[2,4,4096]{2,1,0:T(4,128)S(1)}, u32[]{:S(2)}, u32[]{:S(2)}) collective-permute-start(f32[2,4,4096]{2,1,0:T(4,128)S(1)} %get-tuple-element.28), channel_id=1, source_target_pairs={{0,0},{2,4},{4,2},{6,8},{8,6},{10,12},{12,10},{14,16},{16,14},{18,... | collective-permute-start | bytes 393224 | tf_op jit(solution)/shard_map/ppermute | solution.py:415
  6.5 2.9 %collective-permute-start.1 = (f32[2,4,4096]{2,1,0:T(4,128)S(1)}, f32[2,4,4096]{2,1,0:T(4,128)S(1)}, u32[]{:S(2)}, u32[]{:S(2)}) collective-permute-start(f32[2,4,4096]{2,1,0:T(4,128)S(1)} %get-tuple-element.53), channel_id=1, source_target_pairs={{0,2},{2,0},{4,6},{6,4},{8,10},{10,8},{12,14},{14,12},{16,18},{18,... | collective-permute-start | bytes 393224 | tf_op jit(solution)/shard_map/ppermute | solution.py:415
  10.1 0.0 collective-permute-done.2
  10.1 1.0 %collective-permute-start.3 = (f32[8,4096]{1,0:T(8,128)S(1)}, f32[8,4096]{1,0:T(8,128)S(1)}, u32[]{:S(2)}, u32[]{:S(2)}) collective-permute-start(f32[8,4096]{1,0:T(8,128)S(1)} %get-tuple-element.32), channel_id=1, source_target_pairs={{0,1},{1,0},{2,3},{3,2},{4,5},{5,4},{6,7},{7,6},{8,9},{9,8},{10,11... | collective-permute-start | bytes 393224 | tf_op jit(solution)/shard_map/ppermute | solution.py:415
  11.1 0.7 %collective-permute-start.4 = (f32[8,4096]{1,0:T(8,128)S(1)}, f32[8,4096]{1,0:T(8,128)S(1)}, u32[]{:S(2)}, u32[]{:S(2)}) collective-permute-start(f32[8,4096]{1,0:T(8,128)S(1)} %broadcast_select_fusion.1.own_odd), channel_id=1, source_target_pairs={{0,0},{2,4},{4,2},{6,8},{8,6},{10,12},{12,10},{14,16},{16,14},{18,... | collective-permute-start | bytes 393224 | tf_op jit(solution)/shard_map/ppermute | solution.py:415
  11.8 0.0 collective-permute-done.from_odd
  11.8 2.6 %smooth.1 = (f32[2,16,4096]{2,1,0:T(8,128)S(1)}, bf16[448,4352]{1,0:T(8,128)(2,1)S(1)}, f32[16,128]{1,0:T(8,128)S(1)}) custom-call(f32[2,16,4096]{2,1,0:T(8,128)S(1)} %broadcast_maximum_fusion.frames, f32[2,4,4096]{2,1,0:T(4,128)S(1)} %collective-permute-done.from_odd, f32[2,4,4096]{2,1,0:T(4,128)S(1)} %collective-permute-done.1.from_even), custom_call_target="tpu_custom_call" | custom-call | bytes 8388608 | tf_op jit(solution)/shard_map/smooth/pallas_call | solution.py:469
  14.4 1.2 %collective-permute-done.3 = f32[8,4096]{1,0:T(8,128)S(1)} collective-permute-done((f32[8,4096]{1,0:T(8,128)S(1)}, f32[8,4096]{1,0:T(8,128)S(1)}, u32[]{:S(2)}, u32[]{:S(2)}) %collective-permute-start.3) | collective-permute-done | bytes 131104 | tf_op jit(solution)/shard_map/ppermute | solution.py:415
  15.6 1.7 %collective-permute-start.5 = (f32[8,4096]{1,0:T(8,128)S(1)}, f32[8,4096]{1,0:T(8,128)S(1)}, u32[]{:S(2)}, u32[]{:S(2)}) collective-permute-start(f32[8,4096]{1,0:T(8,128)S(1)} %broadcast_select_fusion.own_even), channel_id=1, source_target_pairs={{0,2},{2,0},{4,6},{6,4},{8,10},{10,8},{12,14},{14,12},{16,18},{18,... | collective-permute-start | bytes 393224 | tf_op jit(solution)/shard_map/ppermute | solution.py:415
  17.3 1.0 %collective-permute-done.5.from_even = f32[8,4096]{1,0:T(8,128)S(1)} collective-permute-done((f32[8,4096]{1,0:T(8,128)S(1)}, f32[8,4096]{1,0:T(8,128)S(1)}, u32[]{:S(2)}, u32[]{:S(2)}) %collective-permute-start.5) | collective-permute-done | bytes 131104 | tf_op jit(solution)/shard_map/ppermute | solution.py:415
  18.3 3.8 %match.1 = (bf16[34,64,128]{2,1,0:T(8,128)(2,1)S(1)}, f32[16,128]{1,0:T(8,128)S(1)}) custom-call(s32[1,2]{1,0:T(1,128)S(1)} %get-tuple-element.58.base, f32[8,4096]{1,0:T(8,128)S(1)} %broadcast_select_fusion.1.own_odd, f32[8,4096]{1,0:T(8,128)S(1)} %broadcast_select_fusion.own_even, f32[8,4096]{1,0:T(8,128)S(1)} %collective-permute-done.4.from_odd, ...), custom_call_target="tpu_custom_call" | custom-call | bytes 12582912 | tf_op jit(solution)/shard_map/match/pallas_call | solution.py:491
  22.1 1.2 %collective-permute-start.7 = (f32[2,16,4096]{2,1,0:T(8,128)S(1)}, f32[2,16,4096]{2,1,0:T(8,128)S(1)}, u32[]{:S(2)}, u32[]{:S(2)}) collective-permute-start(f32[2,16,4096]{2,1,0:T(8,128)S(1)} %get-tuple-element.44.inverse), channel_id=1, source_target_pairs={{0,1},{1,0},{2,3},{3,2},{4,5},{5,4},{6,7},{7,6},{8,9},{9,8},{10,11... | collective-permute-start | bytes 1572872 | tf_op jit(solution)/shard_map/ppermute | solution.py:415
  23.3 11.6 %all_to_all.21 = f32[16,1,128]{2,1,0:T(1,128)S(1)} all-to-all(f32[16,1,128]{2,1,0:T(1,128)S(1)} %bitcast.12), channel_id=1, replica_groups=mesh['rows'=16,'frames'=2] {'rows'}, dimensions={0} | all-to-all | bytes 16384 | tf_op jit(solution)/shard_map/all_to_all | solution.py:511
  34.9 4.3 %pressure.1 = (f32[2,16,4096]{2,1,0:T(8,128)}, f32[2,16,4096]{2,1,0:T(8,128)S(1)}, f32[16,128]{1,0:T(8,128)}) custom-call(s32[1,2]{1,0:T(1,128)S(1)} %get-tuple-element.58.base, f32[1,128]{1,0:T(1,128)S(1)} %bitcast.13, bf16[34,64,128]{2,1,0:T(8,128)(2,1)S(1)} %get-tuple-element.39.clean, f32[2,16,4096]{2,1,0:T(8,128)S(1)} %get-tuple-element.44.inverse), custom_call_target="tpu_custom_call" | custom-call | bytes 12582912 | tf_op jit(solution)/shard_map/pressure/pallas_call | solution.py:514
  39.2 0.1 pad_maximum_fusion
  39.3 0.9 %collective-permute-start.6 = (f32[1,128]{1,0:T(1,128)S(1)}, f32[1,128]{1,0:T(1,128)S(1)}, u32[]{:S(2)}, u32[]{:S(2)}) collective-permute-start(f32[1,128]{1,0:T(1,128)S(1)} %pad_maximum_fusion), channel_id=1, source_target_pairs={{0,1},{1,0},{2,3},{3,2},{4,5},{5,4},{6,7},{7,6},{8,9},{9,8},{10,11... | collective-permute-start | bytes 1544 | tf_op jit(solution)/shard_map/ppermute | solution.py:415
  40.1 3.4 %all-to-all-start.1 = ((f32[16,1,128]{2,1,0:T(1,128)}), f32[16,1,128]{2,1,0:T(1,128)S(1)}, u32[]{:S(2)}, u32[]{:S(2)}) async-start(f32[16,1,128]{2,1,0:T(1,128)} %bitcast.6), calls=%async_computation.1 | async-start | bytes 16384 | tf_op jit(solution)/shard_map/all_to_all | solution.py:543
  43.6 0.1 slice_convert_fusion.base
  43.6 4.3 %time.1 = (f32[16,4096]{1,0:T(8,128)}, f32[16,4096]{1,0:T(8,128)}) custom-call(s32[1,2]{1,0:T(1,128)S(1)} %slice_convert_fusion.base, f32[1,128]{1,0:T(1,128)S(1)} %collective-permute-done.6.totals, bf16[34,64,128]{2,1,0:T(8,128)(2,1)S(1)} %get-tuple-element.39.clean, f32[2,16,4096]{2,1,0:T(8,128)S(1)} %collective-permute-done.7.inverse, ...), custom_call_target="tpu_custom_call" | custom-call | bytes 12582912 | tf_op jit(solution)/shard_map/time/pallas_call | solution.py:528
  47.9 2.0 %all-to-all-done.1 = f32[16,1,128]{2,1,0:T(1,128)S(1)} async-done(((f32[16,1,128]{2,1,0:T(1,128)}), f32[16,1,128]{2,1,0:T(1,128)S(1)}, u32[]{:S(2)}, u32[]{:S(2)}) %all-to-all-start.1) | async-done | bytes 8224 | tf_op jit(solution)/shard_map/all_to_all | solution.py:543
  49.9 0.6 %subtract_sqrt_fusion = (f32[2]{0:T(128)}, f32[2]{0:T(128)}) fusion(f32[128]{0:T(128)S(1)} %reduce_sum.19), kind=kLoop, calls=%fused_computation.9 | loop fusion | flops 8 | bytes 32 | tf_op jit(solution)/shard_map/sqrt | solution.py:548
  (13 shorter events, 0.2 us)
Async XLA Ops:
  0.6 16.7 %copy-start = (s32[1,2]{1,0:T(1,128)S(1)}, s32[1,2]{1,0:T(1,128)}, u32[]{:S(2)}) copy-start(s32[1,2]{1,0:T(1,128)} %param.7) | copy-start | bytes 28
  2.8 7.3 %collective-permute-start.2 = (f32[8,4096]{1,0:T(8,128)S(1)}, f32[8,4096]{1,0:T(8,128)S(1)}, u32[]{:S(2)}, u32[]{:S(2)}) collective-permute-start(f32[8,4096]{1,0:T(8,128)S(1)} %get-tuple-element.56), channel_id=1, source_target_pairs={{0,1},{1,0},{2,3},{3,2},{4,5},{5,4},{6,7},{7,6},{8,9},{9,8},{10,11... | collective-permute-start | bytes 393224 | tf_op jit(solution)/shard_map/ppermute | solution.py:415
  5.8 5.9 %collective-permute-start = (f32[2,4,4096]{2,1,0:T(4,128)S(1)}, f32[2,4,4096]{2,1,0:T(4,128)S(1)}, u32[]{:S(2)}, u32[]{:S(2)}) collective-permute-start(f32[2,4,4096]{2,1,0:T(4,128)S(1)} %get-tuple-element.28), channel_id=1, source_target_pairs={{0,0},{2,4},{4,2},{6,8},{8,6},{10,12},{12,10},{14,16},{16,14},{18,... | collective-permute-start | bytes 393224 | tf_op jit(solution)/shard_map/ppermute | solution.py:415
  6.5 5.3 %collective-permute-start.1 = (f32[2,4,4096]{2,1,0:T(4,128)S(1)}, f32[2,4,4096]{2,1,0:T(4,128)S(1)}, u32[]{:S(2)}, u32[]{:S(2)}) collective-permute-start(f32[2,4,4096]{2,1,0:T(4,128)S(1)} %get-tuple-element.53), channel_id=1, source_target_pairs={{0,2},{2,0},{4,6},{6,4},{8,10},{10,8},{12,14},{14,12},{16,18},{18,... | collective-permute-start | bytes 393224 | tf_op jit(solution)/shard_map/ppermute | solution.py:415
  10.1 5.5 %collective-permute-start.3 = (f32[8,4096]{1,0:T(8,128)S(1)}, f32[8,4096]{1,0:T(8,128)S(1)}, u32[]{:S(2)}, u32[]{:S(2)}) collective-permute-start(f32[8,4096]{1,0:T(8,128)S(1)} %get-tuple-element.32), channel_id=1, source_target_pairs={{0,1},{1,0},{2,3},{3,2},{4,5},{5,4},{6,7},{7,6},{8,9},{9,8},{10,11... | collective-permute-start | bytes 393224 | tf_op jit(solution)/shard_map/ppermute | solution.py:415
  11.1 6.2 %collective-permute-start.4 = (f32[8,4096]{1,0:T(8,128)S(1)}, f32[8,4096]{1,0:T(8,128)S(1)}, u32[]{:S(2)}, u32[]{:S(2)}) collective-permute-start(f32[8,4096]{1,0:T(8,128)S(1)} %broadcast_select_fusion.1.own_odd), channel_id=1, source_target_pairs={{0,0},{2,4},{4,2},{6,8},{8,6},{10,12},{12,10},{14,16},{16,14},{18,... | collective-permute-start | bytes 393224 | tf_op jit(solution)/shard_map/ppermute | solution.py:415
  15.6 2.7 %collective-permute-start.5 = (f32[8,4096]{1,0:T(8,128)S(1)}, f32[8,4096]{1,0:T(8,128)S(1)}, u32[]{:S(2)}, u32[]{:S(2)}) collective-permute-start(f32[8,4096]{1,0:T(8,128)S(1)} %broadcast_select_fusion.own_even), channel_id=1, source_target_pairs={{0,2},{2,0},{4,6},{6,4},{8,10},{10,8},{12,14},{14,12},{16,18},{18,... | collective-permute-start | bytes 393224 | tf_op jit(solution)/shard_map/ppermute | solution.py:415
  22.1 21.5 %collective-permute-start.7 = (f32[2,16,4096]{2,1,0:T(8,128)S(1)}, f32[2,16,4096]{2,1,0:T(8,128)S(1)}, u32[]{:S(2)}, u32[]{:S(2)}) collective-permute-start(f32[2,16,4096]{2,1,0:T(8,128)S(1)} %get-tuple-element.44.inverse), channel_id=1, source_target_pairs={{0,1},{1,0},{2,3},{3,2},{4,5},{5,4},{6,7},{7,6},{8,9},{9,8},{10,11... | collective-permute-start | bytes 1572872 | tf_op jit(solution)/shard_map/ppermute | solution.py:415
  39.3 4.3 %collective-permute-start.6 = (f32[1,128]{1,0:T(1,128)S(1)}, f32[1,128]{1,0:T(1,128)S(1)}, u32[]{:S(2)}, u32[]{:S(2)}) collective-permute-start(f32[1,128]{1,0:T(1,128)S(1)} %pad_maximum_fusion), channel_id=1, source_target_pairs={{0,1},{1,0},{2,3},{3,2},{4,5},{5,4},{6,7},{7,6},{8,9},{9,8},{10,11... | collective-permute-start | bytes 1544 | tf_op jit(solution)/shard_map/ppermute | solution.py:415
  40.1 9.8 %all-to-all-start.1 = ((f32[16,1,128]{2,1,0:T(1,128)}), f32[16,1,128]{2,1,0:T(1,128)S(1)}, u32[]{:S(2)}, u32[]{:S(2)}) async-start(f32[16,1,128]{2,1,0:T(1,128)} %bitcast.6), calls=%async_computation.1 | async-start | bytes 16384 | tf_op jit(solution)/shard_map/all_to_all | solution.py:543

commit v9 on v8

--- a/solution.py
+++ b/solution.py
@@ -117,7 +117,7 @@
     return (index == 0) | (index == lax.axis_size("rows") - 1)
 
 
-def smooth_kernel(frames, from_odd, from_even, inverse, stack, power, rows_in, wide, band, pieces):
+def smooth_kernel(frames, from_odd, from_even, inverse, stack, power, band, rows_in, wide, pieces):
     count, rows, columns = frames.shape
     tiles = columns // lanes
     ring = tiles + 2
@@ -193,7 +193,7 @@
 
 
 def match_kernel(
-    base, own_odd, own_even, from_odd, from_even, stack, power, clean, part, rows_in, padded, band, fine, stream, lags
+    base, own_odd, own_even, from_odd, from_even, stack, power, band, clean, part, rows_in, padded, fine, stream, lags
 ):
     rows = own_odd.shape[0] * 2
     tiles = own_odd.shape[1] // lanes
@@ -207,7 +207,6 @@
     empty = jnp.zeros((2 * slot, lanes), jnp.bfloat16)
     padded[:, tile_of(0)] = empty
     padded[:, tile_of(tiles + 1)] = empty
-    fill_band(band)
     for array in (clean, fine):
         array[0] = empty
         array[tiles + 1] = empty
@@ -281,7 +280,7 @@
     lags[count : count + 1, :] = jnp.sum(ref_power, axis=0, keepdims=True)
     powers = jnp.sum(lags[0:8, :], axis=1, keepdims=True)
     packed = packed + jnp.where(lane == count * reach * reach + across, powers, 0.0)
-    part[...] = jnp.broadcast_to(jnp.sum(packed, axis=0, keepdims=True), part.shape)
+    part[...] = jnp.sum(packed, axis=0, keepdims=True)
 
 
 def spread_columns(clean, spread, base_col):
@@ -384,7 +383,7 @@
     for k in range(2 * count):
         value = jnp.sum(jnp.sum(sums[k], axis=0, keepdims=True), axis=1, keepdims=True)
         line = line + jnp.where(lane_of(line.shape) == k, value, 0.0)
-    part[...] = jnp.broadcast_to(line[0:1], part.shape)
+    part[...] = line[0:1]
 
 
 def time_kernel(base, totals, clean, inverse, moments, time_mean, time_rms, spread):
@@ -422,18 +421,23 @@
     return jnp.where(odd, high, low), jnp.where(odd, low, high)
 
 
-def from_owner(shard, odd, axis, root):
+def from_owner(shard, here, odd, axis, root):
     mine = lax.axis_index(axis) == root
     height = shard.shape[0] // 2
     if lax.axis_size(axis) != 2:
         whole = lax.psum(jnp.where(mine, shard, jnp.zeros_like(shard)), axis)
         return by_parity(odd, whole, height, 0)
-    here = lax.optimization_barrier(jnp.maximum(shard, 0.0))
-    odd_here, even_here = by_parity(odd, here, height, 0)
-    odd_there = paired(odd_here, axis, 0)
-    even_here, odd_there = lax.optimization_barrier((even_here, odd_there))
-    even_there = paired(even_here, axis, 0)
-    return jnp.where(mine, odd_here, odd_there), jnp.where(mine, even_here, even_there)
+    there = by_parity(odd, paired(shard, axis, 0), height, 0)
+    here = by_parity(odd, here, height, 0)
+    return [jnp.where(mine, own, other) for own, other in zip(here, there)]
+
+
+def total_over_rows(row):
+    size = lax.axis_size("rows")
+    row = row + paired(row, "rows", 0)
+    groups = [list(range(core, size, 2)) for core in range(2)]
+    rows = jnp.broadcast_to(row, (size // 2, lanes))
+    return lax.all_to_all(rows, "rows", 0, 0, axis_index_groups=groups, tiled=True)
 
 
 def total_over(value, axis):
@@ -458,45 +462,42 @@
     bf16 = jnp.bfloat16
     struct = functools.partial(jax.ShapeDtypeStruct, dtype=f32)
     odd = lax.axis_index("rows") % 2 == 1
-    raw = lax.optimization_barrier(jnp.maximum(frames_raw, 0.0))
+    raw, run = lax.optimization_barrier((jnp.maximum(frames_raw, 0.0), jnp.maximum(wind_off[0], 0.0)))
+    own_odd, own_even = from_owner(wind_off[0], run, odd, "frames", run_owner[0])
+    from_odd = paired(own_odd, "rows", 1)
+    from_even = paired(own_even, "rows", 0)
     offsets = jnp.clip(search_base, -8, 8)
     frames_odd, frames_even = by_parity(odd, raw, 4, 1)
-    frames_odd, run = lax.optimization_barrier((frames_odd, wind_off[0]))
     frames_odd = paired(frames_odd, "rows", 1)
     frames_even = paired(frames_even, "rows", 0)
-    own_odd, own_even = from_owner(run, odd, "frames", run_owner[0])
-    from_odd = paired(own_odd, "rows", 1)
-    inverse, stack, power = pl.pallas_call(
+    inverse, stack, power, band = pl.pallas_call(
         smooth_kernel,
         out_shape=(
             struct((count, rows, columns)),
             jax.ShapeDtypeStruct((2 * depth, ring * lanes), bf16),
             struct((8 * count, lanes)),
+            jax.ShapeDtypeStruct((4 * lanes, 2 * lanes), bf16),
         ),
         in_specs=[vmem] * 3,
-        out_specs=(vmem,) * 3,
+        out_specs=(vmem,) * 4,
         scratch_shapes=[
             pltpu.VMEM((count, tiles, rows + 16, lanes), f32),
             pltpu.VMEM((2 * count * rows, (tiles + 2) * lanes), bf16),
-            pltpu.VMEM((4 * lanes, 2 * lanes), bf16),
             pltpu.VMEM((ring + 2, 2 * count * rows, lanes), bf16),
         ],
         compiler_params=params,
         cost_estimate=cost(8),
         name="smooth",
     )(raw, frames_odd, frames_even)
-    own_even, power = lax.optimization_barrier((own_even, power))
-    from_even = paired(own_even, "rows", 0)
     blocks = lax.axis_size("frames")
     clean, part = pl.pallas_call(
         match_kernel,
-        out_shape=(jax.ShapeDtypeStruct((tiles + 2, 2 * slot, lanes), bf16), struct((size, lanes))),
-        in_specs=[smem] + [vmem] * 6,
+        out_shape=(jax.ShapeDtypeStruct((tiles + 2, 2 * slot, lanes), bf16), struct((1, lanes))),
+        in_specs=[smem] + [vmem] * 7,
         out_specs=(vmem, vmem),
         scratch_shapes=[
             pltpu.VMEM((tiles, rows + 16, lanes), f32),
             pltpu.VMEM((2 * slot, (tiles + 2) * lanes), bf16),
-            pltpu.VMEM((4 * lanes, 2 * lanes), bf16),
             pltpu.VMEM((ring + 2, 2 * slot, lanes), bf16),
             pltpu.VMEM((4 * slot, ring * lanes), bf16),
             pltpu.VMEM((8 * count, lanes), f32),
@@ -504,16 +505,16 @@
         compiler_params=params,
         cost_estimate=cost(12),
         name="match",
-    )(offsets, own_odd, own_even, from_odd, from_even, stack, power)
+    )(offsets, own_odd, own_even, from_odd, from_even, stack, power, band)
     if blocks == 2:
         inverse_out, part = lax.optimization_barrier((inverse, part))
         other_inverse = paired(inverse_out, "frames", 0)
-    parts = lax.all_to_all(part, "rows", 0, 0, tiled=True)
+    parts = total_over_rows(part)
     totals = jnp.sum(parts, axis=0, keepdims=True)
     spread = pltpu.VMEM((2 * 8 * slot, columns), bf16)
     pressure, moments, part = pl.pallas_call(
         pressure_kernel,
-        out_shape=(struct((count, rows, columns)), struct((2, rows, columns)), struct((size, lanes))),
+        out_shape=(struct((count, rows, columns)), struct((2, rows, columns)), struct((1, lanes))),
         in_specs=[smem] + [vmem] * 3,
         out_specs=(vmem, vmem, vmem),
         scratch_shapes=[spread],
@@ -540,7 +541,7 @@
         total_frames = count * blocks
         time_mean = whole[0] / total_frames
         time_rms = jnp.sqrt(jnp.maximum(whole[1] / total_frames - time_mean * time_mean, 0.0))
-    sums = lax.all_to_all(part, "rows", 0, 0, tiled=True)
+    sums = total_over_rows(part)
     sums, time_mean, time_rms = lax.optimization_barrier((sums, time_mean, time_rms))
     spatial = jnp.sum(sums, axis=0)
     cell_count = rows * columns * size

time: 50.8 us -> 52.1 us (1.026)
  blocking collectives: 11.6 us -> 0 us
  starting transfers between devices: 15.5 us -> 22.5 us
  waiting for transfers between devices: 4.16 us -> 8.13 us
  local copies, waits for them, and re-layouts: 0.01 us -> 1.2 us
  other arithmetic: 2.95 us -> 3.6 us
    all_to_all x1 -> x0, blocking collectives: 11.6 us -> none  [shards(): parts = lax.all_to_all(part, 'rows', 0, 0, tiled=True)]
    all_to_all x1 -> x2, starting transfers between devices: 3.42 us -> 8.95 us  [total_over_rows(): lax.all_to_all(rows, 'rows', 0, 0, axis_index_groups=groups, tiled=True)]
    all_to_all x1 -> x2, waiting for transfers between devices: 1.99 us -> 6.91 us  [total_over_rows(): lax.all_to_all(rows, 'rows', 0, 0, axis_index_groups=groups, tiled=True)]
    ppermute x8 -> x9, starting transfers between devices: 12.1 us -> 13.6 us  [paired(): return lax.ppermute(value, axis, list(enumerate(partner)))]
    broadcast_in_dim x0 -> x2, local copies, waits for them, and re-layouts: none -> 1.2 us  [total_over_rows(): rows = jnp.broadcast_to(row, (size // 2, lanes))]
    ppermute x8 -> x9, waiting for transfers between devices: 2.17 us -> 1.23 us  [paired(): return lax.ppermute(value, axis, list(enumerate(partner)))]
    convert_element_type x1, other arithmetic: 0.01 us -> 0.66 us  [shards(): row = jnp.concatenate([totals[:, :lanes - 2], offsets.astype(f32)], axis=1)]
  transfers between devices with their start and end apart: 9 -> 11, of which waited for: 3 -> 4; matrix products, arithmetic and copies ran while one was open for 0% -> 7% of each run, Pallas kernels for 22% -> 21%
where the time goes in v9:
time: 52.1 us; the launch traced here: 51.7 us
  starting transfers between devices  22.5 us (43%)
  Pallas kernels  14.9 us (29%)
  waiting for transfers between devices  8.13 us (16%)
  other arithmetic  3.6 us (7%)
  between operations  1.4 us (3%)
  local copies, waits for them, and re-layouts  1.2 us (2%)
    ppermute x9, starting transfers between devices, paired(): return lax.ppermute(value, axis, list(enumerate(partner)))  13.6 us
    all_to_all x2, starting transfers between devices, total_over_rows(): lax.all_to_all(rows, 'rows', 0, 0, axis_index_groups=groups, tiled=True)  8.95 us
    all_to_all x2, waiting for transfers between devices, total_over_rows(): lax.all_to_all(rows, 'rows', 0, 0, axis_index_groups=groups, tiled=True)  6.91 us
    pallas_call x1, Pallas kernels, shards(): pl.pallas_call(time_kernel, out_shape=(struct((rows, columns)), struct((r...  4.28 us
    pallas_call x1, Pallas kernels, shards(): pl.pallas_call(pressure_kernel, out_shape=(struct((count, rows, columns))...  4.26 us
    pallas_call x1, Pallas kernels, shards(): pl.pallas_call(match_kernel, out_shape=(jax.ShapeDtypeStruct((tiles + 2,...  3.76 us
    pallas_call x1, Pallas kernels, shards(): pl.pallas_call(smooth_kernel, out_shape=(struct((count, rows, columns)),...  2.57 us
    ppermute x9, waiting for transfers between devices, paired(): return lax.ppermute(value, axis, list(enumerate(partner)))  1.23 us
  transfers between devices with their start and end apart: 11, of which 4 were waited for; matrix products, arithmetic and copies ran while one was open for 7% of the time, Pallas kernels for 21%

profile of v9, /device:TPU:0, one launch (start us, length us, event | category | flops | bytes accessed | tf_op | source)
XLA Modules:
  0.0 51.7 jit_solution(9682207947666892984)
XLA Ops:
  0.6 3.0 %collective-permute-start.2 = (f32[16,4096]{1,0:T(8,128)}, f32[16,4096]{1,0:T(8,128)S(1)}, u32[]{:S(2)}, u32[]{:S(2)}) collective-permute-start(f32[16,4096]{1,0:T(8,128)} %bitcast.14), channel_id=1, source_target_pairs={{0,1},{1,0},{2,3},{3,2},{4,5},{5,4},{6,7},{7,6},{8,9},{9,8},{10,11... | collective-permute-start | bytes 786440 | tf_op jit(solution)/shard_map/ppermute | solution.py:414
  3.7 1.0 %broadcast_maximum_fusion.1 = f32[16,4096]{1,0:T(8,128)S(1)} fusion(f32[1,16,4096]{2,1,0:T(8,128)} %param.5), kind=kLoop, calls=%fused_computation.3 | loop fusion | flops 65536 | bytes 524288 | tf_op jit(solution)/shard_map/max | solution.py:465
  4.7 1.1 %broadcast_maximum_fusion.frames = f32[2,16,4096]{2,1,0:T(8,128)S(1)} fusion(f32[2,16,4096]{2,1,0:T(8,128)} %param.4), kind=kLoop, calls=%fused_computation | loop fusion | flops 131072 | bytes 1048576 | tf_op jit(solution)/shard_map/max | solution.py:465
  5.8 0.7 %collective-permute-start = (f32[2,4,4096]{2,1,0:T(4,128)S(1)}, f32[2,4,4096]{2,1,0:T(4,128)S(1)}, u32[]{:S(2)}, u32[]{:S(2)}) collective-permute-start(f32[2,4,4096]{2,1,0:T(4,128)S(1)} %get-tuple-element.50), channel_id=1, source_target_pairs={{0,0},{2,4},{4,2},{6,8},{8,6},{10,12},{12,10},{14,16},{16,14},{18,... | collective-permute-start | bytes 393224 | tf_op jit(solution)/shard_map/ppermute | solution.py:414
  6.5 2.9 %collective-permute-start.1 = (f32[2,4,4096]{2,1,0:T(4,128)S(1)}, f32[2,4,4096]{2,1,0:T(4,128)S(1)}, u32[]{:S(2)}, u32[]{:S(2)}) collective-permute-start(f32[2,4,4096]{2,1,0:T(4,128)S(1)} %get-tuple-element.49), channel_id=1, source_target_pairs={{0,2},{2,0},{4,6},{6,4},{8,10},{10,8},{12,14},{14,12},{16,18},{18,... | collective-permute-start | bytes 393224 | tf_op jit(solution)/shard_map/ppermute | solution.py:414
  10.1 0.1 collective-permute-done.2
  10.2 0.7 %collective-permute-start.3 = (f32[8,4096]{1,0:T(8,128)S(1)}, f32[8,4096]{1,0:T(8,128)S(1)}, u32[]{:S(2)}, u32[]{:S(2)}) collective-permute-start(f32[8,4096]{1,0:T(8,128)S(1)} %get-tuple-element.48.own_odd), channel_id=1, source_target_pairs={{0,0},{2,4},{4,2},{6,8},{8,6},{10,12},{12,10},{14,16},{16,14},{18,... | collective-permute-start | bytes 393224 | tf_op jit(solution)/shard_map/ppermute | solution.py:414
  10.9 3.1 %collective-permute-start.4 = (f32[8,4096]{1,0:T(8,128)S(1)}, f32[8,4096]{1,0:T(8,128)S(1)}, u32[]{:S(2)}, u32[]{:S(2)}) collective-permute-start(f32[8,4096]{1,0:T(8,128)S(1)} %get-tuple-element.47.own_even), channel_id=1, source_target_pairs={{0,2},{2,0},{4,6},{6,4},{8,10},{10,8},{12,14},{14,12},{16,18},{18,... | collective-permute-start | bytes 393224 | tf_op jit(solution)/shard_map/ppermute | solution.py:414
  14.0 0.7 %fusion = (f32[1,2]{1,0:T(1,128)S(1)}, s32[1,2]{1,0:T(1,128)S(1)}) fusion(s32[1,2]{1,0:T(1,128)} %param.7), kind=kLoop, calls=%fused_computation.13 | loop fusion | flops 4 | bytes 24 | tf_op jit(solution)/shard_map/convert_element_type | solution.py:526
  14.7 2.6 %smooth.1 = (f32[2,16,4096]{2,1,0:T(8,128)S(1)}, bf16[448,4352]{1,0:T(8,128)(2,1)S(1)}, f32[16,128]{1,0:T(8,128)S(1)}, bf16[512,256]{1,0:T(8,128)(2,1)S(1)}) custom-call(f32[2,16,4096]{2,1,0:T(8,128)S(1)} %broadcast_maximum_fusion.frames, f32[2,4,4096]{2,1,0:T(4,128)S(1)} %collective-permute-done.from_odd, f32[2,4,4096]{2,1,0:T(4,128)S(1)} %collective-permute-done.1.from_even), custom_call_target="tpu_custom_call" | custom-call | bytes 8388608 | tf_op jit(solution)/shard_map/smooth/pallas_call | solution.py:473
  17.3 3.8 %match.1 = (bf16[34,64,128]{2,1,0:T(8,128)(2,1)S(1)}, f32[1,128]{1,0:T(1,128)S(1)}) custom-call(s32[1,2]{1,0:T(1,128)S(1)} %get-tuple-element.52.base, f32[8,4096]{1,0:T(8,128)S(1)} %get-tuple-element.48.own_odd, f32[8,4096]{1,0:T(8,128)S(1)} %get-tuple-element.47.own_even, f32[8,4096]{1,0:T(8,128)S(1)} %collective-permute-done.3.from_odd, ...), custom_call_target="tpu_custom_call" | custom-call | bytes 12582912 | tf_op jit(solution)/shard_map/match/pallas_call | solution.py:493
  21.1 1.1 %collective-permute-done.5 = f32[1,128]{1,0:T(1,128)S(1)} collective-permute-done((f32[1,128]{1,0:T(1,128)S(1)}, f32[1,128]{1,0:T(1,128)S(1)}, u32[]{:S(2)}, u32[]{:S(2)}) %collective-permute-start.5) | collective-permute-done | bytes 544 | tf_op jit(solution)/shard_map/ppermute | solution.py:414
  22.2 0.6 %broadcast_in_dim.6 = f32[8,1,128]{2,1,0:T(1,128)} broadcast(f32[128]{0:T(128)S(1)} %add_bitcast_fusion.1), dimensions={2} | broadcast | bytes 4608 | tf_op jit(solution)/shard_map/broadcast_in_dim | solution.py:439
  22.8 5.6 %all-to-all-start = ((f32[8,1,128]{2,1,0:T(1,128)}), f32[8,1,128]{2,1,0:T(1,128)S(1)}, u32[]{:S(2)}, u32[]{:S(2)}) async-start(f32[8,1,128]{2,1,0:T(1,128)} %broadcast_in_dim.6), calls=%async_computation | async-start | bytes 8192 | tf_op jit(solution)/shard_map/all_to_all | solution.py:440
  28.5 1.5 %collective-permute-start.8 = (f32[2,16,4096]{2,1,0:T(8,128)S(1)}, f32[2,16,4096]{2,1,0:T(8,128)S(1)}, u32[]{:S(2)}, u32[]{:S(2)}) collective-permute-start(f32[2,16,4096]{2,1,0:T(8,128)S(1)} %get-tuple-element.38.inverse), channel_id=1, source_target_pairs={{0,1},{1,0},{2,3},{3,2},{4,5},{5,4},{6,7},{7,6},{8,9},{9,8},{10,11... | collective-permute-start | bytes 1572872 | tf_op jit(solution)/shard_map/ppermute | solution.py:414
  30.0 4.9 %all-to-all-done = f32[8,1,128]{2,1,0:T(1,128)S(1)} async-done(((f32[8,1,128]{2,1,0:T(1,128)}), f32[8,1,128]{2,1,0:T(1,128)S(1)}, u32[]{:S(2)}, u32[]{:S(2)}) %all-to-all-start) | async-done | bytes 4128 | tf_op jit(solution)/shard_map/all_to_all | solution.py:440
  34.9 4.3 %pressure.1 = (f32[2,16,4096]{2,1,0:T(8,128)}, f32[2,16,4096]{2,1,0:T(8,128)S(1)}, f32[1,128]{1,0:T(1,128)S(1)}) custom-call(s32[1,2]{1,0:T(1,128)S(1)} %get-tuple-element.52.base, f32[1,128]{1,0:T(1,128)S(1)} %bitcast.12, bf16[34,64,128]{2,1,0:T(8,128)(2,1)S(1)} %get-tuple-element.33.clean, f32[2,16,4096]{2,1,0:T(8,128)S(1)} %get-tuple-element.38.inverse), custom_call_target="tpu_custom_call" | custom-call | bytes 12582912 | tf_op jit(solution)/shard_map/pressure/pallas_call | solution.py:515
  39.2 1.6 %collective-permute-start.7 = (f32[1,128]{1,0:T(1,128)S(1)}, f32[1,128]{1,0:T(1,128)S(1)}, u32[]{:S(2)}, u32[]{:S(2)}) collective-permute-start(f32[1,128]{1,0:T(1,128)S(1)} %pad_maximum_fusion), channel_id=1, source_target_pairs={{0,1},{1,0},{2,3},{3,2},{4,5},{5,4},{6,7},{7,6},{8,9},{9,8},{10,11... | collective-permute-start | bytes 1544 | tf_op jit(solution)/shard_map/ppermute | solution.py:414
  40.8 0.6 %broadcast_in_dim.15 = f32[8,1,128]{2,1,0:T(1,128)} broadcast(f32[128]{0:T(128)S(1)} %add_bitcast_fusion), dimensions={2} | broadcast | bytes 4608 | tf_op jit(solution)/shard_map/broadcast_in_dim | solution.py:439
  41.4 3.3 %all-to-all-start.1 = ((f32[8,1,128]{2,1,0:T(1,128)}), f32[8,1,128]{2,1,0:T(1,128)S(1)}, u32[]{:S(2)}, u32[]{:S(2)}) async-start(f32[8,1,128]{2,1,0:T(1,128)} %broadcast_in_dim.15), calls=%async_computation.1 | async-start | bytes 8192 | tf_op jit(solution)/shard_map/all_to_all | solution.py:440
  44.7 0.1 slice_convert_fusion.base
  44.8 4.3 %time.1 = (f32[16,4096]{1,0:T(8,128)}, f32[16,4096]{1,0:T(8,128)}) custom-call(s32[1,2]{1,0:T(1,128)S(1)} %slice_convert_fusion.base, f32[1,128]{1,0:T(1,128)S(1)} %collective-permute-done.7.totals, bf16[34,64,128]{2,1,0:T(8,128)(2,1)S(1)} %get-tuple-element.33.clean, f32[2,16,4096]{2,1,0:T(8,128)S(1)} %collective-permute-done.8.inverse, ...), custom_call_target="tpu_custom_call" | custom-call | bytes 12582912 | tf_op jit(solution)/shard_map/time/pallas_call | solution.py:529
  49.1 2.0 %all-to-all-done.1 = f32[8,1,128]{2,1,0:T(1,128)S(1)} async-done(((f32[8,1,128]{2,1,0:T(1,128)}), f32[8,1,128]{2,1,0:T(1,128)S(1)}, u32[]{:S(2)}, u32[]{:S(2)}) %all-to-all-start.1) | async-done | bytes 4128 | tf_op jit(solution)/shard_map/all_to_all | solution.py:440
  51.1 0.6 %subtract_sqrt_fusion = (f32[2]{0:T(128)}, f32[2]{0:T(128)}) fusion(f32[128]{0:T(128)S(1)} %reduce_sum.19), kind=kLoop, calls=%fused_computation.7 | loop fusion | flops 8 | bytes 32 | tf_op jit(solution)/shard_map/sqrt | solution.py:549
  (16 shorter events, 0.3 us)
Async XLA Ops:
  0.6 9.5 %collective-permute-start.2 = (f32[16,4096]{1,0:T(8,128)}, f32[16,4096]{1,0:T(8,128)S(1)}, u32[]{:S(2)}, u32[]{:S(2)}) collective-permute-start(f32[16,4096]{1,0:T(8,128)} %bitcast.14), channel_id=1, source_target_pairs={{0,1},{1,0},{2,3},{3,2},{4,5},{5,4},{6,7},{7,6},{8,9},{9,8},{10,11... | collective-permute-start | bytes 786440 | tf_op jit(solution)/shard_map/ppermute | solution.py:414
  5.8 8.9 %collective-permute-start = (f32[2,4,4096]{2,1,0:T(4,128)S(1)}, f32[2,4,4096]{2,1,0:T(4,128)S(1)}, u32[]{:S(2)}, u32[]{:S(2)}) collective-permute-start(f32[2,4,4096]{2,1,0:T(4,128)S(1)} %get-tuple-element.50), channel_id=1, source_target_pairs={{0,0},{2,4},{4,2},{6,8},{8,6},{10,12},{12,10},{14,16},{16,14},{18,... | collective-permute-start | bytes 393224 | tf_op jit(solution)/shard_map/ppermute | solution.py:414
  6.5 8.2 %collective-permute-start.1 = (f32[2,4,4096]{2,1,0:T(4,128)S(1)}, f32[2,4,4096]{2,1,0:T(4,128)S(1)}, u32[]{:S(2)}, u32[]{:S(2)}) collective-permute-start(f32[2,4,4096]{2,1,0:T(4,128)S(1)} %get-tuple-element.49), channel_id=1, source_target_pairs={{0,2},{2,0},{4,6},{6,4},{8,10},{10,8},{12,14},{14,12},{16,18},{18,... | collective-permute-start | bytes 393224 | tf_op jit(solution)/shard_map/ppermute | solution.py:414
  10.2 7.1 %collective-permute-start.3 = (f32[8,4096]{1,0:T(8,128)S(1)}, f32[8,4096]{1,0:T(8,128)S(1)}, u32[]{:S(2)}, u32[]{:S(2)}) collective-permute-start(f32[8,4096]{1,0:T(8,128)S(1)} %get-tuple-element.48.own_odd), channel_id=1, source_target_pairs={{0,0},{2,4},{4,2},{6,8},{8,6},{10,12},{12,10},{14,16},{16,14},{18,... | collective-permute-start | bytes 393224 | tf_op jit(solution)/shard_map/ppermute | solution.py:414
  10.9 6.4 %collective-permute-start.4 = (f32[8,4096]{1,0:T(8,128)S(1)}, f32[8,4096]{1,0:T(8,128)S(1)}, u32[]{:S(2)}, u32[]{:S(2)}) collective-permute-start(f32[8,4096]{1,0:T(8,128)S(1)} %get-tuple-element.47.own_even), channel_id=1, source_target_pairs={{0,2},{2,0},{4,6},{6,4},{8,10},{10,8},{12,14},{14,12},{16,18},{18,... | collective-permute-start | bytes 393224 | tf_op jit(solution)/shard_map/ppermute | solution.py:414
  21.1 1.2 %collective-permute-start.5 = (f32[1,128]{1,0:T(1,128)S(1)}, f32[1,128]{1,0:T(1,128)S(1)}, u32[]{:S(2)}, u32[]{:S(2)}) collective-permute-start(f32[1,128]{1,0:T(1,128)S(1)} %get-tuple-element.32), channel_id=1, source_target_pairs={{0,2},{2,0},{4,6},{6,4},{8,10},{10,8},{12,14},{14,12},{16,18},{18,... | collective-permute-start | bytes 1544 | tf_op jit(solution)/shard_map/ppermute | solution.py:414
  22.8 12.0 %all-to-all-start = ((f32[8,1,128]{2,1,0:T(1,128)}), f32[8,1,128]{2,1,0:T(1,128)S(1)}, u32[]{:S(2)}, u32[]{:S(2)}) async-start(f32[8,1,128]{2,1,0:T(1,128)} %broadcast_in_dim.6), calls=%async_computation | async-start | bytes 8192 | tf_op jit(solution)/shard_map/all_to_all | solution.py:440
  28.5 16.4 %collective-permute-start.8 = (f32[2,16,4096]{2,1,0:T(8,128)S(1)}, f32[2,16,4096]{2,1,0:T(8,128)S(1)}, u32[]{:S(2)}, u32[]{:S(2)}) collective-permute-start(f32[2,16,4096]{2,1,0:T(8,128)S(1)} %get-tuple-element.38.inverse), channel_id=1, source_target_pairs={{0,1},{1,0},{2,3},{3,2},{4,5},{5,4},{6,7},{7,6},{8,9},{9,8},{10,11... | collective-permute-start | bytes 1572872 | tf_op jit(solution)/shard_map/ppermute | solution.py:414
  39.2 1.6 %collective-permute-start.6 = (f32[1,128]{1,0:T(1,128)S(1)}, f32[1,128]{1,0:T(1,128)S(1)}, u32[]{:S(2)}, u32[]{:S(2)}) collective-permute-start(f32[1,128]{1,0:T(1,128)S(1)} %get-tuple-element.36), channel_id=1, source_target_pairs={{0,2},{2,0},{4,6},{6,4},{8,10},{10,8},{12,14},{14,12},{16,18},{18,... | collective-permute-start | bytes 1544 | tf_op jit(solution)/shard_map/ppermute | solution.py:414
  39.2 5.5 %collective-permute-start.7 = (f32[1,128]{1,0:T(1,128)S(1)}, f32[1,128]{1,0:T(1,128)S(1)}, u32[]{:S(2)}, u32[]{:S(2)}) collective-permute-start(f32[1,128]{1,0:T(1,128)S(1)} %pad_maximum_fusion), channel_id=1, source_target_pairs={{0,1},{1,0},{2,3},{3,2},{4,5},{5,4},{6,7},{7,6},{8,9},{9,8},{10,11... | collective-permute-start | bytes 1544 | tf_op jit(solution)/shard_map/ppermute | solution.py:414
  41.4 9.7 %all-to-all-start.1 = ((f32[8,1,128]{2,1,0:T(1,128)}), f32[8,1,128]{2,1,0:T(1,128)S(1)}, u32[]{:S(2)}, u32[]{:S(2)}) async-start(f32[8,1,128]{2,1,0:T(1,128)} %broadcast_in_dim.15), calls=%async_computation.1 | async-start | bytes 8192 | tf_op jit(solution)/shard_map/all_to_all | solution.py:440

commit v10 on v9

--- a/solution.py
+++ b/solution.py
@@ -280,15 +280,15 @@
     lags[count : count + 1, :] = jnp.sum(ref_power, axis=0, keepdims=True)
     powers = jnp.sum(lags[0:8, :], axis=1, keepdims=True)
     packed = packed + jnp.where(lane == count * reach * reach + across, powers, 0.0)
-    part[...] = jnp.sum(packed, axis=0, keepdims=True)
-
-
-def spread_columns(clean, spread, base_col):
+    part[...] = jnp.broadcast_to(jnp.sum(packed, axis=0, keepdims=True), part.shape)
+
+
+def spread_columns(clean, high, low, base_col):
     tiles = clean.shape[0] - 2
-    full = spread.shape[0] // 2
+    full = high.shape[0]
     spare = jnp.zeros((full - reach * slot, tiles * lanes), jnp.bfloat16)
-    spread[reach * slot : full, :] = spare
-    spread[full + reach * slot : 2 * full, :] = spare
+    high[reach * slot : full, :] = spare
+    low[reach * slot : full, :] = spare
 
     def per_offset(j, carry):
         shift = column_shift(base_col + j - 3)
@@ -296,14 +296,18 @@
 
         def step(t, inner):
             turned = shift(clean, t)
-            spread[pl.ds(at, slot), tile_of(t)] = turned[:slot]
-            spread[pl.ds(full + at, slot), tile_of(t)] = turned[slot:]
+            high[pl.ds(at, slot), tile_of(t)] = turned[:slot]
+            low[pl.ds(at, slot), tile_of(t)] = turned[slot:]
             return inner
 
         by_tiles(step, tiles, 32)
         return carry
 
     lax.fori_loop(0, reach, per_offset, 0)
+
+
+def spread_kernel(base, clean, high, low):
+    spread_columns(clean, high, low, base[0, 1])
 
 
 def blend_weights(totals, count):
@@ -339,17 +343,14 @@
     return jnp.concatenate(tiles, axis=1)
 
 
-def pressures(base, totals, clean, spread, inverse):
+def pressures(base, totals, high, low, inverse):
     count, rows, columns = inverse.shape
-    full = spread.shape[0] // 2
     weights = blend_weights(jnp.broadcast_to(totals[0:1, :], (8, lanes)), count)
     bands = [banded(weights[f], f, rows, 1 + base[0, 0]) for f in range(count)]
     mixing = jnp.concatenate(halves(jnp.concatenate(bands, axis=0)), axis=0)
-    spread_columns(clean, spread, base[0, 1])
-
     def chunk_values(where):
-        product = jnp.dot(mixing, spread[0:full, where], preferred_element_type=jnp.float32)
-        product = product + jnp.dot(mixing, spread[full : 2 * full, where], preferred_element_type=jnp.float32)
+        product = jnp.dot(mixing, high[:, where], preferred_element_type=jnp.float32)
+        product = product + jnp.dot(mixing, low[:, where], preferred_element_type=jnp.float32)
         registered = product[: count * rows] + product[count * rows :]
         values = []
         for f in range(count):
@@ -360,9 +361,9 @@
     return chunk_values
 
 
-def pressure_kernel(base, totals, clean, inverse, pressure, moments, part, spread):
+def pressure_kernel(base, totals, high, low, inverse, pressure, moments, part):
     count, rows, columns = inverse.shape
-    chunk_values = pressures(base, totals, clean, spread, inverse)
+    chunk_values = pressures(base, totals, high, low, inverse)
 
     def step(t, sums):
         where = chunk_of(t)
@@ -383,12 +384,13 @@
     for k in range(2 * count):
         value = jnp.sum(jnp.sum(sums[k], axis=0, keepdims=True), axis=1, keepdims=True)
         line = line + jnp.where(lane_of(line.shape) == k, value, 0.0)
-    part[...] = line[0:1]
-
-
-def time_kernel(base, totals, clean, inverse, moments, time_mean, time_rms, spread):
+    part[...] = jnp.broadcast_to(line[0:1], part.shape)
+
+
+def time_kernel(base, totals, clean, inverse, moments, time_mean, time_rms, high, low):
     count, rows, columns = inverse.shape
-    chunk_values = pressures(base, totals, clean, spread, inverse)
+    spread_columns(clean, high, low, base[0, 1])
+    chunk_values = pressures(base, totals, high, low, inverse)
     frames = 2 * count
 
     def step(t, carry):
@@ -430,14 +432,6 @@
     there = by_parity(odd, paired(shard, axis, 0), height, 0)
     here = by_parity(odd, here, height, 0)
     return [jnp.where(mine, own, other) for own, other in zip(here, there)]
-
-
-def total_over_rows(row):
-    size = lax.axis_size("rows")
-    row = row + paired(row, "rows", 0)
-    groups = [list(range(core, size, 2)) for core in range(2)]
-    rows = jnp.broadcast_to(row, (size // 2, lanes))
-    return lax.all_to_all(rows, "rows", 0, 0, axis_index_groups=groups, tiled=True)
 
 
 def total_over(value, axis):
@@ -466,7 +460,6 @@
     own_odd, own_even = from_owner(wind_off[0], run, odd, "frames", run_owner[0])
     from_odd = paired(own_odd, "rows", 1)
     from_even = paired(own_even, "rows", 0)
-    offsets = jnp.clip(search_base, -8, 8)
     frames_odd, frames_even = by_parity(odd, raw, 4, 1)
     frames_odd = paired(frames_odd, "rows", 1)
     frames_even = paired(frames_even, "rows", 0)
@@ -489,10 +482,11 @@
         cost_estimate=cost(8),
         name="smooth",
     )(raw, frames_odd, frames_even)
+    offsets = jnp.clip(search_base, -8, 8)
     blocks = lax.axis_size("frames")
     clean, part = pl.pallas_call(
         match_kernel,
-        out_shape=(jax.ShapeDtypeStruct((tiles + 2, 2 * slot, lanes), bf16), struct((1, lanes))),
+        out_shape=(jax.ShapeDtypeStruct((tiles + 2, 2 * slot, lanes), bf16), struct((size, lanes))),
         in_specs=[smem] + [vmem] * 7,
         out_specs=(vmem, vmem),
         scratch_shapes=[
@@ -509,19 +503,27 @@
     if blocks == 2:
         inverse_out, part = lax.optimization_barrier((inverse, part))
         other_inverse = paired(inverse_out, "frames", 0)
-    parts = total_over_rows(part)
+    parts = lax.all_to_all(part, "rows", 0, 0, tiled=True)
     totals = jnp.sum(parts, axis=0, keepdims=True)
-    spread = pltpu.VMEM((2 * 8 * slot, columns), bf16)
+    spread = (8 * slot, columns)
+    high, low = pl.pallas_call(
+        spread_kernel,
+        out_shape=(jax.ShapeDtypeStruct(spread, bf16),) * 2,
+        in_specs=[smem, vmem],
+        out_specs=(vmem,) * 2,
+        compiler_params=params,
+        cost_estimate=cost(4),
+        name="spread",
+    )(offsets, clean)
     pressure, moments, part = pl.pallas_call(
         pressure_kernel,
-        out_shape=(struct((count, rows, columns)), struct((2, rows, columns)), struct((1, lanes))),
-        in_specs=[smem] + [vmem] * 3,
+        out_shape=(struct((count, rows, columns)), struct((2, rows, columns)), struct((size, lanes))),
+        in_specs=[smem] + [vmem] * 4,
         out_specs=(vmem, vmem, vmem),
-        scratch_shapes=[spread],
         compiler_params=params,
         cost_estimate=cost(12),
         name="pressure",
-    )(offsets, totals, clean, inverse)
+    )(offsets, totals, high, low, inverse)
     if blocks == 2:
         row = jnp.concatenate([totals[:, : lanes - 2], offsets.astype(f32)], axis=1)
         row, part = lax.optimization_barrier((row, part))
@@ -531,7 +533,7 @@
             out_shape=(struct((rows, columns)), struct((rows, columns))),
             in_specs=[smem] + [vmem] * 4,
             out_specs=(vmem, vmem),
-            scratch_shapes=[spread],
+            scratch_shapes=[pltpu.VMEM(spread, bf16)] * 2,
             compiler_params=params,
             cost_estimate=cost(12),
             name="time",
@@ -541,7 +543,7 @@
         total_frames = count * blocks
         time_mean = whole[0] / total_frames
         time_rms = jnp.sqrt(jnp.maximum(whole[1] / total_frames - time_mean * time_mean, 0.0))
-    sums = total_over_rows(part)
+    sums = lax.all_to_all(part, "rows", 0, 0, tiled=True)
     sums, time_mean, time_rms = lax.optimization_barrier((sums, time_mean, time_rms))
     spatial = jnp.sum(sums, axis=0)
     cell_count = rows * columns * size

time: 52.1 us -> 52 us (level)
  waiting for transfers between devices: 8.13 us -> 3.52 us
  local copies, waits for them, and re-layouts: 1.2 us -> 4.77 us
  Pallas kernels: 14.9 us -> 16.6 us
  other arithmetic: 3.6 us -> 2.96 us
    unnamed x0 -> x10, local copies, waits for them, and re-layouts: none -> 4.77 us
    all_to_all x2, waiting for transfers between devices: 6.91 us -> 3.38 us  [the longest x1 2.95 us: shards(): parts = lax.all_to_all(part, 'rows', 0, 0, tiled=True)]
    pallas_call x0 -> x1, Pallas kernels: none -> 2.03 us  [shards(): pl.pallas_call(spread_kernel, out_shape=(jax.ShapeDtypeStruct(spread, bf1...]
    pallas_call x1, Pallas kernels: 4.26 us -> 2.85 us  [shards(): pl.pallas_call(pressure_kernel, out_shape=(struct((count, rows, columns))...]
    broadcast_in_dim x2 -> x0, local copies, waits for them, and re-layouts: 1.2 us -> none  [total_over_rows(): rows = jnp.broadcast_to(row, (size // 2, lanes))]
    ppermute x9 -> x7, starting transfers between devices: 13.6 us -> 12.4 us  [paired(): return lax.ppermute(value, axis, list(enumerate(partner)))]
    ppermute x9 -> x7, waiting for transfers between devices: 1.23 us -> 0.13 us  [paired(): return lax.ppermute(value, axis, list(enumerate(partner)))]
    all_to_all x2, starting transfers between devices: 8.95 us -> 9.81 us  [the longest x1 6.38 us: shards(): parts = lax.all_to_all(part, 'rows', 0, 0, tiled=True)]
  transfers between devices with their start and end apart: 11 -> 9, of which waited for: 4 -> 3; matrix products, arithmetic and copies ran while one was open for 7% -> 5% of each run, Pallas kernels for 21% -> 24%
where the time goes in v10:
time: 52 us; the launch traced here: 51.5 us
  starting transfers between devices  22.3 us (43%)
  Pallas kernels  16.6 us (32%)
  local copies, waits for them, and re-layouts  4.77 us (9%)
  waiting for transfers between devices  3.52 us (7%)
  other arithmetic  2.96 us (6%)
  between operations  1.43 us (3%)
    ppermute x7, starting transfers between devices, paired(): return lax.ppermute(value, axis, list(enumerate(partner)))  12.4 us
    all_to_all x1, starting transfers between devices, shards(): parts = lax.all_to_all(part, 'rows', 0, 0, tiled=True)  6.38 us
    pallas_call x1, Pallas kernels, shards(): pl.pallas_call(time_kernel, out_shape=(struct((rows, columns)), struct((r...  4.79 us
    unnamed x10, local copies, waits for them, and re-layouts  4.77 us
    pallas_call x1, Pallas kernels, shards(): pl.pallas_call(match_kernel, out_shape=(jax.ShapeDtypeStruct((tiles + 2,...  4.36 us
    all_to_all x1, starting transfers between devices, shards(): sums = lax.all_to_all(part, 'rows', 0, 0, tiled=True)  3.43 us
    all_to_all x1, waiting for transfers between devices, shards(): parts = lax.all_to_all(part, 'rows', 0, 0, tiled=True)  2.95 us
    pallas_call x1, Pallas kernels, shards(): pl.pallas_call(pressure_kernel, out_shape=(struct((count, rows, columns))...  2.85 us
  transfers between devices with their start and end apart: 9, of which 3 were waited for; matrix products, arithmetic and copies ran while one was open for 5% of the time, Pallas kernels for 24%

profile of v10, /device:TPU:0, one launch (start us, length us, event | category | flops | bytes accessed | tf_op | source)
XLA Modules:
  0.0 51.5 jit_solution(1490100517421407276)
XLA Ops:
  0.6 3.0 %collective-permute-start.2 = (f32[16,4096]{1,0:T(8,128)}, f32[16,4096]{1,0:T(8,128)S(1)}, u32[]{:S(2)}, u32[]{:S(2)}) collective-permute-start(f32[16,4096]{1,0:T(8,128)} %bitcast.15), channel_id=1, source_target_pairs={{0,1},{1,0},{2,3},{3,2},{4,5},{5,4},{6,7},{7,6},{8,9},{9,8},{10,11... | collective-permute-start | bytes 786440 | tf_op jit(solution)/shard_map/ppermute | solution.py:416
  3.7 1.0 %broadcast_maximum_fusion.1 = f32[16,4096]{1,0:T(8,128)S(1)} fusion(f32[1,16,4096]{2,1,0:T(8,128)} %param.5), kind=kLoop, calls=%fused_computation.3 | loop fusion | flops 65536 | bytes 524288 | tf_op jit(solution)/shard_map/max | solution.py:459
  4.7 1.1 %broadcast_maximum_fusion.frames = f32[2,16,4096]{2,1,0:T(8,128)S(1)} fusion(f32[2,16,4096]{2,1,0:T(8,128)} %param.4), kind=kLoop, calls=%fused_computation | loop fusion | flops 131072 | bytes 1048576 | tf_op jit(solution)/shard_map/max | solution.py:459
  5.8 0.7 %collective-permute-start = (f32[2,4,4096]{2,1,0:T(4,128)S(1)}, f32[2,4,4096]{2,1,0:T(4,128)S(1)}, u32[]{:S(2)}, u32[]{:S(2)}) collective-permute-start(f32[2,4,4096]{2,1,0:T(4,128)S(1)} %get-tuple-element.54), channel_id=1, source_target_pairs={{0,0},{2,4},{4,2},{6,8},{8,6},{10,12},{12,10},{14,16},{16,14},{18,... | collective-permute-start | bytes 393224 | tf_op jit(solution)/shard_map/ppermute | solution.py:416
  6.5 2.9 %collective-permute-start.1 = (f32[2,4,4096]{2,1,0:T(4,128)S(1)}, f32[2,4,4096]{2,1,0:T(4,128)S(1)}, u32[]{:S(2)}, u32[]{:S(2)}) collective-permute-start(f32[2,4,4096]{2,1,0:T(4,128)S(1)} %get-tuple-element.53), channel_id=1, source_target_pairs={{0,2},{2,0},{4,6},{6,4},{8,10},{10,8},{12,14},{14,12},{16,18},{18,... | collective-permute-start | bytes 393224 | tf_op jit(solution)/shard_map/ppermute | solution.py:416
  10.1 0.1 collective-permute-done.2
  10.2 0.7 %collective-permute-start.3 = (f32[8,4096]{1,0:T(8,128)S(1)}, f32[8,4096]{1,0:T(8,128)S(1)}, u32[]{:S(2)}, u32[]{:S(2)}) collective-permute-start(f32[8,4096]{1,0:T(8,128)S(1)} %get-tuple-element.52.own_odd), channel_id=1, source_target_pairs={{0,0},{2,4},{4,2},{6,8},{8,6},{10,12},{12,10},{14,16},{16,14},{18,... | collective-permute-start | bytes 393224 | tf_op jit(solution)/shard_map/ppermute | solution.py:416
  10.9 3.1 %collective-permute-start.4 = (f32[8,4096]{1,0:T(8,128)S(1)}, f32[8,4096]{1,0:T(8,128)S(1)}, u32[]{:S(2)}, u32[]{:S(2)}) collective-permute-start(f32[8,4096]{1,0:T(8,128)S(1)} %get-tuple-element.51.own_even), channel_id=1, source_target_pairs={{0,2},{2,0},{4,6},{6,4},{8,10},{10,8},{12,14},{14,12},{16,18},{18,... | collective-permute-start | bytes 393224 | tf_op jit(solution)/shard_map/ppermute | solution.py:416
  14.1 2.6 %smooth.1 = (f32[2,16,4096]{2,1,0:T(8,128)S(1)}, bf16[448,4352]{1,0:T(8,128)(2,1)S(1)}, f32[16,128]{1,0:T(8,128)S(1)}, bf16[512,256]{1,0:T(8,128)(2,1)S(1)}) custom-call(f32[2,16,4096]{2,1,0:T(8,128)S(1)} %broadcast_maximum_fusion.frames, f32[2,4,4096]{2,1,0:T(4,128)S(1)} %collective-permute-done.from_odd, f32[2,4,4096]{2,1,0:T(4,128)S(1)} %collective-permute-done.1.from_even), custom_call_target="tpu_custom_call" | custom-call | bytes 8388608 | tf_op jit(solution)/shard_map/smooth/pallas_call | solution.py:466
  16.7 4.4 %match.1 = (bf16[34,64,128]{2,1,0:T(8,128)(2,1)S(1)}, f32[16,128]{1,0:T(8,128)}) custom-call(s32[1,2]{1,0:T(1,128)S(1)} %get-tuple-element.56.base, f32[8,4096]{1,0:T(8,128)S(1)} %get-tuple-element.52.own_odd, f32[8,4096]{1,0:T(8,128)S(1)} %get-tuple-element.51.own_even, f32[8,4096]{1,0:T(8,128)S(1)} %collective-permute-done.3.from_odd, ...), custom_call_target="tpu_custom_call" | custom-call | bytes 12582912 | tf_op jit(solution)/shard_map/match/pallas_call | solution.py:487
  21.0 1.5 %collective-permute-start.6 = (f32[2,16,4096]{2,1,0:T(8,128)S(1)}, f32[2,16,4096]{2,1,0:T(8,128)}, u32[]{:S(2)}, u32[]{:S(2)}) collective-permute-start(f32[2,16,4096]{2,1,0:T(8,128)S(1)} %get-tuple-element.42.inverse), channel_id=1, source_target_pairs={{0,1},{1,0},{2,3},{3,2},{4,5},{5,4},{6,7},{7,6},{8,9},{9,8},{10,11... | collective-permute-start | bytes 1572872 | tf_op jit(solution)/shard_map/ppermute | solution.py:416
  22.5 6.4 %all-to-all-start = ((f32[16,1,128]{2,1,0:T(1,128)}), f32[16,1,128]{2,1,0:T(1,128)S(1)}, u32[]{:S(2)}, u32[]{:S(2)}) async-start(f32[16,1,128]{2,1,0:T(1,128)} %bitcast.3), calls=%async_computation | async-start | bytes 16384 | tf_op jit(solution)/shard_map/all_to_all | solution.py:506
  28.9 2.0 %spread.1 = (bf16[256,4096]{1,0:T(8,128)(2,1)S(1)}, bf16[256,4096]{1,0:T(8,128)(2,1)S(1)}) custom-call(s32[1,2]{1,0:T(1,128)S(1)} %get-tuple-element.56.base, bf16[34,64,128]{2,1,0:T(8,128)(2,1)S(1)} %get-tuple-element.35.clean), custom_call_target="tpu_custom_call" | custom-call | bytes 4194304 | tf_op jit(solution)/shard_map/spread/pallas_call | solution.py:509
  31.0 1.3 %copy-done = bf16[256,4096]{1,0:T(8,128)(2,1)} copy-done((bf16[256,4096]{1,0:T(8,128)(2,1)}, bf16[256,4096]{1,0:T(8,128)(2,1)S(1)}, u32[]{:S(2)}) %copy-start) | copy-done | bytes 2097176
  32.3 3.0 %all-to-all-done = f32[16,1,128]{2,1,0:T(1,128)S(1)} async-done(((f32[16,1,128]{2,1,0:T(1,128)}), f32[16,1,128]{2,1,0:T(1,128)S(1)}, u32[]{:S(2)}, u32[]{:S(2)}) %all-to-all-start) | async-done | bytes 8224 | tf_op jit(solution)/shard_map/all_to_all | solution.py:506
  35.3 1.6 %copy-done.1 = bf16[256,4096]{1,0:T(8,128)(2,1)S(1)} copy-done((bf16[256,4096]{1,0:T(8,128)(2,1)S(1)}, bf16[256,4096]{1,0:T(8,128)(2,1)}, u32[]{:S(2)}) %copy-start.1) | copy-done | bytes 2097176
  36.9 2.8 %pressure.1 = (f32[2,16,4096]{2,1,0:T(8,128)}, f32[2,16,4096]{2,1,0:T(8,128)S(1)}, f32[16,128]{1,0:T(8,128)}) custom-call(s32[1,2]{1,0:T(1,128)S(1)} %get-tuple-element.56.base, f32[1,128]{1,0:T(1,128)S(1)} %bitcast.13, bf16[256,4096]{1,0:T(8,128)(2,1)S(1)} %get-tuple-element.36.high, bf16[256,4096]{1,0:T(8,128)(2,1)S(1)} %copy-done.1, ...), custom_call_target="tpu_custom_call" | custom-call | bytes 12582912 | tf_op jit(solution)/shard_map/pressure/pallas_call | solution.py:518
  39.7 0.8 %copy-done.2 = f32[2,16,4096]{2,1,0:T(8,128)} copy-done((f32[2,16,4096]{2,1,0:T(8,128)}, f32[2,16,4096]{2,1,0:T(8,128)S(1)}, u32[]{:S(2)}) %copy-start.2) | copy-done | bytes 524312
  40.6 0.5 collective-permute-start.5
  41.1 3.4 %all-to-all-start.1 = ((f32[16,1,128]{2,1,0:T(1,128)}), f32[16,1,128]{2,1,0:T(1,128)S(1)}, u32[]{:S(2)}, u32[]{:S(2)}) async-start(f32[16,1,128]{2,1,0:T(1,128)} %bitcast.6), calls=%async_computation.1 | async-start | bytes 16384 | tf_op jit(solution)/shard_map/all_to_all | solution.py:546
  44.6 1.0 %copy-done.3 = f32[2,16,4096]{2,1,0:T(8,128)S(1)} copy-done((f32[2,16,4096]{2,1,0:T(8,128)S(1)}, f32[2,16,4096]{2,1,0:T(8,128)}, u32[]{:S(2)}) %copy-start.3) | copy-done | bytes 524312
  45.7 4.8 %time.1 = (f32[16,4096]{1,0:T(8,128)}, f32[16,4096]{1,0:T(8,128)}) custom-call(s32[1,2]{1,0:T(1,128)S(1)} %slice_convert_fusion.base, f32[1,128]{1,0:T(1,128)S(1)} %collective-permute-done.5.totals, bf16[34,64,128]{2,1,0:T(8,128)(2,1)S(1)} %get-tuple-element.35.clean, f32[2,16,4096]{2,1,0:T(8,128)} %collective-permute-done.6.inverse, ...), custom_call_target="tpu_custom_call" | custom-call | bytes 12582912 | tf_op jit(solution)/shard_map/time/pallas_call | solution.py:531
  50.5 0.4 all-to-all-done.1
  50.9 0.6 %subtract_sqrt_fusion = (f32[2]{0:T(128)}, f32[2]{0:T(128)}) fusion(f32[128]{0:T(128)S(1)} %reduce_sum.19), kind=kLoop, calls=%fused_computation.7 | loop fusion | flops 8 | bytes 32 | tf_op jit(solution)/shard_map/sqrt | solution.py:551
  (19 shorter events, 0.3 us)
Async XLA Ops:
  0.6 13.4 %copy-start.4 = (s32[1,2]{1,0:T(1,128)S(1)}, s32[1,2]{1,0:T(1,128)}, u32[]{:S(2)}) copy-start(s32[1,2]{1,0:T(1,128)} %param.7) | copy-start | bytes 28
  0.6 9.5 %collective-permute-start.2 = (f32[16,4096]{1,0:T(8,128)}, f32[16,4096]{1,0:T(8,128)S(1)}, u32[]{:S(2)}, u32[]{:S(2)}) collective-permute-start(f32[16,4096]{1,0:T(8,128)} %bitcast.15), channel_id=1, source_target_pairs={{0,1},{1,0},{2,3},{3,2},{4,5},{5,4},{6,7},{7,6},{8,9},{9,8},{10,11... | collective-permute-start | bytes 786440 | tf_op jit(solution)/shard_map/ppermute | solution.py:416
  5.8 8.2 %collective-permute-start = (f32[2,4,4096]{2,1,0:T(4,128)S(1)}, f32[2,4,4096]{2,1,0:T(4,128)S(1)}, u32[]{:S(2)}, u32[]{:S(2)}) collective-permute-start(f32[2,4,4096]{2,1,0:T(4,128)S(1)} %get-tuple-element.54), channel_id=1, source_target_pairs={{0,0},{2,4},{4,2},{6,8},{8,6},{10,12},{12,10},{14,16},{16,14},{18,... | collective-permute-start | bytes 393224 | tf_op jit(solution)/shard_map/ppermute | solution.py:416
  6.5 7.5 %collective-permute-start.1 = (f32[2,4,4096]{2,1,0:T(4,128)S(1)}, f32[2,4,4096]{2,1,0:T(4,128)S(1)}, u32[]{:S(2)}, u32[]{:S(2)}) collective-permute-start(f32[2,4,4096]{2,1,0:T(4,128)S(1)} %get-tuple-element.53), channel_id=1, source_target_pairs={{0,2},{2,0},{4,6},{6,4},{8,10},{10,8},{12,14},{14,12},{16,18},{18,... | collective-permute-start | bytes 393224 | tf_op jit(solution)/shard_map/ppermute | solution.py:416
  10.2 6.4 %collective-permute-start.3 = (f32[8,4096]{1,0:T(8,128)S(1)}, f32[8,4096]{1,0:T(8,128)S(1)}, u32[]{:S(2)}, u32[]{:S(2)}) collective-permute-start(f32[8,4096]{1,0:T(8,128)S(1)} %get-tuple-element.52.own_odd), channel_id=1, source_target_pairs={{0,0},{2,4},{4,2},{6,8},{8,6},{10,12},{12,10},{14,16},{16,14},{18,... | collective-permute-start | bytes 393224 | tf_op jit(solution)/shard_map/ppermute | solution.py:416
  10.9 5.7 %collective-permute-start.4 = (f32[8,4096]{1,0:T(8,128)S(1)}, f32[8,4096]{1,0:T(8,128)S(1)}, u32[]{:S(2)}, u32[]{:S(2)}) collective-permute-start(f32[8,4096]{1,0:T(8,128)S(1)} %get-tuple-element.51.own_even), channel_id=1, source_target_pairs={{0,2},{2,0},{4,6},{6,4},{8,10},{10,8},{12,14},{14,12},{16,18},{18,... | collective-permute-start | bytes 393224 | tf_op jit(solution)/shard_map/ppermute | solution.py:416
  21.0 23.6 %collective-permute-start.6 = (f32[2,16,4096]{2,1,0:T(8,128)S(1)}, f32[2,16,4096]{2,1,0:T(8,128)}, u32[]{:S(2)}, u32[]{:S(2)}) collective-permute-start(f32[2,16,4096]{2,1,0:T(8,128)S(1)} %get-tuple-element.42.inverse), channel_id=1, source_target_pairs={{0,1},{1,0},{2,3},{3,2},{4,5},{5,4},{6,7},{7,6},{8,9},{9,8},{10,11... | collective-permute-start | bytes 1572872 | tf_op jit(solution)/shard_map/ppermute | solution.py:416
  22.5 12.7 %all-to-all-start = ((f32[16,1,128]{2,1,0:T(1,128)}), f32[16,1,128]{2,1,0:T(1,128)S(1)}, u32[]{:S(2)}, u32[]{:S(2)}) async-start(f32[16,1,128]{2,1,0:T(1,128)} %bitcast.3), calls=%async_computation | async-start | bytes 16384 | tf_op jit(solution)/shard_map/all_to_all | solution.py:506
  31.0 1.3 %copy-start = (bf16[256,4096]{1,0:T(8,128)(2,1)}, bf16[256,4096]{1,0:T(8,128)(2,1)S(1)}, u32[]{:S(2)}) copy-start(bf16[256,4096]{1,0:T(8,128)(2,1)S(1)} %get-tuple-element.37.low) | copy-start | bytes 6291460
  35.3 1.6 %copy-start.1 = (bf16[256,4096]{1,0:T(8,128)(2,1)S(1)}, bf16[256,4096]{1,0:T(8,128)(2,1)}, u32[]{:S(2)}) copy-start(bf16[256,4096]{1,0:T(8,128)(2,1)} %copy-done) | copy-start | bytes 6291460
  39.7 0.8 %copy-start.2 = (f32[2,16,4096]{2,1,0:T(8,128)}, f32[2,16,4096]{2,1,0:T(8,128)S(1)}, u32[]{:S(2)}) copy-start(f32[2,16,4096]{2,1,0:T(8,128)S(1)} %get-tuple-element.43.moments) | copy-start | bytes 1572868
  40.6 4.0 %collective-permute-start.5 = (f32[1,128]{1,0:T(1,128)S(1)}, f32[1,128]{1,0:T(1,128)S(1)}, u32[]{:S(2)}, u32[]{:S(2)}) collective-permute-start(f32[1,128]{1,0:T(1,128)S(1)} %pad_maximum_fusion), channel_id=1, source_target_pairs={{0,1},{1,0},{2,3},{3,2},{4,5},{5,4},{6,7},{7,6},{8,9},{9,8},{10,11... | collective-permute-start | bytes 1544 | tf_op jit(solution)/shard_map/ppermute | solution.py:416
  41.1 9.8 %all-to-all-start.1 = ((f32[16,1,128]{2,1,0:T(1,128)}), f32[16,1,128]{2,1,0:T(1,128)S(1)}, u32[]{:S(2)}, u32[]{:S(2)}) async-start(f32[16,1,128]{2,1,0:T(1,128)} %bitcast.6), calls=%async_computation.1 | async-start | bytes 16384 | tf_op jit(solution)/shard_map/all_to_all | solution.py:546
  44.6 1.0 %copy-start.3 = (f32[2,16,4096]{2,1,0:T(8,128)S(1)}, f32[2,16,4096]{2,1,0:T(8,128)}, u32[]{:S(2)}) copy-start(f32[2,16,4096]{2,1,0:T(8,128)} %copy-done.2) | copy-start | bytes 1572868

commit v11 on v9

--- a/solution.py
+++ b/solution.py
@@ -13,7 +13,6 @@
 calib_square = 0.15
 lanes = 128
 reach = 7
-slot = 32
 params = pltpu.CompilerParams(vmem_limit_bytes=14 * 1024 * 1024)
 vmem = pl.BlockSpec(memory_space=pltpu.VMEM)
 smem = pl.BlockSpec(memory_space=pltpu.SMEM)
@@ -105,7 +104,7 @@
         result = value
         for times in range(1, 4):
             amount = times * unit
-            turned = pltpu.roll(value, amount if direction > 0 else lanes - amount, 1)
+            turned = pltpu.roll(value, amount if direction > 0 else value.shape[1] - amount, 1)
             result = jnp.where(digit == times, turned, result)
         value = result
         unit *= 4
@@ -193,7 +192,7 @@
 
 
 def match_kernel(
-    base, own_odd, own_even, from_odd, from_even, stack, power, band, clean, part, rows_in, padded, fine, stream, lags
+    base, own_odd, own_even, from_odd, from_even, stack, power, band, clean, part, rows_in, padded, fine, stream, folded, lags
 ):
     rows = own_odd.shape[0] * 2
     tiles = own_odd.shape[1] // lanes
@@ -204,17 +203,16 @@
     last_row = lax.axis_size("rows") - 1
     odd = row_index % 2 == 1
     edge = at_edge()
-    empty = jnp.zeros((2 * slot, lanes), jnp.bfloat16)
+    empty = jnp.zeros((2 * wide, lanes), jnp.bfloat16)
     padded[:, tile_of(0)] = empty
     padded[:, tile_of(tiles + 1)] = empty
     for array in (clean, fine):
         array[0] = empty
         array[tiles + 1] = empty
     fine[tiles + 2] = empty
-    spare = jnp.zeros((slot - wide, lanes), jnp.float32)
-    place = lax.broadcasted_iota(jnp.int32, (slot, 2 * lanes), 0)
+    place = lax.broadcasted_iota(jnp.int32, (wide, 2 * lanes), 0)
     own = (place >= 4) & (place < rows + 4)
-    inside = ((place >= 4) | (row_index > 0)) & ((place < rows + 4) | (row_index < last_row)) & (place < wide)
+    inside = ((place >= 4) | (row_index > 0)) & ((place < rows + 4) | (row_index < last_row))
 
     def load_step(t, carry):
         outer = [jnp.where(edge, 0.0, from_odd[:, tile_of(t)]), own_odd[:, tile_of(t)]]
@@ -226,13 +224,12 @@
         return carry
 
     def vertical_step(t, carry):
-        value = vertical(lambda s: rows_in[t, pl.ds(s, wide), :])
-        padded[:, tile_of(t + 1)] = cut(jnp.concatenate([value, spare], axis=0))
+        padded[:, tile_of(t + 1)] = cut(vertical(lambda s: rows_in[t, pl.ds(s, wide), :]))
         return carry
 
     def horizontal_step(t, total):
         smooth = jnp.where(inside, horizontal(padded, band, t), 0.0)
-        raw = [jnp.concatenate([rows_in[2 * t + c, pl.ds(4, wide), :], spare], axis=0) for c in range(2)]
+        raw = [rows_in[2 * t + c, pl.ds(4, wide), :] for c in range(2)]
         detail = jnp.concatenate(raw, axis=1) - smooth
         square = jnp.where(own, detail * detail, 0.0)
         for array, value in ((clean, cut(smooth)), (fine, cut(detail))):
@@ -245,10 +242,9 @@
     ref_power = by_tiles(horizontal_step, tiles // 2, 8, jnp.zeros((8, lanes), jnp.float32))
     fine[tiles + 3] = fine[1]
     shift = column_shift(base[0, 1])
-    stream[2 * slot : 4 * slot, :] = jnp.zeros((2 * slot, ring * lanes), jnp.bfloat16)
 
     def stream_step(t, carry):
-        stream[0 : 2 * slot, tile_of(t)] = shift(fine, t)
+        stream[:, tile_of(t)] = shift(fine, t)
         return carry
 
     by_tiles(stream_step, ring, ring // 2)
@@ -256,8 +252,9 @@
         stack[...], stream[...], (((1,), (1,)), ((), ())), preferred_element_type=jnp.float32
     )
     size = reach * count * rows
-    product = product[:size] + product[size:]
-    product = by_row_shift(product, rows, -1)
+    folded[...] = jnp.zeros(folded.shape, jnp.float32)
+    folded[:, 0 : 2 * wide] = product[:size] + product[size:]
+    product = by_row_shift(folded[...], rows, -1)
     lags[...] = jnp.zeros(lags.shape, jnp.float32)
     for j in range(reach):
         for f in range(count):
@@ -272,7 +269,7 @@
         for j in range(reach):
             at = (f * reach + j) * reach
             high = pltpu.roll(block, (back + at) & (lanes - 1), 1)
-            low = pltpu.roll(block, (back + at - slot) & (lanes - 1), 1)
+            low = pltpu.roll(block, (back + at - wide) & (lanes - 1), 1)
             packed = packed + jnp.where((across == j) & (lane >= at) & (lane < at + reach), high + low, 0.0)
     lags[0:8, :] = jnp.zeros((8, lanes), jnp.float32)
     for f in range(count):
@@ -280,24 +277,21 @@
     lags[count : count + 1, :] = jnp.sum(ref_power, axis=0, keepdims=True)
     powers = jnp.sum(lags[0:8, :], axis=1, keepdims=True)
     packed = packed + jnp.where(lane == count * reach * reach + across, powers, 0.0)
-    part[...] = jnp.sum(packed, axis=0, keepdims=True)
+    part[...] = jnp.broadcast_to(jnp.sum(packed, axis=0, keepdims=True), part.shape)
 
 
 def spread_columns(clean, spread, base_col):
     tiles = clean.shape[0] - 2
-    full = spread.shape[0] // 2
-    spare = jnp.zeros((full - reach * slot, tiles * lanes), jnp.bfloat16)
-    spread[reach * slot : full, :] = spare
-    spread[full + reach * slot : 2 * full, :] = spare
+    size = clean.shape[1]
+    spare = spread.shape[0] - reach * size
+    spread[reach * size :, :] = jnp.zeros((spare, tiles * lanes), jnp.bfloat16)
 
     def per_offset(j, carry):
         shift = column_shift(base_col + j - 3)
-        at = pl.multiple_of(j * slot, slot)
+        at = pl.multiple_of(j * size, size)
 
         def step(t, inner):
-            turned = shift(clean, t)
-            spread[pl.ds(at, slot), tile_of(t)] = turned[:slot]
-            spread[pl.ds(full + at, slot), tile_of(t)] = turned[slot:]
+            spread[pl.ds(at, size), tile_of(t)] = shift(clean, t)
             return inner
 
         by_tiles(step, tiles, 32)
@@ -325,31 +319,31 @@
     return weights
 
 
-def banded(weights, f, rows, first_row):
+def banded(weights, f, rows, first_row, depth):
+    wide = rows + 8
+    blank = jnp.zeros((weights.shape[0], depth - lanes), jnp.float32)
+    weights = jnp.concatenate([weights, blank], axis=1)
     lane = lane_of(weights.shape)
-    tiles = []
-    for group in (range(4), range(4, reach)):
-        line = jnp.zeros_like(weights)
-        for j in group:
-            at = first_row + (j % 4) * slot
-            turned = pltpu.roll(weights, (at + 2 * lanes - (f * reach + j) * reach) & (lanes - 1), 1)
-            line = jnp.where((lane >= at) & (lane < at + reach), turned, line)
-        line = jnp.broadcast_to(line[0:1], (rows, lanes))
-        tiles.append(by_row_shift(line, rows, 1))
-    return jnp.concatenate(tiles, axis=1)
+    line = jnp.zeros_like(weights)
+    for j in range(reach):
+        at = first_row + j * 2 * wide
+        amount = at - (f * reach + j) * reach
+        amount = jnp.where(amount < 0, amount + depth, amount)
+        line = jnp.where((lane >= at) & (lane < at + reach), pltpu.roll(weights, amount, 1), line)
+    line = line + pltpu.roll(line, wide, 1)
+    return by_row_shift(jnp.broadcast_to(line[0:1], (rows, depth)), rows, 1)
 
 
 def pressures(base, totals, clean, spread, inverse):
     count, rows, columns = inverse.shape
-    full = spread.shape[0] // 2
+    depth = spread.shape[0]
     weights = blend_weights(jnp.broadcast_to(totals[0:1, :], (8, lanes)), count)
-    bands = [banded(weights[f], f, rows, 1 + base[0, 0]) for f in range(count)]
-    mixing = jnp.concatenate(halves(jnp.concatenate(bands, axis=0)), axis=0)
+    bands = [banded(weights[f], f, rows, 1 + base[0, 0], depth) for f in range(count)]
+    mixing = cut(jnp.concatenate(bands, axis=0))
     spread_columns(clean, spread, base[0, 1])
 
     def chunk_values(where):
-        product = jnp.dot(mixing, spread[0:full, where], preferred_element_type=jnp.float32)
-        product = product + jnp.dot(mixing, spread[full : 2 * full, where], preferred_element_type=jnp.float32)
+        product = jnp.dot(mixing, spread[:, where], preferred_element_type=jnp.float32)
         registered = product[: count * rows] + product[count * rows :]
         values = []
         for f in range(count):
@@ -360,7 +354,7 @@
     return chunk_values
 
 
-def pressure_kernel(base, totals, clean, inverse, pressure, moments, part, spread):
+def pressure_kernel(base, totals, clean, inverse, pressure, moments, part, spread, held, sent):
     count, rows, columns = inverse.shape
     chunk_values = pressures(base, totals, clean, spread, inverse)
 
@@ -369,7 +363,7 @@
         values = chunk_values(where)
         squares = [value * value for value in values]
         for f in range(count):
-            pressure[f, :, where] = values[f]
+            held[f, :, where] = values[f]
         moments[0, :, where] = sum(values[1:], values[0])
         moments[1, :, where] = sum(squares[1:], squares[0])
         result = []
@@ -379,11 +373,14 @@
 
     zero = jnp.zeros((8, lanes), jnp.float32)
     sums = by_tiles(step, columns // (2 * lanes), 8, (zero,) * (2 * count))
+    copy = pltpu.make_async_copy(held, pressure, sent)
+    copy.start()
     line = zero
     for k in range(2 * count):
         value = jnp.sum(jnp.sum(sums[k], axis=0, keepdims=True), axis=1, keepdims=True)
         line = line + jnp.where(lane_of(line.shape) == k, value, 0.0)
-    part[...] = line[0:1]
+    part[...] = jnp.broadcast_to(line[0:1], part.shape)
+    copy.wait()
 
 
 def time_kernel(base, totals, clean, inverse, moments, time_mean, time_rms, spread):
@@ -430,14 +427,6 @@
     there = by_parity(odd, paired(shard, axis, 0), height, 0)
     here = by_parity(odd, here, height, 0)
     return [jnp.where(mine, own, other) for own, other in zip(here, there)]
-
-
-def total_over_rows(row):
-    size = lax.axis_size("rows")
-    row = row + paired(row, "rows", 0)
-    groups = [list(range(core, size, 2)) for core in range(2)]
-    rows = jnp.broadcast_to(row, (size // 2, lanes))
-    return lax.all_to_all(rows, "rows", 0, 0, axis_index_groups=groups, tiled=True)
 
 
 def total_over(value, axis):
@@ -466,7 +455,6 @@
     own_odd, own_even = from_owner(wind_off[0], run, odd, "frames", run_owner[0])
     from_odd = paired(own_odd, "rows", 1)
     from_even = paired(own_even, "rows", 0)
-    offsets = jnp.clip(search_base, -8, 8)
     frames_odd, frames_even = by_parity(odd, raw, 4, 1)
     frames_odd = paired(frames_odd, "rows", 1)
     frames_even = paired(frames_even, "rows", 0)
@@ -489,17 +477,19 @@
         cost_estimate=cost(8),
         name="smooth",
     )(raw, frames_odd, frames_even)
+    offsets = jnp.clip(search_base, -8, 8)
     blocks = lax.axis_size("frames")
     clean, part = pl.pallas_call(
         match_kernel,
-        out_shape=(jax.ShapeDtypeStruct((tiles + 2, 2 * slot, lanes), bf16), struct((1, lanes))),
+        out_shape=(jax.ShapeDtypeStruct((tiles + 2, 2 * wide, lanes), bf16), struct((size, lanes))),
         in_specs=[smem] + [vmem] * 7,
         out_specs=(vmem, vmem),
         scratch_shapes=[
             pltpu.VMEM((tiles, rows + 16, lanes), f32),
-            pltpu.VMEM((2 * slot, (tiles + 2) * lanes), bf16),
-            pltpu.VMEM((ring + 2, 2 * slot, lanes), bf16),
-            pltpu.VMEM((4 * slot, ring * lanes), bf16),
+            pltpu.VMEM((2 * wide, (tiles + 2) * lanes), bf16),
+            pltpu.VMEM((ring + 2, 2 * wide, lanes), bf16),
+            pltpu.VMEM((2 * wide, ring * lanes), bf16),
+            pltpu.VMEM((depth, lanes), f32),
             pltpu.VMEM((8 * count, lanes), f32),
         ],
         compiler_params=params,
@@ -509,15 +499,16 @@
     if blocks == 2:
         inverse_out, part = lax.optimization_barrier((inverse, part))
         other_inverse = paired(inverse_out, "frames", 0)
-    parts = total_over_rows(part)
+    parts = lax.all_to_all(part, "rows", 0, 0, tiled=True)
     totals = jnp.sum(parts, axis=0, keepdims=True)
-    spread = pltpu.VMEM((2 * 8 * slot, columns), bf16)
+    depth = -(-reach * 2 * wide // lanes) * lanes
+    spread = pltpu.VMEM((depth, columns), bf16)
     pressure, moments, part = pl.pallas_call(
         pressure_kernel,
-        out_shape=(struct((count, rows, columns)), struct((2, rows, columns)), struct((1, lanes))),
+        out_shape=(struct((count, rows, columns)), struct((2, rows, columns)), struct((size, lanes))),
         in_specs=[smem] + [vmem] * 3,
-        out_specs=(vmem, vmem, vmem),
-        scratch_shapes=[spread],
+        out_specs=(pl.BlockSpec(memory_space=pl.ANY), vmem, vmem),
+        scratch_shapes=[spread, pltpu.VMEM((count, rows, columns), f32), pltpu.SemaphoreType.DMA],
         compiler_params=params,
         cost_estimate=cost(12),
         name="pressure",
@@ -541,7 +532,7 @@
         total_frames = count * blocks
         time_mean = whole[0] / total_frames
         time_rms = jnp.sqrt(jnp.maximum(whole[1] / total_frames - time_mean * time_mean, 0.0))
-    sums = total_over_rows(part)
+    sums = lax.all_to_all(part, "rows", 0, 0, tiled=True)
     sums, time_mean, time_rms = lax.optimization_barrier((sums, time_mean, time_rms))
     spatial = jnp.sum(sums, axis=0)
     cell_count = rows * columns * size

time: 52.1 us -> 50.5 us (0.969)
  blocking collectives: 0 us -> 11.9 us
  starting transfers between devices: 22.5 us -> 16 us
  waiting for transfers between devices: 8.13 us -> 2.43 us
  local copies, waits for them, and re-layouts: 1.2 us -> 0 us
    all_to_all x0 -> x1, blocking collectives: none -> 11.9 us  [shards(): parts = lax.all_to_all(part, 'rows', 0, 0, tiled=True)]
    all_to_all x2 -> x1, starting transfers between devices: 8.95 us -> 3.48 us  [shards(): sums = lax.all_to_all(part, 'rows', 0, 0, tiled=True)]
    all_to_all x2 -> x1, waiting for transfers between devices: 6.91 us -> 2.3 us  [shards(): sums = lax.all_to_all(part, 'rows', 0, 0, tiled=True)]
    broadcast_in_dim x2 -> x0, local copies, waits for them, and re-layouts: 1.2 us -> none  [total_over_rows(): rows = jnp.broadcast_to(row, (size // 2, lanes))]
    ppermute x9 -> x7, starting transfers between devices: 13.6 us -> 12.5 us  [paired(): return lax.ppermute(value, axis, list(enumerate(partner)))]
    ppermute x9 -> x7, waiting for transfers between devices: 1.23 us -> 0.13 us  [paired(): return lax.ppermute(value, axis, list(enumerate(partner)))]
  transfers between devices with their start and end apart: 11 -> 8, of which waited for: 4 -> 2; matrix products, arithmetic and copies ran while one was open for 7% -> 6% of each run, Pallas kernels for 21% -> 22%
where the time goes in v11:
time: 50.5 us; the launch traced here: 50.1 us
  starting transfers between devices  16 us (32%)
  Pallas kernels  14.8 us (29%)
  blocking collectives  11.9 us (24%)
  other arithmetic  3.62 us (7%)
  waiting for transfers between devices  2.43 us (5%)
  between operations  1.39 us (3%)
    ppermute x7, starting transfers between devices, paired(): return lax.ppermute(value, axis, list(enumerate(partner)))  12.5 us
    all_to_all x1, blocking collectives, shards(): parts = lax.all_to_all(part, 'rows', 0, 0, tiled=True)  11.9 us
    pallas_call x1, Pallas kernels, shards(): pl.pallas_call(pressure_kernel, out_shape=(struct((count, rows, columns))...  4.56 us
    pallas_call x1, Pallas kernels, shards(): pl.pallas_call(time_kernel, out_shape=(struct((rows, columns)), struct((r...  3.98 us
    pallas_call x1, Pallas kernels, shards(): pl.pallas_call(match_kernel, out_shape=(jax.ShapeDtypeStruct((tiles + 2,...  3.69 us
    all_to_all x1, starting transfers between devices, shards(): sums = lax.all_to_all(part, 'rows', 0, 0, tiled=True)  3.48 us
    pallas_call x1, Pallas kernels, shards(): pl.pallas_call(smooth_kernel, out_shape=(struct((count, rows, columns)),...  2.57 us
    all_to_all x1, waiting for transfers between devices, shards(): sums = lax.all_to_all(part, 'rows', 0, 0, tiled=True)  2.3 us
  transfers between devices with their start and end apart: 8, of which 2 were waited for; matrix products, arithmetic and copies ran while one was open for 6% of the time, Pallas kernels for 22%

profile of v11, /device:TPU:0, one launch (start us, length us, event | category | flops | bytes accessed | tf_op | source)
XLA Modules:
  0.0 50.1 jit_solution(1473112753005082985)
XLA Ops:
  0.6 3.0 %collective-permute-start.2 = (f32[16,4096]{1,0:T(8,128)}, f32[16,4096]{1,0:T(8,128)S(1)}, u32[]{:S(2)}, u32[]{:S(2)}) collective-permute-start(f32[16,4096]{1,0:T(8,128)} %bitcast.16), channel_id=1, source_target_pairs={{0,1},{1,0},{2,3},{3,2},{4,5},{5,4},{6,7},{7,6},{8,9},{9,8},{10,11... | collective-permute-start | bytes 786440 | tf_op jit(solution)/shard_map/ppermute | solution.py:411
  3.7 1.0 %broadcast_maximum_fusion.1 = f32[16,4096]{1,0:T(8,128)S(1)} fusion(f32[1,16,4096]{2,1,0:T(8,128)} %param.5), kind=kLoop, calls=%fused_computation.3 | loop fusion | flops 65536 | bytes 524288 | tf_op jit(solution)/shard_map/max | solution.py:454
  4.7 1.1 %broadcast_maximum_fusion.frames = f32[2,16,4096]{2,1,0:T(8,128)S(1)} fusion(f32[2,16,4096]{2,1,0:T(8,128)} %param.4), kind=kLoop, calls=%fused_computation | loop fusion | flops 131072 | bytes 1048576 | tf_op jit(solution)/shard_map/max | solution.py:454
  5.8 0.7 %collective-permute-start = (f32[2,4,4096]{2,1,0:T(4,128)S(1)}, f32[2,4,4096]{2,1,0:T(4,128)S(1)}, u32[]{:S(2)}, u32[]{:S(2)}) collective-permute-start(f32[2,4,4096]{2,1,0:T(4,128)S(1)} %get-tuple-element.50), channel_id=1, source_target_pairs={{0,0},{2,4},{4,2},{6,8},{8,6},{10,12},{12,10},{14,16},{16,14},{18,... | collective-permute-start | bytes 393224 | tf_op jit(solution)/shard_map/ppermute | solution.py:411
  6.5 2.9 %collective-permute-start.1 = (f32[2,4,4096]{2,1,0:T(4,128)S(1)}, f32[2,4,4096]{2,1,0:T(4,128)S(1)}, u32[]{:S(2)}, u32[]{:S(2)}) collective-permute-start(f32[2,4,4096]{2,1,0:T(4,128)S(1)} %get-tuple-element.49), channel_id=1, source_target_pairs={{0,2},{2,0},{4,6},{6,4},{8,10},{10,8},{12,14},{14,12},{16,18},{18,... | collective-permute-start | bytes 393224 | tf_op jit(solution)/shard_map/ppermute | solution.py:411
  10.1 0.1 collective-permute-done.2
  10.2 0.7 %collective-permute-start.3 = (f32[8,4096]{1,0:T(8,128)S(1)}, f32[8,4096]{1,0:T(8,128)S(1)}, u32[]{:S(2)}, u32[]{:S(2)}) collective-permute-start(f32[8,4096]{1,0:T(8,128)S(1)} %get-tuple-element.48.own_odd), channel_id=1, source_target_pairs={{0,0},{2,4},{4,2},{6,8},{8,6},{10,12},{12,10},{14,16},{16,14},{18,... | collective-permute-start | bytes 393224 | tf_op jit(solution)/shard_map/ppermute | solution.py:411
  10.9 3.1 %collective-permute-start.4 = (f32[8,4096]{1,0:T(8,128)S(1)}, f32[8,4096]{1,0:T(8,128)S(1)}, u32[]{:S(2)}, u32[]{:S(2)}) collective-permute-start(f32[8,4096]{1,0:T(8,128)S(1)} %get-tuple-element.47.own_even), channel_id=1, source_target_pairs={{0,2},{2,0},{4,6},{6,4},{8,10},{10,8},{12,14},{14,12},{16,18},{18,... | collective-permute-start | bytes 393224 | tf_op jit(solution)/shard_map/ppermute | solution.py:411
  14.0 0.7 %fusion = (f32[1,2]{1,0:T(1,128)S(1)}, s32[1,2]{1,0:T(1,128)S(1)}) fusion(s32[1,2]{1,0:T(1,128)} %param.7), kind=kLoop, calls=%fused_computation.11 | loop fusion | flops 4 | bytes 24 | tf_op jit(solution)/shard_map/convert_element_type | solution.py:517
  14.7 0.0 collective-permute-done.from_odd
  14.7 0.0 collective-permute-done.1.from_even
  14.7 2.6 %smooth.1 = (f32[2,16,4096]{2,1,0:T(8,128)S(1)}, bf16[448,4352]{1,0:T(8,128)(2,1)S(1)}, f32[16,128]{1,0:T(8,128)S(1)}, bf16[512,256]{1,0:T(8,128)(2,1)S(1)}) custom-call(f32[2,16,4096]{2,1,0:T(8,128)S(1)} %broadcast_maximum_fusion.frames, f32[2,4,4096]{2,1,0:T(4,128)S(1)} %collective-permute-done.from_odd, f32[2,4,4096]{2,1,0:T(4,128)S(1)} %collective-permute-done.1.from_even), custom_call_target="tpu_custom_call" | custom-call | bytes 8388608 | tf_op jit(solution)/shard_map/smooth/pallas_call | solution.py:461
  17.3 0.0 collective-permute-done.3.from_odd
  17.3 3.7 %match.1 = (bf16[34,48,128]{2,1,0:T(8,128)(2,1)S(1)}, f32[16,128]{1,0:T(8,128)S(1)}) custom-call(s32[1,2]{1,0:T(1,128)S(1)} %get-tuple-element.52.base, f32[8,4096]{1,0:T(8,128)S(1)} %get-tuple-element.48.own_odd, f32[8,4096]{1,0:T(8,128)S(1)} %get-tuple-element.47.own_even, f32[8,4096]{1,0:T(8,128)S(1)} %collective-permute-done.3.from_odd, ...), custom_call_target="tpu_custom_call" | custom-call | bytes 12582912 | tf_op jit(solution)/shard_map/match/pallas_call | solution.py:482
  21.0 1.6 %collective-permute-start.6 = (f32[2,16,4096]{2,1,0:T(8,128)S(1)}, f32[2,16,4096]{2,1,0:T(8,128)S(1)}, u32[]{:S(2)}, u32[]{:S(2)}) collective-permute-start(f32[2,16,4096]{2,1,0:T(8,128)S(1)} %get-tuple-element.38.inverse), channel_id=1, source_target_pairs={{0,1},{1,0},{2,3},{3,2},{4,5},{5,4},{6,7},{7,6},{8,9},{9,8},{10,11... | collective-permute-start | bytes 1572872 | tf_op jit(solution)/shard_map/ppermute | solution.py:411
  22.5 11.9 %all_to_all.21 = f32[16,1,128]{2,1,0:T(1,128)S(1)} all-to-all(f32[16,1,128]{2,1,0:T(1,128)S(1)} %bitcast.13), channel_id=1, replica_groups=mesh['rows'=16,'frames'=2] {'rows'}, dimensions={0} | all-to-all | bytes 16384 | tf_op jit(solution)/shard_map/all_to_all | solution.py:502
  34.5 4.6 %pressure.1 = (f32[2,16,4096]{2,1,0:T(8,128)}, f32[2,16,4096]{2,1,0:T(8,128)S(1)}, f32[16,128]{1,0:T(8,128)}) custom-call(s32[1,2]{1,0:T(1,128)S(1)} %get-tuple-element.52.base, f32[1,128]{1,0:T(1,128)S(1)} %bitcast.14, bf16[34,48,128]{2,1,0:T(8,128)(2,1)S(1)} %get-tuple-element.33.clean, f32[2,16,4096]{2,1,0:T(8,128)S(1)} %get-tuple-element.38.inverse), custom_call_target="tpu_custom_call" | custom-call | bytes 12582912 | tf_op jit(solution)/shard_map/pressure/pallas_call | solution.py:506
  39.1 0.1 pad_maximum_fusion
  39.2 0.5 %collective-permute-start.5 = (f32[1,128]{1,0:T(1,128)S(1)}, f32[1,128]{1,0:T(1,128)S(1)}, u32[]{:S(2)}, u32[]{:S(2)}) collective-permute-start(f32[1,128]{1,0:T(1,128)S(1)} %pad_maximum_fusion), channel_id=1, source_target_pairs={{0,1},{1,0},{2,3},{3,2},{4,5},{5,4},{6,7},{7,6},{8,9},{9,8},{10,11... | collective-permute-start | bytes 1544 | tf_op jit(solution)/shard_map/ppermute | solution.py:411
  39.7 3.5 %all-to-all-start.1 = ((f32[16,1,128]{2,1,0:T(1,128)}), f32[16,1,128]{2,1,0:T(1,128)S(1)}, u32[]{:S(2)}, u32[]{:S(2)}) async-start(f32[16,1,128]{2,1,0:T(1,128)} %bitcast.6), calls=%async_computation.1 | async-start | bytes 16384 | tf_op jit(solution)/shard_map/all_to_all | solution.py:535
  43.2 0.1 slice_convert_fusion.base
  43.3 4.0 %time.1 = (f32[16,4096]{1,0:T(8,128)}, f32[16,4096]{1,0:T(8,128)}) custom-call(s32[1,2]{1,0:T(1,128)S(1)} %slice_convert_fusion.base, f32[1,128]{1,0:T(1,128)S(1)} %collective-permute-done.5.totals, bf16[34,48,128]{2,1,0:T(8,128)(2,1)S(1)} %get-tuple-element.33.clean, f32[2,16,4096]{2,1,0:T(8,128)S(1)} %collective-permute-done.6.inverse, ...), custom_call_target="tpu_custom_call" | custom-call | bytes 12582912 | tf_op jit(solution)/shard_map/time/pallas_call | solution.py:520
  47.2 2.3 %all-to-all-done.1 = f32[16,1,128]{2,1,0:T(1,128)S(1)} async-done(((f32[16,1,128]{2,1,0:T(1,128)}), f32[16,1,128]{2,1,0:T(1,128)S(1)}, u32[]{:S(2)}, u32[]{:S(2)}) %all-to-all-start.1) | async-done | bytes 8224 | tf_op jit(solution)/shard_map/all_to_all | solution.py:535
  49.6 0.6 %subtract_sqrt_fusion = (f32[2]{0:T(128)}, f32[2]{0:T(128)}) fusion(f32[128]{0:T(128)S(1)} %reduce_sum.19), kind=kLoop, calls=%fused_computation.7 | loop fusion | flops 8 | bytes 32 | tf_op jit(solution)/shard_map/sqrt | solution.py:540
  (7 shorter events, 0.1 us)
Async XLA Ops:
  0.6 9.5 %collective-permute-start.2 = (f32[16,4096]{1,0:T(8,128)}, f32[16,4096]{1,0:T(8,128)S(1)}, u32[]{:S(2)}, u32[]{:S(2)}) collective-permute-start(f32[16,4096]{1,0:T(8,128)} %bitcast.16), channel_id=1, source_target_pairs={{0,1},{1,0},{2,3},{3,2},{4,5},{5,4},{6,7},{7,6},{8,9},{9,8},{10,11... | collective-permute-start | bytes 786440 | tf_op jit(solution)/shard_map/ppermute | solution.py:411
  5.8 8.9 %collective-permute-start = (f32[2,4,4096]{2,1,0:T(4,128)S(1)}, f32[2,4,4096]{2,1,0:T(4,128)S(1)}, u32[]{:S(2)}, u32[]{:S(2)}) collective-permute-start(f32[2,4,4096]{2,1,0:T(4,128)S(1)} %get-tuple-element.50), channel_id=1, source_target_pairs={{0,0},{2,4},{4,2},{6,8},{8,6},{10,12},{12,10},{14,16},{16,14},{18,... | collective-permute-start | bytes 393224 | tf_op jit(solution)/shard_map/ppermute | solution.py:411
  6.5 8.2 %collective-permute-start.1 = (f32[2,4,4096]{2,1,0:T(4,128)S(1)}, f32[2,4,4096]{2,1,0:T(4,128)S(1)}, u32[]{:S(2)}, u32[]{:S(2)}) collective-permute-start(f32[2,4,4096]{2,1,0:T(4,128)S(1)} %get-tuple-element.49), channel_id=1, source_target_pairs={{0,2},{2,0},{4,6},{6,4},{8,10},{10,8},{12,14},{14,12},{16,18},{18,... | collective-permute-start | bytes 393224 | tf_op jit(solution)/shard_map/ppermute | solution.py:411
  10.2 7.1 %collective-permute-start.3 = (f32[8,4096]{1,0:T(8,128)S(1)}, f32[8,4096]{1,0:T(8,128)S(1)}, u32[]{:S(2)}, u32[]{:S(2)}) collective-permute-start(f32[8,4096]{1,0:T(8,128)S(1)} %get-tuple-element.48.own_odd), channel_id=1, source_target_pairs={{0,0},{2,4},{4,2},{6,8},{8,6},{10,12},{12,10},{14,16},{16,14},{18,... | collective-permute-start | bytes 393224 | tf_op jit(solution)/shard_map/ppermute | solution.py:411
  10.9 6.4 %collective-permute-start.4 = (f32[8,4096]{1,0:T(8,128)S(1)}, f32[8,4096]{1,0:T(8,128)S(1)}, u32[]{:S(2)}, u32[]{:S(2)}) collective-permute-start(f32[8,4096]{1,0:T(8,128)S(1)} %get-tuple-element.47.own_even), channel_id=1, source_target_pairs={{0,2},{2,0},{4,6},{6,4},{8,10},{10,8},{12,14},{14,12},{16,18},{18,... | collective-permute-start | bytes 393224 | tf_op jit(solution)/shard_map/ppermute | solution.py:411
  21.0 22.3 %collective-permute-start.6 = (f32[2,16,4096]{2,1,0:T(8,128)S(1)}, f32[2,16,4096]{2,1,0:T(8,128)S(1)}, u32[]{:S(2)}, u32[]{:S(2)}) collective-permute-start(f32[2,16,4096]{2,1,0:T(8,128)S(1)} %get-tuple-element.38.inverse), channel_id=1, source_target_pairs={{0,1},{1,0},{2,3},{3,2},{4,5},{5,4},{6,7},{7,6},{8,9},{9,8},{10,11... | collective-permute-start | bytes 1572872 | tf_op jit(solution)/shard_map/ppermute | solution.py:411
  39.2 4.0 %collective-permute-start.5 = (f32[1,128]{1,0:T(1,128)S(1)}, f32[1,128]{1,0:T(1,128)S(1)}, u32[]{:S(2)}, u32[]{:S(2)}) collective-permute-start(f32[1,128]{1,0:T(1,128)S(1)} %pad_maximum_fusion), channel_id=1, source_target_pairs={{0,1},{1,0},{2,3},{3,2},{4,5},{5,4},{6,7},{7,6},{8,9},{9,8},{10,11... | collective-permute-start | bytes 1544 | tf_op jit(solution)/shard_map/ppermute | solution.py:411
  39.7 9.9 %all-to-all-start.1 = ((f32[16,1,128]{2,1,0:T(1,128)}), f32[16,1,128]{2,1,0:T(1,128)S(1)}, u32[]{:S(2)}, u32[]{:S(2)}) async-start(f32[16,1,128]{2,1,0:T(1,128)} %bitcast.6), calls=%async_computation.1 | async-start | bytes 16384 | tf_op jit(solution)/shard_map/all_to_all | solution.py:535

commit v12 on v11

--- a/solution.py
+++ b/solution.py
@@ -354,7 +354,7 @@
     return chunk_values
 
 
-def pressure_kernel(base, totals, clean, inverse, pressure, moments, part, spread, held, sent):
+def pressure_kernel(base, totals, clean, inverse, pressure, moments, part, spread):
     count, rows, columns = inverse.shape
     chunk_values = pressures(base, totals, clean, spread, inverse)
 
@@ -363,7 +363,7 @@
         values = chunk_values(where)
         squares = [value * value for value in values]
         for f in range(count):
-            held[f, :, where] = values[f]
+            pressure[f, :, where] = values[f]
         moments[0, :, where] = sum(values[1:], values[0])
         moments[1, :, where] = sum(squares[1:], squares[0])
         result = []
@@ -373,14 +373,11 @@
 
     zero = jnp.zeros((8, lanes), jnp.float32)
     sums = by_tiles(step, columns // (2 * lanes), 8, (zero,) * (2 * count))
-    copy = pltpu.make_async_copy(held, pressure, sent)
-    copy.start()
     line = zero
     for k in range(2 * count):
         value = jnp.sum(jnp.sum(sums[k], axis=0, keepdims=True), axis=1, keepdims=True)
         line = line + jnp.where(lane_of(line.shape) == k, value, 0.0)
     part[...] = jnp.broadcast_to(line[0:1], part.shape)
-    copy.wait()
 
 
 def time_kernel(base, totals, clean, inverse, moments, time_mean, time_rms, spread):
@@ -458,6 +455,7 @@
     frames_odd, frames_even = by_parity(odd, raw, 4, 1)
     frames_odd = paired(frames_odd, "rows", 1)
     frames_even = paired(frames_even, "rows", 0)
+    frames_odd, own_odd = lax.optimization_barrier((frames_odd, own_odd))
     inverse, stack, power, band = pl.pallas_call(
         smooth_kernel,
         out_shape=(
@@ -479,6 +477,8 @@
     )(raw, frames_odd, frames_even)
     offsets = jnp.clip(search_base, -8, 8)
     blocks = lax.axis_size("frames")
+    if blocks == 2:
+        other_inverse = paired(inverse, "frames", 0)
     clean, part = pl.pallas_call(
         match_kernel,
         out_shape=(jax.ShapeDtypeStruct((tiles + 2, 2 * wide, lanes), bf16), struct((size, lanes))),
@@ -496,9 +496,6 @@
         cost_estimate=cost(12),
         name="match",
     )(offsets, own_odd, own_even, from_odd, from_even, stack, power, band)
-    if blocks == 2:
-        inverse_out, part = lax.optimization_barrier((inverse, part))
-        other_inverse = paired(inverse_out, "frames", 0)
     parts = lax.all_to_all(part, "rows", 0, 0, tiled=True)
     totals = jnp.sum(parts, axis=0, keepdims=True)
     depth = -(-reach * 2 * wide // lanes) * lanes
@@ -507,8 +504,8 @@
         pressure_kernel,
         out_shape=(struct((count, rows, columns)), struct((2, rows, columns)), struct((size, lanes))),
         in_specs=[smem] + [vmem] * 3,
-        out_specs=(pl.BlockSpec(memory_space=pl.ANY), vmem, vmem),
-        scratch_shapes=[spread, pltpu.VMEM((count, rows, columns), f32), pltpu.SemaphoreType.DMA],
+        out_specs=(vmem, vmem, vmem),
+        scratch_shapes=[spread],
         compiler_params=params,
         cost_estimate=cost(12),
         name="pressure",

time: 50.5 us -> 49.3 us (0.976)
  blocking collectives: 11.9 us -> 11.2 us
  Pallas kernels: 14.8 us -> 14.2 us
    all_to_all x1, blocking collectives: 11.9 us -> 11.2 us  [shards(): parts = lax.all_to_all(part, 'rows', 0, 0, tiled=True)]
    pallas_call x1, Pallas kernels: 4.56 us -> 3.97 us  [shards(): pl.pallas_call(pressure_kernel, out_shape=(struct((count, rows, columns))...]
  transfers between devices with their start and end apart: 8 -> 8, of which waited for: 2 -> 2; matrix products, arithmetic and copies ran while one was open for 6% -> 6% of each run, Pallas kernels for 22% -> 29%
where the time goes in v12:
time: 49.3 us; the launch traced here: 49 us
  starting transfers between devices  16.2 us (33%)
  Pallas kernels  14.2 us (29%)
  blocking collectives  11.2 us (23%)
  other arithmetic  3.62 us (7%)
  waiting for transfers between devices  2.43 us (5%)
  between operations  1.37 us (3%)
    ppermute x7, starting transfers between devices, paired(): return lax.ppermute(value, axis, list(enumerate(partner)))  12.7 us
    all_to_all x1, blocking collectives, shards(): parts = lax.all_to_all(part, 'rows', 0, 0, tiled=True)  11.2 us
    pallas_call x1, Pallas kernels, shards(): pl.pallas_call(time_kernel, out_shape=(struct((rows, columns)), struct((r...  3.98 us
    pallas_call x1, Pallas kernels, shards(): pl.pallas_call(pressure_kernel, out_shape=(struct((count, rows, columns))...  3.97 us
    pallas_call x1, Pallas kernels, shards(): pl.pallas_call(match_kernel, out_shape=(jax.ShapeDtypeStruct((tiles + 2,...  3.69 us
    all_to_all x1, starting transfers between devices, shards(): sums = lax.all_to_all(part, 'rows', 0, 0, tiled=True)  3.48 us
    pallas_call x1, Pallas kernels, shards(): pl.pallas_call(smooth_kernel, out_shape=(struct((count, rows, columns)),...  2.56 us
    all_to_all x1, waiting for transfers between devices, shards(): sums = lax.all_to_all(part, 'rows', 0, 0, tiled=True)  2.3 us
  transfers between devices with their start and end apart: 8, of which 2 were waited for; matrix products, arithmetic and copies ran while one was open for 6% of the time, Pallas kernels for 29%

profile of v12, /device:TPU:0, one launch (start us, length us, event | category | flops | bytes accessed | tf_op | source)
XLA Modules:
  0.0 49.0 jit_solution(14013827619968924224)
XLA Ops:
  0.6 3.0 %collective-permute-start.1 = (f32[16,4096]{1,0:T(8,128)}, f32[16,4096]{1,0:T(8,128)S(1)}, u32[]{:S(2)}, u32[]{:S(2)}) collective-permute-start(f32[16,4096]{1,0:T(8,128)} %bitcast.16), channel_id=1, source_target_pairs={{0,1},{1,0},{2,3},{3,2},{4,5},{5,4},{6,7},{7,6},{8,9},{9,8},{10,11... | collective-permute-start | bytes 786440 | tf_op jit(solution)/shard_map/ppermute | solution.py:408
  3.7 1.0 %broadcast_maximum_fusion.1 = f32[16,4096]{1,0:T(8,128)S(1)} fusion(f32[1,16,4096]{2,1,0:T(8,128)} %param.5), kind=kLoop, calls=%fused_computation.3 | loop fusion | flops 65536 | bytes 524288 | tf_op jit(solution)/shard_map/max | solution.py:451
  4.7 1.1 %broadcast_maximum_fusion.frames = f32[2,16,4096]{2,1,0:T(8,128)S(1)} fusion(f32[2,16,4096]{2,1,0:T(8,128)} %param.4), kind=kLoop, calls=%fused_computation | loop fusion | flops 131072 | bytes 1048576 | tf_op jit(solution)/shard_map/max | solution.py:451
  5.8 0.7 %collective-permute-start = (f32[2,4,4096]{2,1,0:T(4,128)S(1)}, f32[2,4,4096]{2,1,0:T(4,128)S(1)}, u32[]{:S(2)}, u32[]{:S(2)}) collective-permute-start(f32[2,4,4096]{2,1,0:T(4,128)S(1)} %get-tuple-element.48), channel_id=1, source_target_pairs={{0,0},{2,4},{4,2},{6,8},{8,6},{10,12},{12,10},{14,16},{16,14},{18,... | collective-permute-start | bytes 393224 | tf_op jit(solution)/shard_map/ppermute | solution.py:408
  6.5 2.9 %collective-permute-start.4 = (f32[2,4,4096]{2,1,0:T(4,128)S(1)}, f32[2,4,4096]{2,1,0:T(4,128)S(1)}, u32[]{:S(2)}, u32[]{:S(2)}) collective-permute-start(f32[2,4,4096]{2,1,0:T(4,128)S(1)} %get-tuple-element.47), channel_id=1, source_target_pairs={{0,2},{2,0},{4,6},{6,4},{8,10},{10,8},{12,14},{14,12},{16,18},{18,... | collective-permute-start | bytes 393224 | tf_op jit(solution)/shard_map/ppermute | solution.py:408
  10.1 0.1 collective-permute-done.1
  10.2 0.7 %collective-permute-start.2 = (f32[8,4096]{1,0:T(8,128)S(1)}, f32[8,4096]{1,0:T(8,128)S(1)}, u32[]{:S(2)}, u32[]{:S(2)}) collective-permute-start(f32[8,4096]{1,0:T(8,128)S(1)} %get-tuple-element.27.own_odd), channel_id=1, source_target_pairs={{0,0},{2,4},{4,2},{6,8},{8,6},{10,12},{12,10},{14,16},{16,14},{18,... | collective-permute-start | bytes 393224 | tf_op jit(solution)/shard_map/ppermute | solution.py:408
  10.9 0.0 collective-permute-done.from_odd
  10.9 3.1 %collective-permute-start.3 = (f32[8,4096]{1,0:T(8,128)S(1)}, f32[8,4096]{1,0:T(8,128)S(1)}, u32[]{:S(2)}, u32[]{:S(2)}) collective-permute-start(f32[8,4096]{1,0:T(8,128)S(1)} %get-tuple-element.49.own_even), channel_id=1, source_target_pairs={{0,2},{2,0},{4,6},{6,4},{8,10},{10,8},{12,14},{14,12},{16,18},{18,... | collective-permute-start | bytes 393224 | tf_op jit(solution)/shard_map/ppermute | solution.py:408
  14.0 0.0 collective-permute-done.4.from_even
  14.0 2.6 %smooth.1 = (f32[2,16,4096]{2,1,0:T(8,128)S(1)}, bf16[448,4352]{1,0:T(8,128)(2,1)S(1)}, f32[16,128]{1,0:T(8,128)S(1)}, bf16[512,256]{1,0:T(8,128)(2,1)S(1)}) custom-call(f32[2,16,4096]{2,1,0:T(8,128)S(1)} %broadcast_maximum_fusion.frames, f32[2,4,4096]{2,1,0:T(4,128)S(1)} %collective-permute-done.from_odd, f32[2,4,4096]{2,1,0:T(4,128)S(1)} %collective-permute-done.4.from_even), custom_call_target="tpu_custom_call" | custom-call | bytes 8388608 | tf_op jit(solution)/shard_map/smooth/pallas_call | solution.py:459
  16.6 1.6 %collective-permute-start.6 = (f32[2,16,4096]{2,1,0:T(8,128)S(1)}, f32[2,16,4096]{2,1,0:T(8,128)S(1)}, u32[]{:S(2)}, u32[]{:S(2)}) collective-permute-start(f32[2,16,4096]{2,1,0:T(8,128)S(1)} %get-tuple-element.34.inverse), channel_id=1, source_target_pairs={{0,1},{1,0},{2,3},{3,2},{4,5},{5,4},{6,7},{7,6},{8,9},{9,8},{10,11... | collective-permute-start | bytes 1572872 | tf_op jit(solution)/shard_map/ppermute | solution.py:408
  18.2 0.7 %fusion = (f32[1,2]{1,0:T(1,128)S(1)}, s32[1,2]{1,0:T(1,128)S(1)}) fusion(s32[1,2]{1,0:T(1,128)} %param.7), kind=kLoop, calls=%fused_computation.11 | loop fusion | flops 4 | bytes 24 | tf_op jit(solution)/shard_map/convert_element_type | solution.py:514
  18.9 0.0 collective-permute-done.2.from_odd
  18.9 3.7 %match.1 = (bf16[34,48,128]{2,1,0:T(8,128)(2,1)S(1)}, f32[16,128]{1,0:T(8,128)S(1)}) custom-call(s32[1,2]{1,0:T(1,128)S(1)} %get-tuple-element.52.base, f32[8,4096]{1,0:T(8,128)S(1)} %get-tuple-element.27.own_odd, f32[8,4096]{1,0:T(8,128)S(1)} %get-tuple-element.49.own_even, f32[8,4096]{1,0:T(8,128)S(1)} %collective-permute-done.2.from_odd, ...), custom_call_target="tpu_custom_call" | custom-call | bytes 12582912 | tf_op jit(solution)/shard_map/match/pallas_call | solution.py:482
  22.6 11.2 %all_to_all.21 = f32[16,1,128]{2,1,0:T(1,128)S(1)} all-to-all(f32[16,1,128]{2,1,0:T(1,128)S(1)} %bitcast.13), channel_id=1, replica_groups=mesh['rows'=16,'frames'=2] {'rows'}, dimensions={0} | all-to-all | bytes 16384 | tf_op jit(solution)/shard_map/all_to_all | solution.py:499
  33.8 4.0 %pressure.1 = (f32[2,16,4096]{2,1,0:T(8,128)}, f32[2,16,4096]{2,1,0:T(8,128)S(1)}, f32[16,128]{1,0:T(8,128)}) custom-call(s32[1,2]{1,0:T(1,128)S(1)} %get-tuple-element.52.base, f32[1,128]{1,0:T(1,128)S(1)} %bitcast.14, bf16[34,48,128]{2,1,0:T(8,128)(2,1)S(1)} %get-tuple-element.33.clean, f32[2,16,4096]{2,1,0:T(8,128)S(1)} %get-tuple-element.34.inverse), custom_call_target="tpu_custom_call" | custom-call | bytes 12582912 | tf_op jit(solution)/shard_map/pressure/pallas_call | solution.py:503
  37.7 0.1 pad_maximum_fusion
  37.8 0.7 %collective-permute-start.5 = (f32[1,128]{1,0:T(1,128)S(1)}, f32[1,128]{1,0:T(1,128)S(1)}, u32[]{:S(2)}, u32[]{:S(2)}) collective-permute-start(f32[1,128]{1,0:T(1,128)S(1)} %pad_maximum_fusion), channel_id=1, source_target_pairs={{0,1},{1,0},{2,3},{3,2},{4,5},{5,4},{6,7},{7,6},{8,9},{9,8},{10,11... | collective-permute-start | bytes 1544 | tf_op jit(solution)/shard_map/ppermute | solution.py:408
  38.5 3.5 %all-to-all-start.1 = ((f32[16,1,128]{2,1,0:T(1,128)}), f32[16,1,128]{2,1,0:T(1,128)S(1)}, u32[]{:S(2)}, u32[]{:S(2)}) async-start(f32[16,1,128]{2,1,0:T(1,128)} %bitcast.6), calls=%async_computation.1 | async-start | bytes 16384 | tf_op jit(solution)/shard_map/all_to_all | solution.py:532
  42.0 0.1 slice_convert_fusion.base
  42.1 4.0 %time.1 = (f32[16,4096]{1,0:T(8,128)}, f32[16,4096]{1,0:T(8,128)}) custom-call(s32[1,2]{1,0:T(1,128)S(1)} %slice_convert_fusion.base, f32[1,128]{1,0:T(1,128)S(1)} %collective-permute-done.5.totals, bf16[34,48,128]{2,1,0:T(8,128)(2,1)S(1)} %get-tuple-element.33.clean, f32[2,16,4096]{2,1,0:T(8,128)S(1)} %collective-permute-done.6.inverse, ...), custom_call_target="tpu_custom_call" | custom-call | bytes 12582912 | tf_op jit(solution)/shard_map/time/pallas_call | solution.py:517
  46.1 2.3 %all-to-all-done.1 = f32[16,1,128]{2,1,0:T(1,128)S(1)} async-done(((f32[16,1,128]{2,1,0:T(1,128)}), f32[16,1,128]{2,1,0:T(1,128)S(1)}, u32[]{:S(2)}, u32[]{:S(2)}) %all-to-all-start.1) | async-done | bytes 8224 | tf_op jit(solution)/shard_map/all_to_all | solution.py:532
  48.4 0.6 %subtract_sqrt_fusion = (f32[2]{0:T(128)}, f32[2]{0:T(128)}) fusion(f32[128]{0:T(128)S(1)} %reduce_sum.19), kind=kLoop, calls=%fused_computation.7 | loop fusion | flops 8 | bytes 32 | tf_op jit(solution)/shard_map/sqrt | solution.py:537
  (7 shorter events, 0.1 us)
Async XLA Ops:
  0.6 9.5 %collective-permute-start.1 = (f32[16,4096]{1,0:T(8,128)}, f32[16,4096]{1,0:T(8,128)S(1)}, u32[]{:S(2)}, u32[]{:S(2)}) collective-permute-start(f32[16,4096]{1,0:T(8,128)} %bitcast.16), channel_id=1, source_target_pairs={{0,1},{1,0},{2,3},{3,2},{4,5},{5,4},{6,7},{7,6},{8,9},{9,8},{10,11... | collective-permute-start | bytes 786440 | tf_op jit(solution)/shard_map/ppermute | solution.py:408
  5.8 5.1 %collective-permute-start = (f32[2,4,4096]{2,1,0:T(4,128)S(1)}, f32[2,4,4096]{2,1,0:T(4,128)S(1)}, u32[]{:S(2)}, u32[]{:S(2)}) collective-permute-start(f32[2,4,4096]{2,1,0:T(4,128)S(1)} %get-tuple-element.48), channel_id=1, source_target_pairs={{0,0},{2,4},{4,2},{6,8},{8,6},{10,12},{12,10},{14,16},{16,14},{18,... | collective-permute-start | bytes 393224 | tf_op jit(solution)/shard_map/ppermute | solution.py:408
  6.5 7.5 %collective-permute-start.4 = (f32[2,4,4096]{2,1,0:T(4,128)S(1)}, f32[2,4,4096]{2,1,0:T(4,128)S(1)}, u32[]{:S(2)}, u32[]{:S(2)}) collective-permute-start(f32[2,4,4096]{2,1,0:T(4,128)S(1)} %get-tuple-element.47), channel_id=1, source_target_pairs={{0,2},{2,0},{4,6},{6,4},{8,10},{10,8},{12,14},{14,12},{16,18},{18,... | collective-permute-start | bytes 393224 | tf_op jit(solution)/shard_map/ppermute | solution.py:408
  10.2 8.6 %collective-permute-start.2 = (f32[8,4096]{1,0:T(8,128)S(1)}, f32[8,4096]{1,0:T(8,128)S(1)}, u32[]{:S(2)}, u32[]{:S(2)}) collective-permute-start(f32[8,4096]{1,0:T(8,128)S(1)} %get-tuple-element.27.own_odd), channel_id=1, source_target_pairs={{0,0},{2,4},{4,2},{6,8},{8,6},{10,12},{12,10},{14,16},{16,14},{18,... | collective-permute-start | bytes 393224 | tf_op jit(solution)/shard_map/ppermute | solution.py:408
  10.9 8.0 %collective-permute-start.3 = (f32[8,4096]{1,0:T(8,128)S(1)}, f32[8,4096]{1,0:T(8,128)S(1)}, u32[]{:S(2)}, u32[]{:S(2)}) collective-permute-start(f32[8,4096]{1,0:T(8,128)S(1)} %get-tuple-element.49.own_even), channel_id=1, source_target_pairs={{0,2},{2,0},{4,6},{6,4},{8,10},{10,8},{12,14},{14,12},{16,18},{18,... | collective-permute-start | bytes 393224 | tf_op jit(solution)/shard_map/ppermute | solution.py:408
  16.6 25.5 %collective-permute-start.6 = (f32[2,16,4096]{2,1,0:T(8,128)S(1)}, f32[2,16,4096]{2,1,0:T(8,128)S(1)}, u32[]{:S(2)}, u32[]{:S(2)}) collective-permute-start(f32[2,16,4096]{2,1,0:T(8,128)S(1)} %get-tuple-element.34.inverse), channel_id=1, source_target_pairs={{0,1},{1,0},{2,3},{3,2},{4,5},{5,4},{6,7},{7,6},{8,9},{9,8},{10,11... | collective-permute-start | bytes 1572872 | tf_op jit(solution)/shard_map/ppermute | solution.py:408
  37.8 4.2 %collective-permute-start.5 = (f32[1,128]{1,0:T(1,128)S(1)}, f32[1,128]{1,0:T(1,128)S(1)}, u32[]{:S(2)}, u32[]{:S(2)}) collective-permute-start(f32[1,128]{1,0:T(1,128)S(1)} %pad_maximum_fusion), channel_id=1, source_target_pairs={{0,1},{1,0},{2,3},{3,2},{4,5},{5,4},{6,7},{7,6},{8,9},{9,8},{10,11... | collective-permute-start | bytes 1544 | tf_op jit(solution)/shard_map/ppermute | solution.py:408
  38.5 9.9 %all-to-all-start.1 = ((f32[16,1,128]{2,1,0:T(1,128)}), f32[16,1,128]{2,1,0:T(1,128)S(1)}, u32[]{:S(2)}, u32[]{:S(2)}) async-start(f32[16,1,128]{2,1,0:T(1,128)} %bitcast.6), calls=%async_computation.1 | async-start | bytes 16384 | tf_op jit(solution)/shard_map/all_to_all | solution.py:532

commit v13 on v12

--- a/solution.py
+++ b/solution.py
@@ -13,6 +13,8 @@
 calib_square = 0.15
 lanes = 128
 reach = 7
+near = 4
+far = 2
 params = pltpu.CompilerParams(vmem_limit_bytes=14 * 1024 * 1024)
 vmem = pl.BlockSpec(memory_space=pltpu.VMEM)
 smem = pl.BlockSpec(memory_space=pltpu.SMEM)
@@ -162,10 +164,10 @@
     def stack_step(t, carry):
         before, here, after = pieces[t], pieces[t + 1], pieces[t + 2]
         size = count * rows
-        for j in range(reach):
-            turned = moved(before, here, after, 3 - j)
-            stack[j * size : (j + 1) * size, tile_of(t)] = turned[:size]
-            stack[(reach + j) * size : (reach + j + 1) * size, tile_of(t)] = turned[size:]
+        for a in range(near):
+            turned = moved(before, here, after, 1 - a)
+            stack[a * size : (a + 1) * size, tile_of(t)] = turned[:size]
+            stack[(near + a) * size : (near + a + 1) * size, tile_of(t)] = turned[size:]
         return carry
 
     by_tiles(load_step, tiles, 8)
@@ -241,26 +243,27 @@
     by_tiles(vertical_step, tiles, 8)
     ref_power = by_tiles(horizontal_step, tiles // 2, 8, jnp.zeros((8, lanes), jnp.float32))
     fine[tiles + 3] = fine[1]
-    shift = column_shift(base[0, 1])
+    shifts = [column_shift(base[0, 1] + near * b - 2) for b in range(far)]
 
     def stream_step(t, carry):
-        stream[:, tile_of(t)] = shift(fine, t)
+        for b, shift in enumerate(shifts):
+            stream[b * 2 * wide : (b + 1) * 2 * wide, tile_of(t)] = shift(fine, t)
         return carry
 
     by_tiles(stream_step, ring, ring // 2)
     product = lax.dot_general(
         stack[...], stream[...], (((1,), (1,)), ((), ())), preferred_element_type=jnp.float32
     )
-    size = reach * count * rows
+    size = near * count * rows
     folded[...] = jnp.zeros(folded.shape, jnp.float32)
-    folded[:, 0 : 2 * wide] = product[:size] + product[size:]
+    folded[:, 0 : far * 2 * wide] = product[:size] + product[size:]
     product = by_row_shift(folded[...], rows, -1)
     lags[...] = jnp.zeros(lags.shape, jnp.float32)
-    for j in range(reach):
+    for a in range(near):
         for f in range(count):
-            start = (j * count + f) * rows
-            lags[f * 8 + j : f * 8 + j + 1, :] = jnp.sum(product[start : start + rows], axis=0, keepdims=True)
-    back = 2 * lanes - 1 - base[0, 0]
+            start = (a * count + f) * rows
+            lags[f * 8 + a : f * 8 + a + 1, :] = jnp.sum(product[start : start + rows], axis=0, keepdims=True)
+    back = 4 * lanes - 1 - base[0, 0]
     across = lax.broadcasted_iota(jnp.int32, (8, lanes), 0)
     lane = lane_of((8, lanes))
     packed = jnp.zeros((8, lanes), jnp.float32)
@@ -268,9 +271,11 @@
         block = lags[f * 8 : f * 8 + 8, :]
         for j in range(reach):
             at = (f * reach + j) * reach
-            high = pltpu.roll(block, (back + at) & (lanes - 1), 1)
-            low = pltpu.roll(block, (back + at - wide) & (lanes - 1), 1)
-            packed = packed + jnp.where((across == j) & (lane >= at) & (lane < at + reach), high + low, 0.0)
+            there = back + at - (j // near) * 2 * wide
+            high = pltpu.roll(block, there & (lanes - 1), 1)
+            low = pltpu.roll(block, (there - wide) & (lanes - 1), 1)
+            member = (across == j % near) & (lane >= at) & (lane < at + reach)
+            packed = packed + jnp.where(member, high + low, 0.0)
     lags[0:8, :] = jnp.zeros((8, lanes), jnp.float32)
     for f in range(count):
         lags[f : f + 1, :] = jnp.sum(power[f * 8 : f * 8 + 8, :], axis=0, keepdims=True)
@@ -442,14 +447,15 @@
     tiles = columns // lanes
     ring = tiles + 2
     wide = rows + 8
-    depth = reach * count * rows
+    depth = near * count * rows
     size = lax.axis_size("rows")
     f32 = jnp.float32
     bf16 = jnp.bfloat16
     struct = functools.partial(jax.ShapeDtypeStruct, dtype=f32)
     odd = lax.axis_index("rows") % 2 == 1
     raw, run = lax.optimization_barrier((jnp.maximum(frames_raw, 0.0), jnp.maximum(wind_off[0], 0.0)))
-    own_odd, own_even = from_owner(wind_off[0], run, odd, "frames", run_owner[0])
+    owner, offsets = lax.optimization_barrier((run_owner, jnp.clip(search_base, -8, 8)))
+    own_odd, own_even = from_owner(wind_off[0], run, odd, "frames", owner[0])
     from_odd = paired(own_odd, "rows", 1)
     from_even = paired(own_even, "rows", 0)
     frames_odd, frames_even = by_parity(odd, raw, 4, 1)
@@ -475,7 +481,6 @@
         cost_estimate=cost(8),
         name="smooth",
     )(raw, frames_odd, frames_even)
-    offsets = jnp.clip(search_base, -8, 8)
     blocks = lax.axis_size("frames")
     if blocks == 2:
         other_inverse = paired(inverse, "frames", 0)
@@ -488,7 +493,7 @@
             pltpu.VMEM((tiles, rows + 16, lanes), f32),
             pltpu.VMEM((2 * wide, (tiles + 2) * lanes), bf16),
             pltpu.VMEM((ring + 2, 2 * wide, lanes), bf16),
-            pltpu.VMEM((2 * wide, ring * lanes), bf16),
+            pltpu.VMEM((far * 2 * wide, ring * lanes), bf16),
             pltpu.VMEM((depth, lanes), f32),
             pltpu.VMEM((8 * count, lanes), f32),
         ],

time: 49.3 us -> 49.6 us (level)
  blocking collectives: 11.2 us -> 0 us
  waiting for transfers between devices: 2.43 us -> 8.74 us
  starting transfers between devices: 16.2 us -> 22.2 us
  other arithmetic: 3.62 us -> 2.96 us
    all_to_all x1 -> x0, blocking collectives: 11.2 us -> none  [shards(): parts = lax.all_to_all(part, 'rows', 0, 0, tiled=True)]
    all_to_all x0 -> x1, waiting for transfers between devices: none -> 6.32 us  [shards(): parts = lax.all_to_all(part, 'rows', 0, 0, tiled=True)]
    all_to_all x0 -> x1, starting transfers between devices: none -> 5.24 us  [shards(): parts = lax.all_to_all(part, 'rows', 0, 0, tiled=True)]
    ppermute x7, starting transfers between devices: 12.7 us -> 13.5 us  [paired(): return lax.ppermute(value, axis, list(enumerate(partner)))]
    convert_element_type x1, other arithmetic: 0.66 us -> 0.01 us  [shards(): row = jnp.concatenate([totals[:, :lanes - 2], offsets.astype(f32)], axis=1)]
  transfers between devices with their start and end apart: 8 -> 9, of which waited for: 2 -> 3; matrix products, arithmetic and copies ran while one was open for 6% -> 5% of each run, Pallas kernels for 29% -> 28%
where the time goes in v13:
time: 49.6 us; the launch traced here: 49.3 us
  starting transfers between devices  22.2 us (45%)
  Pallas kernels  14 us (28%)
  waiting for transfers between devices  8.74 us (18%)
  other arithmetic  2.96 us (6%)
  between operations  1.41 us (3%)
    ppermute x7, starting transfers between devices, paired(): return lax.ppermute(value, axis, list(enumerate(partner)))  13.5 us
    all_to_all x1, waiting for transfers between devices, shards(): parts = lax.all_to_all(part, 'rows', 0, 0, tiled=True)  6.32 us
    all_to_all x1, starting transfers between devices, shards(): parts = lax.all_to_all(part, 'rows', 0, 0, tiled=True)  5.24 us
    pallas_call x1, Pallas kernels, shards(): pl.pallas_call(time_kernel, out_shape=(struct((rows, columns)), struct((r...  3.98 us
    pallas_call x1, Pallas kernels, shards(): pl.pallas_call(pressure_kernel, out_shape=(struct((count, rows, columns))...  3.96 us
    pallas_call x1, Pallas kernels, shards(): pl.pallas_call(match_kernel, out_shape=(jax.ShapeDtypeStruct((tiles + 2,...  3.95 us
    all_to_all x1, starting transfers between devices, shards(): sums = lax.all_to_all(part, 'rows', 0, 0, tiled=True)  3.42 us
    all_to_all x1, waiting for transfers between devices, shards(): sums = lax.all_to_all(part, 'rows', 0, 0, tiled=True)  2.29 us
  transfers between devices with their start and end apart: 9, of which 3 were waited for; matrix products, arithmetic and copies ran while one was open for 5% of the time, Pallas kernels for 28%

profile of v13, /device:TPU:0, one launch (start us, length us, event | category | flops | bytes accessed | tf_op | source)
XLA Modules:
  0.0 49.3 jit_solution(11684283072456771227)
XLA Ops:
  0.6 3.0 %collective-permute-start.1 = (f32[16,4096]{1,0:T(8,128)}, f32[16,4096]{1,0:T(8,128)S(1)}, u32[]{:S(2)}, u32[]{:S(2)}) collective-permute-start(f32[16,4096]{1,0:T(8,128)} %bitcast.15), channel_id=1, source_target_pairs={{0,1},{1,0},{2,3},{3,2},{4,5},{5,4},{6,7},{7,6},{8,9},{9,8},{10,11... | collective-permute-start | bytes 786440 | tf_op jit(solution)/shard_map/ppermute | solution.py:413
  3.7 1.0 %broadcast_maximum_fusion.1 = f32[16,4096]{1,0:T(8,128)S(1)} fusion(f32[1,16,4096]{2,1,0:T(8,128)} %param.5), kind=kLoop, calls=%fused_computation.3 | loop fusion | flops 65536 | bytes 524288 | tf_op jit(solution)/shard_map/max | solution.py:456
  4.7 1.1 %broadcast_maximum_fusion.frames = f32[2,16,4096]{2,1,0:T(8,128)S(1)} fusion(f32[2,16,4096]{2,1,0:T(8,128)} %param.4), kind=kLoop, calls=%fused_computation | loop fusion | flops 131072 | bytes 1048576 | tf_op jit(solution)/shard_map/max | solution.py:456
  5.8 0.7 %collective-permute-start = (f32[2,4,4096]{2,1,0:T(4,128)S(1)}, f32[2,4,4096]{2,1,0:T(4,128)S(1)}, u32[]{:S(2)}, u32[]{:S(2)}) collective-permute-start(f32[2,4,4096]{2,1,0:T(4,128)S(1)} %get-tuple-element.52), channel_id=1, source_target_pairs={{0,0},{2,4},{4,2},{6,8},{8,6},{10,12},{12,10},{14,16},{16,14},{18,... | collective-permute-start | bytes 393224 | tf_op jit(solution)/shard_map/ppermute | solution.py:413
  6.5 2.9 %collective-permute-start.4 = (f32[2,4,4096]{2,1,0:T(4,128)S(1)}, f32[2,4,4096]{2,1,0:T(4,128)S(1)}, u32[]{:S(2)}, u32[]{:S(2)}) collective-permute-start(f32[2,4,4096]{2,1,0:T(4,128)S(1)} %get-tuple-element.51), channel_id=1, source_target_pairs={{0,2},{2,0},{4,6},{6,4},{8,10},{10,8},{12,14},{14,12},{16,18},{18,... | collective-permute-start | bytes 393224 | tf_op jit(solution)/shard_map/ppermute | solution.py:413
  10.1 0.1 collective-permute-done.1
  10.2 0.7 %collective-permute-start.2 = (f32[8,4096]{1,0:T(8,128)S(1)}, f32[8,4096]{1,0:T(8,128)S(1)}, u32[]{:S(2)}, u32[]{:S(2)}) collective-permute-start(f32[8,4096]{1,0:T(8,128)S(1)} %get-tuple-element.31.own_odd), channel_id=1, source_target_pairs={{0,0},{2,4},{4,2},{6,8},{8,6},{10,12},{12,10},{14,16},{16,14},{18,... | collective-permute-start | bytes 393224 | tf_op jit(solution)/shard_map/ppermute | solution.py:413
  10.9 3.1 %collective-permute-start.3 = (f32[8,4096]{1,0:T(8,128)S(1)}, f32[8,4096]{1,0:T(8,128)S(1)}, u32[]{:S(2)}, u32[]{:S(2)}) collective-permute-start(f32[8,4096]{1,0:T(8,128)S(1)} %get-tuple-element.53.own_even), channel_id=1, source_target_pairs={{0,2},{2,0},{4,6},{6,4},{8,10},{10,8},{12,14},{14,12},{16,18},{18,... | collective-permute-start | bytes 393224 | tf_op jit(solution)/shard_map/ppermute | solution.py:413
  14.0 0.0 collective-permute-done.4.from_even
  14.0 2.1 %smooth.1 = (f32[2,16,4096]{2,1,0:T(8,128)S(1)}, bf16[256,4352]{1,0:T(8,128)(2,1)S(1)}, f32[16,128]{1,0:T(8,128)S(1)}, bf16[512,256]{1,0:T(8,128)(2,1)S(1)}) custom-call(f32[2,16,4096]{2,1,0:T(8,128)S(1)} %broadcast_maximum_fusion.frames, f32[2,4,4096]{2,1,0:T(4,128)S(1)} %collective-permute-done.from_odd, f32[2,4,4096]{2,1,0:T(4,128)S(1)} %collective-permute-done.4.from_even), custom_call_target="tpu_custom_call" | custom-call | bytes 8388608 | tf_op jit(solution)/shard_map/smooth/pallas_call | solution.py:465
  16.2 1.6 %collective-permute-start.6 = (f32[2,16,4096]{2,1,0:T(8,128)S(1)}, f32[2,16,4096]{2,1,0:T(8,128)S(1)}, u32[]{:S(2)}, u32[]{:S(2)}) collective-permute-start(f32[2,16,4096]{2,1,0:T(8,128)S(1)} %get-tuple-element.38.inverse), channel_id=1, source_target_pairs={{0,1},{1,0},{2,3},{3,2},{4,5},{5,4},{6,7},{7,6},{8,9},{9,8},{10,11... | collective-permute-start | bytes 1572872 | tf_op jit(solution)/shard_map/ppermute | solution.py:413
  17.8 0.0 collective-permute-done.2.from_odd
  17.8 0.0 collective-permute-done.3.from_even
  17.8 3.9 %match.1 = (bf16[34,48,128]{2,1,0:T(8,128)(2,1)S(1)}, f32[16,128]{1,0:T(8,128)}) custom-call(s32[1,2]{1,0:T(1,128)S(1)} %broadcast_clamp_fusion.base, f32[8,4096]{1,0:T(8,128)S(1)} %get-tuple-element.31.own_odd, f32[8,4096]{1,0:T(8,128)S(1)} %get-tuple-element.53.own_even, f32[8,4096]{1,0:T(8,128)S(1)} %collective-permute-done.2.from_odd, ...), custom_call_target="tpu_custom_call" | custom-call | bytes 12582912 | tf_op jit(solution)/shard_map/match/pallas_call | solution.py:487
  21.7 5.2 %all-to-all-start = ((f32[16,1,128]{2,1,0:T(1,128)}), f32[16,1,128]{2,1,0:T(1,128)S(1)}, u32[]{:S(2)}, u32[]{:S(2)}) async-start(f32[16,1,128]{2,1,0:T(1,128)} %bitcast.3), calls=%async_computation | async-start | bytes 16384 | tf_op jit(solution)/shard_map/all_to_all | solution.py:504
  27.0 6.3 %all-to-all-done = f32[16,1,128]{2,1,0:T(1,128)S(1)} async-done(((f32[16,1,128]{2,1,0:T(1,128)}), f32[16,1,128]{2,1,0:T(1,128)S(1)}, u32[]{:S(2)}, u32[]{:S(2)}) %all-to-all-start) | async-done | bytes 8224 | tf_op jit(solution)/shard_map/all_to_all | solution.py:504
  33.4 4.0 %pressure.1 = (f32[2,16,4096]{2,1,0:T(8,128)}, f32[2,16,4096]{2,1,0:T(8,128)S(1)}, f32[16,128]{1,0:T(8,128)}) custom-call(s32[1,2]{1,0:T(1,128)S(1)} %broadcast_clamp_fusion.base, f32[1,128]{1,0:T(1,128)S(1)} %bitcast.13, bf16[34,48,128]{2,1,0:T(8,128)(2,1)S(1)} %get-tuple-element.37.clean, f32[2,16,4096]{2,1,0:T(8,128)S(1)} %get-tuple-element.38.inverse), custom_call_target="tpu_custom_call" | custom-call | bytes 12582912 | tf_op jit(solution)/shard_map/pressure/pallas_call | solution.py:508
  37.3 0.1 pad_maximum_fusion
  37.4 1.5 %collective-permute-start.5 = (f32[1,128]{1,0:T(1,128)S(1)}, f32[1,128]{1,0:T(1,128)S(1)}, u32[]{:S(2)}, u32[]{:S(2)}) collective-permute-start(f32[1,128]{1,0:T(1,128)S(1)} %pad_maximum_fusion), channel_id=1, source_target_pairs={{0,1},{1,0},{2,3},{3,2},{4,5},{5,4},{6,7},{7,6},{8,9},{9,8},{10,11... | collective-permute-start | bytes 1544 | tf_op jit(solution)/shard_map/ppermute | solution.py:413
  38.9 3.4 %all-to-all-start.1 = ((f32[16,1,128]{2,1,0:T(1,128)}), f32[16,1,128]{2,1,0:T(1,128)S(1)}, u32[]{:S(2)}, u32[]{:S(2)}) async-start(f32[16,1,128]{2,1,0:T(1,128)} %bitcast.6), calls=%async_computation.1 | async-start | bytes 16384 | tf_op jit(solution)/shard_map/all_to_all | solution.py:537
  42.4 0.1 slice_convert_fusion.base
  42.4 4.0 %time.1 = (f32[16,4096]{1,0:T(8,128)}, f32[16,4096]{1,0:T(8,128)}) custom-call(s32[1,2]{1,0:T(1,128)S(1)} %slice_convert_fusion.base, f32[1,128]{1,0:T(1,128)S(1)} %collective-permute-done.5.totals, bf16[34,48,128]{2,1,0:T(8,128)(2,1)S(1)} %get-tuple-element.37.clean, f32[2,16,4096]{2,1,0:T(8,128)S(1)} %collective-permute-done.6.inverse, ...), custom_call_target="tpu_custom_call" | custom-call | bytes 12582912 | tf_op jit(solution)/shard_map/time/pallas_call | solution.py:522
  46.4 2.3 %all-to-all-done.1 = f32[16,1,128]{2,1,0:T(1,128)S(1)} async-done(((f32[16,1,128]{2,1,0:T(1,128)}), f32[16,1,128]{2,1,0:T(1,128)S(1)}, u32[]{:S(2)}, u32[]{:S(2)}) %all-to-all-start.1) | async-done | bytes 8224 | tf_op jit(solution)/shard_map/all_to_all | solution.py:537
  48.7 0.6 %subtract_sqrt_fusion = (f32[2]{0:T(128)}, f32[2]{0:T(128)}) fusion(f32[128]{0:T(128)S(1)} %reduce_sum.19), kind=kLoop, calls=%fused_computation.7 | loop fusion | flops 8 | bytes 32 | tf_op jit(solution)/shard_map/sqrt | solution.py:542
  (11 shorter events, 0.2 us)
Async XLA Ops:
  0.6 17.1 %copy-start = (s32[1,2]{1,0:T(1,128)S(1)}, s32[1,2]{1,0:T(1,128)}, u32[]{:S(2)}) copy-start(s32[1,2]{1,0:T(1,128)} %param.7) | copy-start | bytes 28
  0.6 9.5 %collective-permute-start.1 = (f32[16,4096]{1,0:T(8,128)}, f32[16,4096]{1,0:T(8,128)S(1)}, u32[]{:S(2)}, u32[]{:S(2)}) collective-permute-start(f32[16,4096]{1,0:T(8,128)} %bitcast.15), channel_id=1, source_target_pairs={{0,1},{1,0},{2,3},{3,2},{4,5},{5,4},{6,7},{7,6},{8,9},{9,8},{10,11... | collective-permute-start | bytes 786440 | tf_op jit(solution)/shard_map/ppermute | solution.py:413
  5.8 5.1 %collective-permute-start = (f32[2,4,4096]{2,1,0:T(4,128)S(1)}, f32[2,4,4096]{2,1,0:T(4,128)S(1)}, u32[]{:S(2)}, u32[]{:S(2)}) collective-permute-start(f32[2,4,4096]{2,1,0:T(4,128)S(1)} %get-tuple-element.52), channel_id=1, source_target_pairs={{0,0},{2,4},{4,2},{6,8},{8,6},{10,12},{12,10},{14,16},{16,14},{18,... | collective-permute-start | bytes 393224 | tf_op jit(solution)/shard_map/ppermute | solution.py:413
  6.5 7.5 %collective-permute-start.4 = (f32[2,4,4096]{2,1,0:T(4,128)S(1)}, f32[2,4,4096]{2,1,0:T(4,128)S(1)}, u32[]{:S(2)}, u32[]{:S(2)}) collective-permute-start(f32[2,4,4096]{2,1,0:T(4,128)S(1)} %get-tuple-element.51), channel_id=1, source_target_pairs={{0,2},{2,0},{4,6},{6,4},{8,10},{10,8},{12,14},{14,12},{16,18},{18,... | collective-permute-start | bytes 393224 | tf_op jit(solution)/shard_map/ppermute | solution.py:413
  10.2 7.6 %collective-permute-start.2 = (f32[8,4096]{1,0:T(8,128)S(1)}, f32[8,4096]{1,0:T(8,128)S(1)}, u32[]{:S(2)}, u32[]{:S(2)}) collective-permute-start(f32[8,4096]{1,0:T(8,128)S(1)} %get-tuple-element.31.own_odd), channel_id=1, source_target_pairs={{0,0},{2,4},{4,2},{6,8},{8,6},{10,12},{12,10},{14,16},{16,14},{18,... | collective-permute-start | bytes 393224 | tf_op jit(solution)/shard_map/ppermute | solution.py:413
  10.9 6.9 %collective-permute-start.3 = (f32[8,4096]{1,0:T(8,128)S(1)}, f32[8,4096]{1,0:T(8,128)S(1)}, u32[]{:S(2)}, u32[]{:S(2)}) collective-permute-start(f32[8,4096]{1,0:T(8,128)S(1)} %get-tuple-element.53.own_even), channel_id=1, source_target_pairs={{0,2},{2,0},{4,6},{6,4},{8,10},{10,8},{12,14},{14,12},{16,18},{18,... | collective-permute-start | bytes 393224 | tf_op jit(solution)/shard_map/ppermute | solution.py:413
  16.2 26.2 %collective-permute-start.6 = (f32[2,16,4096]{2,1,0:T(8,128)S(1)}, f32[2,16,4096]{2,1,0:T(8,128)S(1)}, u32[]{:S(2)}, u32[]{:S(2)}) collective-permute-start(f32[2,16,4096]{2,1,0:T(8,128)S(1)} %get-tuple-element.38.inverse), channel_id=1, source_target_pairs={{0,1},{1,0},{2,3},{3,2},{4,5},{5,4},{6,7},{7,6},{8,9},{9,8},{10,11... | collective-permute-start | bytes 1572872 | tf_op jit(solution)/shard_map/ppermute | solution.py:413
  21.7 11.6 %all-to-all-start = ((f32[16,1,128]{2,1,0:T(1,128)}), f32[16,1,128]{2,1,0:T(1,128)S(1)}, u32[]{:S(2)}, u32[]{:S(2)}) async-start(f32[16,1,128]{2,1,0:T(1,128)} %bitcast.3), calls=%async_computation | async-start | bytes 16384 | tf_op jit(solution)/shard_map/all_to_all | solution.py:504
  37.4 4.9 %collective-permute-start.5 = (f32[1,128]{1,0:T(1,128)S(1)}, f32[1,128]{1,0:T(1,128)S(1)}, u32[]{:S(2)}, u32[]{:S(2)}) collective-permute-start(f32[1,128]{1,0:T(1,128)S(1)} %pad_maximum_fusion), channel_id=1, source_target_pairs={{0,1},{1,0},{2,3},{3,2},{4,5},{5,4},{6,7},{7,6},{8,9},{9,8},{10,11... | collective-permute-start | bytes 1544 | tf_op jit(solution)/shard_map/ppermute | solution.py:413
  38.9 9.8 %all-to-all-start.1 = ((f32[16,1,128]{2,1,0:T(1,128)}), f32[16,1,128]{2,1,0:T(1,128)S(1)}, u32[]{:S(2)}, u32[]{:S(2)}) async-start(f32[16,1,128]{2,1,0:T(1,128)} %bitcast.6), calls=%async_computation.1 | async-start | bytes 16384 | tf_op jit(solution)/shard_map/all_to_all | solution.py:537

commit v14 on v13

--- a/solution.py
+++ b/solution.py
@@ -282,7 +282,11 @@
     lags[count : count + 1, :] = jnp.sum(ref_power, axis=0, keepdims=True)
     powers = jnp.sum(lags[0:8, :], axis=1, keepdims=True)
     packed = packed + jnp.where(lane == count * reach * reach + across, powers, 0.0)
-    part[...] = jnp.broadcast_to(jnp.sum(packed, axis=0, keepdims=True), part.shape)
+    packed = jnp.sum(packed, axis=0, keepdims=True)
+    for place in range(2):
+        offset = base[0, place].astype(jnp.float32)
+        packed = jnp.where(lane[0:1] == lanes - 2 + place, offset, packed)
+    part[...] = jnp.broadcast_to(packed, part.shape)
 
 
 def spread_columns(clean, spread, base_col):
@@ -291,18 +295,10 @@
     spare = spread.shape[0] - reach * size
     spread[reach * size :, :] = jnp.zeros((spare, tiles * lanes), jnp.bfloat16)
 
-    def per_offset(j, carry):
+    for j in range(reach):
         shift = column_shift(base_col + j - 3)
-        at = pl.multiple_of(j * size, size)
-
-        def step(t, inner):
-            spread[pl.ds(at, size), tile_of(t)] = shift(clean, t)
-            return inner
-
-        by_tiles(step, tiles, 32)
-        return carry
-
-    lax.fori_loop(0, reach, per_offset, 0)
+        for t in range(tiles):
+            spread[j * size : (j + 1) * size, t * lanes : (t + 1) * lanes] = shift(clean, t)
 
 
 def blend_weights(totals, count):
@@ -482,11 +478,12 @@
         name="smooth",
     )(raw, frames_odd, frames_even)
     blocks = lax.axis_size("frames")
+    peers = size * blocks if blocks == 2 else size
     if blocks == 2:
         other_inverse = paired(inverse, "frames", 0)
     clean, part = pl.pallas_call(
         match_kernel,
-        out_shape=(jax.ShapeDtypeStruct((tiles + 2, 2 * wide, lanes), bf16), struct((size, lanes))),
+        out_shape=(jax.ShapeDtypeStruct((tiles + 2, 2 * wide, lanes), bf16), struct((peers, lanes))),
         in_specs=[smem] + [vmem] * 7,
         out_specs=(vmem, vmem),
         scratch_shapes=[
@@ -501,8 +498,15 @@
         cost_estimate=cost(12),
         name="match",
     )(offsets, own_odd, own_even, from_odd, from_even, stack, power, band)
-    parts = lax.all_to_all(part, "rows", 0, 0, tiled=True)
-    totals = jnp.sum(parts, axis=0, keepdims=True)
+    if blocks == 2:
+        parts = lax.all_to_all(part, ("rows", "frames"), 0, 0, tiled=True).reshape(size, blocks, lanes)
+        mine = lax.axis_index("frames") == 0
+        both = jnp.sum(parts, axis=0)
+        totals = jnp.where(mine, both[0:1], both[1:2])
+        row = jnp.where(mine, both[1:2], both[0:1])
+        place = jnp.where(mine, parts[0, 1:2], parts[0, 0:1])[:, lanes - 2 :].astype(jnp.int32)
+    else:
+        totals = jnp.sum(lax.all_to_all(part, "rows", 0, 0, tiled=True), axis=0, keepdims=True)
     depth = -(-reach * 2 * wide // lanes) * lanes
     spread = pltpu.VMEM((depth, columns), bf16)
     pressure, moments, part = pl.pallas_call(
@@ -516,9 +520,6 @@
         name="pressure",
     )(offsets, totals, clean, inverse)
     if blocks == 2:
-        row = jnp.concatenate([totals[:, : lanes - 2], offsets.astype(f32)], axis=1)
-        row, part = lax.optimization_barrier((row, part))
-        row = paired(row, "frames", 0)
         time_mean, time_rms = pl.pallas_call(
             time_kernel,
             out_shape=(struct((rows, columns)), struct((rows, columns))),
@@ -528,7 +529,7 @@
             compiler_params=params,
             cost_estimate=cost(12),
             name="time",
-        )(row[:, lanes - 2 :].astype(jnp.int32), row, clean, other_inverse, moments)
+        )(place, row, clean, other_inverse, moments)
     else:
         whole = total_over(moments, "frames")
         total_frames = count * blocks

time: 49.6 us -> 48 us (0.968)
  Pallas kernels: 14 us -> 12.5 us
    all_to_all x1, starting transfers between devices: 5.24 us -> 6.75 us  [shards(): lax.all_to_all(part, ('rows', 'frames'), 0, 0, tiled=True)]
    ppermute x7 -> x6, starting transfers between devices: 13.5 us -> 12.2 us  [paired(): return lax.ppermute(value, axis, list(enumerate(partner)))]
    all_to_all x1, waiting for transfers between devices: 6.32 us -> 5.29 us  [shards(): lax.all_to_all(part, ('rows', 'frames'), 0, 0, tiled=True)]
    pallas_call x1, Pallas kernels: 3.98 us -> 3.23 us  [shards(): pl.pallas_call(time_kernel, out_shape=(struct((rows, columns)), struct((r...]
    pallas_call x1, Pallas kernels: 3.96 us -> 3.21 us  [shards(): pl.pallas_call(pressure_kernel, out_shape=(struct((count, rows, columns))...]
  transfers between devices with their start and end apart: 9 -> 8, of which waited for: 3 -> 4; matrix products, arithmetic and copies ran while one was open for 5% -> 5% of each run, Pallas kernels for 28% -> 18%
where the time goes in v14:
time: 48 us; the launch traced here: 47.7 us
  starting transfers between devices  22.4 us (47%)
  Pallas kernels  12.5 us (26%)
  waiting for transfers between devices  8.45 us (18%)
  other arithmetic  2.89 us (6%)
  between operations  1.41 us (3%)
    ppermute x6, starting transfers between devices, paired(): return lax.ppermute(value, axis, list(enumerate(partner)))  12.2 us
    all_to_all x1, starting transfers between devices, shards(): lax.all_to_all(part, ('rows', 'frames'), 0, 0, tiled=True)  6.75 us
    all_to_all x1, waiting for transfers between devices, shards(): lax.all_to_all(part, ('rows', 'frames'), 0, 0, tiled=True)  5.29 us
    pallas_call x1, Pallas kernels, shards(): pl.pallas_call(match_kernel, out_shape=(jax.ShapeDtypeStruct((tiles + 2,...  3.96 us
    all_to_all x1, starting transfers between devices, shards(): sums = lax.all_to_all(part, 'rows', 0, 0, tiled=True)  3.42 us
    pallas_call x1, Pallas kernels, shards(): pl.pallas_call(time_kernel, out_shape=(struct((rows, columns)), struct((r...  3.23 us
    pallas_call x1, Pallas kernels, shards(): pl.pallas_call(pressure_kernel, out_shape=(struct((count, rows, columns))...  3.21 us
    all_to_all x1, waiting for transfers between devices, shards(): sums = lax.all_to_all(part, 'rows', 0, 0, tiled=True)  2.61 us
  transfers between devices with their start and end apart: 8, of which 4 were waited for; matrix products, arithmetic and copies ran while one was open for 5% of the time, Pallas kernels for 18%

profile of v14, /device:TPU:0, one launch (start us, length us, event | category | flops | bytes accessed | tf_op | source)
XLA Modules:
  0.0 47.7 jit_solution(11260089396770833171)
XLA Ops:
  0.6 3.0 %collective-permute-start.1 = (f32[16,4096]{1,0:T(8,128)}, f32[16,4096]{1,0:T(8,128)S(1)}, u32[]{:S(2)}, u32[]{:S(2)}) collective-permute-start(f32[16,4096]{1,0:T(8,128)} %bitcast.14), channel_id=1, source_target_pairs={{0,1},{1,0},{2,3},{3,2},{4,5},{5,4},{6,7},{7,6},{8,9},{9,8},{10,11... | collective-permute-start | bytes 786440 | tf_op jit(solution)/shard_map/ppermute | solution.py:409
  3.7 1.0 %broadcast_maximum_fusion.1 = f32[16,4096]{1,0:T(8,128)S(1)} fusion(f32[1,16,4096]{2,1,0:T(8,128)} %param.5), kind=kLoop, calls=%fused_computation.3 | loop fusion | flops 65536 | bytes 524288 | tf_op jit(solution)/shard_map/max | solution.py:452
  4.7 1.1 %broadcast_maximum_fusion.frames = f32[2,16,4096]{2,1,0:T(8,128)S(1)} fusion(f32[2,16,4096]{2,1,0:T(8,128)} %param.4), kind=kLoop, calls=%fused_computation | loop fusion | flops 131072 | bytes 1048576 | tf_op jit(solution)/shard_map/max | solution.py:452
  5.8 0.7 %collective-permute-start = (f32[2,4,4096]{2,1,0:T(4,128)S(1)}, f32[2,4,4096]{2,1,0:T(4,128)S(1)}, u32[]{:S(2)}, u32[]{:S(2)}) collective-permute-start(f32[2,4,4096]{2,1,0:T(4,128)S(1)} %get-tuple-element.48), channel_id=1, source_target_pairs={{0,0},{2,4},{4,2},{6,8},{8,6},{10,12},{12,10},{14,16},{16,14},{18,... | collective-permute-start | bytes 393224 | tf_op jit(solution)/shard_map/ppermute | solution.py:409
  6.5 2.9 %collective-permute-start.4 = (f32[2,4,4096]{2,1,0:T(4,128)S(1)}, f32[2,4,4096]{2,1,0:T(4,128)S(1)}, u32[]{:S(2)}, u32[]{:S(2)}) collective-permute-start(f32[2,4,4096]{2,1,0:T(4,128)S(1)} %get-tuple-element.47), channel_id=1, source_target_pairs={{0,2},{2,0},{4,6},{6,4},{8,10},{10,8},{12,14},{14,12},{16,18},{18,... | collective-permute-start | bytes 393224 | tf_op jit(solution)/shard_map/ppermute | solution.py:409
  10.1 0.1 collective-permute-done.1
  10.2 0.7 %collective-permute-start.2 = (f32[8,4096]{1,0:T(8,128)S(1)}, f32[8,4096]{1,0:T(8,128)S(1)}, u32[]{:S(2)}, u32[]{:S(2)}) collective-permute-start(f32[8,4096]{1,0:T(8,128)S(1)} %get-tuple-element.29.own_odd), channel_id=1, source_target_pairs={{0,0},{2,4},{4,2},{6,8},{8,6},{10,12},{12,10},{14,16},{16,14},{18,... | collective-permute-start | bytes 393224 | tf_op jit(solution)/shard_map/ppermute | solution.py:409
  10.9 3.1 %collective-permute-start.3 = (f32[8,4096]{1,0:T(8,128)S(1)}, f32[8,4096]{1,0:T(8,128)S(1)}, u32[]{:S(2)}, u32[]{:S(2)}) collective-permute-start(f32[8,4096]{1,0:T(8,128)S(1)} %get-tuple-element.49.own_even), channel_id=1, source_target_pairs={{0,2},{2,0},{4,6},{6,4},{8,10},{10,8},{12,14},{14,12},{16,18},{18,... | collective-permute-start | bytes 393224 | tf_op jit(solution)/shard_map/ppermute | solution.py:409
  14.0 0.0 collective-permute-done.from_odd
  14.0 0.0 collective-permute-done.4.from_even
  14.1 2.1 %smooth.1 = (f32[2,16,4096]{2,1,0:T(8,128)S(1)}, bf16[256,4352]{1,0:T(8,128)(2,1)S(1)}, f32[16,128]{1,0:T(8,128)S(1)}, bf16[512,256]{1,0:T(8,128)(2,1)S(1)}) custom-call(f32[2,16,4096]{2,1,0:T(8,128)S(1)} %broadcast_maximum_fusion.frames, f32[2,4,4096]{2,1,0:T(4,128)S(1)} %collective-permute-done.from_odd, f32[2,4,4096]{2,1,0:T(4,128)S(1)} %collective-permute-done.4.from_even), custom_call_target="tpu_custom_call" | custom-call | bytes 8388608 | tf_op jit(solution)/shard_map/smooth/pallas_call | solution.py:461
  16.2 0.0 collective-permute-done.2.from_odd
  16.2 0.0 collective-permute-done.3.from_even
  16.2 4.0 %match.1 = (bf16[34,48,128]{2,1,0:T(8,128)(2,1)S(1)}, f32[32,128]{1,0:T(8,128)}) custom-call(s32[1,2]{1,0:T(1,128)S(1)} %broadcast_clamp_fusion.base, f32[8,4096]{1,0:T(8,128)S(1)} %get-tuple-element.29.own_odd, f32[8,4096]{1,0:T(8,128)S(1)} %get-tuple-element.49.own_even, f32[8,4096]{1,0:T(8,128)S(1)} %collective-permute-done.2.from_odd, ...), custom_call_target="tpu_custom_call" | custom-call | bytes 12582912 | tf_op jit(solution)/shard_map/match/pallas_call | solution.py:484
  20.2 6.7 %all-to-all-start = ((f32[32,1,128]{2,1,0:T(1,128)}), f32[32,1,128]{2,1,0:T(1,128)S(1)}, u32[]{:S(2)}, u32[]{:S(2)}) async-start(f32[32,1,128]{2,1,0:T(1,128)} %bitcast.3), calls=%async_computation | async-start | bytes 32768 | tf_op jit(solution)/shard_map/all_to_all | solution.py:502
  26.9 1.8 %collective-permute-start.5 = (f32[2,16,4096]{2,1,0:T(8,128)S(1)}, f32[2,16,4096]{2,1,0:T(8,128)S(1)}, u32[]{:S(2)}, u32[]{:S(2)}) collective-permute-start(f32[2,16,4096]{2,1,0:T(8,128)S(1)} %get-tuple-element.36.inverse), channel_id=1, source_target_pairs={{0,1},{1,0},{2,3},{3,2},{4,5},{5,4},{6,7},{7,6},{8,9},{9,8},{10,11... | collective-permute-start | bytes 1572872 | tf_op jit(solution)/shard_map/ppermute | solution.py:409
  28.8 5.3 %all-to-all-done = f32[32,1,128]{2,1,0:T(1,128)S(1)} async-done(((f32[32,1,128]{2,1,0:T(1,128)}), f32[32,1,128]{2,1,0:T(1,128)S(1)}, u32[]{:S(2)}, u32[]{:S(2)}) %all-to-all-start) | async-done | bytes 16416 | tf_op jit(solution)/shard_map/all_to_all | solution.py:502
  34.1 3.2 %pressure.1 = (f32[2,16,4096]{2,1,0:T(8,128)}, f32[2,16,4096]{2,1,0:T(8,128)S(1)}, f32[16,128]{1,0:T(8,128)}) custom-call(s32[1,2]{1,0:T(1,128)S(1)} %broadcast_clamp_fusion.base, f32[1,128]{1,0:T(1,128)S(1)} %get-tuple-element.52.totals, bf16[34,48,128]{2,1,0:T(8,128)(2,1)S(1)} %get-tuple-element.35.clean, f32[2,16,4096]{2,1,0:T(8,128)S(1)} %get-tuple-element.36.inverse), custom_call_target="tpu_custom_call" | custom-call | bytes 12582912 | tf_op jit(solution)/shard_map/pressure/pallas_call | solution.py:512
  37.3 3.4 %all-to-all-start.1 = ((f32[16,1,128]{2,1,0:T(1,128)}), f32[16,1,128]{2,1,0:T(1,128)S(1)}, u32[]{:S(2)}, u32[]{:S(2)}) async-start(f32[16,1,128]{2,1,0:T(1,128)} %bitcast.6), calls=%async_computation.1 | async-start | bytes 16384 | tf_op jit(solution)/shard_map/all_to_all | solution.py:538
  40.8 0.1 slice_convert_fusion.base
  40.8 0.4 collective-permute-done.5.inverse
  41.3 3.2 %time.1 = (f32[16,4096]{1,0:T(8,128)}, f32[16,4096]{1,0:T(8,128)}) custom-call(s32[1,2]{1,0:T(1,128)S(1)} %slice_convert_fusion.base, f32[1,128]{1,0:T(1,128)S(1)} %get-tuple-element.51.totals, bf16[34,48,128]{2,1,0:T(8,128)(2,1)S(1)} %get-tuple-element.35.clean, f32[2,16,4096]{2,1,0:T(8,128)S(1)} %collective-permute-done.5.inverse, ...), custom_call_target="tpu_custom_call" | custom-call | bytes 12582912 | tf_op jit(solution)/shard_map/time/pallas_call | solution.py:523
  44.5 2.6 %all-to-all-done.1 = f32[16,1,128]{2,1,0:T(1,128)S(1)} async-done(((f32[16,1,128]{2,1,0:T(1,128)}), f32[16,1,128]{2,1,0:T(1,128)S(1)}, u32[]{:S(2)}, u32[]{:S(2)}) %all-to-all-start.1) | async-done | bytes 8224 | tf_op jit(solution)/shard_map/all_to_all | solution.py:538
  47.1 0.6 %subtract_sqrt_fusion = (f32[2]{0:T(128)}, f32[2]{0:T(128)}) fusion(f32[128]{0:T(128)S(1)} %reduce_sum.19), kind=kLoop, calls=%fused_computation.10 | loop fusion | flops 8 | bytes 32 | tf_op jit(solution)/shard_map/sqrt | solution.py:543
  (9 shorter events, 0.1 us)
Async XLA Ops:
  0.6 13.4 %copy-start = (s32[1,2]{1,0:T(1,128)S(1)}, s32[1,2]{1,0:T(1,128)}, u32[]{:S(2)}) copy-start(s32[1,2]{1,0:T(1,128)} %param.7) | copy-start | bytes 28
  0.6 9.5 %collective-permute-start.1 = (f32[16,4096]{1,0:T(8,128)}, f32[16,4096]{1,0:T(8,128)S(1)}, u32[]{:S(2)}, u32[]{:S(2)}) collective-permute-start(f32[16,4096]{1,0:T(8,128)} %bitcast.14), channel_id=1, source_target_pairs={{0,1},{1,0},{2,3},{3,2},{4,5},{5,4},{6,7},{7,6},{8,9},{9,8},{10,11... | collective-permute-start | bytes 786440 | tf_op jit(solution)/shard_map/ppermute | solution.py:409
  5.8 8.2 %collective-permute-start = (f32[2,4,4096]{2,1,0:T(4,128)S(1)}, f32[2,4,4096]{2,1,0:T(4,128)S(1)}, u32[]{:S(2)}, u32[]{:S(2)}) collective-permute-start(f32[2,4,4096]{2,1,0:T(4,128)S(1)} %get-tuple-element.48), channel_id=1, source_target_pairs={{0,0},{2,4},{4,2},{6,8},{8,6},{10,12},{12,10},{14,16},{16,14},{18,... | collective-permute-start | bytes 393224 | tf_op jit(solution)/shard_map/ppermute | solution.py:409
  6.5 7.5 %collective-permute-start.4 = (f32[2,4,4096]{2,1,0:T(4,128)S(1)}, f32[2,4,4096]{2,1,0:T(4,128)S(1)}, u32[]{:S(2)}, u32[]{:S(2)}) collective-permute-start(f32[2,4,4096]{2,1,0:T(4,128)S(1)} %get-tuple-element.47), channel_id=1, source_target_pairs={{0,2},{2,0},{4,6},{6,4},{8,10},{10,8},{12,14},{14,12},{16,18},{18,... | collective-permute-start | bytes 393224 | tf_op jit(solution)/shard_map/ppermute | solution.py:409
  10.2 6.0 %collective-permute-start.2 = (f32[8,4096]{1,0:T(8,128)S(1)}, f32[8,4096]{1,0:T(8,128)S(1)}, u32[]{:S(2)}, u32[]{:S(2)}) collective-permute-start(f32[8,4096]{1,0:T(8,128)S(1)} %get-tuple-element.29.own_odd), channel_id=1, source_target_pairs={{0,0},{2,4},{4,2},{6,8},{8,6},{10,12},{12,10},{14,16},{16,14},{18,... | collective-permute-start | bytes 393224 | tf_op jit(solution)/shard_map/ppermute | solution.py:409
  10.9 5.3 %collective-permute-start.3 = (f32[8,4096]{1,0:T(8,128)S(1)}, f32[8,4096]{1,0:T(8,128)S(1)}, u32[]{:S(2)}, u32[]{:S(2)}) collective-permute-start(f32[8,4096]{1,0:T(8,128)S(1)} %get-tuple-element.49.own_even), channel_id=1, source_target_pairs={{0,2},{2,0},{4,6},{6,4},{8,10},{10,8},{12,14},{14,12},{16,18},{18,... | collective-permute-start | bytes 393224 | tf_op jit(solution)/shard_map/ppermute | solution.py:409
  20.2 13.9 %all-to-all-start = ((f32[32,1,128]{2,1,0:T(1,128)}), f32[32,1,128]{2,1,0:T(1,128)S(1)}, u32[]{:S(2)}, u32[]{:S(2)}) async-start(f32[32,1,128]{2,1,0:T(1,128)} %bitcast.3), calls=%async_computation | async-start | bytes 32768 | tf_op jit(solution)/shard_map/all_to_all | solution.py:502
  26.9 14.3 %collective-permute-start.5 = (f32[2,16,4096]{2,1,0:T(8,128)S(1)}, f32[2,16,4096]{2,1,0:T(8,128)S(1)}, u32[]{:S(2)}, u32[]{:S(2)}) collective-permute-start(f32[2,16,4096]{2,1,0:T(8,128)S(1)} %get-tuple-element.36.inverse), channel_id=1, source_target_pairs={{0,1},{1,0},{2,3},{3,2},{4,5},{5,4},{6,7},{7,6},{8,9},{9,8},{10,11... | collective-permute-start | bytes 1572872 | tf_op jit(solution)/shard_map/ppermute | solution.py:409
  37.3 9.8 %all-to-all-start.1 = ((f32[16,1,128]{2,1,0:T(1,128)}), f32[16,1,128]{2,1,0:T(1,128)S(1)}, u32[]{:S(2)}, u32[]{:S(2)}) async-start(f32[16,1,128]{2,1,0:T(1,128)} %bitcast.6), calls=%async_computation.1 | async-start | bytes 16384 | tf_op jit(solution)/shard_map/all_to_all | solution.py:538

commit v15 on v14

--- a/solution.py
+++ b/solution.py
@@ -25,10 +25,17 @@
 
 
 def tile_of(index):
+    if isinstance(index, int):
+        return slice(index * lanes, (index + 1) * lanes)
     return pl.ds(pl.multiple_of(index * lanes, lanes), lanes)
 
 
 def by_tiles(step, tiles, group, init=()):
+    if group == tiles:
+        for index in range(tiles):
+            init = step(index, init)
+        return init
+
     def body(index, carry):
         for inner in range(group):
             carry = step(index * group + inner, carry)
@@ -88,11 +95,13 @@
 
 
 def chunk_of(t):
+    if isinstance(t, int):
+        return slice(t * 2 * lanes, (t + 1) * 2 * lanes)
     return pl.ds(pl.multiple_of(t * 2 * lanes, 2 * lanes), 2 * lanes)
 
 
 def horizontal(wide, band, t):
-    window = wide[:, pl.ds(pl.multiple_of(t * 2 * lanes, 2 * lanes), 4 * lanes)]
+    window = wide[:, t * 2 * lanes : (t + 2) * 2 * lanes]
     product = jnp.dot(window, band[...], preferred_element_type=jnp.float32)
     half = product.shape[0] // 2
     return product[:half] + product[half:]
@@ -170,13 +179,13 @@
             stack[(near + a) * size : (near + a + 1) * size, tile_of(t)] = turned[size:]
         return carry
 
-    by_tiles(load_step, tiles, 8)
-    by_tiles(vertical_step, tiles, 8)
-    powers = by_tiles(horizontal_step, tiles // 2, 8, (jnp.zeros((8, lanes), jnp.float32),) * count)
+    by_tiles(load_step, tiles, tiles)
+    by_tiles(vertical_step, tiles, tiles)
+    powers = by_tiles(horizontal_step, tiles // 2, tiles // 2, (jnp.zeros((8, lanes), jnp.float32),) * count)
     for f in range(count):
         power[f * 8 : f * 8 + 8, :] = powers[f]
     pieces[tiles + 3] = pieces[1]
-    by_tiles(stack_step, ring, ring // 2)
+    by_tiles(stack_step, ring, ring)
 
 
 def column_shift(offset):
@@ -239,9 +248,9 @@
             array[2 * t + 2] = value[:, lanes:]
         return total + fold(square[:, :lanes]) + fold(square[:, lanes:])
 
-    by_tiles(load_step, tiles, 8)
-    by_tiles(vertical_step, tiles, 8)
-    ref_power = by_tiles(horizontal_step, tiles // 2, 8, jnp.zeros((8, lanes), jnp.float32))
+    by_tiles(load_step, tiles, tiles)
+    by_tiles(vertical_step, tiles, tiles)
+    ref_power = by_tiles(horizontal_step, tiles // 2, tiles // 2, jnp.zeros((8, lanes), jnp.float32))
     fine[tiles + 3] = fine[1]
     shifts = [column_shift(base[0, 1] + near * b - 2) for b in range(far)]
 
@@ -250,7 +259,7 @@
             stream[b * 2 * wide : (b + 1) * 2 * wide, tile_of(t)] = shift(fine, t)
         return carry
 
-    by_tiles(stream_step, ring, ring // 2)
+    by_tiles(stream_step, ring, ring)
     product = lax.dot_general(
         stack[...], stream[...], (((1,), (1,)), ((), ())), preferred_element_type=jnp.float32
     )
@@ -373,7 +382,7 @@
         return tuple(result)
 
     zero = jnp.zeros((8, lanes), jnp.float32)
-    sums = by_tiles(step, columns // (2 * lanes), 8, (zero,) * (2 * count))
+    sums = by_tiles(step, columns // (2 * lanes), columns // (2 * lanes), (zero,) * (2 * count))
     line = zero
     for k in range(2 * count):
         value = jnp.sum(jnp.sum(sums[k], axis=0, keepdims=True), axis=1, keepdims=True)
@@ -398,7 +407,7 @@
         time_rms[:, where] = jnp.sqrt(jnp.maximum(second * (1.0 / frames) - mean * mean, 0.0))
         return carry
 
-    by_tiles(step, columns // (2 * lanes), 8)
+    by_tiles(step, columns // (2 * lanes), columns // (2 * lanes))
 
 
 def paired(value, axis, first):

time: 48 us -> 46.9 us (0.977)
  Pallas kernels: 12.5 us -> 10.3 us
  starting transfers between devices: 22.4 us -> 23.2 us
    pallas_call x1, Pallas kernels: 3.96 us -> 3.14 us  [shards(): pl.pallas_call(match_kernel, out_shape=(jax.ShapeDtypeStruct((tiles + 2,...]
    pallas_call x1, Pallas kernels: 2.14 us -> 1.33 us  [shards(): pl.pallas_call(smooth_kernel, out_shape=(struct((count, rows, columns)),...]
    all_to_all x1, starting transfers between devices: 6.75 us -> 7.55 us  [shards(): lax.all_to_all(part, ('rows', 'frames'), 0, 0, tiled=True)]
  transfers between devices with their start and end apart: 8 -> 8, of which waited for: 4 -> 4; matrix products, arithmetic and copies ran while one was open for 5% -> 5% of each run, Pallas kernels for 18% -> 15%
where the time goes in v15:
time: 46.9 us; the launch traced here: 46.6 us
  starting transfers between devices  23.2 us (49%)
  Pallas kernels  10.3 us (22%)
  waiting for transfers between devices  8.8 us (19%)
  other arithmetic  2.89 us (6%)
  between operations  1.41 us (3%)
    ppermute x6, starting transfers between devices, paired(): return lax.ppermute(value, axis, list(enumerate(partner)))  12.2 us
    all_to_all x1, starting transfers between devices, shards(): lax.all_to_all(part, ('rows', 'frames'), 0, 0, tiled=True)  7.55 us
    all_to_all x1, waiting for transfers between devices, shards(): lax.all_to_all(part, ('rows', 'frames'), 0, 0, tiled=True)  5.29 us
    all_to_all x1, starting transfers between devices, shards(): sums = lax.all_to_all(part, 'rows', 0, 0, tiled=True)  3.42 us
    pallas_call x1, Pallas kernels, shards(): pl.pallas_call(match_kernel, out_shape=(jax.ShapeDtypeStruct((tiles + 2,...  3.14 us
    pallas_call x1, Pallas kernels, shards(): pl.pallas_call(pressure_kernel, out_shape=(struct((count, rows, columns))...  2.94 us
    pallas_call x1, Pallas kernels, shards(): pl.pallas_call(time_kernel, out_shape=(struct((rows, columns)), struct((r...  2.87 us
    all_to_all x1, waiting for transfers between devices, shards(): sums = lax.all_to_all(part, 'rows', 0, 0, tiled=True)  2.69 us
  transfers between devices with their start and end apart: 8, of which 4 were waited for; matrix products, arithmetic and copies ran while one was open for 5% of the time, Pallas kernels for 15%

profile of v15, /device:TPU:0, one launch (start us, length us, event | category | flops | bytes accessed | tf_op | source)
XLA Modules:
  0.0 46.6 jit_solution(9668220473151824655)
XLA Ops:
  0.6 3.0 %collective-permute-start.1 = (f32[16,4096]{1,0:T(8,128)}, f32[16,4096]{1,0:T(8,128)S(1)}, u32[]{:S(2)}, u32[]{:S(2)}) collective-permute-start(f32[16,4096]{1,0:T(8,128)} %bitcast.14), channel_id=1, source_target_pairs={{0,1},{1,0},{2,3},{3,2},{4,5},{5,4},{6,7},{7,6},{8,9},{9,8},{10,11... | collective-permute-start | bytes 786440 | tf_op jit(solution)/shard_map/ppermute | solution.py:418
  3.7 1.0 %broadcast_maximum_fusion.1 = f32[16,4096]{1,0:T(8,128)S(1)} fusion(f32[1,16,4096]{2,1,0:T(8,128)} %param.5), kind=kLoop, calls=%fused_computation.3 | loop fusion | flops 65536 | bytes 524288 | tf_op jit(solution)/shard_map/max | solution.py:461
  4.7 1.1 %broadcast_maximum_fusion.frames = f32[2,16,4096]{2,1,0:T(8,128)S(1)} fusion(f32[2,16,4096]{2,1,0:T(8,128)} %param.4), kind=kLoop, calls=%fused_computation | loop fusion | flops 131072 | bytes 1048576 | tf_op jit(solution)/shard_map/max | solution.py:461
  5.8 0.7 %collective-permute-start = (f32[2,4,4096]{2,1,0:T(4,128)S(1)}, f32[2,4,4096]{2,1,0:T(4,128)S(1)}, u32[]{:S(2)}, u32[]{:S(2)}) collective-permute-start(f32[2,4,4096]{2,1,0:T(4,128)S(1)} %get-tuple-element.48), channel_id=1, source_target_pairs={{0,0},{2,4},{4,2},{6,8},{8,6},{10,12},{12,10},{14,16},{16,14},{18,... | collective-permute-start | bytes 393224 | tf_op jit(solution)/shard_map/ppermute | solution.py:418
  6.5 2.9 %collective-permute-start.4 = (f32[2,4,4096]{2,1,0:T(4,128)S(1)}, f32[2,4,4096]{2,1,0:T(4,128)S(1)}, u32[]{:S(2)}, u32[]{:S(2)}) collective-permute-start(f32[2,4,4096]{2,1,0:T(4,128)S(1)} %get-tuple-element.47), channel_id=1, source_target_pairs={{0,2},{2,0},{4,6},{6,4},{8,10},{10,8},{12,14},{14,12},{16,18},{18,... | collective-permute-start | bytes 393224 | tf_op jit(solution)/shard_map/ppermute | solution.py:418
  10.1 0.1 collective-permute-done.1
  10.2 0.7 %collective-permute-start.2 = (f32[8,4096]{1,0:T(8,128)S(1)}, f32[8,4096]{1,0:T(8,128)S(1)}, u32[]{:S(2)}, u32[]{:S(2)}) collective-permute-start(f32[8,4096]{1,0:T(8,128)S(1)} %get-tuple-element.29.own_odd), channel_id=1, source_target_pairs={{0,0},{2,4},{4,2},{6,8},{8,6},{10,12},{12,10},{14,16},{16,14},{18,... | collective-permute-start | bytes 393224 | tf_op jit(solution)/shard_map/ppermute | solution.py:418
  10.9 3.1 %collective-permute-start.3 = (f32[8,4096]{1,0:T(8,128)S(1)}, f32[8,4096]{1,0:T(8,128)S(1)}, u32[]{:S(2)}, u32[]{:S(2)}) collective-permute-start(f32[8,4096]{1,0:T(8,128)S(1)} %get-tuple-element.49.own_even), channel_id=1, source_target_pairs={{0,2},{2,0},{4,6},{6,4},{8,10},{10,8},{12,14},{14,12},{16,18},{18,... | collective-permute-start | bytes 393224 | tf_op jit(solution)/shard_map/ppermute | solution.py:418
  14.0 0.0 collective-permute-done.from_odd
  14.0 0.0 collective-permute-done.4.from_even
  14.1 1.3 %smooth.1 = (f32[2,16,4096]{2,1,0:T(8,128)S(1)}, bf16[256,4352]{1,0:T(8,128)(2,1)S(1)}, f32[16,128]{1,0:T(8,128)S(1)}, bf16[512,256]{1,0:T(8,128)(2,1)S(1)}) custom-call(f32[2,16,4096]{2,1,0:T(8,128)S(1)} %broadcast_maximum_fusion.frames, f32[2,4,4096]{2,1,0:T(4,128)S(1)} %collective-permute-done.from_odd, f32[2,4,4096]{2,1,0:T(4,128)S(1)} %collective-permute-done.4.from_even), custom_call_target="tpu_custom_call" | custom-call | bytes 8388608 | tf_op jit(solution)/shard_map/smooth/pallas_call | solution.py:470
  15.4 0.0 collective-permute-done.2.from_odd
  15.4 0.0 collective-permute-done.3.from_even
  15.4 3.1 %match.1 = (bf16[34,48,128]{2,1,0:T(8,128)(2,1)S(1)}, f32[32,128]{1,0:T(8,128)}) custom-call(s32[1,2]{1,0:T(1,128)S(1)} %broadcast_clamp_fusion.base, f32[8,4096]{1,0:T(8,128)S(1)} %get-tuple-element.29.own_odd, f32[8,4096]{1,0:T(8,128)S(1)} %get-tuple-element.49.own_even, f32[8,4096]{1,0:T(8,128)S(1)} %collective-permute-done.2.from_odd, ...), custom_call_target="tpu_custom_call" | custom-call | bytes 12582912 | tf_op jit(solution)/shard_map/match/pallas_call | solution.py:493
  18.6 7.6 %all-to-all-start = ((f32[32,1,128]{2,1,0:T(1,128)}), f32[32,1,128]{2,1,0:T(1,128)S(1)}, u32[]{:S(2)}, u32[]{:S(2)}) async-start(f32[32,1,128]{2,1,0:T(1,128)} %bitcast.3), calls=%async_computation | async-start | bytes 32768 | tf_op jit(solution)/shard_map/all_to_all | solution.py:511
  26.1 1.8 %collective-permute-start.5 = (f32[2,16,4096]{2,1,0:T(8,128)S(1)}, f32[2,16,4096]{2,1,0:T(8,128)S(1)}, u32[]{:S(2)}, u32[]{:S(2)}) collective-permute-start(f32[2,16,4096]{2,1,0:T(8,128)S(1)} %get-tuple-element.36.inverse), channel_id=1, source_target_pairs={{0,1},{1,0},{2,3},{3,2},{4,5},{5,4},{6,7},{7,6},{8,9},{9,8},{10,11... | collective-permute-start | bytes 1572872 | tf_op jit(solution)/shard_map/ppermute | solution.py:418
  28.0 5.3 %all-to-all-done = f32[32,1,128]{2,1,0:T(1,128)S(1)} async-done(((f32[32,1,128]{2,1,0:T(1,128)}), f32[32,1,128]{2,1,0:T(1,128)S(1)}, u32[]{:S(2)}, u32[]{:S(2)}) %all-to-all-start) | async-done | bytes 16416 | tf_op jit(solution)/shard_map/all_to_all | solution.py:511
  33.3 2.9 %pressure.1 = (f32[2,16,4096]{2,1,0:T(8,128)}, f32[2,16,4096]{2,1,0:T(8,128)S(1)}, f32[16,128]{1,0:T(8,128)}) custom-call(s32[1,2]{1,0:T(1,128)S(1)} %broadcast_clamp_fusion.base, f32[1,128]{1,0:T(1,128)S(1)} %get-tuple-element.52.totals, bf16[34,48,128]{2,1,0:T(8,128)(2,1)S(1)} %get-tuple-element.35.clean, f32[2,16,4096]{2,1,0:T(8,128)S(1)} %get-tuple-element.36.inverse), custom_call_target="tpu_custom_call" | custom-call | bytes 12582912 | tf_op jit(solution)/shard_map/pressure/pallas_call | solution.py:521
  36.2 3.4 %all-to-all-start.1 = ((f32[16,1,128]{2,1,0:T(1,128)}), f32[16,1,128]{2,1,0:T(1,128)S(1)}, u32[]{:S(2)}, u32[]{:S(2)}) async-start(f32[16,1,128]{2,1,0:T(1,128)} %bitcast.6), calls=%async_computation.1 | async-start | bytes 16384 | tf_op jit(solution)/shard_map/all_to_all | solution.py:547
  39.7 0.1 slice_convert_fusion.base
  39.7 0.7 %collective-permute-done.5.inverse = f32[2,16,4096]{2,1,0:T(8,128)S(1)} collective-permute-done((f32[2,16,4096]{2,1,0:T(8,128)S(1)}, f32[2,16,4096]{2,1,0:T(8,128)S(1)}, u32[]{:S(2)}, u32[]{:S(2)}) %collective-permute-start.5) | collective-permute-done | bytes 524320 | tf_op jit(solution)/shard_map/ppermute | solution.py:418
  40.4 2.9 %time.1 = (f32[16,4096]{1,0:T(8,128)}, f32[16,4096]{1,0:T(8,128)}) custom-call(s32[1,2]{1,0:T(1,128)S(1)} %slice_convert_fusion.base, f32[1,128]{1,0:T(1,128)S(1)} %get-tuple-element.51.totals, bf16[34,48,128]{2,1,0:T(8,128)(2,1)S(1)} %get-tuple-element.35.clean, f32[2,16,4096]{2,1,0:T(8,128)S(1)} %collective-permute-done.5.inverse, ...), custom_call_target="tpu_custom_call" | custom-call | bytes 12582912 | tf_op jit(solution)/shard_map/time/pallas_call | solution.py:532
  43.3 2.7 %all-to-all-done.1 = f32[16,1,128]{2,1,0:T(1,128)S(1)} async-done(((f32[16,1,128]{2,1,0:T(1,128)}), f32[16,1,128]{2,1,0:T(1,128)S(1)}, u32[]{:S(2)}, u32[]{:S(2)}) %all-to-all-start.1) | async-done | bytes 8224 | tf_op jit(solution)/shard_map/all_to_all | solution.py:547
  46.0 0.6 %subtract_sqrt_fusion = (f32[2]{0:T(128)}, f32[2]{0:T(128)}) fusion(f32[128]{0:T(128)S(1)} %reduce_sum.19), kind=kLoop, calls=%fused_computation.10 | loop fusion | flops 8 | bytes 32 | tf_op jit(solution)/shard_map/sqrt | solution.py:552
  (9 shorter events, 0.1 us)
Async XLA Ops:
  0.6 13.4 %copy-start = (s32[1,2]{1,0:T(1,128)S(1)}, s32[1,2]{1,0:T(1,128)}, u32[]{:S(2)}) copy-start(s32[1,2]{1,0:T(1,128)} %param.7) | copy-start | bytes 28
  0.6 9.5 %collective-permute-start.1 = (f32[16,4096]{1,0:T(8,128)}, f32[16,4096]{1,0:T(8,128)S(1)}, u32[]{:S(2)}, u32[]{:S(2)}) collective-permute-start(f32[16,4096]{1,0:T(8,128)} %bitcast.14), channel_id=1, source_target_pairs={{0,1},{1,0},{2,3},{3,2},{4,5},{5,4},{6,7},{7,6},{8,9},{9,8},{10,11... | collective-permute-start | bytes 786440 | tf_op jit(solution)/shard_map/ppermute | solution.py:418
  5.8 8.2 %collective-permute-start = (f32[2,4,4096]{2,1,0:T(4,128)S(1)}, f32[2,4,4096]{2,1,0:T(4,128)S(1)}, u32[]{:S(2)}, u32[]{:S(2)}) collective-permute-start(f32[2,4,4096]{2,1,0:T(4,128)S(1)} %get-tuple-element.48), channel_id=1, source_target_pairs={{0,0},{2,4},{4,2},{6,8},{8,6},{10,12},{12,10},{14,16},{16,14},{18,... | collective-permute-start | bytes 393224 | tf_op jit(solution)/shard_map/ppermute | solution.py:418
  6.5 7.5 %collective-permute-start.4 = (f32[2,4,4096]{2,1,0:T(4,128)S(1)}, f32[2,4,4096]{2,1,0:T(4,128)S(1)}, u32[]{:S(2)}, u32[]{:S(2)}) collective-permute-start(f32[2,4,4096]{2,1,0:T(4,128)S(1)} %get-tuple-element.47), channel_id=1, source_target_pairs={{0,2},{2,0},{4,6},{6,4},{8,10},{10,8},{12,14},{14,12},{16,18},{18,... | collective-permute-start | bytes 393224 | tf_op jit(solution)/shard_map/ppermute | solution.py:418
  10.2 5.2 %collective-permute-start.2 = (f32[8,4096]{1,0:T(8,128)S(1)}, f32[8,4096]{1,0:T(8,128)S(1)}, u32[]{:S(2)}, u32[]{:S(2)}) collective-permute-start(f32[8,4096]{1,0:T(8,128)S(1)} %get-tuple-element.29.own_odd), channel_id=1, source_target_pairs={{0,0},{2,4},{4,2},{6,8},{8,6},{10,12},{12,10},{14,16},{16,14},{18,... | collective-permute-start | bytes 393224 | tf_op jit(solution)/shard_map/ppermute | solution.py:418
  10.9 4.5 %collective-permute-start.3 = (f32[8,4096]{1,0:T(8,128)S(1)}, f32[8,4096]{1,0:T(8,128)S(1)}, u32[]{:S(2)}, u32[]{:S(2)}) collective-permute-start(f32[8,4096]{1,0:T(8,128)S(1)} %get-tuple-element.49.own_even), channel_id=1, source_target_pairs={{0,2},{2,0},{4,6},{6,4},{8,10},{10,8},{12,14},{14,12},{16,18},{18,... | collective-permute-start | bytes 393224 | tf_op jit(solution)/shard_map/ppermute | solution.py:418
  18.6 14.7 %all-to-all-start = ((f32[32,1,128]{2,1,0:T(1,128)}), f32[32,1,128]{2,1,0:T(1,128)S(1)}, u32[]{:S(2)}, u32[]{:S(2)}) async-start(f32[32,1,128]{2,1,0:T(1,128)} %bitcast.3), calls=%async_computation | async-start | bytes 32768 | tf_op jit(solution)/shard_map/all_to_all | solution.py:511
  26.1 14.3 %collective-permute-start.5 = (f32[2,16,4096]{2,1,0:T(8,128)S(1)}, f32[2,16,4096]{2,1,0:T(8,128)S(1)}, u32[]{:S(2)}, u32[]{:S(2)}) collective-permute-start(f32[2,16,4096]{2,1,0:T(8,128)S(1)} %get-tuple-element.36.inverse), channel_id=1, source_target_pairs={{0,1},{1,0},{2,3},{3,2},{4,5},{5,4},{6,7},{7,6},{8,9},{9,8},{10,11... | collective-permute-start | bytes 1572872 | tf_op jit(solution)/shard_map/ppermute | solution.py:418
  36.2 9.8 %all-to-all-start.1 = ((f32[16,1,128]{2,1,0:T(1,128)}), f32[16,1,128]{2,1,0:T(1,128)S(1)}, u32[]{:S(2)}, u32[]{:S(2)}) async-start(f32[16,1,128]{2,1,0:T(1,128)} %bitcast.6), calls=%async_computation.1 | async-start | bytes 16384 | tf_op jit(solution)/shard_map/all_to_all | solution.py:547

commit v16 on v15

--- a/solution.py
+++ b/solution.py
@@ -179,9 +179,13 @@
             stack[(near + a) * size : (near + a + 1) * size, tile_of(t)] = turned[size:]
         return carry
 
-    by_tiles(load_step, tiles, tiles)
-    by_tiles(vertical_step, tiles, tiles)
-    powers = by_tiles(horizontal_step, tiles // 2, tiles // 2, (jnp.zeros((8, lanes), jnp.float32),) * count)
+    powers = (jnp.zeros((8, lanes), jnp.float32),) * count
+    for t in range(tiles + 1):
+        if t < tiles:
+            load_step(t, 0)
+            vertical_step(t, 0)
+        if t % 2 == 0 and t > 0:
+            powers = horizontal_step(t // 2 - 1, powers)
     for f in range(count):
         power[f * 8 : f * 8 + 8, :] = powers[f]
     pieces[tiles + 3] = pieces[1]
@@ -248,9 +252,13 @@
             array[2 * t + 2] = value[:, lanes:]
         return total + fold(square[:, :lanes]) + fold(square[:, lanes:])
 
-    by_tiles(load_step, tiles, tiles)
-    by_tiles(vertical_step, tiles, tiles)
-    ref_power = by_tiles(horizontal_step, tiles // 2, tiles // 2, jnp.zeros((8, lanes), jnp.float32))
+    ref_power = jnp.zeros((8, lanes), jnp.float32)
+    for t in range(tiles + 1):
+        if t < tiles:
+            load_step(t, 0)
+            vertical_step(t, 0)
+        if t % 2 == 0 and t > 0:
+            ref_power = horizontal_step(t // 2 - 1, ref_power)
     fine[tiles + 3] = fine[1]
     shifts = [column_shift(base[0, 1] + near * b - 2) for b in range(far)]
 
@@ -260,9 +268,13 @@
         return carry
 
     by_tiles(stream_step, ring, ring)
-    product = lax.dot_general(
-        stack[...], stream[...], (((1,), (1,)), ((), ())), preferred_element_type=jnp.float32
-    )
+    product = None
+    for half in range(2):
+        at = slice(half * ring * lanes // 2, (half + 1) * ring * lanes // 2)
+        term = lax.dot_general(
+            stack[:, at], stream[:, at], (((1,), (1,)), ((), ())), preferred_element_type=jnp.float32
+        )
+        product = term if product is None else product + term
     size = near * count * rows
     folded[...] = jnp.zeros(folded.shape, jnp.float32)
     folded[:, 0 : far * 2 * wide] = product[:size] + product[size:]
@@ -298,16 +310,18 @@
     part[...] = jnp.broadcast_to(packed, part.shape)
 
 
-def spread_columns(clean, spread, base_col):
-    tiles = clean.shape[0] - 2
+def spreader(clean, spread, base_col):
     size = clean.shape[1]
     spare = spread.shape[0] - reach * size
-    spread[reach * size :, :] = jnp.zeros((spare, tiles * lanes), jnp.bfloat16)
-
-    for j in range(reach):
-        shift = column_shift(base_col + j - 3)
-        for t in range(tiles):
-            spread[j * size : (j + 1) * size, t * lanes : (t + 1) * lanes] = shift(clean, t)
+    shifts = [column_shift(base_col + j - 3) for j in range(reach)]
+
+    def spread_tile(t):
+        at = tile_of(t)
+        for j, shift in enumerate(shifts):
+            spread[j * size : (j + 1) * size, at] = shift(clean, t)
+        spread[reach * size :, at] = jnp.zeros((spare, lanes), jnp.bfloat16)
+
+    return spread_tile
 
 
 def blend_weights(totals, count):
@@ -350,9 +364,12 @@
     weights = blend_weights(jnp.broadcast_to(totals[0:1, :], (8, lanes)), count)
     bands = [banded(weights[f], f, rows, 1 + base[0, 0], depth) for f in range(count)]
     mixing = cut(jnp.concatenate(bands, axis=0))
-    spread_columns(clean, spread, base[0, 1])
-
-    def chunk_values(where):
+    spread_tile = spreader(clean, spread, base[0, 1])
+
+    def chunk_values(t):
+        where = chunk_of(t)
+        spread_tile(2 * t)
+        spread_tile(2 * t + 1)
         product = jnp.dot(mixing, spread[:, where], preferred_element_type=jnp.float32)
         registered = product[: count * rows] + product[count * rows :]
         values = []
@@ -370,7 +387,7 @@
 
     def step(t, sums):
         where = chunk_of(t)
-        values = chunk_values(where)
+        values = chunk_values(t)
         squares = [value * value for value in values]
         for f in range(count):
             pressure[f, :, where] = values[f]
@@ -399,7 +416,7 @@
         where = chunk_of(t)
         first = moments[0, :, where]
         second = moments[1, :, where]
-        for value in chunk_values(where):
+        for value in chunk_values(t):
             first = first + value
             second = second + value * value
         mean = first * (1.0 / frames)

time: 46.9 us -> 46.9 us (level)
  transfers between devices with their start and end apart: 8 -> 8, of which waited for: 4 -> 4; matrix products, arithmetic and copies ran while one was open for 5% -> 5% of each run, Pallas kernels for 15% -> 16%
where the time goes in v16:
time: 46.9 us; the launch traced here: 46.6 us
  starting transfers between devices  23.2 us (49%)
  Pallas kernels  10.4 us (22%)
  waiting for transfers between devices  8.65 us (18%)
  other arithmetic  2.89 us (6%)
  between operations  1.41 us (3%)
    ppermute x6, starting transfers between devices, paired(): return lax.ppermute(value, axis, list(enumerate(partner)))  12.2 us
    all_to_all x1, starting transfers between devices, shards(): lax.all_to_all(part, ('rows', 'frames'), 0, 0, tiled=True)  7.57 us
    all_to_all x1, waiting for transfers between devices, shards(): lax.all_to_all(part, ('rows', 'frames'), 0, 0, tiled=True)  5.29 us
    all_to_all x1, starting transfers between devices, shards(): sums = lax.all_to_all(part, 'rows', 0, 0, tiled=True)  3.42 us
    pallas_call x1, Pallas kernels, shards(): pl.pallas_call(match_kernel, out_shape=(jax.ShapeDtypeStruct((tiles + 2,...  3.12 us
    pallas_call x1, Pallas kernels, shards(): pl.pallas_call(time_kernel, out_shape=(struct((rows, columns)), struct((r...  3.03 us
    pallas_call x1, Pallas kernels, shards(): pl.pallas_call(pressure_kernel, out_shape=(struct((count, rows, columns))...  2.93 us
    all_to_all x1, waiting for transfers between devices, shards(): sums = lax.all_to_all(part, 'rows', 0, 0, tiled=True)  2.53 us
  transfers between devices with their start and end apart: 8, of which 4 were waited for; matrix products, arithmetic and copies ran while one was open for 5% of the time, Pallas kernels for 16%

profile of v16, /device:TPU:0, one launch (start us, length us, event | category | flops | bytes accessed | tf_op | source)
XLA Modules:
  0.0 46.6 jit_solution(6481538212489369133)
XLA Ops:
  0.6 3.0 %collective-permute-start.1 = (f32[16,4096]{1,0:T(8,128)}, f32[16,4096]{1,0:T(8,128)S(1)}, u32[]{:S(2)}, u32[]{:S(2)}) collective-permute-start(f32[16,4096]{1,0:T(8,128)} %bitcast.14), channel_id=1, source_target_pairs={{0,1},{1,0},{2,3},{3,2},{4,5},{5,4},{6,7},{7,6},{8,9},{9,8},{10,11... | collective-permute-start | bytes 786440 | tf_op jit(solution)/shard_map/ppermute | solution.py:435
  3.7 1.0 %broadcast_maximum_fusion.1 = f32[16,4096]{1,0:T(8,128)S(1)} fusion(f32[1,16,4096]{2,1,0:T(8,128)} %param.5), kind=kLoop, calls=%fused_computation.3 | loop fusion | flops 65536 | bytes 524288 | tf_op jit(solution)/shard_map/max | solution.py:478
  4.7 1.1 %broadcast_maximum_fusion.frames = f32[2,16,4096]{2,1,0:T(8,128)S(1)} fusion(f32[2,16,4096]{2,1,0:T(8,128)} %param.4), kind=kLoop, calls=%fused_computation | loop fusion | flops 131072 | bytes 1048576 | tf_op jit(solution)/shard_map/max | solution.py:478
  5.8 0.7 %collective-permute-start = (f32[2,4,4096]{2,1,0:T(4,128)S(1)}, f32[2,4,4096]{2,1,0:T(4,128)S(1)}, u32[]{:S(2)}, u32[]{:S(2)}) collective-permute-start(f32[2,4,4096]{2,1,0:T(4,128)S(1)} %get-tuple-element.48), channel_id=1, source_target_pairs={{0,0},{2,4},{4,2},{6,8},{8,6},{10,12},{12,10},{14,16},{16,14},{18,... | collective-permute-start | bytes 393224 | tf_op jit(solution)/shard_map/ppermute | solution.py:435
  6.5 2.9 %collective-permute-start.4 = (f32[2,4,4096]{2,1,0:T(4,128)S(1)}, f32[2,4,4096]{2,1,0:T(4,128)S(1)}, u32[]{:S(2)}, u32[]{:S(2)}) collective-permute-start(f32[2,4,4096]{2,1,0:T(4,128)S(1)} %get-tuple-element.47), channel_id=1, source_target_pairs={{0,2},{2,0},{4,6},{6,4},{8,10},{10,8},{12,14},{14,12},{16,18},{18,... | collective-permute-start | bytes 393224 | tf_op jit(solution)/shard_map/ppermute | solution.py:435
  10.1 0.1 collective-permute-done.1
  10.2 0.7 %collective-permute-start.2 = (f32[8,4096]{1,0:T(8,128)S(1)}, f32[8,4096]{1,0:T(8,128)S(1)}, u32[]{:S(2)}, u32[]{:S(2)}) collective-permute-start(f32[8,4096]{1,0:T(8,128)S(1)} %get-tuple-element.29.own_odd), channel_id=1, source_target_pairs={{0,0},{2,4},{4,2},{6,8},{8,6},{10,12},{12,10},{14,16},{16,14},{18,... | collective-permute-start | bytes 393224 | tf_op jit(solution)/shard_map/ppermute | solution.py:435
  10.9 3.1 %collective-permute-start.3 = (f32[8,4096]{1,0:T(8,128)S(1)}, f32[8,4096]{1,0:T(8,128)S(1)}, u32[]{:S(2)}, u32[]{:S(2)}) collective-permute-start(f32[8,4096]{1,0:T(8,128)S(1)} %get-tuple-element.49.own_even), channel_id=1, source_target_pairs={{0,2},{2,0},{4,6},{6,4},{8,10},{10,8},{12,14},{14,12},{16,18},{18,... | collective-permute-start | bytes 393224 | tf_op jit(solution)/shard_map/ppermute | solution.py:435
  14.0 0.0 collective-permute-done.from_odd
  14.0 0.0 collective-permute-done.4.from_even
  14.1 1.3 %smooth.1 = (f32[2,16,4096]{2,1,0:T(8,128)S(1)}, bf16[256,4352]{1,0:T(8,128)(2,1)S(1)}, f32[16,128]{1,0:T(8,128)S(1)}, bf16[512,256]{1,0:T(8,128)(2,1)S(1)}) custom-call(f32[2,16,4096]{2,1,0:T(8,128)S(1)} %broadcast_maximum_fusion.frames, f32[2,4,4096]{2,1,0:T(4,128)S(1)} %collective-permute-done.from_odd, f32[2,4,4096]{2,1,0:T(4,128)S(1)} %collective-permute-done.4.from_even), custom_call_target="tpu_custom_call" | custom-call | bytes 8388608 | tf_op jit(solution)/shard_map/smooth/pallas_call | solution.py:487
  15.4 0.0 collective-permute-done.2.from_odd
  15.4 0.0 collective-permute-done.3.from_even
  15.4 3.1 %match.1 = (bf16[34,48,128]{2,1,0:T(8,128)(2,1)S(1)}, f32[32,128]{1,0:T(8,128)}) custom-call(s32[1,2]{1,0:T(1,128)S(1)} %broadcast_clamp_fusion.base, f32[8,4096]{1,0:T(8,128)S(1)} %get-tuple-element.29.own_odd, f32[8,4096]{1,0:T(8,128)S(1)} %get-tuple-element.49.own_even, f32[8,4096]{1,0:T(8,128)S(1)} %collective-permute-done.2.from_odd, ...), custom_call_target="tpu_custom_call" | custom-call | bytes 12582912 | tf_op jit(solution)/shard_map/match/pallas_call | solution.py:510
  18.5 7.6 %all-to-all-start = ((f32[32,1,128]{2,1,0:T(1,128)}), f32[32,1,128]{2,1,0:T(1,128)S(1)}, u32[]{:S(2)}, u32[]{:S(2)}) async-start(f32[32,1,128]{2,1,0:T(1,128)} %bitcast.3), calls=%async_computation | async-start | bytes 32768 | tf_op jit(solution)/shard_map/all_to_all | solution.py:528
  26.1 1.8 %collective-permute-start.5 = (f32[2,16,4096]{2,1,0:T(8,128)S(1)}, f32[2,16,4096]{2,1,0:T(8,128)S(1)}, u32[]{:S(2)}, u32[]{:S(2)}) collective-permute-start(f32[2,16,4096]{2,1,0:T(8,128)S(1)} %get-tuple-element.36.inverse), channel_id=1, source_target_pairs={{0,1},{1,0},{2,3},{3,2},{4,5},{5,4},{6,7},{7,6},{8,9},{9,8},{10,11... | collective-permute-start | bytes 1572872 | tf_op jit(solution)/shard_map/ppermute | solution.py:435
  28.0 5.3 %all-to-all-done = f32[32,1,128]{2,1,0:T(1,128)S(1)} async-done(((f32[32,1,128]{2,1,0:T(1,128)}), f32[32,1,128]{2,1,0:T(1,128)S(1)}, u32[]{:S(2)}, u32[]{:S(2)}) %all-to-all-start) | async-done | bytes 16416 | tf_op jit(solution)/shard_map/all_to_all | solution.py:528
  33.3 2.9 %pressure.1 = (f32[2,16,4096]{2,1,0:T(8,128)}, f32[2,16,4096]{2,1,0:T(8,128)S(1)}, f32[16,128]{1,0:T(8,128)}) custom-call(s32[1,2]{1,0:T(1,128)S(1)} %broadcast_clamp_fusion.base, f32[1,128]{1,0:T(1,128)S(1)} %get-tuple-element.52.totals, bf16[34,48,128]{2,1,0:T(8,128)(2,1)S(1)} %get-tuple-element.35.clean, f32[2,16,4096]{2,1,0:T(8,128)S(1)} %get-tuple-element.36.inverse), custom_call_target="tpu_custom_call" | custom-call | bytes 12582912 | tf_op jit(solution)/shard_map/pressure/pallas_call | solution.py:538
  36.2 3.4 %all-to-all-start.1 = ((f32[16,1,128]{2,1,0:T(1,128)}), f32[16,1,128]{2,1,0:T(1,128)S(1)}, u32[]{:S(2)}, u32[]{:S(2)}) async-start(f32[16,1,128]{2,1,0:T(1,128)} %bitcast.6), calls=%async_computation.1 | async-start | bytes 16384 | tf_op jit(solution)/shard_map/all_to_all | solution.py:564
  39.6 0.1 slice_convert_fusion.base
  39.7 0.7 %collective-permute-done.5.inverse = f32[2,16,4096]{2,1,0:T(8,128)S(1)} collective-permute-done((f32[2,16,4096]{2,1,0:T(8,128)S(1)}, f32[2,16,4096]{2,1,0:T(8,128)S(1)}, u32[]{:S(2)}, u32[]{:S(2)}) %collective-permute-start.5) | collective-permute-done | bytes 524320 | tf_op jit(solution)/shard_map/ppermute | solution.py:435
  40.4 3.0 %time.1 = (f32[16,4096]{1,0:T(8,128)}, f32[16,4096]{1,0:T(8,128)}) custom-call(s32[1,2]{1,0:T(1,128)S(1)} %slice_convert_fusion.base, f32[1,128]{1,0:T(1,128)S(1)} %get-tuple-element.51.totals, bf16[34,48,128]{2,1,0:T(8,128)(2,1)S(1)} %get-tuple-element.35.clean, f32[2,16,4096]{2,1,0:T(8,128)S(1)} %collective-permute-done.5.inverse, ...), custom_call_target="tpu_custom_call" | custom-call | bytes 12582912 | tf_op jit(solution)/shard_map/time/pallas_call | solution.py:549
  43.5 2.5 %all-to-all-done.1 = f32[16,1,128]{2,1,0:T(1,128)S(1)} async-done(((f32[16,1,128]{2,1,0:T(1,128)}), f32[16,1,128]{2,1,0:T(1,128)S(1)}, u32[]{:S(2)}, u32[]{:S(2)}) %all-to-all-start.1) | async-done | bytes 8224 | tf_op jit(solution)/shard_map/all_to_all | solution.py:564
  46.0 0.6 %subtract_sqrt_fusion = (f32[2]{0:T(128)}, f32[2]{0:T(128)}) fusion(f32[128]{0:T(128)S(1)} %reduce_sum.19), kind=kLoop, calls=%fused_computation.10 | loop fusion | flops 8 | bytes 32 | tf_op jit(solution)/shard_map/sqrt | solution.py:569
  (9 shorter events, 0.1 us)
Async XLA Ops:
  0.6 13.4 %copy-start = (s32[1,2]{1,0:T(1,128)S(1)}, s32[1,2]{1,0:T(1,128)}, u32[]{:S(2)}) copy-start(s32[1,2]{1,0:T(1,128)} %param.7) | copy-start | bytes 28
  0.6 9.5 %collective-permute-start.1 = (f32[16,4096]{1,0:T(8,128)}, f32[16,4096]{1,0:T(8,128)S(1)}, u32[]{:S(2)}, u32[]{:S(2)}) collective-permute-start(f32[16,4096]{1,0:T(8,128)} %bitcast.14), channel_id=1, source_target_pairs={{0,1},{1,0},{2,3},{3,2},{4,5},{5,4},{6,7},{7,6},{8,9},{9,8},{10,11... | collective-permute-start | bytes 786440 | tf_op jit(solution)/shard_map/ppermute | solution.py:435
  5.8 8.2 %collective-permute-start = (f32[2,4,4096]{2,1,0:T(4,128)S(1)}, f32[2,4,4096]{2,1,0:T(4,128)S(1)}, u32[]{:S(2)}, u32[]{:S(2)}) collective-permute-start(f32[2,4,4096]{2,1,0:T(4,128)S(1)} %get-tuple-element.48), channel_id=1, source_target_pairs={{0,0},{2,4},{4,2},{6,8},{8,6},{10,12},{12,10},{14,16},{16,14},{18,... | collective-permute-start | bytes 393224 | tf_op jit(solution)/shard_map/ppermute | solution.py:435
  6.5 7.5 %collective-permute-start.4 = (f32[2,4,4096]{2,1,0:T(4,128)S(1)}, f32[2,4,4096]{2,1,0:T(4,128)S(1)}, u32[]{:S(2)}, u32[]{:S(2)}) collective-permute-start(f32[2,4,4096]{2,1,0:T(4,128)S(1)} %get-tuple-element.47), channel_id=1, source_target_pairs={{0,2},{2,0},{4,6},{6,4},{8,10},{10,8},{12,14},{14,12},{16,18},{18,... | collective-permute-start | bytes 393224 | tf_op jit(solution)/shard_map/ppermute | solution.py:435
  10.2 5.2 %collective-permute-start.2 = (f32[8,4096]{1,0:T(8,128)S(1)}, f32[8,4096]{1,0:T(8,128)S(1)}, u32[]{:S(2)}, u32[]{:S(2)}) collective-permute-start(f32[8,4096]{1,0:T(8,128)S(1)} %get-tuple-element.29.own_odd), channel_id=1, source_target_pairs={{0,0},{2,4},{4,2},{6,8},{8,6},{10,12},{12,10},{14,16},{16,14},{18,... | collective-permute-start | bytes 393224 | tf_op jit(solution)/shard_map/ppermute | solution.py:435
  10.9 4.5 %collective-permute-start.3 = (f32[8,4096]{1,0:T(8,128)S(1)}, f32[8,4096]{1,0:T(8,128)S(1)}, u32[]{:S(2)}, u32[]{:S(2)}) collective-permute-start(f32[8,4096]{1,0:T(8,128)S(1)} %get-tuple-element.49.own_even), channel_id=1, source_target_pairs={{0,2},{2,0},{4,6},{6,4},{8,10},{10,8},{12,14},{14,12},{16,18},{18,... | collective-permute-start | bytes 393224 | tf_op jit(solution)/shard_map/ppermute | solution.py:435
  18.5 14.7 %all-to-all-start = ((f32[32,1,128]{2,1,0:T(1,128)}), f32[32,1,128]{2,1,0:T(1,128)S(1)}, u32[]{:S(2)}, u32[]{:S(2)}) async-start(f32[32,1,128]{2,1,0:T(1,128)} %bitcast.3), calls=%async_computation | async-start | bytes 32768 | tf_op jit(solution)/shard_map/all_to_all | solution.py:528
  26.1 14.3 %collective-permute-start.5 = (f32[2,16,4096]{2,1,0:T(8,128)S(1)}, f32[2,16,4096]{2,1,0:T(8,128)S(1)}, u32[]{:S(2)}, u32[]{:S(2)}) collective-permute-start(f32[2,16,4096]{2,1,0:T(8,128)S(1)} %get-tuple-element.36.inverse), channel_id=1, source_target_pairs={{0,1},{1,0},{2,3},{3,2},{4,5},{5,4},{6,7},{7,6},{8,9},{9,8},{10,11... | collective-permute-start | bytes 1572872 | tf_op jit(solution)/shard_map/ppermute | solution.py:435
  36.2 9.8 %all-to-all-start.1 = ((f32[16,1,128]{2,1,0:T(1,128)}), f32[16,1,128]{2,1,0:T(1,128)S(1)}, u32[]{:S(2)}, u32[]{:S(2)}) async-start(f32[16,1,128]{2,1,0:T(1,128)} %bitcast.6), calls=%async_computation.1 | async-start | bytes 16384 | tf_op jit(solution)/shard_map/all_to_all | solution.py:564

commit v17 on v16

--- a/solution.py
+++ b/solution.py
@@ -15,6 +15,7 @@
 reach = 7
 near = 4
 far = 2
+slot = 32
 params = pltpu.CompilerParams(vmem_limit_bytes=14 * 1024 * 1024)
 vmem = pl.BlockSpec(memory_space=pltpu.VMEM)
 smem = pl.BlockSpec(memory_space=pltpu.SMEM)
@@ -100,11 +101,20 @@
     return pl.ds(pl.multiple_of(t * 2 * lanes, 2 * lanes), 2 * lanes)
 
 
-def horizontal(wide, band, t):
-    window = wide[:, t * 2 * lanes : (t + 2) * 2 * lanes]
-    product = jnp.dot(window, band[...], preferred_element_type=jnp.float32)
-    half = product.shape[0] // 2
-    return product[:half] + product[half:]
+def place_tile(windows, index, value):
+    for c in (index // 2 - 1, index // 2):
+        at = index - 2 * c
+        if 0 <= c < windows.shape[0] and at < 4:
+            windows[c, :, at * lanes : (at + 1) * lanes] = value
+
+
+def horizontal(windows, band):
+    chunks, height, width = windows.shape
+    product = jnp.dot(
+        windows[...].reshape(chunks * height, width), band[...], preferred_element_type=jnp.float32
+    )
+    product = product.reshape(chunks, height, 2 * lanes)
+    return product[:, : height // 2] + product[:, height // 2 :]
 
 
 def by_row_shift(value, rows, direction):
@@ -134,8 +144,8 @@
     odd = lax.axis_index("rows") % 2 == 1
     edge = at_edge()
     blank = jnp.zeros((2 * count * rows, lanes), jnp.bfloat16)
-    wide[:, tile_of(0)] = blank
-    wide[:, tile_of(tiles + 1)] = blank
+    place_tile(wide, 0, blank)
+    place_tile(wide, tiles + 1, blank)
     fill_band(band)
     pieces[0] = blank
     pieces[tiles + 1] = blank
@@ -152,11 +162,11 @@
 
     def vertical_step(t, carry):
         parts = [vertical(lambda s: rows_in[f, t, pl.ds(4 + s, rows), :]) for f in range(count)]
-        wide[:, tile_of(t + 1)] = cut(jnp.concatenate(parts, axis=0))
+        place_tile(wide, t + 1, cut(jnp.concatenate(parts, axis=0)))
         return carry
 
     def horizontal_step(t, totals):
-        smooth = horizontal(wide, band, t)
+        smooth = smoothed[t]
         result = []
         details = []
         for f in range(count):
@@ -180,12 +190,12 @@
         return carry
 
     powers = (jnp.zeros((8, lanes), jnp.float32),) * count
-    for t in range(tiles + 1):
-        if t < tiles:
-            load_step(t, 0)
-            vertical_step(t, 0)
-        if t % 2 == 0 and t > 0:
-            powers = horizontal_step(t // 2 - 1, powers)
+    for t in range(tiles):
+        load_step(t, 0)
+        vertical_step(t, 0)
+    smoothed = horizontal(wide, band)
+    for t in range(tiles // 2):
+        powers = horizontal_step(t, powers)
     for f in range(count):
         power[f * 8 : f * 8 + 8, :] = powers[f]
     pieces[tiles + 3] = pieces[1]
@@ -206,79 +216,112 @@
     return shift
 
 
-def match_kernel(
-    base, own_odd, own_even, from_odd, from_even, stack, power, band, clean, part, rows_in, padded, fine, stream, folded, lags
-):
-    rows = own_odd.shape[0] * 2
-    tiles = own_odd.shape[1] // lanes
-    count = power.shape[0] // 8
-    ring = tiles + 2
-    wide = rows + 8
-    row_index = lax.axis_index("rows")
-    last_row = lax.axis_size("rows") - 1
-    odd = row_index % 2 == 1
-    edge = at_edge()
-    empty = jnp.zeros((2 * wide, lanes), jnp.bfloat16)
-    padded[:, tile_of(0)] = empty
-    padded[:, tile_of(tiles + 1)] = empty
+def reference_rows(raw, smooth, clean, fine, tiles):
+    height = clean.shape[1] // 2
+    empty = jnp.zeros((2 * height, lanes), jnp.bfloat16)
     for array in (clean, fine):
         array[0] = empty
         array[tiles + 1] = empty
     fine[tiles + 2] = empty
-    place = lax.broadcasted_iota(jnp.int32, (wide, 2 * lanes), 0)
-    own = (place >= 4) & (place < rows + 4)
-    inside = ((place >= 4) | (row_index > 0)) & ((place < rows + 4) | (row_index < last_row))
-
-    def load_step(t, carry):
-        outer = [jnp.where(edge, 0.0, from_odd[:, tile_of(t)]), own_odd[:, tile_of(t)]]
-        inner = [array[:, tile_of(t)] for array in (own_even, from_even)]
-        rows_in[t, 0:8, :] = jnp.where(odd, inner[1], outer[0])
-        rows_in[t, 8:16, :] = jnp.where(odd, inner[0], outer[1])
-        rows_in[t, 16:24, :] = jnp.where(odd, outer[1], inner[0])
-        rows_in[t, 24:32, :] = jnp.where(odd, outer[0], inner[1])
-        return carry
-
-    def vertical_step(t, carry):
-        padded[:, tile_of(t + 1)] = cut(vertical(lambda s: rows_in[t, pl.ds(s, wide), :]))
-        return carry
-
-    def horizontal_step(t, total):
-        smooth = jnp.where(inside, horizontal(padded, band, t), 0.0)
-        raw = [rows_in[2 * t + c, pl.ds(4, wide), :] for c in range(2)]
-        detail = jnp.concatenate(raw, axis=1) - smooth
-        square = jnp.where(own, detail * detail, 0.0)
-        for array, value in ((clean, cut(smooth)), (fine, cut(detail))):
+    squares = []
+    for t in range(tiles // 2):
+        detail = jnp.concatenate([raw(2 * t), raw(2 * t + 1)], axis=1) - smooth(t)
+        for array, value in ((clean, cut(smooth(t))), (fine, cut(detail))):
             array[2 * t + 1] = value[:, :lanes]
             array[2 * t + 2] = value[:, lanes:]
-        return total + fold(square[:, :lanes]) + fold(square[:, lanes:])
-
-    ref_power = jnp.zeros((8, lanes), jnp.float32)
-    for t in range(tiles + 1):
-        if t < tiles:
-            load_step(t, 0)
-            vertical_step(t, 0)
-        if t % 2 == 0 and t > 0:
-            ref_power = horizontal_step(t // 2 - 1, ref_power)
+        squares.append(detail * detail)
     fine[tiles + 3] = fine[1]
-    shifts = [column_shift(base[0, 1] + near * b - 2) for b in range(far)]
-
-    def stream_step(t, carry):
+    return squares
+
+
+def lag_products(stack, fine, stream, folded, base_col, start):
+    height = fine.shape[1]
+    half = height // 2
+    shifts = [column_shift(base_col + near * b - 2) for b in range(far)]
+    for t in range(fine.shape[0] - 2):
         for b, shift in enumerate(shifts):
-            stream[b * 2 * wide : (b + 1) * 2 * wide, tile_of(t)] = shift(fine, t)
-        return carry
-
-    by_tiles(stream_step, ring, ring)
-    product = None
-    for half in range(2):
-        at = slice(half * ring * lanes // 2, (half + 1) * ring * lanes // 2)
-        term = lax.dot_general(
-            stack[:, at], stream[:, at], (((1,), (1,)), ((), ())), preferred_element_type=jnp.float32
-        )
-        product = term if product is None else product + term
-    size = near * count * rows
+            stream[b * height : (b + 1) * height, tile_of(t)] = shift(fine, t)
+    product = lax.dot_general(
+        stack[...], stream[...], (((1,), (1,)), ((), ())), preferred_element_type=jnp.float32
+    )
+    size = product.shape[0] // 2
     folded[...] = jnp.zeros(folded.shape, jnp.float32)
-    folded[:, 0 : far * 2 * wide] = product[:size] + product[size:]
-    product = by_row_shift(folded[...], rows, -1)
+    folded[:, 0 : far * height] = product[:size] + product[size:]
+    product = folded[...]
+    lane = lane_of(product.shape)
+    placed = jnp.zeros_like(product)
+    for s in range(2 * far):
+        at = s * slot + start
+        turned = pltpu.roll(product, at - s * half, 1)
+        placed = jnp.where((lane >= at) & (lane < at + half), turned, placed)
+    return placed
+
+
+def near_kernel(
+    base, own_odd, own_even, from_even, stack, band, clean, lags, power, rows_in, windows, fine, stream, folded
+):
+    tiles = own_odd.shape[1] // lanes
+    odd = lax.axis_index("rows") % 2 == 1
+    height = clean.shape[1] // 2
+    empty = jnp.zeros((2 * height, lanes), jnp.bfloat16)
+    place_tile(windows, 0, empty)
+    place_tile(windows, tiles + 1, empty)
+    for t in range(tiles):
+        at = tile_of(t)
+        outer = own_odd[:, at]
+        inner = from_even[:, at]
+        rows_in[t, 0:8, :] = jnp.where(odd, inner, outer)
+        rows_in[t, 8:16, :] = own_even[:, at]
+        rows_in[t, 16:24, :] = jnp.where(odd, outer, inner)
+        place_tile(windows, t + 1, cut(vertical(lambda s: rows_in[t, pl.ds(s, height), :])))
+    smooth = horizontal(windows, band)
+    squares = reference_rows(lambda t: rows_in[t, pl.ds(4, height), :], lambda t: smooth[t], clean, fine, tiles)
+    place = lax.broadcasted_iota(jnp.int32, squares[0].shape, 0)
+    first = jnp.where(odd, 4, 0)
+    own = (place >= first) & (place < first + height - 4)
+    total = jnp.zeros((8, lanes), jnp.float32)
+    for square in squares:
+        square = jnp.where(own, square, 0.0)
+        total = total + fold(square[:, :lanes]) + fold(square[:, lanes:])
+    power[...] = total
+    lags[...] = lag_products(stack, fine, stream, folded, base[0, 1], jnp.where(odd, 0, 8))
+
+
+def match_kernel(
+    base, own_odd, from_odd, near_lags, near_power, stack, power, band, clean, part, rows_in, windows, fine, stream, folded, lags
+):
+    tiles = own_odd.shape[1] // lanes
+    count = power.shape[0] // 8
+    rows = folded.shape[0] // (near * count)
+    odd = lax.axis_index("rows") % 2 == 1
+    edge = at_edge()
+    height = clean.shape[1] // 2
+    empty = jnp.zeros((2 * height, lanes), jnp.bfloat16)
+    place_tile(windows, 0, empty)
+    place_tile(windows, tiles + 1, empty)
+    for t in range(tiles):
+        at = tile_of(t)
+        outer = jnp.where(edge, 0.0, from_odd[:, at])
+        inner = own_odd[:, at]
+        rows_in[t, 0:8, :] = jnp.where(odd, inner, outer)
+        rows_in[t, 8:16, :] = jnp.where(odd, outer, inner)
+        place_tile(windows, t + 1, cut(vertical(lambda s: rows_in[t, pl.ds(s, height), :])))
+    smooth = horizontal(windows, band)
+    place = lax.broadcasted_iota(jnp.int32, (height, 2 * lanes), 0)
+    first = jnp.where(odd, 0, 4)
+    own = (place >= first) & (place < first + 4)
+    inside = (place >= jnp.where(edge, first, 0)) & (place < jnp.where(edge, first + 4, height))
+
+    def masked(t):
+        return jnp.where(inside, smooth[t], 0.0)
+
+    squares = reference_rows(lambda t: rows_in[t, pl.ds(4, height), :], masked, clean, fine, tiles)
+    ref_power = near_power[...]
+    for square in squares:
+        square = jnp.where(own, square, 0.0)
+        ref_power = ref_power + fold(square[:, :lanes]) + fold(square[:, lanes:])
+    product = lag_products(stack, fine, stream, folded, base[0, 1], jnp.where(odd, 16, 0))
+    product = by_row_shift(product + near_lags[...], rows, -1)
     lags[...] = jnp.zeros(lags.shape, jnp.float32)
     for a in range(near):
         for f in range(count):
@@ -292,9 +335,9 @@
         block = lags[f * 8 : f * 8 + 8, :]
         for j in range(reach):
             at = (f * reach + j) * reach
-            there = back + at - (j // near) * 2 * wide
+            there = back + at - (j // near) * 2 * slot
             high = pltpu.roll(block, there & (lanes - 1), 1)
-            low = pltpu.roll(block, (there - wide) & (lanes - 1), 1)
+            low = pltpu.roll(block, (there - slot) & (lanes - 1), 1)
             member = (across == j % near) & (lane >= at) & (lane < at + reach)
             packed = packed + jnp.where(member, high + low, 0.0)
     lags[0:8, :] = jnp.zeros((8, lanes), jnp.float32)
@@ -310,15 +353,17 @@
     part[...] = jnp.broadcast_to(packed, part.shape)
 
 
-def spreader(clean, spread, base_col):
-    size = clean.shape[1]
+def spreader(clean, other, spread, base_col):
+    height = clean.shape[1]
+    size = height + other.shape[1]
     spare = spread.shape[0] - reach * size
     shifts = [column_shift(base_col + j - 3) for j in range(reach)]
 
     def spread_tile(t):
         at = tile_of(t)
         for j, shift in enumerate(shifts):
-            spread[j * size : (j + 1) * size, at] = shift(clean, t)
+            spread[j * size : j * size + height, at] = shift(clean, t)
+            spread[j * size + height : (j + 1) * size, at] = shift(other, t)
         spread[reach * size :, at] = jnp.zeros((spare, lanes), jnp.bfloat16)
 
     return spread_tile
@@ -354,17 +399,23 @@
         amount = at - (f * reach + j) * reach
         amount = jnp.where(amount < 0, amount + depth, amount)
         line = jnp.where((lane >= at) & (lane < at + reach), pltpu.roll(weights, amount, 1), line)
-    line = line + pltpu.roll(line, wide, 1)
-    return by_row_shift(jnp.broadcast_to(line[0:1], (rows, depth)), rows, 1)
-
-
-def pressures(base, totals, clean, spread, inverse):
+    band = by_row_shift(jnp.broadcast_to(line[0:1], (rows, depth)), rows, 1)
+    odd = lax.axis_index("rows") % 2 == 1
+    row = lane_of(band.shape) % (2 * wide)
+    start = jnp.where(odd, 0, 8)
+    inner = (row >= start) & (row < start + rows)
+    first = pltpu.roll(jnp.where(inner, band, 0.0), jnp.where(odd, 0, depth - 8), 1)
+    second = pltpu.roll(jnp.where(inner, 0.0, band), jnp.where(odd, 2 * rows - 16, 2 * rows), 1)
+    return first + pltpu.roll(first, rows, 1) + second + pltpu.roll(second, 8, 1)
+
+
+def pressures(base, totals, clean, other, spread, inverse):
     count, rows, columns = inverse.shape
     depth = spread.shape[0]
     weights = blend_weights(jnp.broadcast_to(totals[0:1, :], (8, lanes)), count)
     bands = [banded(weights[f], f, rows, 1 + base[0, 0], depth) for f in range(count)]
     mixing = cut(jnp.concatenate(bands, axis=0))
-    spread_tile = spreader(clean, spread, base[0, 1])
+    spread_tile = spreader(clean, other, spread, base[0, 1])
 
     def chunk_values(t):
         where = chunk_of(t)
@@ -381,9 +432,9 @@
     return chunk_values
 
 
-def pressure_kernel(base, totals, clean, inverse, pressure, moments, part, spread):
+def pressure_kernel(base, totals, clean, other, inverse, pressure, moments, part, spread):
     count, rows, columns = inverse.shape
-    chunk_values = pressures(base, totals, clean, spread, inverse)
+    chunk_values = pressures(base, totals, clean, other, spread, inverse)
 
     def step(t, sums):
         where = chunk_of(t)
@@ -407,9 +458,9 @@
     part[...] = jnp.broadcast_to(line[0:1], part.shape)
 
 
-def time_kernel(base, totals, clean, inverse, moments, time_mean, time_rms, spread):
+def time_kernel(base, totals, clean, other, inverse, moments, time_mean, time_rms, spread):
     count, rows, columns = inverse.shape
-    chunk_values = pressures(base, totals, clean, spread, inverse)
+    chunk_values = pressures(base, totals, clean, other, spread, inverse)
     frames = 2 * count
 
     def step(t, carry):
@@ -496,7 +547,7 @@
         out_specs=(vmem,) * 4,
         scratch_shapes=[
             pltpu.VMEM((count, tiles, rows + 16, lanes), f32),
-            pltpu.VMEM((2 * count * rows, (tiles + 2) * lanes), bf16),
+            pltpu.VMEM((tiles // 2, 2 * count * rows, 4 * lanes), bf16),
             pltpu.VMEM((ring + 2, 2 * count * rows, lanes), bf16),
         ],
         compiler_params=params,
@@ -507,23 +558,39 @@
     peers = size * blocks if blocks == 2 else size
     if blocks == 2:
         other_inverse = paired(inverse, "frames", 0)
-    clean, part = pl.pallas_call(
+    def reference_scratch(height):
+        return [
+            pltpu.VMEM((tiles, height + 8, lanes), f32),
+            pltpu.VMEM((tiles // 2, 2 * height, 4 * lanes), bf16),
+            pltpu.VMEM((ring + 2, 2 * height, lanes), bf16),
+            pltpu.VMEM((far * 2 * height, ring * lanes), bf16),
+            pltpu.VMEM((depth, lanes), f32),
+        ]
+
+    clean, near_lags, near_power = pl.pallas_call(
+        near_kernel,
+        out_shape=(
+            jax.ShapeDtypeStruct((tiles + 2, 2 * rows, lanes), bf16),
+            struct((depth, lanes)),
+            struct((8, lanes)),
+        ),
+        in_specs=[smem] + [vmem] * 5,
+        out_specs=(vmem,) * 3,
+        scratch_shapes=reference_scratch(rows),
+        compiler_params=params,
+        cost_estimate=cost(8),
+        name="near",
+    )(offsets, own_odd, own_even, from_even, stack, band)
+    other, part = pl.pallas_call(
         match_kernel,
-        out_shape=(jax.ShapeDtypeStruct((tiles + 2, 2 * wide, lanes), bf16), struct((peers, lanes))),
+        out_shape=(jax.ShapeDtypeStruct((tiles + 2, 16, lanes), bf16), struct((peers, lanes))),
         in_specs=[smem] + [vmem] * 7,
-        out_specs=(vmem, vmem),
-        scratch_shapes=[
-            pltpu.VMEM((tiles, rows + 16, lanes), f32),
-            pltpu.VMEM((2 * wide, (tiles + 2) * lanes), bf16),
-            pltpu.VMEM((ring + 2, 2 * wide, lanes), bf16),
-            pltpu.VMEM((far * 2 * wide, ring * lanes), bf16),
-            pltpu.VMEM((depth, lanes), f32),
-            pltpu.VMEM((8 * count, lanes), f32),
-        ],
+        out_specs=(vmem,) * 2,
+        scratch_shapes=reference_scratch(8) + [pltpu.VMEM((8 * count, lanes), f32)],
         compiler_params=params,
-        cost_estimate=cost(12),
+        cost_estimate=cost(8),
         name="match",
-    )(offsets, own_odd, own_even, from_odd, from_even, stack, power, band)
+    )(offsets, own_odd, from_odd, near_lags, near_power, stack, power, band)
     if blocks == 2:
         parts = lax.all_to_all(part, ("rows", "frames"), 0, 0, tiled=True).reshape(size, blocks, lanes)
         mine = lax.axis_index("frames") == 0
@@ -538,24 +605,24 @@
     pressure, moments, part = pl.pallas_call(
         pressure_kernel,
         out_shape=(struct((count, rows, columns)), struct((2, rows, columns)), struct((size, lanes))),
-        in_specs=[smem] + [vmem] * 3,
+        in_specs=[smem] + [vmem] * 4,
         out_specs=(vmem, vmem, vmem),
         scratch_shapes=[spread],
         compiler_params=params,
         cost_estimate=cost(12),
         name="pressure",
-    )(offsets, totals, clean, inverse)
+    )(offsets, totals, clean, other, inverse)
     if blocks == 2:
         time_mean, time_rms = pl.pallas_call(
             time_kernel,
             out_shape=(struct((rows, columns)), struct((rows, columns))),
-            in_specs=[smem] + [vmem] * 4,
+            in_specs=[smem] + [vmem] * 5,
             out_specs=(vmem, vmem),
             scratch_shapes=[spread],
             compiler_params=params,
             cost_estimate=cost(12),
             name="time",
-        )(place, row, clean, other_inverse, moments)
+        )(place, row, clean, other, other_inverse, moments)
     else:
         whole = total_over(moments, "frames")
         total_frames = count * blocks

time: 46.9 us -> 46.9 us (level)
  Pallas kernels: 10.4 us -> 12.2 us
  starting transfers between devices: 23.2 us -> 21.5 us
    ppermute x6, starting transfers between devices: 12.2 us -> 9.19 us  [paired(): return lax.ppermute(value, axis, list(enumerate(partner)))]
    pallas_call x0 -> x1, Pallas kernels: none -> 2.12 us  [shards(): pl.pallas_call(near_kernel, out_shape=(jax.ShapeDtypeStruct((tiles + 2, 2...]
    all_to_all x1, starting transfers between devices: 7.57 us -> 8.87 us  [shards(): lax.all_to_all(part, ('rows', 'frames'), 0, 0, tiled=True)]
  transfers between devices with their start and end apart: 8 -> 8, of which waited for: 4 -> 4; matrix products, arithmetic and copies ran while one was open for 5% -> 5% of each run, Pallas kernels for 16% -> 20%
where the time goes in v17:
time: 46.9 us; the launch traced here: 46.6 us
  starting transfers between devices  21.5 us (46%)
  Pallas kernels  12.2 us (26%)
  waiting for transfers between devices  8.57 us (18%)
  other arithmetic  2.89 us (6%)
  between operations  1.45 us (3%)
    ppermute x6, starting transfers between devices, paired(): return lax.ppermute(value, axis, list(enumerate(partner)))  9.19 us
    all_to_all x1, starting transfers between devices, shards(): lax.all_to_all(part, ('rows', 'frames'), 0, 0, tiled=True)  8.87 us
    all_to_all x1, waiting for transfers between devices, shards(): lax.all_to_all(part, ('rows', 'frames'), 0, 0, tiled=True)  5.29 us
    all_to_all x1, starting transfers between devices, shards(): sums = lax.all_to_all(part, 'rows', 0, 0, tiled=True)  3.45 us
    pallas_call x1, Pallas kernels, shards(): pl.pallas_call(time_kernel, out_shape=(struct((rows, columns)), struct((r...  3.13 us
    pallas_call x1, Pallas kernels, shards(): pl.pallas_call(pressure_kernel, out_shape=(struct((count, rows, columns))...  3 us
    pallas_call x1, Pallas kernels, shards(): pl.pallas_call(match_kernel, out_shape=(jax.ShapeDtypeStruct((tiles + 2,...  2.77 us
    all_to_all x1, waiting for transfers between devices, shards(): sums = lax.all_to_all(part, 'rows', 0, 0, tiled=True)  2.55 us
  transfers between devices with their start and end apart: 8, of which 4 were waited for; matrix products, arithmetic and copies ran while one was open for 5% of the time, Pallas kernels for 20%

profile of v17, /device:TPU:0, one launch (start us, length us, event | category | flops | bytes accessed | tf_op | source)
XLA Modules:
  0.0 46.6 jit_solution(2671978036307710807)
XLA Ops:
  0.6 3.0 %collective-permute-start.1 = (f32[16,4096]{1,0:T(8,128)}, f32[16,4096]{1,0:T(8,128)S(1)}, u32[]{:S(2)}, u32[]{:S(2)}) collective-permute-start(f32[16,4096]{1,0:T(8,128)} %bitcast.14), channel_id=1, source_target_pairs={{0,1},{1,0},{2,3},{3,2},{4,5},{5,4},{6,7},{7,6},{8,9},{9,8},{10,11... | collective-permute-start | bytes 786440 | tf_op jit(solution)/shard_map/ppermute | solution.py:486
  3.7 1.0 %broadcast_maximum_fusion.1 = f32[16,4096]{1,0:T(8,128)S(1)} fusion(f32[1,16,4096]{2,1,0:T(8,128)} %param.5), kind=kLoop, calls=%fused_computation.3 | loop fusion | flops 65536 | bytes 524288 | tf_op jit(solution)/shard_map/max | solution.py:529
  4.7 1.1 %broadcast_maximum_fusion.frames = f32[2,16,4096]{2,1,0:T(8,128)S(1)} fusion(f32[2,16,4096]{2,1,0:T(8,128)} %param.4), kind=kLoop, calls=%fused_computation | loop fusion | flops 131072 | bytes 1048576 | tf_op jit(solution)/shard_map/max | solution.py:529
  5.8 0.7 %collective-permute-start = (f32[2,4,4096]{2,1,0:T(4,128)S(1)}, f32[2,4,4096]{2,1,0:T(4,128)S(1)}, u32[]{:S(2)}, u32[]{:S(2)}) collective-permute-start(f32[2,4,4096]{2,1,0:T(4,128)S(1)} %get-tuple-element.54), channel_id=1, source_target_pairs={{0,0},{2,4},{4,2},{6,8},{8,6},{10,12},{12,10},{14,16},{16,14},{18,... | collective-permute-start | bytes 393224 | tf_op jit(solution)/shard_map/ppermute | solution.py:486
  6.5 2.9 %collective-permute-start.4 = (f32[2,4,4096]{2,1,0:T(4,128)S(1)}, f32[2,4,4096]{2,1,0:T(4,128)S(1)}, u32[]{:S(2)}, u32[]{:S(2)}) collective-permute-start(f32[2,4,4096]{2,1,0:T(4,128)S(1)} %get-tuple-element.53), channel_id=1, source_target_pairs={{0,2},{2,0},{4,6},{6,4},{8,10},{10,8},{12,14},{14,12},{16,18},{18,... | collective-permute-start | bytes 393224 | tf_op jit(solution)/shard_map/ppermute | solution.py:486
  10.1 0.1 collective-permute-done.1
  10.2 0.1 collective-permute-start.3
  10.3 0.7 %collective-permute-start.2 = (f32[8,4096]{1,0:T(8,128)S(1)}, f32[8,4096]{1,0:T(8,128)S(1)}, u32[]{:S(2)}, u32[]{:S(2)}) collective-permute-start(f32[8,4096]{1,0:T(8,128)S(1)} %get-tuple-element.32.own_odd), channel_id=1, source_target_pairs={{0,0},{2,4},{4,2},{6,8},{8,6},{10,12},{12,10},{14,16},{16,14},{18,... | collective-permute-start | bytes 393224 | tf_op jit(solution)/shard_map/ppermute | solution.py:486
  11.0 0.0 collective-permute-done.from_odd
  11.0 0.0 collective-permute-done.4.from_even
  11.0 1.2 %smooth.1 = (f32[2,16,4096]{2,1,0:T(8,128)S(1)}, bf16[256,4352]{1,0:T(8,128)(2,1)S(1)}, f32[16,128]{1,0:T(8,128)S(1)}, bf16[512,256]{1,0:T(8,128)(2,1)S(1)}) custom-call(f32[2,16,4096]{2,1,0:T(8,128)S(1)} %broadcast_maximum_fusion.frames, f32[2,4,4096]{2,1,0:T(4,128)S(1)} %collective-permute-done.from_odd, f32[2,4,4096]{2,1,0:T(4,128)S(1)} %collective-permute-done.4.from_even), custom_call_target="tpu_custom_call" | custom-call | bytes 8388608 | tf_op jit(solution)/shard_map/smooth/pallas_call | solution.py:538
  12.2 2.1 %near.1 = (bf16[34,32,128]{2,1,0:T(8,128)(2,1)S(1)}, f32[128,128]{1,0:T(8,128)S(1)}, f32[8,128]{1,0:T(8,128)S(1)}) custom-call(s32[1,2]{1,0:T(1,128)S(1)} %broadcast_clamp_fusion.base, f32[8,4096]{1,0:T(8,128)S(1)} %get-tuple-element.32.own_odd, f32[8,4096]{1,0:T(8,128)S(1)} %get-tuple-element.55.own_even, f32[8,4096]{1,0:T(8,128)S(1)} %collective-permute-done.3.from_even, ...), custom_call_target="tpu_custom_call" | custom-call | bytes 8388608 | tf_op jit(solution)/shard_map/near/pallas_call | solution.py:570
  14.3 0.0 collective-permute-done.2.from_odd
  14.4 2.8 %match.1 = (bf16[34,16,128]{2,1,0:T(8,128)(2,1)S(1)}, f32[32,128]{1,0:T(8,128)}) custom-call(s32[1,2]{1,0:T(1,128)S(1)} %broadcast_clamp_fusion.base, f32[8,4096]{1,0:T(8,128)S(1)} %get-tuple-element.32.own_odd, f32[8,4096]{1,0:T(8,128)S(1)} %collective-permute-done.2.from_odd, f32[128,128]{1,0:T(8,128)S(1)} %get-tuple-element.36.near_lags, ...), custom_call_target="tpu_custom_call" | custom-call | bytes 8388608 | tf_op jit(solution)/shard_map/match/pallas_call | solution.py:584
  17.1 8.9 %all-to-all-start = ((f32[32,1,128]{2,1,0:T(1,128)}), f32[32,1,128]{2,1,0:T(1,128)S(1)}, u32[]{:S(2)}, u32[]{:S(2)}) async-start(f32[32,1,128]{2,1,0:T(1,128)} %bitcast.3), calls=%async_computation | async-start | bytes 32768 | tf_op jit(solution)/shard_map/all_to_all | solution.py:595
  26.0 1.8 %collective-permute-start.5 = (f32[2,16,4096]{2,1,0:T(8,128)S(1)}, f32[2,16,4096]{2,1,0:T(8,128)S(1)}, u32[]{:S(2)}, u32[]{:S(2)}) collective-permute-start(f32[2,16,4096]{2,1,0:T(8,128)S(1)} %get-tuple-element.42.inverse), channel_id=1, source_target_pairs={{0,1},{1,0},{2,3},{3,2},{4,5},{5,4},{6,7},{7,6},{8,9},{9,8},{10,11... | collective-permute-start | bytes 1572872 | tf_op jit(solution)/shard_map/ppermute | solution.py:486
  27.8 5.3 %all-to-all-done = f32[32,1,128]{2,1,0:T(1,128)S(1)} async-done(((f32[32,1,128]{2,1,0:T(1,128)}), f32[32,1,128]{2,1,0:T(1,128)S(1)}, u32[]{:S(2)}, u32[]{:S(2)}) %all-to-all-start) | async-done | bytes 16416 | tf_op jit(solution)/shard_map/all_to_all | solution.py:595
  33.2 3.0 %pressure.1 = (f32[2,16,4096]{2,1,0:T(8,128)}, f32[2,16,4096]{2,1,0:T(8,128)S(1)}, f32[16,128]{1,0:T(8,128)}) custom-call(s32[1,2]{1,0:T(1,128)S(1)} %broadcast_clamp_fusion.base, f32[1,128]{1,0:T(1,128)S(1)} %get-tuple-element.58.totals, bf16[34,32,128]{2,1,0:T(8,128)(2,1)S(1)} %get-tuple-element.40.clean, ...), custom_call_target="tpu_custom_call" | custom-call | bytes 12582912 | tf_op jit(solution)/shard_map/pressure/pallas_call | solution.py:605
  36.2 3.5 %all-to-all-start.1 = ((f32[16,1,128]{2,1,0:T(1,128)}), f32[16,1,128]{2,1,0:T(1,128)S(1)}, u32[]{:S(2)}, u32[]{:S(2)}) async-start(f32[16,1,128]{2,1,0:T(1,128)} %bitcast.6), calls=%async_computation.1 | async-start | bytes 16384 | tf_op jit(solution)/shard_map/all_to_all | solution.py:631
  39.6 0.1 slice_convert_fusion.base
  39.7 0.6 %collective-permute-done.5.inverse = f32[2,16,4096]{2,1,0:T(8,128)S(1)} collective-permute-done((f32[2,16,4096]{2,1,0:T(8,128)S(1)}, f32[2,16,4096]{2,1,0:T(8,128)S(1)}, u32[]{:S(2)}, u32[]{:S(2)}) %collective-permute-start.5) | collective-permute-done | bytes 524320 | tf_op jit(solution)/shard_map/ppermute | solution.py:486
  40.3 3.1 %time.1 = (f32[16,4096]{1,0:T(8,128)}, f32[16,4096]{1,0:T(8,128)}) custom-call(s32[1,2]{1,0:T(1,128)S(1)} %slice_convert_fusion.base, f32[1,128]{1,0:T(1,128)S(1)} %get-tuple-element.57.totals, bf16[34,32,128]{2,1,0:T(8,128)(2,1)S(1)} %get-tuple-element.40.clean, bf16[34,16,128]{2,1,0:T(8,128)(2,1)S(1)} %get-tuple-element.41.other, ...), custom_call_target="tpu_custom_call" | custom-call | bytes 12582912 | tf_op jit(solution)/shard_map/time/pallas_call | solution.py:616
  43.5 2.5 %all-to-all-done.1 = f32[16,1,128]{2,1,0:T(1,128)S(1)} async-done(((f32[16,1,128]{2,1,0:T(1,128)}), f32[16,1,128]{2,1,0:T(1,128)S(1)}, u32[]{:S(2)}, u32[]{:S(2)}) %all-to-all-start.1) | async-done | bytes 8224 | tf_op jit(solution)/shard_map/all_to_all | solution.py:631
  46.0 0.6 %subtract_sqrt_fusion = (f32[2]{0:T(128)}, f32[2]{0:T(128)}) fusion(f32[128]{0:T(128)S(1)} %reduce_sum.19), kind=kLoop, calls=%fused_computation.10 | loop fusion | flops 8 | bytes 32 | tf_op jit(solution)/shard_map/sqrt | solution.py:636
  (10 shorter events, 0.1 us)
Async XLA Ops:
  0.6 10.4 %copy-start = (s32[1,2]{1,0:T(1,128)S(1)}, s32[1,2]{1,0:T(1,128)}, u32[]{:S(2)}) copy-start(s32[1,2]{1,0:T(1,128)} %param.7) | copy-start | bytes 28
  0.6 9.5 %collective-permute-start.1 = (f32[16,4096]{1,0:T(8,128)}, f32[16,4096]{1,0:T(8,128)S(1)}, u32[]{:S(2)}, u32[]{:S(2)}) collective-permute-start(f32[16,4096]{1,0:T(8,128)} %bitcast.14), channel_id=1, source_target_pairs={{0,1},{1,0},{2,3},{3,2},{4,5},{5,4},{6,7},{7,6},{8,9},{9,8},{10,11... | collective-permute-start | bytes 786440 | tf_op jit(solution)/shard_map/ppermute | solution.py:486
  5.8 5.2 %collective-permute-start = (f32[2,4,4096]{2,1,0:T(4,128)S(1)}, f32[2,4,4096]{2,1,0:T(4,128)S(1)}, u32[]{:S(2)}, u32[]{:S(2)}) collective-permute-start(f32[2,4,4096]{2,1,0:T(4,128)S(1)} %get-tuple-element.54), channel_id=1, source_target_pairs={{0,0},{2,4},{4,2},{6,8},{8,6},{10,12},{12,10},{14,16},{16,14},{18,... | collective-permute-start | bytes 393224 | tf_op jit(solution)/shard_map/ppermute | solution.py:486
  6.5 4.5 %collective-permute-start.4 = (f32[2,4,4096]{2,1,0:T(4,128)S(1)}, f32[2,4,4096]{2,1,0:T(4,128)S(1)}, u32[]{:S(2)}, u32[]{:S(2)}) collective-permute-start(f32[2,4,4096]{2,1,0:T(4,128)S(1)} %get-tuple-element.53), channel_id=1, source_target_pairs={{0,2},{2,0},{4,6},{6,4},{8,10},{10,8},{12,14},{14,12},{16,18},{18,... | collective-permute-start | bytes 393224 | tf_op jit(solution)/shard_map/ppermute | solution.py:486
  10.2 2.0 %collective-permute-start.3 = (f32[8,4096]{1,0:T(8,128)S(1)}, f32[8,4096]{1,0:T(8,128)S(1)}, u32[]{:S(2)}, u32[]{:S(2)}) collective-permute-start(f32[8,4096]{1,0:T(8,128)S(1)} %get-tuple-element.55.own_even), channel_id=1, source_target_pairs={{0,2},{2,0},{4,6},{6,4},{8,10},{10,8},{12,14},{14,12},{16,18},{18,... | collective-permute-start | bytes 393224 | tf_op jit(solution)/shard_map/ppermute | solution.py:486
  10.3 4.0 %collective-permute-start.2 = (f32[8,4096]{1,0:T(8,128)S(1)}, f32[8,4096]{1,0:T(8,128)S(1)}, u32[]{:S(2)}, u32[]{:S(2)}) collective-permute-start(f32[8,4096]{1,0:T(8,128)S(1)} %get-tuple-element.32.own_odd), channel_id=1, source_target_pairs={{0,0},{2,4},{4,2},{6,8},{8,6},{10,12},{12,10},{14,16},{16,14},{18,... | collective-permute-start | bytes 393224 | tf_op jit(solution)/shard_map/ppermute | solution.py:486
  17.1 16.0 %all-to-all-start = ((f32[32,1,128]{2,1,0:T(1,128)}), f32[32,1,128]{2,1,0:T(1,128)S(1)}, u32[]{:S(2)}, u32[]{:S(2)}) async-start(f32[32,1,128]{2,1,0:T(1,128)} %bitcast.3), calls=%async_computation | async-start | bytes 32768 | tf_op jit(solution)/shard_map/all_to_all | solution.py:595
  26.0 14.3 %collective-permute-start.5 = (f32[2,16,4096]{2,1,0:T(8,128)S(1)}, f32[2,16,4096]{2,1,0:T(8,128)S(1)}, u32[]{:S(2)}, u32[]{:S(2)}) collective-permute-start(f32[2,16,4096]{2,1,0:T(8,128)S(1)} %get-tuple-element.42.inverse), channel_id=1, source_target_pairs={{0,1},{1,0},{2,3},{3,2},{4,5},{5,4},{6,7},{7,6},{8,9},{9,8},{10,11... | collective-permute-start | bytes 1572872 | tf_op jit(solution)/shard_map/ppermute | solution.py:486
  36.2 9.8 %all-to-all-start.1 = ((f32[16,1,128]{2,1,0:T(1,128)}), f32[16,1,128]{2,1,0:T(1,128)S(1)}, u32[]{:S(2)}, u32[]{:S(2)}) async-start(f32[16,1,128]{2,1,0:T(1,128)} %bitcast.6), calls=%async_computation.1 | async-start | bytes 16384 | tf_op jit(solution)/shard_map/all_to_all | solution.py:631

commit v18 on v17

--- a/solution.py
+++ b/solution.py
@@ -353,20 +353,23 @@
     part[...] = jnp.broadcast_to(packed, part.shape)
 
 
-def spreader(clean, other, spread, base_col):
-    height = clean.shape[1]
-    size = height + other.shape[1]
-    spare = spread.shape[0] - reach * size
+def spreader(clean, spread, base_col):
+    size = clean.shape[1]
     shifts = [column_shift(base_col + j - 3) for j in range(reach)]
 
     def spread_tile(t):
         at = tile_of(t)
         for j, shift in enumerate(shifts):
-            spread[j * size : j * size + height, at] = shift(clean, t)
-            spread[j * size + height : (j + 1) * size, at] = shift(other, t)
-        spread[reach * size :, at] = jnp.zeros((spare, lanes), jnp.bfloat16)
+            spread[j * size : (j + 1) * size, at] = shift(clean, t)
+        spread[reach * size :, at] = jnp.zeros((spread.shape[0] - reach * size, lanes), jnp.bfloat16)
 
     return spread_tile
+
+
+def shift_kernel(base, clean, spread):
+    spread_tile = spreader(clean, spread, base[0, 1])
+    for t in range(clean.shape[0] - 2):
+        spread_tile(t)
 
 
 def blend_weights(totals, count):
@@ -388,40 +391,45 @@
     return weights
 
 
-def banded(weights, f, rows, first_row, depth):
-    wide = rows + 8
+def banded(weights, f, rows, first_row):
+    depth = 8 * slot
     blank = jnp.zeros((weights.shape[0], depth - lanes), jnp.float32)
     weights = jnp.concatenate([weights, blank], axis=1)
     lane = lane_of(weights.shape)
     line = jnp.zeros_like(weights)
     for j in range(reach):
-        at = first_row + j * 2 * wide
-        amount = at - (f * reach + j) * reach
-        amount = jnp.where(amount < 0, amount + depth, amount)
+        at = first_row + j * slot
+        amount = (at + depth - (f * reach + j) * reach) & (depth - 1)
         line = jnp.where((lane >= at) & (lane < at + reach), pltpu.roll(weights, amount, 1), line)
     band = by_row_shift(jnp.broadcast_to(line[0:1], (rows, depth)), rows, 1)
     odd = lax.axis_index("rows") % 2 == 1
-    row = lane_of(band.shape) % (2 * wide)
+    lane = lane_of(band.shape)
+    row = lane & (slot - 1)
     start = jnp.where(odd, 0, 8)
     inner = (row >= start) & (row < start + rows)
-    first = pltpu.roll(jnp.where(inner, band, 0.0), jnp.where(odd, 0, depth - 8), 1)
-    second = pltpu.roll(jnp.where(inner, 0.0, band), jnp.where(odd, 2 * rows - 16, 2 * rows), 1)
-    return first + pltpu.roll(first, rows, 1) + second + pltpu.roll(second, 8, 1)
-
-
-def pressures(base, totals, clean, other, spread, inverse):
+    first = pltpu.roll(jnp.where(inner, band, 0.0), (depth - start) & (depth - 1), 1)
+    outer = jnp.where(inner, 0.0, band)
+    start = jnp.where(odd, 16, 0)
+    second = jnp.zeros_like(band)
+    for j in range(reach):
+        turned = pltpu.roll(outer, (depth - start - j * 16) & (depth - 1), 1)
+        second = jnp.where((lane >= j * 16) & (lane < j * 16 + 8), turned, second)
+    second = second[:, :lanes]
+    return first + pltpu.roll(first, rows, 1), second + pltpu.roll(second, 8, 1)
+
+
+def pressures(base, totals, first, second, inverse, prepare):
     count, rows, columns = inverse.shape
-    depth = spread.shape[0]
     weights = blend_weights(jnp.broadcast_to(totals[0:1, :], (8, lanes)), count)
-    bands = [banded(weights[f], f, rows, 1 + base[0, 0], depth) for f in range(count)]
-    mixing = cut(jnp.concatenate(bands, axis=0))
-    spread_tile = spreader(clean, other, spread, base[0, 1])
+    bands = [banded(weights[f], f, rows, 1 + base[0, 0]) for f in range(count)]
+    inner, outer = [cut(jnp.concatenate(parts, axis=0)) for parts in zip(*bands)]
 
     def chunk_values(t):
         where = chunk_of(t)
-        spread_tile(2 * t)
-        spread_tile(2 * t + 1)
-        product = jnp.dot(mixing, spread[:, where], preferred_element_type=jnp.float32)
+        prepare(2 * t)
+        prepare(2 * t + 1)
+        product = jnp.dot(inner, first[:, where], preferred_element_type=jnp.float32)
+        product = product + jnp.dot(outer, second[:, where], preferred_element_type=jnp.float32)
         registered = product[: count * rows] + product[count * rows :]
         values = []
         for f in range(count):
@@ -432,9 +440,9 @@
     return chunk_values
 
 
-def pressure_kernel(base, totals, clean, other, inverse, pressure, moments, part, spread):
+def pressure_kernel(base, totals, first, other, inverse, pressure, moments, part, second):
     count, rows, columns = inverse.shape
-    chunk_values = pressures(base, totals, clean, other, spread, inverse)
+    chunk_values = pressures(base, totals, first, second, inverse, spreader(other, second, base[0, 1]))
 
     def step(t, sums):
         where = chunk_of(t)
@@ -458,21 +466,27 @@
     part[...] = jnp.broadcast_to(line[0:1], part.shape)
 
 
-def time_kernel(base, totals, clean, other, inverse, moments, time_mean, time_rms, spread):
+def time_kernel(base, totals, clean, other, inverse, moments, time_mean, time_rms, first, second):
     count, rows, columns = inverse.shape
-    chunk_values = pressures(base, totals, clean, other, spread, inverse)
+    steps = [spreader(clean, first, base[0, 1]), spreader(other, second, base[0, 1])]
+
+    def prepare(t):
+        for step in steps:
+            step(t)
+
+    chunk_values = pressures(base, totals, first, second, inverse, prepare)
     frames = 2 * count
 
     def step(t, carry):
         where = chunk_of(t)
-        first = moments[0, :, where]
-        second = moments[1, :, where]
+        total = moments[0, :, where]
+        squares = moments[1, :, where]
         for value in chunk_values(t):
-            first = first + value
-            second = second + value * value
-        mean = first * (1.0 / frames)
+            total = total + value
+            squares = squares + value * value
+        mean = total * (1.0 / frames)
         time_mean[:, where] = mean
-        time_rms[:, where] = jnp.sqrt(jnp.maximum(second * (1.0 / frames) - mean * mean, 0.0))
+        time_rms[:, where] = jnp.sqrt(jnp.maximum(squares * (1.0 / frames) - mean * mean, 0.0))
         return carry
 
     by_tiles(step, columns // (2 * lanes), columns // (2 * lanes))
@@ -600,25 +614,33 @@
         place = jnp.where(mine, parts[0, 1:2], parts[0, 0:1])[:, lanes - 2 :].astype(jnp.int32)
     else:
         totals = jnp.sum(lax.all_to_all(part, "rows", 0, 0, tiled=True), axis=0, keepdims=True)
-    depth = -(-reach * 2 * wide // lanes) * lanes
-    spread = pltpu.VMEM((depth, columns), bf16)
+    spreads = [(8 * 2 * rows, columns), (8 * 16, columns)]
+    first = pl.pallas_call(
+        shift_kernel,
+        out_shape=jax.ShapeDtypeStruct(spreads[0], bf16),
+        in_specs=[smem, vmem],
+        out_specs=vmem,
+        compiler_params=params,
+        cost_estimate=cost(3),
+        name="shift",
+    )(offsets, clean)
     pressure, moments, part = pl.pallas_call(
         pressure_kernel,
         out_shape=(struct((count, rows, columns)), struct((2, rows, columns)), struct((size, lanes))),
         in_specs=[smem] + [vmem] * 4,
         out_specs=(vmem, vmem, vmem),
-        scratch_shapes=[spread],
+        scratch_shapes=[pltpu.VMEM(spreads[1], bf16)],
         compiler_params=params,
         cost_estimate=cost(12),
         name="pressure",
-    )(offsets, totals, clean, other, inverse)
+    )(offsets, totals, first, other, inverse)
     if blocks == 2:
         time_mean, time_rms = pl.pallas_call(
             time_kernel,
             out_shape=(struct((rows, columns)), struct((rows, columns))),
             in_specs=[smem] + [vmem] * 5,
             out_specs=(vmem, vmem),
-            scratch_shapes=[spread],
+            scratch_shapes=[pltpu.VMEM(shape, bf16) for shape in spreads],
             compiler_params=params,
             cost_estimate=cost(12),
             name="time",

time: 46.9 us -> 47.2 us (level)
  waiting for transfers between devices: 8.57 us -> 6.03 us
  local copies, waits for them, and re-layouts: 0.01 us -> 1.85 us
  Pallas kernels: 12.2 us -> 13.4 us
    all_to_all x1, starting transfers between devices: 8.87 us -> 5.58 us  [shards(): lax.all_to_all(part, ('rows', 'frames'), 0, 0, tiled=True)]
    ppermute x6, starting transfers between devices: 9.19 us -> 12.2 us  [paired(): return lax.ppermute(value, axis, list(enumerate(partner)))]
    unnamed x2 -> x6, local copies, waits for them, and re-layouts: 0.01 us -> 1.85 us
    all_to_all x1, waiting for transfers between devices: 5.29 us -> 4.16 us  [shards(): lax.all_to_all(part, ('rows', 'frames'), 0, 0, tiled=True)]
    pallas_call x0 -> x1, Pallas kernels: none -> 1.12 us  [shards(): pl.pallas_call(shift_kernel, out_shape=jax.ShapeDtypeStruct(spreads[0], b...]
    all_to_all x1, waiting for transfers between devices: 2.55 us -> 1.54 us  [shards(): sums = lax.all_to_all(part, 'rows', 0, 0, tiled=True)]
  transfers between devices with their start and end apart: 8 -> 8, of which waited for: 4 -> 4; matrix products, arithmetic and copies ran while one was open for 5% -> 5% of each run, Pallas kernels for 20% -> 23%
where the time goes in v18:
time: 47.2 us; the launch traced here: 46.9 us
  starting transfers between devices  21.3 us (45%)
  Pallas kernels  13.4 us (28%)
  waiting for transfers between devices  6.03 us (13%)
  other arithmetic  2.89 us (6%)
  local copies, waits for them, and re-layouts  1.85 us (4%)
  between operations  1.44 us (3%)
    ppermute x6, starting transfers between devices, paired(): return lax.ppermute(value, axis, list(enumerate(partner)))  12.2 us
    all_to_all x1, starting transfers between devices, shards(): lax.all_to_all(part, ('rows', 'frames'), 0, 0, tiled=True)  5.58 us
    all_to_all x1, waiting for transfers between devices, shards(): lax.all_to_all(part, ('rows', 'frames'), 0, 0, tiled=True)  4.16 us
    pallas_call x1, Pallas kernels, shards(): pl.pallas_call(time_kernel, out_shape=(struct((rows, columns)), struct((r...  3.48 us
    all_to_all x1, starting transfers between devices, shards(): sums = lax.all_to_all(part, 'rows', 0, 0, tiled=True)  3.42 us
    pallas_call x1, Pallas kernels, shards(): pl.pallas_call(match_kernel, out_shape=(jax.ShapeDtypeStruct((tiles + 2,...  2.77 us
    pallas_call x1, Pallas kernels, shards(): pl.pallas_call(pressure_kernel, out_shape=(struct((count, rows, columns))...  2.73 us
    pallas_call x1, Pallas kernels, shards(): pl.pallas_call(near_kernel, out_shape=(jax.ShapeDtypeStruct((tiles + 2, 2...  2.13 us
  transfers between devices with their start and end apart: 8, of which 4 were waited for; matrix products, arithmetic and copies ran while one was open for 5% of the time, Pallas kernels for 23%

profile of v18, /device:TPU:0, one launch (start us, length us, event | category | flops | bytes accessed | tf_op | source)
XLA Modules:
  0.0 46.9 jit_solution(4181118929025168435)
XLA Ops:
  0.6 3.0 %collective-permute-start.1 = (f32[16,4096]{1,0:T(8,128)}, f32[16,4096]{1,0:T(8,128)S(1)}, u32[]{:S(2)}, u32[]{:S(2)}) collective-permute-start(f32[16,4096]{1,0:T(8,128)} %bitcast.14), channel_id=1, source_target_pairs={{0,1},{1,0},{2,3},{3,2},{4,5},{5,4},{6,7},{7,6},{8,9},{9,8},{10,11... | collective-permute-start | bytes 786440 | tf_op jit(solution)/shard_map/ppermute | solution.py:500
  3.7 1.0 %broadcast_maximum_fusion.1 = f32[16,4096]{1,0:T(8,128)S(1)} fusion(f32[1,16,4096]{2,1,0:T(8,128)} %param.5), kind=kLoop, calls=%fused_computation.3 | loop fusion | flops 65536 | bytes 524288 | tf_op jit(solution)/shard_map/max | solution.py:543
  4.7 1.1 %broadcast_maximum_fusion.frames = f32[2,16,4096]{2,1,0:T(8,128)S(1)} fusion(f32[2,16,4096]{2,1,0:T(8,128)} %param.4), kind=kLoop, calls=%fused_computation | loop fusion | flops 131072 | bytes 1048576 | tf_op jit(solution)/shard_map/max | solution.py:543
  5.8 0.7 %collective-permute-start = (f32[2,4,4096]{2,1,0:T(4,128)S(1)}, f32[2,4,4096]{2,1,0:T(4,128)S(1)}, u32[]{:S(2)}, u32[]{:S(2)}) collective-permute-start(f32[2,4,4096]{2,1,0:T(4,128)S(1)} %get-tuple-element.54), channel_id=1, source_target_pairs={{0,0},{2,4},{4,2},{6,8},{8,6},{10,12},{12,10},{14,16},{16,14},{18,... | collective-permute-start | bytes 393224 | tf_op jit(solution)/shard_map/ppermute | solution.py:500
  6.5 2.9 %collective-permute-start.4 = (f32[2,4,4096]{2,1,0:T(4,128)S(1)}, f32[2,4,4096]{2,1,0:T(4,128)S(1)}, u32[]{:S(2)}, u32[]{:S(2)}) collective-permute-start(f32[2,4,4096]{2,1,0:T(4,128)S(1)} %get-tuple-element.53), channel_id=1, source_target_pairs={{0,2},{2,0},{4,6},{6,4},{8,10},{10,8},{12,14},{14,12},{16,18},{18,... | collective-permute-start | bytes 393224 | tf_op jit(solution)/shard_map/ppermute | solution.py:500
  10.1 0.1 collective-permute-done.1
  10.2 0.7 %collective-permute-start.2 = (f32[8,4096]{1,0:T(8,128)S(1)}, f32[8,4096]{1,0:T(8,128)S(1)}, u32[]{:S(2)}, u32[]{:S(2)}) collective-permute-start(f32[8,4096]{1,0:T(8,128)S(1)} %get-tuple-element.32.own_odd), channel_id=1, source_target_pairs={{0,0},{2,4},{4,2},{6,8},{8,6},{10,12},{12,10},{14,16},{16,14},{18,... | collective-permute-start | bytes 393224 | tf_op jit(solution)/shard_map/ppermute | solution.py:500
  10.9 3.1 %collective-permute-start.3 = (f32[8,4096]{1,0:T(8,128)S(1)}, f32[8,4096]{1,0:T(8,128)S(1)}, u32[]{:S(2)}, u32[]{:S(2)}) collective-permute-start(f32[8,4096]{1,0:T(8,128)S(1)} %get-tuple-element.55.own_even), channel_id=1, source_target_pairs={{0,2},{2,0},{4,6},{6,4},{8,10},{10,8},{12,14},{14,12},{16,18},{18,... | collective-permute-start | bytes 393224 | tf_op jit(solution)/shard_map/ppermute | solution.py:500
  14.1 1.2 %smooth.1 = (f32[2,16,4096]{2,1,0:T(8,128)S(1)}, bf16[256,4352]{1,0:T(8,128)(2,1)S(1)}, f32[16,128]{1,0:T(8,128)S(1)}, bf16[512,256]{1,0:T(8,128)(2,1)S(1)}) custom-call(f32[2,16,4096]{2,1,0:T(8,128)S(1)} %broadcast_maximum_fusion.frames, f32[2,4,4096]{2,1,0:T(4,128)S(1)} %collective-permute-done.from_odd, f32[2,4,4096]{2,1,0:T(4,128)S(1)} %collective-permute-done.4.from_even), custom_call_target="tpu_custom_call" | custom-call | bytes 8388608 | tf_op jit(solution)/shard_map/smooth/pallas_call | solution.py:552
  15.2 2.1 %near.1 = (bf16[34,32,128]{2,1,0:T(8,128)(2,1)S(1)}, f32[128,128]{1,0:T(8,128)S(1)}, f32[8,128]{1,0:T(8,128)S(1)}) custom-call(s32[1,2]{1,0:T(1,128)S(1)} %broadcast_clamp_fusion.base, f32[8,4096]{1,0:T(8,128)S(1)} %get-tuple-element.32.own_odd, f32[8,4096]{1,0:T(8,128)S(1)} %get-tuple-element.55.own_even, f32[8,4096]{1,0:T(8,128)S(1)} %collective-permute-done.3.from_even, ...), custom_call_target="tpu_custom_call" | custom-call | bytes 8388608 | tf_op jit(solution)/shard_map/near/pallas_call | solution.py:584
  17.4 2.8 %match.1 = (bf16[34,16,128]{2,1,0:T(8,128)(2,1)S(1)}, f32[32,128]{1,0:T(8,128)}) custom-call(s32[1,2]{1,0:T(1,128)S(1)} %broadcast_clamp_fusion.base, f32[8,4096]{1,0:T(8,128)S(1)} %get-tuple-element.32.own_odd, f32[8,4096]{1,0:T(8,128)S(1)} %collective-permute-done.2.from_odd, f32[128,128]{1,0:T(8,128)S(1)} %get-tuple-element.36.near_lags, ...), custom_call_target="tpu_custom_call" | custom-call | bytes 8388608 | tf_op jit(solution)/shard_map/match/pallas_call | solution.py:598
  20.2 5.6 %all-to-all-start = ((f32[32,1,128]{2,1,0:T(1,128)}), f32[32,1,128]{2,1,0:T(1,128)S(1)}, u32[]{:S(2)}, u32[]{:S(2)}) async-start(f32[32,1,128]{2,1,0:T(1,128)} %bitcast.3), calls=%async_computation | async-start | bytes 32768 | tf_op jit(solution)/shard_map/all_to_all | solution.py:609
  25.8 1.8 %collective-permute-start.5 = (f32[2,16,4096]{2,1,0:T(8,128)S(1)}, f32[2,16,4096]{2,1,0:T(8,128)}, u32[]{:S(2)}, u32[]{:S(2)}) collective-permute-start(f32[2,16,4096]{2,1,0:T(8,128)S(1)} %get-tuple-element.42.inverse), channel_id=1, source_target_pairs={{0,1},{1,0},{2,3},{3,2},{4,5},{5,4},{6,7},{7,6},{8,9},{9,8},{10,11... | collective-permute-start | bytes 1572872 | tf_op jit(solution)/shard_map/ppermute | solution.py:500
  27.6 1.1 %shift.1.first = bf16[256,4096]{1,0:T(8,128)(2,1)S(1)} custom-call(s32[1,2]{1,0:T(1,128)S(1)} %broadcast_clamp_fusion.base, bf16[34,32,128]{2,1,0:T(8,128)(2,1)S(1)} %get-tuple-element.40.clean), custom_call_target="tpu_custom_call" | custom-call | bytes 3145728 | tf_op jit(solution)/shard_map/shift/pallas_call | solution.py:618
  28.7 4.2 %all-to-all-done = f32[32,1,128]{2,1,0:T(1,128)S(1)} async-done(((f32[32,1,128]{2,1,0:T(1,128)}), f32[32,1,128]{2,1,0:T(1,128)S(1)}, u32[]{:S(2)}, u32[]{:S(2)}) %all-to-all-start) | async-done | bytes 16416 | tf_op jit(solution)/shard_map/all_to_all | solution.py:609
  32.9 2.7 %pressure.1 = (f32[2,16,4096]{2,1,0:T(8,128)}, f32[2,16,4096]{2,1,0:T(8,128)S(1)}, f32[16,128]{1,0:T(8,128)}) custom-call(s32[1,2]{1,0:T(1,128)S(1)} %broadcast_clamp_fusion.base, f32[1,128]{1,0:T(1,128)S(1)} %get-tuple-element.58.totals, bf16[256,4096]{1,0:T(8,128)(2,1)S(1)} %shift.1.first, bf16[34,16,128]{2,1,0:T(8,128)(2,1)S(1)} %get-tuple-element.41.other, ...), custom_call_target="tpu_custom_call" | custom-call | bytes 12582912 | tf_op jit(solution)/shard_map/pressure/pallas_call | solution.py:627
  35.6 0.8 %copy-done = f32[2,16,4096]{2,1,0:T(8,128)} copy-done((f32[2,16,4096]{2,1,0:T(8,128)}, f32[2,16,4096]{2,1,0:T(8,128)S(1)}, u32[]{:S(2)}) %copy-start) | copy-done | bytes 524312
  36.4 3.4 %all-to-all-start.1 = ((f32[16,1,128]{2,1,0:T(1,128)}), f32[16,1,128]{2,1,0:T(1,128)S(1)}, u32[]{:S(2)}, u32[]{:S(2)}) async-start(f32[16,1,128]{2,1,0:T(1,128)} %bitcast.6), calls=%async_computation.1 | async-start | bytes 16384 | tf_op jit(solution)/shard_map/all_to_all | solution.py:653
  39.9 0.1 slice_convert_fusion.base
  40.0 0.2 collective-permute-done.5.inverse
  40.2 1.0 %copy-done.1 = f32[2,16,4096]{2,1,0:T(8,128)S(1)} copy-done((f32[2,16,4096]{2,1,0:T(8,128)S(1)}, f32[2,16,4096]{2,1,0:T(8,128)}, u32[]{:S(2)}) %copy-start.1) | copy-done | bytes 524312
  41.2 3.5 %time.1 = (f32[16,4096]{1,0:T(8,128)}, f32[16,4096]{1,0:T(8,128)}) custom-call(s32[1,2]{1,0:T(1,128)S(1)} %slice_convert_fusion.base, f32[1,128]{1,0:T(1,128)S(1)} %get-tuple-element.57.totals, bf16[34,32,128]{2,1,0:T(8,128)(2,1)S(1)} %get-tuple-element.40.clean, bf16[34,16,128]{2,1,0:T(8,128)(2,1)S(1)} %get-tuple-element.41.other, ...), custom_call_target="tpu_custom_call" | custom-call | bytes 12582912 | tf_op jit(solution)/shard_map/time/pallas_call | solution.py:638
  44.7 1.5 %all-to-all-done.1 = f32[16,1,128]{2,1,0:T(1,128)S(1)} async-done(((f32[16,1,128]{2,1,0:T(1,128)}), f32[16,1,128]{2,1,0:T(1,128)S(1)}, u32[]{:S(2)}, u32[]{:S(2)}) %all-to-all-start.1) | async-done | bytes 8224 | tf_op jit(solution)/shard_map/all_to_all | solution.py:653
  46.3 0.6 %subtract_sqrt_fusion = (f32[2]{0:T(128)}, f32[2]{0:T(128)}) fusion(f32[128]{0:T(128)S(1)} %reduce_sum.19), kind=kLoop, calls=%fused_computation.10 | loop fusion | flops 8 | bytes 32 | tf_op jit(solution)/shard_map/sqrt | solution.py:658
  (15 shorter events, 0.2 us)
Async XLA Ops:
  0.6 13.4 %copy-start.2 = (s32[1,2]{1,0:T(1,128)S(1)}, s32[1,2]{1,0:T(1,128)}, u32[]{:S(2)}) copy-start(s32[1,2]{1,0:T(1,128)} %param.7) | copy-start | bytes 28
  0.6 9.5 %collective-permute-start.1 = (f32[16,4096]{1,0:T(8,128)}, f32[16,4096]{1,0:T(8,128)S(1)}, u32[]{:S(2)}, u32[]{:S(2)}) collective-permute-start(f32[16,4096]{1,0:T(8,128)} %bitcast.14), channel_id=1, source_target_pairs={{0,1},{1,0},{2,3},{3,2},{4,5},{5,4},{6,7},{7,6},{8,9},{9,8},{10,11... | collective-permute-start | bytes 786440 | tf_op jit(solution)/shard_map/ppermute | solution.py:500
  5.8 8.2 %collective-permute-start = (f32[2,4,4096]{2,1,0:T(4,128)S(1)}, f32[2,4,4096]{2,1,0:T(4,128)S(1)}, u32[]{:S(2)}, u32[]{:S(2)}) collective-permute-start(f32[2,4,4096]{2,1,0:T(4,128)S(1)} %get-tuple-element.54), channel_id=1, source_target_pairs={{0,0},{2,4},{4,2},{6,8},{8,6},{10,12},{12,10},{14,16},{16,14},{18,... | collective-permute-start | bytes 393224 | tf_op jit(solution)/shard_map/ppermute | solution.py:500
  6.5 7.5 %collective-permute-start.4 = (f32[2,4,4096]{2,1,0:T(4,128)S(1)}, f32[2,4,4096]{2,1,0:T(4,128)S(1)}, u32[]{:S(2)}, u32[]{:S(2)}) collective-permute-start(f32[2,4,4096]{2,1,0:T(4,128)S(1)} %get-tuple-element.53), channel_id=1, source_target_pairs={{0,2},{2,0},{4,6},{6,4},{8,10},{10,8},{12,14},{14,12},{16,18},{18,... | collective-permute-start | bytes 393224 | tf_op jit(solution)/shard_map/ppermute | solution.py:500
  10.2 7.2 %collective-permute-start.2 = (f32[8,4096]{1,0:T(8,128)S(1)}, f32[8,4096]{1,0:T(8,128)S(1)}, u32[]{:S(2)}, u32[]{:S(2)}) collective-permute-start(f32[8,4096]{1,0:T(8,128)S(1)} %get-tuple-element.32.own_odd), channel_id=1, source_target_pairs={{0,0},{2,4},{4,2},{6,8},{8,6},{10,12},{12,10},{14,16},{16,14},{18,... | collective-permute-start | bytes 393224 | tf_op jit(solution)/shard_map/ppermute | solution.py:500
  10.9 4.3 %collective-permute-start.3 = (f32[8,4096]{1,0:T(8,128)S(1)}, f32[8,4096]{1,0:T(8,128)S(1)}, u32[]{:S(2)}, u32[]{:S(2)}) collective-permute-start(f32[8,4096]{1,0:T(8,128)S(1)} %get-tuple-element.55.own_even), channel_id=1, source_target_pairs={{0,2},{2,0},{4,6},{6,4},{8,10},{10,8},{12,14},{14,12},{16,18},{18,... | collective-permute-start | bytes 393224 | tf_op jit(solution)/shard_map/ppermute | solution.py:500
  20.2 12.7 %all-to-all-start = ((f32[32,1,128]{2,1,0:T(1,128)}), f32[32,1,128]{2,1,0:T(1,128)S(1)}, u32[]{:S(2)}, u32[]{:S(2)}) async-start(f32[32,1,128]{2,1,0:T(1,128)} %bitcast.3), calls=%async_computation | async-start | bytes 32768 | tf_op jit(solution)/shard_map/all_to_all | solution.py:609
  25.8 14.4 %collective-permute-start.5 = (f32[2,16,4096]{2,1,0:T(8,128)S(1)}, f32[2,16,4096]{2,1,0:T(8,128)}, u32[]{:S(2)}, u32[]{:S(2)}) collective-permute-start(f32[2,16,4096]{2,1,0:T(8,128)S(1)} %get-tuple-element.42.inverse), channel_id=1, source_target_pairs={{0,1},{1,0},{2,3},{3,2},{4,5},{5,4},{6,7},{7,6},{8,9},{9,8},{10,11... | collective-permute-start | bytes 1572872 | tf_op jit(solution)/shard_map/ppermute | solution.py:500
  35.6 0.8 %copy-start = (f32[2,16,4096]{2,1,0:T(8,128)}, f32[2,16,4096]{2,1,0:T(8,128)S(1)}, u32[]{:S(2)}) copy-start(f32[2,16,4096]{2,1,0:T(8,128)S(1)} %get-tuple-element.45.moments) | copy-start | bytes 1572868
  36.4 9.8 %all-to-all-start.1 = ((f32[16,1,128]{2,1,0:T(1,128)}), f32[16,1,128]{2,1,0:T(1,128)S(1)}, u32[]{:S(2)}, u32[]{:S(2)}) async-start(f32[16,1,128]{2,1,0:T(1,128)} %bitcast.6), calls=%async_computation.1 | async-start | bytes 16384 | tf_op jit(solution)/shard_map/all_to_all | solution.py:653
  40.2 1.0 %copy-start.1 = (f32[2,16,4096]{2,1,0:T(8,128)S(1)}, f32[2,16,4096]{2,1,0:T(8,128)}, u32[]{:S(2)}) copy-start(f32[2,16,4096]{2,1,0:T(8,128)} %copy-done) | copy-start | bytes 1572868

commit v19 on v17

--- a/solution.py
+++ b/solution.py
@@ -369,26 +369,23 @@
     return spread_tile
 
 
-def blend_weights(totals, count):
+def blend_terms(totals, count):
     lane = lane_of(totals.shape)
     block = reach * reach
-
-    def pick(index):
-        return jnp.sum(jnp.where(lane == index, totals, 0.0), axis=1, keepdims=True)
-
-    ref_power = pick(count * block + count)
-    weights = []
+    squared = totals * totals
+
+    def pick(array, low, size):
+        return jnp.sum(jnp.where((lane >= low) & (lane < low + size), array, 0.0), axis=1, keepdims=True)
+
+    ref_power = pick(totals, count * block + count, 1)
+    terms = []
     for f in range(count):
-        norm_product = jnp.sqrt((pick(count * block + f) + 1e-06) * (ref_power + 1e-06))
-        member = (lane >= f * block) & (lane < (f + 1) * block)
-        rho = jnp.where(member, totals, 0.0) / norm_product
-        squared = rho * rho
-        middle = jnp.where(lane == f * block + block // 2, 0.05, 0.0)
-        weights.append((squared + middle) / (0.05 + jnp.sum(squared, axis=1, keepdims=True)))
-    return weights
-
-
-def banded(weights, f, rows, first_row, depth):
+        norm_product = 0.05 * ((pick(totals, count * block + f, 1) + 1e-06) * (ref_power + 1e-06))
+        terms.append((norm_product, 1.0 / (norm_product + pick(squared, f * block, block))))
+    return squared, terms
+
+
+def banded(weights, terms, f, rows, first_row, depth):
     wide = rows + 8
     blank = jnp.zeros((weights.shape[0], depth - lanes), jnp.float32)
     weights = jnp.concatenate([weights, blank], axis=1)
@@ -400,6 +397,8 @@
         amount = jnp.where(amount < 0, amount + depth, amount)
         line = jnp.where((lane >= at) & (lane < at + reach), pltpu.roll(weights, amount, 1), line)
     band = by_row_shift(jnp.broadcast_to(line[0:1], (rows, depth)), rows, 1)
+    middle = first_row + reach // 2 * (2 * wide + 1) + lax.broadcasted_iota(jnp.int32, band.shape, 0)
+    band = (band + jnp.where(lane_of(band.shape) == middle, terms[0][0:1], 0.0)) * terms[1][0:1]
     odd = lax.axis_index("rows") % 2 == 1
     row = lane_of(band.shape) % (2 * wide)
     start = jnp.where(odd, 0, 8)
@@ -412,8 +411,8 @@
 def pressures(base, totals, clean, other, spread, inverse):
     count, rows, columns = inverse.shape
     depth = spread.shape[0]
-    weights = blend_weights(jnp.broadcast_to(totals[0:1, :], (8, lanes)), count)
-    bands = [banded(weights[f], f, rows, 1 + base[0, 0], depth) for f in range(count)]
+    squared, terms = blend_terms(jnp.broadcast_to(totals[0:1, :], (8, lanes)), count)
+    bands = [banded(squared, terms[f], f, rows, 1 + base[0, 0], depth) for f in range(count)]
     mixing = cut(jnp.concatenate(bands, axis=0))
     spread_tile = spreader(clean, other, spread, base[0, 1])
 

time: 46.9 us -> 46.9 us (level)
  no operation moved by 1% of the time
where the time goes in v19:
time: 46.9 us; the launch traced here: 46.6 us
  starting transfers between devices  21.5 us (46%)
  Pallas kernels  12.1 us (26%)
  waiting for transfers between devices  8.68 us (19%)
  other arithmetic  2.89 us (6%)
  between operations  1.45 us (3%)
    ppermute x6, starting transfers between devices, paired(): return lax.ppermute(value, axis, list(enumerate(partner)))  9.19 us
    all_to_all x1, starting transfers between devices, shards(): lax.all_to_all(part, ('rows', 'frames'), 0, 0, tiled=True)  8.87 us
    all_to_all x1, waiting for transfers between devices, shards(): lax.all_to_all(part, ('rows', 'frames'), 0, 0, tiled=True)  5.29 us
    all_to_all x1, starting transfers between devices, shards(): sums = lax.all_to_all(part, 'rows', 0, 0, tiled=True)  3.45 us
    pallas_call x1, Pallas kernels, shards(): pl.pallas_call(pressure_kernel, out_shape=(struct((count, rows, columns))...  3.02 us
    pallas_call x1, Pallas kernels, shards(): pl.pallas_call(time_kernel, out_shape=(struct((rows, columns)), struct((r...  3.01 us
    pallas_call x1, Pallas kernels, shards(): pl.pallas_call(match_kernel, out_shape=(jax.ShapeDtypeStruct((tiles + 2,...  2.77 us
    all_to_all x1, waiting for transfers between devices, shards(): sums = lax.all_to_all(part, 'rows', 0, 0, tiled=True)  2.69 us
  transfers between devices with their start and end apart: 8, of which 4 were waited for; matrix products, arithmetic and copies ran while one was open for 5% of the time, Pallas kernels for 20%

profile of v19, /device:TPU:0, one launch (start us, length us, event | category | flops | bytes accessed | tf_op | source)
XLA Modules:
  0.0 46.6 jit_solution(1845643442214263974)
XLA Ops:
  0.6 3.0 %collective-permute-start.1 = (f32[16,4096]{1,0:T(8,128)}, f32[16,4096]{1,0:T(8,128)S(1)}, u32[]{:S(2)}, u32[]{:S(2)}) collective-permute-start(f32[16,4096]{1,0:T(8,128)} %bitcast.14), channel_id=1, source_target_pairs={{0,1},{1,0},{2,3},{3,2},{4,5},{5,4},{6,7},{7,6},{8,9},{9,8},{10,11... | collective-permute-start | bytes 786440 | tf_op jit(solution)/shard_map/ppermute | solution.py:485
  3.7 1.0 %broadcast_maximum_fusion.1 = f32[16,4096]{1,0:T(8,128)S(1)} fusion(f32[1,16,4096]{2,1,0:T(8,128)} %param.5), kind=kLoop, calls=%fused_computation.3 | loop fusion | flops 65536 | bytes 524288 | tf_op jit(solution)/shard_map/max | solution.py:528
  4.7 1.1 %broadcast_maximum_fusion.frames = f32[2,16,4096]{2,1,0:T(8,128)S(1)} fusion(f32[2,16,4096]{2,1,0:T(8,128)} %param.4), kind=kLoop, calls=%fused_computation | loop fusion | flops 131072 | bytes 1048576 | tf_op jit(solution)/shard_map/max | solution.py:528
  5.8 0.7 %collective-permute-start = (f32[2,4,4096]{2,1,0:T(4,128)S(1)}, f32[2,4,4096]{2,1,0:T(4,128)S(1)}, u32[]{:S(2)}, u32[]{:S(2)}) collective-permute-start(f32[2,4,4096]{2,1,0:T(4,128)S(1)} %get-tuple-element.54), channel_id=1, source_target_pairs={{0,0},{2,4},{4,2},{6,8},{8,6},{10,12},{12,10},{14,16},{16,14},{18,... | collective-permute-start | bytes 393224 | tf_op jit(solution)/shard_map/ppermute | solution.py:485
  6.5 2.9 %collective-permute-start.4 = (f32[2,4,4096]{2,1,0:T(4,128)S(1)}, f32[2,4,4096]{2,1,0:T(4,128)S(1)}, u32[]{:S(2)}, u32[]{:S(2)}) collective-permute-start(f32[2,4,4096]{2,1,0:T(4,128)S(1)} %get-tuple-element.53), channel_id=1, source_target_pairs={{0,2},{2,0},{4,6},{6,4},{8,10},{10,8},{12,14},{14,12},{16,18},{18,... | collective-permute-start | bytes 393224 | tf_op jit(solution)/shard_map/ppermute | solution.py:485
  10.1 0.1 collective-permute-done.1
  10.2 0.1 collective-permute-start.3
  10.3 0.7 %collective-permute-start.2 = (f32[8,4096]{1,0:T(8,128)S(1)}, f32[8,4096]{1,0:T(8,128)S(1)}, u32[]{:S(2)}, u32[]{:S(2)}) collective-permute-start(f32[8,4096]{1,0:T(8,128)S(1)} %get-tuple-element.32.own_odd), channel_id=1, source_target_pairs={{0,0},{2,4},{4,2},{6,8},{8,6},{10,12},{12,10},{14,16},{16,14},{18,... | collective-permute-start | bytes 393224 | tf_op jit(solution)/shard_map/ppermute | solution.py:485
  11.0 0.0 collective-permute-done.from_odd
  11.0 0.0 collective-permute-done.4.from_even
  11.0 1.2 %smooth.1 = (f32[2,16,4096]{2,1,0:T(8,128)S(1)}, bf16[256,4352]{1,0:T(8,128)(2,1)S(1)}, f32[16,128]{1,0:T(8,128)S(1)}, bf16[512,256]{1,0:T(8,128)(2,1)S(1)}) custom-call(f32[2,16,4096]{2,1,0:T(8,128)S(1)} %broadcast_maximum_fusion.frames, f32[2,4,4096]{2,1,0:T(4,128)S(1)} %collective-permute-done.from_odd, f32[2,4,4096]{2,1,0:T(4,128)S(1)} %collective-permute-done.4.from_even), custom_call_target="tpu_custom_call" | custom-call | bytes 8388608 | tf_op jit(solution)/shard_map/smooth/pallas_call | solution.py:537
  12.2 2.1 %near.1 = (bf16[34,32,128]{2,1,0:T(8,128)(2,1)S(1)}, f32[128,128]{1,0:T(8,128)S(1)}, f32[8,128]{1,0:T(8,128)S(1)}) custom-call(s32[1,2]{1,0:T(1,128)S(1)} %broadcast_clamp_fusion.base, f32[8,4096]{1,0:T(8,128)S(1)} %get-tuple-element.32.own_odd, f32[8,4096]{1,0:T(8,128)S(1)} %get-tuple-element.55.own_even, f32[8,4096]{1,0:T(8,128)S(1)} %collective-permute-done.3.from_even, ...), custom_call_target="tpu_custom_call" | custom-call | bytes 8388608 | tf_op jit(solution)/shard_map/near/pallas_call | solution.py:569
  14.3 0.0 collective-permute-done.2.from_odd
  14.4 2.8 %match.1 = (bf16[34,16,128]{2,1,0:T(8,128)(2,1)S(1)}, f32[32,128]{1,0:T(8,128)}) custom-call(s32[1,2]{1,0:T(1,128)S(1)} %broadcast_clamp_fusion.base, f32[8,4096]{1,0:T(8,128)S(1)} %get-tuple-element.32.own_odd, f32[8,4096]{1,0:T(8,128)S(1)} %collective-permute-done.2.from_odd, f32[128,128]{1,0:T(8,128)S(1)} %get-tuple-element.36.near_lags, ...), custom_call_target="tpu_custom_call" | custom-call | bytes 8388608 | tf_op jit(solution)/shard_map/match/pallas_call | solution.py:583
  17.1 8.9 %all-to-all-start = ((f32[32,1,128]{2,1,0:T(1,128)}), f32[32,1,128]{2,1,0:T(1,128)S(1)}, u32[]{:S(2)}, u32[]{:S(2)}) async-start(f32[32,1,128]{2,1,0:T(1,128)} %bitcast.3), calls=%async_computation | async-start | bytes 32768 | tf_op jit(solution)/shard_map/all_to_all | solution.py:594
  26.0 1.8 %collective-permute-start.5 = (f32[2,16,4096]{2,1,0:T(8,128)S(1)}, f32[2,16,4096]{2,1,0:T(8,128)S(1)}, u32[]{:S(2)}, u32[]{:S(2)}) collective-permute-start(f32[2,16,4096]{2,1,0:T(8,128)S(1)} %get-tuple-element.42.inverse), channel_id=1, source_target_pairs={{0,1},{1,0},{2,3},{3,2},{4,5},{5,4},{6,7},{7,6},{8,9},{9,8},{10,11... | collective-permute-start | bytes 1572872 | tf_op jit(solution)/shard_map/ppermute | solution.py:485
  27.8 5.3 %all-to-all-done = f32[32,1,128]{2,1,0:T(1,128)S(1)} async-done(((f32[32,1,128]{2,1,0:T(1,128)}), f32[32,1,128]{2,1,0:T(1,128)S(1)}, u32[]{:S(2)}, u32[]{:S(2)}) %all-to-all-start) | async-done | bytes 16416 | tf_op jit(solution)/shard_map/all_to_all | solution.py:594
  33.2 3.0 %pressure.1 = (f32[2,16,4096]{2,1,0:T(8,128)}, f32[2,16,4096]{2,1,0:T(8,128)S(1)}, f32[16,128]{1,0:T(8,128)}) custom-call(s32[1,2]{1,0:T(1,128)S(1)} %broadcast_clamp_fusion.base, f32[1,128]{1,0:T(1,128)S(1)} %get-tuple-element.58.totals, bf16[34,32,128]{2,1,0:T(8,128)(2,1)S(1)} %get-tuple-element.40.clean, ...), custom_call_target="tpu_custom_call" | custom-call | bytes 12582912 | tf_op jit(solution)/shard_map/pressure/pallas_call | solution.py:604
  36.2 3.5 %all-to-all-start.1 = ((f32[16,1,128]{2,1,0:T(1,128)}), f32[16,1,128]{2,1,0:T(1,128)S(1)}, u32[]{:S(2)}, u32[]{:S(2)}) async-start(f32[16,1,128]{2,1,0:T(1,128)} %bitcast.6), calls=%async_computation.1 | async-start | bytes 16384 | tf_op jit(solution)/shard_map/all_to_all | solution.py:630
  39.7 0.1 slice_convert_fusion.base
  39.7 0.6 %collective-permute-done.5.inverse = f32[2,16,4096]{2,1,0:T(8,128)S(1)} collective-permute-done((f32[2,16,4096]{2,1,0:T(8,128)S(1)}, f32[2,16,4096]{2,1,0:T(8,128)S(1)}, u32[]{:S(2)}, u32[]{:S(2)}) %collective-permute-start.5) | collective-permute-done | bytes 524320 | tf_op jit(solution)/shard_map/ppermute | solution.py:485
  40.3 3.0 %time.1 = (f32[16,4096]{1,0:T(8,128)}, f32[16,4096]{1,0:T(8,128)}) custom-call(s32[1,2]{1,0:T(1,128)S(1)} %slice_convert_fusion.base, f32[1,128]{1,0:T(1,128)S(1)} %get-tuple-element.57.totals, bf16[34,32,128]{2,1,0:T(8,128)(2,1)S(1)} %get-tuple-element.40.clean, bf16[34,16,128]{2,1,0:T(8,128)(2,1)S(1)} %get-tuple-element.41.other, ...), custom_call_target="tpu_custom_call" | custom-call | bytes 12582912 | tf_op jit(solution)/shard_map/time/pallas_call | solution.py:615
  43.3 2.7 %all-to-all-done.1 = f32[16,1,128]{2,1,0:T(1,128)S(1)} async-done(((f32[16,1,128]{2,1,0:T(1,128)}), f32[16,1,128]{2,1,0:T(1,128)S(1)}, u32[]{:S(2)}, u32[]{:S(2)}) %all-to-all-start.1) | async-done | bytes 8224 | tf_op jit(solution)/shard_map/all_to_all | solution.py:630
  46.0 0.6 %subtract_sqrt_fusion = (f32[2]{0:T(128)}, f32[2]{0:T(128)}) fusion(f32[128]{0:T(128)S(1)} %reduce_sum.19), kind=kLoop, calls=%fused_computation.10 | loop fusion | flops 8 | bytes 32 | tf_op jit(solution)/shard_map/sqrt | solution.py:635
  (10 shorter events, 0.1 us)
Async XLA Ops:
  0.6 10.4 %copy-start = (s32[1,2]{1,0:T(1,128)S(1)}, s32[1,2]{1,0:T(1,128)}, u32[]{:S(2)}) copy-start(s32[1,2]{1,0:T(1,128)} %param.7) | copy-start | bytes 28
  0.6 9.5 %collective-permute-start.1 = (f32[16,4096]{1,0:T(8,128)}, f32[16,4096]{1,0:T(8,128)S(1)}, u32[]{:S(2)}, u32[]{:S(2)}) collective-permute-start(f32[16,4096]{1,0:T(8,128)} %bitcast.14), channel_id=1, source_target_pairs={{0,1},{1,0},{2,3},{3,2},{4,5},{5,4},{6,7},{7,6},{8,9},{9,8},{10,11... | collective-permute-start | bytes 786440 | tf_op jit(solution)/shard_map/ppermute | solution.py:485
  5.8 5.2 %collective-permute-start = (f32[2,4,4096]{2,1,0:T(4,128)S(1)}, f32[2,4,4096]{2,1,0:T(4,128)S(1)}, u32[]{:S(2)}, u32[]{:S(2)}) collective-permute-start(f32[2,4,4096]{2,1,0:T(4,128)S(1)} %get-tuple-element.54), channel_id=1, source_target_pairs={{0,0},{2,4},{4,2},{6,8},{8,6},{10,12},{12,10},{14,16},{16,14},{18,... | collective-permute-start | bytes 393224 | tf_op jit(solution)/shard_map/ppermute | solution.py:485
  6.5 4.5 %collective-permute-start.4 = (f32[2,4,4096]{2,1,0:T(4,128)S(1)}, f32[2,4,4096]{2,1,0:T(4,128)S(1)}, u32[]{:S(2)}, u32[]{:S(2)}) collective-permute-start(f32[2,4,4096]{2,1,0:T(4,128)S(1)} %get-tuple-element.53), channel_id=1, source_target_pairs={{0,2},{2,0},{4,6},{6,4},{8,10},{10,8},{12,14},{14,12},{16,18},{18,... | collective-permute-start | bytes 393224 | tf_op jit(solution)/shard_map/ppermute | solution.py:485
  10.2 2.0 %collective-permute-start.3 = (f32[8,4096]{1,0:T(8,128)S(1)}, f32[8,4096]{1,0:T(8,128)S(1)}, u32[]{:S(2)}, u32[]{:S(2)}) collective-permute-start(f32[8,4096]{1,0:T(8,128)S(1)} %get-tuple-element.55.own_even), channel_id=1, source_target_pairs={{0,2},{2,0},{4,6},{6,4},{8,10},{10,8},{12,14},{14,12},{16,18},{18,... | collective-permute-start | bytes 393224 | tf_op jit(solution)/shard_map/ppermute | solution.py:485
  10.3 4.0 %collective-permute-start.2 = (f32[8,4096]{1,0:T(8,128)S(1)}, f32[8,4096]{1,0:T(8,128)S(1)}, u32[]{:S(2)}, u32[]{:S(2)}) collective-permute-start(f32[8,4096]{1,0:T(8,128)S(1)} %get-tuple-element.32.own_odd), channel_id=1, source_target_pairs={{0,0},{2,4},{4,2},{6,8},{8,6},{10,12},{12,10},{14,16},{16,14},{18,... | collective-permute-start | bytes 393224 | tf_op jit(solution)/shard_map/ppermute | solution.py:485
  17.1 16.0 %all-to-all-start = ((f32[32,1,128]{2,1,0:T(1,128)}), f32[32,1,128]{2,1,0:T(1,128)S(1)}, u32[]{:S(2)}, u32[]{:S(2)}) async-start(f32[32,1,128]{2,1,0:T(1,128)} %bitcast.3), calls=%async_computation | async-start | bytes 32768 | tf_op jit(solution)/shard_map/all_to_all | solution.py:594
  26.0 14.3 %collective-permute-start.5 = (f32[2,16,4096]{2,1,0:T(8,128)S(1)}, f32[2,16,4096]{2,1,0:T(8,128)S(1)}, u32[]{:S(2)}, u32[]{:S(2)}) collective-permute-start(f32[2,16,4096]{2,1,0:T(8,128)S(1)} %get-tuple-element.42.inverse), channel_id=1, source_target_pairs={{0,1},{1,0},{2,3},{3,2},{4,5},{5,4},{6,7},{7,6},{8,9},{9,8},{10,11... | collective-permute-start | bytes 1572872 | tf_op jit(solution)/shard_map/ppermute | solution.py:485
  36.2 9.8 %all-to-all-start.1 = ((f32[16,1,128]{2,1,0:T(1,128)}), f32[16,1,128]{2,1,0:T(1,128)S(1)}, u32[]{:S(2)}, u32[]{:S(2)}) async-start(f32[16,1,128]{2,1,0:T(1,128)} %bitcast.6), calls=%async_computation.1 | async-start | bytes 16384 | tf_op jit(solution)/shard_map/all_to_all | solution.py:630

commit v20 on v19

--- a/solution.py
+++ b/solution.py
@@ -501,6 +501,11 @@
     there = by_parity(odd, paired(shard, axis, 0), height, 0)
     here = by_parity(odd, here, height, 0)
     return [jnp.where(mine, own, other) for own, other in zip(here, there)]
+
+
+def middle_first(size):
+    order = sorted(range(size), key=lambda i: (abs(2 * i + 1 - size), i))
+    return order
 
 
 def total_over(value, axis):
@@ -591,7 +596,9 @@
         name="match",
     )(offsets, own_odd, from_odd, near_lags, near_power, stack, power, band)
     if blocks == 2:
-        parts = lax.all_to_all(part, ("rows", "frames"), 0, 0, tiled=True).reshape(size, blocks, lanes)
+        order = [i * blocks + f for i in middle_first(size) for f in range(blocks)]
+        parts = lax.all_to_all(part, ("rows", "frames"), 0, 0, axis_index_groups=[order], tiled=True)
+        parts = parts.reshape(size, blocks, lanes)
         mine = lax.axis_index("frames") == 0
         both = jnp.sum(parts, axis=0)
         totals = jnp.where(mine, both[0:1], both[1:2])
@@ -627,7 +634,7 @@
         total_frames = count * blocks
         time_mean = whole[0] / total_frames
         time_rms = jnp.sqrt(jnp.maximum(whole[1] / total_frames - time_mean * time_mean, 0.0))
-    sums = lax.all_to_all(part, "rows", 0, 0, tiled=True)
+    sums = lax.all_to_all(part, "rows", 0, 0, axis_index_groups=[middle_first(size)], tiled=True)
     sums, time_mean, time_rms = lax.optimization_barrier((sums, time_mean, time_rms))
     spatial = jnp.sum(sums, axis=0)
     cell_count = rows * columns * size

time: 46.9 us -> 45 us (0.959)
  waiting for transfers between devices: 8.68 us -> 6.25 us
  starting transfers between devices: 21.5 us -> 22 us
    all_to_all x2, waiting for transfers between devices: 7.97 us -> 5.9 us  [the longest x1 5.19 us: shards(): lax.all_to_all(part, ('rows', 'frames'), 0, 0, axis_index_groups=[order],...]
    all_to_all x2, starting transfers between devices: 12.3 us -> 12.8 us  [the longest x1 8.87 us: shards(): lax.all_to_all(part, ('rows', 'frames'), 0, 0, axis_index_groups=[order],...]
  transfers between devices with their start and end apart: 8 -> 8, of which waited for: 4 -> 4; matrix products, arithmetic and copies ran while one was open for 5% -> 5% of each run, Pallas kernels for 20% -> 21%
where the time goes in v20:
time: 45 us; the launch traced here: 44.7 us
  starting transfers between devices  22 us (49%)
  Pallas kernels  12.1 us (27%)
  waiting for transfers between devices  6.25 us (14%)
  other arithmetic  2.89 us (6%)
  between operations  1.43 us (3%)
    ppermute x6, starting transfers between devices, paired(): return lax.ppermute(value, axis, list(enumerate(partner)))  9.19 us
    all_to_all x1, starting transfers between devices, shards(): lax.all_to_all(part, ('rows', 'frames'), 0, 0, axis_index_groups=[order],...  8.87 us
    all_to_all x1, waiting for transfers between devices, shards(): lax.all_to_all(part, ('rows', 'frames'), 0, 0, axis_index_groups=[order],...  5.19 us
    all_to_all x1, starting transfers between devices, shards(): lax.all_to_all(part, 'rows', 0, 0, axis_index_groups=[middle_first(size)]...  3.97 us
    pallas_call x1, Pallas kernels, shards(): pl.pallas_call(time_kernel, out_shape=(struct((rows, columns)), struct((r...  3.06 us
    pallas_call x1, Pallas kernels, shards(): pl.pallas_call(pressure_kernel, out_shape=(struct((count, rows, columns))...  2.98 us
    pallas_call x1, Pallas kernels, shards(): pl.pallas_call(match_kernel, out_shape=(jax.ShapeDtypeStruct((tiles + 2,...  2.77 us
    pallas_call x1, Pallas kernels, shards(): pl.pallas_call(near_kernel, out_shape=(jax.ShapeDtypeStruct((tiles + 2, 2...  2.12 us
  transfers between devices with their start and end apart: 8, of which 4 were waited for; matrix products, arithmetic and copies ran while one was open for 5% of the time, Pallas kernels for 21%

profile of v20, /device:TPU:0, one launch (start us, length us, event | category | flops | bytes accessed | tf_op | source)
XLA Modules:
  0.0 44.7 jit_solution(15036869692751521088)
XLA Ops:
  0.6 3.0 %collective-permute-start.1 = (f32[16,4096]{1,0:T(8,128)}, f32[16,4096]{1,0:T(8,128)S(1)}, u32[]{:S(2)}, u32[]{:S(2)}) collective-permute-start(f32[16,4096]{1,0:T(8,128)} %bitcast.14), channel_id=1, source_target_pairs={{0,1},{1,0},{2,3},{3,2},{4,5},{5,4},{6,7},{7,6},{8,9},{9,8},{10,11... | collective-permute-start | bytes 786440 | tf_op jit(solution)/shard_map/ppermute | solution.py:485
  3.7 1.0 %broadcast_maximum_fusion.1 = f32[16,4096]{1,0:T(8,128)S(1)} fusion(f32[1,16,4096]{2,1,0:T(8,128)} %param.5), kind=kLoop, calls=%fused_computation.3 | loop fusion | flops 65536 | bytes 524288 | tf_op jit(solution)/shard_map/max | solution.py:533
  4.7 1.1 %broadcast_maximum_fusion.frames = f32[2,16,4096]{2,1,0:T(8,128)S(1)} fusion(f32[2,16,4096]{2,1,0:T(8,128)} %param.4), kind=kLoop, calls=%fused_computation | loop fusion | flops 131072 | bytes 1048576 | tf_op jit(solution)/shard_map/max | solution.py:533
  5.8 0.7 %collective-permute-start = (f32[2,4,4096]{2,1,0:T(4,128)S(1)}, f32[2,4,4096]{2,1,0:T(4,128)S(1)}, u32[]{:S(2)}, u32[]{:S(2)}) collective-permute-start(f32[2,4,4096]{2,1,0:T(4,128)S(1)} %get-tuple-element.54), channel_id=1, source_target_pairs={{0,0},{2,4},{4,2},{6,8},{8,6},{10,12},{12,10},{14,16},{16,14},{18,... | collective-permute-start | bytes 393224 | tf_op jit(solution)/shard_map/ppermute | solution.py:485
  6.5 2.9 %collective-permute-start.4 = (f32[2,4,4096]{2,1,0:T(4,128)S(1)}, f32[2,4,4096]{2,1,0:T(4,128)S(1)}, u32[]{:S(2)}, u32[]{:S(2)}) collective-permute-start(f32[2,4,4096]{2,1,0:T(4,128)S(1)} %get-tuple-element.53), channel_id=1, source_target_pairs={{0,2},{2,0},{4,6},{6,4},{8,10},{10,8},{12,14},{14,12},{16,18},{18,... | collective-permute-start | bytes 393224 | tf_op jit(solution)/shard_map/ppermute | solution.py:485
  10.1 0.1 collective-permute-done.1
  10.2 0.1 collective-permute-start.3
  10.3 0.7 %collective-permute-start.2 = (f32[8,4096]{1,0:T(8,128)S(1)}, f32[8,4096]{1,0:T(8,128)S(1)}, u32[]{:S(2)}, u32[]{:S(2)}) collective-permute-start(f32[8,4096]{1,0:T(8,128)S(1)} %get-tuple-element.32.own_odd), channel_id=1, source_target_pairs={{0,0},{2,4},{4,2},{6,8},{8,6},{10,12},{12,10},{14,16},{16,14},{18,... | collective-permute-start | bytes 393224 | tf_op jit(solution)/shard_map/ppermute | solution.py:485
  11.0 0.0 collective-permute-done.from_odd
  11.0 0.0 collective-permute-done.4.from_even
  11.0 1.2 %smooth.1 = (f32[2,16,4096]{2,1,0:T(8,128)S(1)}, bf16[256,4352]{1,0:T(8,128)(2,1)S(1)}, f32[16,128]{1,0:T(8,128)S(1)}, bf16[512,256]{1,0:T(8,128)(2,1)S(1)}) custom-call(f32[2,16,4096]{2,1,0:T(8,128)S(1)} %broadcast_maximum_fusion.frames, f32[2,4,4096]{2,1,0:T(4,128)S(1)} %collective-permute-done.from_odd, f32[2,4,4096]{2,1,0:T(4,128)S(1)} %collective-permute-done.4.from_even), custom_call_target="tpu_custom_call" | custom-call | bytes 8388608 | tf_op jit(solution)/shard_map/smooth/pallas_call | solution.py:542
  12.2 0.0 collective-permute-done.3.from_even
  12.2 2.1 %near.1 = (bf16[34,32,128]{2,1,0:T(8,128)(2,1)S(1)}, f32[128,128]{1,0:T(8,128)S(1)}, f32[8,128]{1,0:T(8,128)S(1)}) custom-call(s32[1,2]{1,0:T(1,128)S(1)} %broadcast_clamp_fusion.base, f32[8,4096]{1,0:T(8,128)S(1)} %get-tuple-element.32.own_odd, f32[8,4096]{1,0:T(8,128)S(1)} %get-tuple-element.55.own_even, f32[8,4096]{1,0:T(8,128)S(1)} %collective-permute-done.3.from_even, ...), custom_call_target="tpu_custom_call" | custom-call | bytes 8388608 | tf_op jit(solution)/shard_map/near/pallas_call | solution.py:574
  14.4 2.8 %match.1 = (bf16[34,16,128]{2,1,0:T(8,128)(2,1)S(1)}, f32[32,128]{1,0:T(8,128)}) custom-call(s32[1,2]{1,0:T(1,128)S(1)} %broadcast_clamp_fusion.base, f32[8,4096]{1,0:T(8,128)S(1)} %get-tuple-element.32.own_odd, f32[8,4096]{1,0:T(8,128)S(1)} %collective-permute-done.2.from_odd, f32[128,128]{1,0:T(8,128)S(1)} %get-tuple-element.36.near_lags, ...), custom_call_target="tpu_custom_call" | custom-call | bytes 8388608 | tf_op jit(solution)/shard_map/match/pallas_call | solution.py:588
  17.1 8.9 %all-to-all-start = ((f32[32,1,128]{2,1,0:T(1,128)}), f32[32,1,128]{2,1,0:T(1,128)S(1)}, u32[]{:S(2)}, u32[]{:S(2)}) async-start(f32[32,1,128]{2,1,0:T(1,128)} %bitcast.3), calls=%async_computation | async-start | bytes 32768 | tf_op jit(solution)/shard_map/all_to_all | solution.py:600
  26.0 1.8 %collective-permute-start.5 = (f32[2,16,4096]{2,1,0:T(8,128)S(1)}, f32[2,16,4096]{2,1,0:T(8,128)S(1)}, u32[]{:S(2)}, u32[]{:S(2)}) collective-permute-start(f32[2,16,4096]{2,1,0:T(8,128)S(1)} %get-tuple-element.42.inverse), channel_id=1, source_target_pairs={{0,1},{1,0},{2,3},{3,2},{4,5},{5,4},{6,7},{7,6},{8,9},{9,8},{10,11... | collective-permute-start | bytes 1572872 | tf_op jit(solution)/shard_map/ppermute | solution.py:485
  27.8 5.2 %all-to-all-done = f32[32,1,128]{2,1,0:T(1,128)S(1)} async-done(((f32[32,1,128]{2,1,0:T(1,128)}), f32[32,1,128]{2,1,0:T(1,128)S(1)}, u32[]{:S(2)}, u32[]{:S(2)}) %all-to-all-start) | async-done | bytes 16416 | tf_op jit(solution)/shard_map/all_to_all | solution.py:600
  33.1 3.0 %pressure.1 = (f32[2,16,4096]{2,1,0:T(8,128)}, f32[2,16,4096]{2,1,0:T(8,128)S(1)}, f32[16,128]{1,0:T(8,128)}) custom-call(s32[1,2]{1,0:T(1,128)S(1)} %broadcast_clamp_fusion.base, f32[1,128]{1,0:T(1,128)S(1)} %get-tuple-element.58.totals, bf16[34,32,128]{2,1,0:T(8,128)(2,1)S(1)} %get-tuple-element.40.clean, ...), custom_call_target="tpu_custom_call" | custom-call | bytes 12582912 | tf_op jit(solution)/shard_map/pressure/pallas_call | solution.py:611
  36.1 4.0 %all-to-all-start.1 = ((f32[16,1,128]{2,1,0:T(1,128)}), f32[16,1,128]{2,1,0:T(1,128)S(1)}, u32[]{:S(2)}, u32[]{:S(2)}) async-start(f32[16,1,128]{2,1,0:T(1,128)} %bitcast.6), calls=%async_computation.1 | async-start | bytes 16384 | tf_op jit(solution)/shard_map/all_to_all | solution.py:637
  40.0 0.1 slice_convert_fusion.base
  40.1 0.2 collective-permute-done.5.inverse
  40.3 3.1 %time.1 = (f32[16,4096]{1,0:T(8,128)}, f32[16,4096]{1,0:T(8,128)}) custom-call(s32[1,2]{1,0:T(1,128)S(1)} %slice_convert_fusion.base, f32[1,128]{1,0:T(1,128)S(1)} %get-tuple-element.57.totals, bf16[34,32,128]{2,1,0:T(8,128)(2,1)S(1)} %get-tuple-element.40.clean, bf16[34,16,128]{2,1,0:T(8,128)(2,1)S(1)} %get-tuple-element.41.other, ...), custom_call_target="tpu_custom_call" | custom-call | bytes 12582912 | tf_op jit(solution)/shard_map/time/pallas_call | solution.py:622
  43.4 0.7 %all-to-all-done.1 = f32[16,1,128]{2,1,0:T(1,128)S(1)} async-done(((f32[16,1,128]{2,1,0:T(1,128)}), f32[16,1,128]{2,1,0:T(1,128)S(1)}, u32[]{:S(2)}, u32[]{:S(2)}) %all-to-all-start.1) | async-done | bytes 8224 | tf_op jit(solution)/shard_map/all_to_all | solution.py:637
  44.1 0.6 %subtract_sqrt_fusion = (f32[2]{0:T(128)}, f32[2]{0:T(128)}) fusion(f32[128]{0:T(128)S(1)} %reduce_sum.19), kind=kLoop, calls=%fused_computation.10 | loop fusion | flops 8 | bytes 32 | tf_op jit(solution)/shard_map/sqrt | solution.py:642
  (10 shorter events, 0.1 us)
Async XLA Ops:
  0.6 10.4 %copy-start = (s32[1,2]{1,0:T(1,128)S(1)}, s32[1,2]{1,0:T(1,128)}, u32[]{:S(2)}) copy-start(s32[1,2]{1,0:T(1,128)} %param.7) | copy-start | bytes 28
  0.6 9.5 %collective-permute-start.1 = (f32[16,4096]{1,0:T(8,128)}, f32[16,4096]{1,0:T(8,128)S(1)}, u32[]{:S(2)}, u32[]{:S(2)}) collective-permute-start(f32[16,4096]{1,0:T(8,128)} %bitcast.14), channel_id=1, source_target_pairs={{0,1},{1,0},{2,3},{3,2},{4,5},{5,4},{6,7},{7,6},{8,9},{9,8},{10,11... | collective-permute-start | bytes 786440 | tf_op jit(solution)/shard_map/ppermute | solution.py:485
  5.8 5.2 %collective-permute-start = (f32[2,4,4096]{2,1,0:T(4,128)S(1)}, f32[2,4,4096]{2,1,0:T(4,128)S(1)}, u32[]{:S(2)}, u32[]{:S(2)}) collective-permute-start(f32[2,4,4096]{2,1,0:T(4,128)S(1)} %get-tuple-element.54), channel_id=1, source_target_pairs={{0,0},{2,4},{4,2},{6,8},{8,6},{10,12},{12,10},{14,16},{16,14},{18,... | collective-permute-start | bytes 393224 | tf_op jit(solution)/shard_map/ppermute | solution.py:485
  6.5 4.5 %collective-permute-start.4 = (f32[2,4,4096]{2,1,0:T(4,128)S(1)}, f32[2,4,4096]{2,1,0:T(4,128)S(1)}, u32[]{:S(2)}, u32[]{:S(2)}) collective-permute-start(f32[2,4,4096]{2,1,0:T(4,128)S(1)} %get-tuple-element.53), channel_id=1, source_target_pairs={{0,2},{2,0},{4,6},{6,4},{8,10},{10,8},{12,14},{14,12},{16,18},{18,... | collective-permute-start | bytes 393224 | tf_op jit(solution)/shard_map/ppermute | solution.py:485
  10.2 2.0 %collective-permute-start.3 = (f32[8,4096]{1,0:T(8,128)S(1)}, f32[8,4096]{1,0:T(8,128)S(1)}, u32[]{:S(2)}, u32[]{:S(2)}) collective-permute-start(f32[8,4096]{1,0:T(8,128)S(1)} %get-tuple-element.55.own_even), channel_id=1, source_target_pairs={{0,2},{2,0},{4,6},{6,4},{8,10},{10,8},{12,14},{14,12},{16,18},{18,... | collective-permute-start | bytes 393224 | tf_op jit(solution)/shard_map/ppermute | solution.py:485
  10.3 4.0 %collective-permute-start.2 = (f32[8,4096]{1,0:T(8,128)S(1)}, f32[8,4096]{1,0:T(8,128)S(1)}, u32[]{:S(2)}, u32[]{:S(2)}) collective-permute-start(f32[8,4096]{1,0:T(8,128)S(1)} %get-tuple-element.32.own_odd), channel_id=1, source_target_pairs={{0,0},{2,4},{4,2},{6,8},{8,6},{10,12},{12,10},{14,16},{16,14},{18,... | collective-permute-start | bytes 393224 | tf_op jit(solution)/shard_map/ppermute | solution.py:485
  17.1 15.9 %all-to-all-start = ((f32[32,1,128]{2,1,0:T(1,128)}), f32[32,1,128]{2,1,0:T(1,128)S(1)}, u32[]{:S(2)}, u32[]{:S(2)}) async-start(f32[32,1,128]{2,1,0:T(1,128)} %bitcast.3), calls=%async_computation | async-start | bytes 32768 | tf_op jit(solution)/shard_map/all_to_all | solution.py:600
  26.0 14.3 %collective-permute-start.5 = (f32[2,16,4096]{2,1,0:T(8,128)S(1)}, f32[2,16,4096]{2,1,0:T(8,128)S(1)}, u32[]{:S(2)}, u32[]{:S(2)}) collective-permute-start(f32[2,16,4096]{2,1,0:T(8,128)S(1)} %get-tuple-element.42.inverse), channel_id=1, source_target_pairs={{0,1},{1,0},{2,3},{3,2},{4,5},{5,4},{6,7},{7,6},{8,9},{9,8},{10,11... | collective-permute-start | bytes 1572872 | tf_op jit(solution)/shard_map/ppermute | solution.py:485
  36.1 8.1 %all-to-all-start.1 = ((f32[16,1,128]{2,1,0:T(1,128)}), f32[16,1,128]{2,1,0:T(1,128)S(1)}, u32[]{:S(2)}, u32[]{:S(2)}) async-start(f32[16,1,128]{2,1,0:T(1,128)} %bitcast.6), calls=%async_computation.1 | async-start | bytes 16384 | tf_op jit(solution)/shard_map/all_to_all | solution.py:637

commit v21 on v20

--- a/solution.py
+++ b/solution.py
@@ -559,9 +559,6 @@
         name="smooth",
     )(raw, frames_odd, frames_even)
     blocks = lax.axis_size("frames")
-    peers = size * blocks if blocks == 2 else size
-    if blocks == 2:
-        other_inverse = paired(inverse, "frames", 0)
     def reference_scratch(height):
         return [
             pltpu.VMEM((tiles, height + 8, lanes), f32),
@@ -587,7 +584,7 @@
     )(offsets, own_odd, own_even, from_even, stack, band)
     other, part = pl.pallas_call(
         match_kernel,
-        out_shape=(jax.ShapeDtypeStruct((tiles + 2, 16, lanes), bf16), struct((peers, lanes))),
+        out_shape=(jax.ShapeDtypeStruct((tiles + 2, 16, lanes), bf16), struct((size, lanes))),
         in_specs=[smem] + [vmem] * 7,
         out_specs=(vmem,) * 2,
         scratch_shapes=reference_scratch(8) + [pltpu.VMEM((8 * count, lanes), f32)],
@@ -596,16 +593,11 @@
         name="match",
     )(offsets, own_odd, from_odd, near_lags, near_power, stack, power, band)
     if blocks == 2:
-        order = [i * blocks + f for i in middle_first(size) for f in range(blocks)]
-        parts = lax.all_to_all(part, ("rows", "frames"), 0, 0, axis_index_groups=[order], tiled=True)
-        parts = parts.reshape(size, blocks, lanes)
-        mine = lax.axis_index("frames") == 0
-        both = jnp.sum(parts, axis=0)
-        totals = jnp.where(mine, both[0:1], both[1:2])
-        row = jnp.where(mine, both[1:2], both[0:1])
-        place = jnp.where(mine, parts[0, 1:2], parts[0, 0:1])[:, lanes - 2 :].astype(jnp.int32)
-    else:
-        totals = jnp.sum(lax.all_to_all(part, "rows", 0, 0, tiled=True), axis=0, keepdims=True)
+        inverse_out, part = lax.optimization_barrier((inverse, part))
+        other_inverse = paired(inverse_out, "frames", 0)
+    order = [middle_first(size)]
+    parts = lax.all_to_all(part, "rows", 0, 0, axis_index_groups=order, tiled=True)
+    totals = jnp.sum(parts, axis=0, keepdims=True)
     depth = -(-reach * 2 * wide // lanes) * lanes
     spread = pltpu.VMEM((depth, columns), bf16)
     pressure, moments, part = pl.pallas_call(
@@ -619,6 +611,9 @@
         name="pressure",
     )(offsets, totals, clean, other, inverse)
     if blocks == 2:
+        row, part = lax.optimization_barrier((totals, part))
+        row = paired(row, "frames", 0)
+        place = (row[:, lanes - 2 :] / size).astype(jnp.int32)
         time_mean, time_rms = pl.pallas_call(
             time_kernel,
             out_shape=(struct((rows, columns)), struct((rows, columns))),
@@ -634,7 +629,7 @@
         total_frames = count * blocks
         time_mean = whole[0] / total_frames
         time_rms = jnp.sqrt(jnp.maximum(whole[1] / total_frames - time_mean * time_mean, 0.0))
-    sums = lax.all_to_all(part, "rows", 0, 0, axis_index_groups=[middle_first(size)], tiled=True)
+    sums = lax.all_to_all(part, "rows", 0, 0, axis_index_groups=order, tiled=True)
     sums, time_mean, time_rms = lax.optimization_barrier((sums, time_mean, time_rms))
     spatial = jnp.sum(sums, axis=0)
     cell_count = rows * columns * size

time: 45 us -> 44.3 us (0.984)
  blocking collectives: 0 us -> 13.4 us
  starting transfers between devices: 22 us -> 13.6 us
  waiting for transfers between devices: 6.25 us -> 1.11 us
  Pallas kernels: 12.1 us -> 11.5 us
    all_to_all x0 -> x1, blocking collectives: none -> 13.4 us  [shards(): lax.all_to_all(part, 'rows', 0, 0, axis_index_groups=order, tiled=True)]
    all_to_all x2 -> x1, starting transfers between devices: 12.8 us -> 4.03 us  [shards(): lax.all_to_all(part, 'rows', 0, 0, axis_index_groups=order, tiled=True)]
    all_to_all x2 -> x1, waiting for transfers between devices: 5.9 us -> 0.98 us  [shards(): lax.all_to_all(part, 'rows', 0, 0, axis_index_groups=order, tiled=True)]
    pallas_call x1, Pallas kernels: 2.77 us -> 2.16 us  [shards(): pl.pallas_call(match_kernel, out_shape=(jax.ShapeDtypeStruct((tiles + 2,...]
    ppermute x6 -> x7, starting transfers between devices: 9.19 us -> 9.6 us  [paired(): return lax.ppermute(value, axis, list(enumerate(partner)))]
  transfers between devices with their start and end apart: 8 -> 8, of which waited for: 4 -> 2; matrix products, arithmetic and copies ran while one was open for 5% -> 5% of each run, Pallas kernels for 21% -> 21%
where the time goes in v21:
time: 44.3 us; the launch traced here: 44 us
  starting transfers between devices  13.6 us (31%)
  blocking collectives  13.4 us (30%)
  Pallas kernels  11.5 us (26%)
  other arithmetic  2.89 us (7%)
  between operations  1.42 us (3%)
  waiting for transfers between devices  1.11 us (3%)
    all_to_all x1, blocking collectives, shards(): lax.all_to_all(part, 'rows', 0, 0, axis_index_groups=order, tiled=True)  13.4 us
    ppermute x7, starting transfers between devices, paired(): return lax.ppermute(value, axis, list(enumerate(partner)))  9.6 us
    all_to_all x1, starting transfers between devices, shards(): lax.all_to_all(part, 'rows', 0, 0, axis_index_groups=order, tiled=True)  4.03 us
    pallas_call x1, Pallas kernels, shards(): pl.pallas_call(pressure_kernel, out_shape=(struct((count, rows, columns))...  3.02 us
    pallas_call x1, Pallas kernels, shards(): pl.pallas_call(time_kernel, out_shape=(struct((rows, columns)), struct((r...  3.02 us
    pallas_call x1, Pallas kernels, shards(): pl.pallas_call(match_kernel, out_shape=(jax.ShapeDtypeStruct((tiles + 2,...  2.16 us
    pallas_call x1, Pallas kernels, shards(): pl.pallas_call(near_kernel, out_shape=(jax.ShapeDtypeStruct((tiles + 2, 2...  2.13 us
    pallas_call x1, Pallas kernels, shards(): pl.pallas_call(smooth_kernel, out_shape=(struct((count, rows, columns)),...  1.17 us
  transfers between devices with their start and end apart: 8, of which 2 were waited for; matrix products, arithmetic and copies ran while one was open for 5% of the time, Pallas kernels for 21%

profile of v21, /device:TPU:0, one launch (start us, length us, event | category | flops | bytes accessed | tf_op | source)
XLA Modules:
  0.0 44.0 jit_solution(10015072826932159648)
XLA Ops:
  0.6 3.0 %collective-permute-start.1 = (f32[16,4096]{1,0:T(8,128)}, f32[16,4096]{1,0:T(8,128)S(1)}, u32[]{:S(2)}, u32[]{:S(2)}) collective-permute-start(f32[16,4096]{1,0:T(8,128)} %bitcast.15), channel_id=1, source_target_pairs={{0,1},{1,0},{2,3},{3,2},{4,5},{5,4},{6,7},{7,6},{8,9},{9,8},{10,11... | collective-permute-start | bytes 786440 | tf_op jit(solution)/shard_map/ppermute | solution.py:485
  3.7 1.0 %broadcast_maximum_fusion.1 = f32[16,4096]{1,0:T(8,128)S(1)} fusion(f32[1,16,4096]{2,1,0:T(8,128)} %param.5), kind=kLoop, calls=%fused_computation.3 | loop fusion | flops 65536 | bytes 524288 | tf_op jit(solution)/shard_map/max | solution.py:533
  4.7 1.1 %broadcast_maximum_fusion.frames = f32[2,16,4096]{2,1,0:T(8,128)S(1)} fusion(f32[2,16,4096]{2,1,0:T(8,128)} %param.4), kind=kLoop, calls=%fused_computation | loop fusion | flops 131072 | bytes 1048576 | tf_op jit(solution)/shard_map/max | solution.py:533
  5.8 0.7 %collective-permute-start = (f32[2,4,4096]{2,1,0:T(4,128)S(1)}, f32[2,4,4096]{2,1,0:T(4,128)S(1)}, u32[]{:S(2)}, u32[]{:S(2)}) collective-permute-start(f32[2,4,4096]{2,1,0:T(4,128)S(1)} %get-tuple-element.64), channel_id=1, source_target_pairs={{0,0},{2,4},{4,2},{6,8},{8,6},{10,12},{12,10},{14,16},{16,14},{18,... | collective-permute-start | bytes 393224 | tf_op jit(solution)/shard_map/ppermute | solution.py:485
  6.5 2.9 %collective-permute-start.2 = (f32[2,4,4096]{2,1,0:T(4,128)S(1)}, f32[2,4,4096]{2,1,0:T(4,128)S(1)}, u32[]{:S(2)}, u32[]{:S(2)}) collective-permute-start(f32[2,4,4096]{2,1,0:T(4,128)S(1)} %get-tuple-element.63), channel_id=1, source_target_pairs={{0,2},{2,0},{4,6},{6,4},{8,10},{10,8},{12,14},{14,12},{16,18},{18,... | collective-permute-start | bytes 393224 | tf_op jit(solution)/shard_map/ppermute | solution.py:485
  10.1 0.1 collective-permute-done.1
  10.2 0.1 collective-permute-start.4
  10.3 0.7 %collective-permute-start.3 = (f32[8,4096]{1,0:T(8,128)S(1)}, f32[8,4096]{1,0:T(8,128)S(1)}, u32[]{:S(2)}, u32[]{:S(2)}) collective-permute-start(f32[8,4096]{1,0:T(8,128)S(1)} %get-tuple-element.38.own_odd), channel_id=1, source_target_pairs={{0,0},{2,4},{4,2},{6,8},{8,6},{10,12},{12,10},{14,16},{16,14},{18,... | collective-permute-start | bytes 393224 | tf_op jit(solution)/shard_map/ppermute | solution.py:485
  11.0 0.0 collective-permute-done.2.from_even
  11.0 1.2 %smooth.1 = (f32[2,16,4096]{2,1,0:T(8,128)S(1)}, bf16[256,4352]{1,0:T(8,128)(2,1)S(1)}, f32[16,128]{1,0:T(8,128)S(1)}, bf16[512,256]{1,0:T(8,128)(2,1)S(1)}) custom-call(f32[2,16,4096]{2,1,0:T(8,128)S(1)} %broadcast_maximum_fusion.frames, f32[2,4,4096]{2,1,0:T(4,128)S(1)} %collective-permute-done.from_odd, f32[2,4,4096]{2,1,0:T(4,128)S(1)} %collective-permute-done.2.from_even), custom_call_target="tpu_custom_call" | custom-call | bytes 8388608 | tf_op jit(solution)/shard_map/smooth/pallas_call | solution.py:542
  12.2 2.1 %near.1 = (bf16[34,32,128]{2,1,0:T(8,128)(2,1)S(1)}, f32[128,128]{1,0:T(8,128)S(1)}, f32[8,128]{1,0:T(8,128)S(1)}) custom-call(s32[1,2]{1,0:T(1,128)S(1)} %broadcast_clamp_fusion.base, f32[8,4096]{1,0:T(8,128)S(1)} %get-tuple-element.38.own_odd, f32[8,4096]{1,0:T(8,128)S(1)} %get-tuple-element.61.own_even, f32[8,4096]{1,0:T(8,128)S(1)} %collective-permute-done.4.from_even, ...), custom_call_target="tpu_custom_call" | custom-call | bytes 8388608 | tf_op jit(solution)/shard_map/near/pallas_call | solution.py:571
  14.3 0.0 collective-permute-done.3.from_odd
  14.4 2.2 %match.1 = (bf16[34,16,128]{2,1,0:T(8,128)(2,1)S(1)}, f32[16,128]{1,0:T(8,128)S(1)}) custom-call(s32[1,2]{1,0:T(1,128)S(1)} %broadcast_clamp_fusion.base, f32[8,4096]{1,0:T(8,128)S(1)} %get-tuple-element.38.own_odd, f32[8,4096]{1,0:T(8,128)S(1)} %collective-permute-done.3.from_odd, f32[128,128]{1,0:T(8,128)S(1)} %get-tuple-element.41.near_lags, ...), custom_call_target="tpu_custom_call" | custom-call | bytes 8388608 | tf_op jit(solution)/shard_map/match/pallas_call | solution.py:585
  16.5 1.8 %collective-permute-start.6 = (f32[2,16,4096]{2,1,0:T(8,128)S(1)}, f32[2,16,4096]{2,1,0:T(8,128)S(1)}, u32[]{:S(2)}, u32[]{:S(2)}) collective-permute-start(f32[2,16,4096]{2,1,0:T(8,128)S(1)} %get-tuple-element.52.inverse), channel_id=1, source_target_pairs={{0,1},{1,0},{2,3},{3,2},{4,5},{5,4},{6,7},{7,6},{8,9},{9,8},{10,11... | collective-permute-start | bytes 1572872 | tf_op jit(solution)/shard_map/ppermute | solution.py:485
  18.3 13.4 %all_to_all.21 = f32[16,1,128]{2,1,0:T(1,128)S(1)} all-to-all(f32[16,1,128]{2,1,0:T(1,128)S(1)} %bitcast.12), channel_id=1, replica_groups={{14,16,12,18,10,20,8,22,6,24,4,26,2,28,0,30},{15,17,13,19,11,21,9,23,7,..., dimensions={0} | all-to-all | bytes 16384 | tf_op jit(solution)/shard_map/all_to_all | solution.py:599
  31.8 3.0 %pressure.1 = (f32[2,16,4096]{2,1,0:T(8,128)}, f32[2,16,4096]{2,1,0:T(8,128)S(1)}, f32[16,128]{1,0:T(8,128)}) custom-call(s32[1,2]{1,0:T(1,128)S(1)} %broadcast_clamp_fusion.base, f32[1,128]{1,0:T(1,128)S(1)} %bitcast.13, bf16[34,32,128]{2,1,0:T(8,128)(2,1)S(1)} %get-tuple-element.46.clean, bf16[34,16,128]{2,1,0:T(8,128)(2,1)S(1)} %get-tuple-element.47.other, ...), custom_call_target="tpu_custom_call" | custom-call | bytes 12582912 | tf_op jit(solution)/shard_map/pressure/pallas_call | solution.py:603
  34.8 0.5 %collective-permute-start.5 = (f32[1,128]{1,0:T(1,128)S(1)}, f32[1,128]{1,0:T(1,128)S(1)}, u32[]{:S(2)}, u32[]{:S(2)}) collective-permute-start(f32[1,128]{1,0:T(1,128)S(1)} %bitcast.14), channel_id=1, source_target_pairs={{0,1},{1,0},{2,3},{3,2},{4,5},{5,4},{6,7},{7,6},{8,9},{9,8},{10,11... | collective-permute-start | bytes 1544 | tf_op jit(solution)/shard_map/ppermute | solution.py:485
  35.2 4.0 %all-to-all-start.1 = ((f32[16,1,128]{2,1,0:T(1,128)}), f32[16,1,128]{2,1,0:T(1,128)S(1)}, u32[]{:S(2)}, u32[]{:S(2)}) async-start(f32[16,1,128]{2,1,0:T(1,128)} %bitcast.6), calls=%async_computation.1 | async-start | bytes 16384 | tf_op jit(solution)/shard_map/all_to_all | solution.py:632
  39.3 0.0 collective-permute-done.5.totals
  39.3 0.1 multiply_convert_fusion.base
  39.4 0.0 collective-permute-done.6.inverse
  39.4 3.0 %time.1 = (f32[16,4096]{1,0:T(8,128)}, f32[16,4096]{1,0:T(8,128)}) custom-call(s32[1,2]{1,0:T(1,128)S(1)} %multiply_convert_fusion.base, f32[1,128]{1,0:T(1,128)S(1)} %collective-permute-done.5.totals, bf16[34,32,128]{2,1,0:T(8,128)(2,1)S(1)} %get-tuple-element.46.clean, bf16[34,16,128]{2,1,0:T(8,128)(2,1)S(1)} %get-tuple-element.47.other, ...), custom_call_target="tpu_custom_call" | custom-call | bytes 12582912 | tf_op jit(solution)/shard_map/time/pallas_call | solution.py:617
  42.4 1.0 %all-to-all-done.1 = f32[16,1,128]{2,1,0:T(1,128)S(1)} async-done(((f32[16,1,128]{2,1,0:T(1,128)}), f32[16,1,128]{2,1,0:T(1,128)S(1)}, u32[]{:S(2)}, u32[]{:S(2)}) %all-to-all-start.1) | async-done | bytes 8224 | tf_op jit(solution)/shard_map/all_to_all | solution.py:632
  43.4 0.6 %subtract_sqrt_fusion = (f32[2]{0:T(128)}, f32[2]{0:T(128)}) fusion(f32[128]{0:T(128)S(1)} %reduce_sum.19), kind=kLoop, calls=%fused_computation.6 | loop fusion | flops 8 | bytes 32 | tf_op jit(solution)/shard_map/sqrt | solution.py:637
  (9 shorter events, 0.1 us)
Async XLA Ops:
  0.6 10.4 %copy-start = (s32[1,2]{1,0:T(1,128)S(1)}, s32[1,2]{1,0:T(1,128)}, u32[]{:S(2)}) copy-start(s32[1,2]{1,0:T(1,128)} %param.7) | copy-start | bytes 28
  0.6 9.5 %collective-permute-start.1 = (f32[16,4096]{1,0:T(8,128)}, f32[16,4096]{1,0:T(8,128)S(1)}, u32[]{:S(2)}, u32[]{:S(2)}) collective-permute-start(f32[16,4096]{1,0:T(8,128)} %bitcast.15), channel_id=1, source_target_pairs={{0,1},{1,0},{2,3},{3,2},{4,5},{5,4},{6,7},{7,6},{8,9},{9,8},{10,11... | collective-permute-start | bytes 786440 | tf_op jit(solution)/shard_map/ppermute | solution.py:485
  5.8 5.2 %collective-permute-start = (f32[2,4,4096]{2,1,0:T(4,128)S(1)}, f32[2,4,4096]{2,1,0:T(4,128)S(1)}, u32[]{:S(2)}, u32[]{:S(2)}) collective-permute-start(f32[2,4,4096]{2,1,0:T(4,128)S(1)} %get-tuple-element.64), channel_id=1, source_target_pairs={{0,0},{2,4},{4,2},{6,8},{8,6},{10,12},{12,10},{14,16},{16,14},{18,... | collective-permute-start | bytes 393224 | tf_op jit(solution)/shard_map/ppermute | solution.py:485
  6.5 4.5 %collective-permute-start.2 = (f32[2,4,4096]{2,1,0:T(4,128)S(1)}, f32[2,4,4096]{2,1,0:T(4,128)S(1)}, u32[]{:S(2)}, u32[]{:S(2)}) collective-permute-start(f32[2,4,4096]{2,1,0:T(4,128)S(1)} %get-tuple-element.63), channel_id=1, source_target_pairs={{0,2},{2,0},{4,6},{6,4},{8,10},{10,8},{12,14},{14,12},{16,18},{18,... | collective-permute-start | bytes 393224 | tf_op jit(solution)/shard_map/ppermute | solution.py:485
  10.2 2.0 %collective-permute-start.4 = (f32[8,4096]{1,0:T(8,128)S(1)}, f32[8,4096]{1,0:T(8,128)S(1)}, u32[]{:S(2)}, u32[]{:S(2)}) collective-permute-start(f32[8,4096]{1,0:T(8,128)S(1)} %get-tuple-element.61.own_even), channel_id=1, source_target_pairs={{0,2},{2,0},{4,6},{6,4},{8,10},{10,8},{12,14},{14,12},{16,18},{18,... | collective-permute-start | bytes 393224 | tf_op jit(solution)/shard_map/ppermute | solution.py:485
  10.3 4.0 %collective-permute-start.3 = (f32[8,4096]{1,0:T(8,128)S(1)}, f32[8,4096]{1,0:T(8,128)S(1)}, u32[]{:S(2)}, u32[]{:S(2)}) collective-permute-start(f32[8,4096]{1,0:T(8,128)S(1)} %get-tuple-element.38.own_odd), channel_id=1, source_target_pairs={{0,0},{2,4},{4,2},{6,8},{8,6},{10,12},{12,10},{14,16},{16,14},{18,... | collective-permute-start | bytes 393224 | tf_op jit(solution)/shard_map/ppermute | solution.py:485
  16.5 22.8 %collective-permute-start.6 = (f32[2,16,4096]{2,1,0:T(8,128)S(1)}, f32[2,16,4096]{2,1,0:T(8,128)S(1)}, u32[]{:S(2)}, u32[]{:S(2)}) collective-permute-start(f32[2,16,4096]{2,1,0:T(8,128)S(1)} %get-tuple-element.52.inverse), channel_id=1, source_target_pairs={{0,1},{1,0},{2,3},{3,2},{4,5},{5,4},{6,7},{7,6},{8,9},{9,8},{10,11... | collective-permute-start | bytes 1572872 | tf_op jit(solution)/shard_map/ppermute | solution.py:485
  34.8 4.5 %collective-permute-start.5 = (f32[1,128]{1,0:T(1,128)S(1)}, f32[1,128]{1,0:T(1,128)S(1)}, u32[]{:S(2)}, u32[]{:S(2)}) collective-permute-start(f32[1,128]{1,0:T(1,128)S(1)} %bitcast.14), channel_id=1, source_target_pairs={{0,1},{1,0},{2,3},{3,2},{4,5},{5,4},{6,7},{7,6},{8,9},{9,8},{10,11... | collective-permute-start | bytes 1544 | tf_op jit(solution)/shard_map/ppermute | solution.py:485
  35.2 8.1 %all-to-all-start.1 = ((f32[16,1,128]{2,1,0:T(1,128)}), f32[16,1,128]{2,1,0:T(1,128)S(1)}, u32[]{:S(2)}, u32[]{:S(2)}) async-start(f32[16,1,128]{2,1,0:T(1,128)} %bitcast.6), calls=%async_computation.1 | async-start | bytes 16384 | tf_op jit(solution)/shard_map/all_to_all | solution.py:632

commit v22 on v21

--- a/solution.py
+++ b/solution.py
@@ -629,7 +629,8 @@
         total_frames = count * blocks
         time_mean = whole[0] / total_frames
         time_rms = jnp.sqrt(jnp.maximum(whole[1] / total_frames - time_mean * time_mean, 0.0))
-    sums = lax.all_to_all(part, "rows", 0, 0, axis_index_groups=order, tiled=True)
+    turned = [[(i + size // 2 - 1) % size for i in range(size)]]
+    sums = lax.all_to_all(part, "rows", 0, 0, axis_index_groups=turned, tiled=True)
     sums, time_mean, time_rms = lax.optimization_barrier((sums, time_mean, time_rms))
     spatial = jnp.sum(sums, axis=0)
     cell_count = rows * columns * size

time: 44.3 us -> 44.3 us (level)
  no operation moved by 1% of the time
where the time goes in v22:
time: 44.3 us; the launch traced here: 44 us
  starting transfers between devices  13.7 us (31%)
  blocking collectives  13.4 us (30%)
  Pallas kernels  11.5 us (26%)
  other arithmetic  2.89 us (7%)
  between operations  1.42 us (3%)
  waiting for transfers between devices  1.11 us (3%)
    all_to_all x1, blocking collectives, shards(): lax.all_to_all(part, 'rows', 0, 0, axis_index_groups=order, tiled=True)  13.4 us
    ppermute x7, starting transfers between devices, paired(): return lax.ppermute(value, axis, list(enumerate(partner)))  9.7 us
    all_to_all x1, starting transfers between devices, shards(): lax.all_to_all(part, 'rows', 0, 0, axis_index_groups=turned, tiled=True)  3.99 us
    pallas_call x1, Pallas kernels, shards(): pl.pallas_call(time_kernel, out_shape=(struct((rows, columns)), struct((r...  3.06 us
    pallas_call x1, Pallas kernels, shards(): pl.pallas_call(pressure_kernel, out_shape=(struct((count, rows, columns))...  2.98 us
    pallas_call x1, Pallas kernels, shards(): pl.pallas_call(match_kernel, out_shape=(jax.ShapeDtypeStruct((tiles + 2,...  2.16 us
    pallas_call x1, Pallas kernels, shards(): pl.pallas_call(near_kernel, out_shape=(jax.ShapeDtypeStruct((tiles + 2, 2...  2.12 us
    pallas_call x1, Pallas kernels, shards(): pl.pallas_call(smooth_kernel, out_shape=(struct((count, rows, columns)),...  1.17 us
  transfers between devices with their start and end apart: 8, of which 2 were waited for; matrix products, arithmetic and copies ran while one was open for 5% of the time, Pallas kernels for 21%

profile of v22, /device:TPU:0, one launch (start us, length us, event | category | flops | bytes accessed | tf_op | source)
XLA Modules:
  0.0 44.0 jit_solution(16435664475597363318)
XLA Ops:
  0.6 3.0 %collective-permute-start.1 = (f32[16,4096]{1,0:T(8,128)}, f32[16,4096]{1,0:T(8,128)S(1)}, u32[]{:S(2)}, u32[]{:S(2)}) collective-permute-start(f32[16,4096]{1,0:T(8,128)} %bitcast.15), channel_id=1, source_target_pairs={{0,1},{1,0},{2,3},{3,2},{4,5},{5,4},{6,7},{7,6},{8,9},{9,8},{10,11... | collective-permute-start | bytes 786440 | tf_op jit(solution)/shard_map/ppermute | solution.py:485
  3.7 1.0 %broadcast_maximum_fusion.1 = f32[16,4096]{1,0:T(8,128)S(1)} fusion(f32[1,16,4096]{2,1,0:T(8,128)} %param.5), kind=kLoop, calls=%fused_computation.3 | loop fusion | flops 65536 | bytes 524288 | tf_op jit(solution)/shard_map/max | solution.py:533
  4.7 1.1 %broadcast_maximum_fusion.frames = f32[2,16,4096]{2,1,0:T(8,128)S(1)} fusion(f32[2,16,4096]{2,1,0:T(8,128)} %param.4), kind=kLoop, calls=%fused_computation | loop fusion | flops 131072 | bytes 1048576 | tf_op jit(solution)/shard_map/max | solution.py:533
  5.8 0.7 %collective-permute-start = (f32[2,4,4096]{2,1,0:T(4,128)S(1)}, f32[2,4,4096]{2,1,0:T(4,128)S(1)}, u32[]{:S(2)}, u32[]{:S(2)}) collective-permute-start(f32[2,4,4096]{2,1,0:T(4,128)S(1)} %get-tuple-element.64), channel_id=1, source_target_pairs={{0,0},{2,4},{4,2},{6,8},{8,6},{10,12},{12,10},{14,16},{16,14},{18,... | collective-permute-start | bytes 393224 | tf_op jit(solution)/shard_map/ppermute | solution.py:485
  6.5 2.9 %collective-permute-start.2 = (f32[2,4,4096]{2,1,0:T(4,128)S(1)}, f32[2,4,4096]{2,1,0:T(4,128)S(1)}, u32[]{:S(2)}, u32[]{:S(2)}) collective-permute-start(f32[2,4,4096]{2,1,0:T(4,128)S(1)} %get-tuple-element.63), channel_id=1, source_target_pairs={{0,2},{2,0},{4,6},{6,4},{8,10},{10,8},{12,14},{14,12},{16,18},{18,... | collective-permute-start | bytes 393224 | tf_op jit(solution)/shard_map/ppermute | solution.py:485
  10.1 0.1 collective-permute-done.1
  10.2 0.1 collective-permute-start.4
  10.3 0.7 %collective-permute-start.3 = (f32[8,4096]{1,0:T(8,128)S(1)}, f32[8,4096]{1,0:T(8,128)S(1)}, u32[]{:S(2)}, u32[]{:S(2)}) collective-permute-start(f32[8,4096]{1,0:T(8,128)S(1)} %get-tuple-element.38.own_odd), channel_id=1, source_target_pairs={{0,0},{2,4},{4,2},{6,8},{8,6},{10,12},{12,10},{14,16},{16,14},{18,... | collective-permute-start | bytes 393224 | tf_op jit(solution)/shard_map/ppermute | solution.py:485
  11.0 0.0 collective-permute-done.from_odd
  11.0 0.0 collective-permute-done.2.from_even
  11.0 1.2 %smooth.1 = (f32[2,16,4096]{2,1,0:T(8,128)S(1)}, bf16[256,4352]{1,0:T(8,128)(2,1)S(1)}, f32[16,128]{1,0:T(8,128)S(1)}, bf16[512,256]{1,0:T(8,128)(2,1)S(1)}) custom-call(f32[2,16,4096]{2,1,0:T(8,128)S(1)} %broadcast_maximum_fusion.frames, f32[2,4,4096]{2,1,0:T(4,128)S(1)} %collective-permute-done.from_odd, f32[2,4,4096]{2,1,0:T(4,128)S(1)} %collective-permute-done.2.from_even), custom_call_target="tpu_custom_call" | custom-call | bytes 8388608 | tf_op jit(solution)/shard_map/smooth/pallas_call | solution.py:542
  12.2 0.0 collective-permute-done.4.from_even
  12.2 2.1 %near.1 = (bf16[34,32,128]{2,1,0:T(8,128)(2,1)S(1)}, f32[128,128]{1,0:T(8,128)S(1)}, f32[8,128]{1,0:T(8,128)S(1)}) custom-call(s32[1,2]{1,0:T(1,128)S(1)} %broadcast_clamp_fusion.base, f32[8,4096]{1,0:T(8,128)S(1)} %get-tuple-element.38.own_odd, f32[8,4096]{1,0:T(8,128)S(1)} %get-tuple-element.61.own_even, f32[8,4096]{1,0:T(8,128)S(1)} %collective-permute-done.4.from_even, ...), custom_call_target="tpu_custom_call" | custom-call | bytes 8388608 | tf_op jit(solution)/shard_map/near/pallas_call | solution.py:571
  14.3 0.0 collective-permute-done.3.from_odd
  14.4 2.2 %match.1 = (bf16[34,16,128]{2,1,0:T(8,128)(2,1)S(1)}, f32[16,128]{1,0:T(8,128)S(1)}) custom-call(s32[1,2]{1,0:T(1,128)S(1)} %broadcast_clamp_fusion.base, f32[8,4096]{1,0:T(8,128)S(1)} %get-tuple-element.38.own_odd, f32[8,4096]{1,0:T(8,128)S(1)} %collective-permute-done.3.from_odd, f32[128,128]{1,0:T(8,128)S(1)} %get-tuple-element.41.near_lags, ...), custom_call_target="tpu_custom_call" | custom-call | bytes 8388608 | tf_op jit(solution)/shard_map/match/pallas_call | solution.py:585
  16.5 1.8 %collective-permute-start.6 = (f32[2,16,4096]{2,1,0:T(8,128)S(1)}, f32[2,16,4096]{2,1,0:T(8,128)S(1)}, u32[]{:S(2)}, u32[]{:S(2)}) collective-permute-start(f32[2,16,4096]{2,1,0:T(8,128)S(1)} %get-tuple-element.52.inverse), channel_id=1, source_target_pairs={{0,1},{1,0},{2,3},{3,2},{4,5},{5,4},{6,7},{7,6},{8,9},{9,8},{10,11... | collective-permute-start | bytes 1572872 | tf_op jit(solution)/shard_map/ppermute | solution.py:485
  18.3 13.4 %all_to_all.21 = f32[16,1,128]{2,1,0:T(1,128)S(1)} all-to-all(f32[16,1,128]{2,1,0:T(1,128)S(1)} %bitcast.12), channel_id=1, replica_groups={{14,16,12,18,10,20,8,22,6,24,4,26,2,28,0,30},{15,17,13,19,11,21,9,23,7,..., dimensions={0} | all-to-all | bytes 16384 | tf_op jit(solution)/shard_map/all_to_all | solution.py:599
  31.8 3.0 %pressure.1 = (f32[2,16,4096]{2,1,0:T(8,128)}, f32[2,16,4096]{2,1,0:T(8,128)S(1)}, f32[16,128]{1,0:T(8,128)}) custom-call(s32[1,2]{1,0:T(1,128)S(1)} %broadcast_clamp_fusion.base, f32[1,128]{1,0:T(1,128)S(1)} %bitcast.13, bf16[34,32,128]{2,1,0:T(8,128)(2,1)S(1)} %get-tuple-element.46.clean, bf16[34,16,128]{2,1,0:T(8,128)(2,1)S(1)} %get-tuple-element.47.other, ...), custom_call_target="tpu_custom_call" | custom-call | bytes 12582912 | tf_op jit(solution)/shard_map/pressure/pallas_call | solution.py:603
  34.7 0.6 %collective-permute-start.5 = (f32[1,128]{1,0:T(1,128)S(1)}, f32[1,128]{1,0:T(1,128)S(1)}, u32[]{:S(2)}, u32[]{:S(2)}) collective-permute-start(f32[1,128]{1,0:T(1,128)S(1)} %bitcast.14), channel_id=1, source_target_pairs={{0,1},{1,0},{2,3},{3,2},{4,5},{5,4},{6,7},{7,6},{8,9},{9,8},{10,11... | collective-permute-start | bytes 1544 | tf_op jit(solution)/shard_map/ppermute | solution.py:485
  35.3 4.0 %all-to-all-start.1 = ((f32[16,1,128]{2,1,0:T(1,128)}), f32[16,1,128]{2,1,0:T(1,128)S(1)}, u32[]{:S(2)}, u32[]{:S(2)}) async-start(f32[16,1,128]{2,1,0:T(1,128)} %bitcast.6), calls=%async_computation.1 | async-start | bytes 16384 | tf_op jit(solution)/shard_map/all_to_all | solution.py:633
  39.3 0.1 multiply_convert_fusion.base
  39.4 3.1 %time.1 = (f32[16,4096]{1,0:T(8,128)}, f32[16,4096]{1,0:T(8,128)}) custom-call(s32[1,2]{1,0:T(1,128)S(1)} %multiply_convert_fusion.base, f32[1,128]{1,0:T(1,128)S(1)} %collective-permute-done.5.totals, bf16[34,32,128]{2,1,0:T(8,128)(2,1)S(1)} %get-tuple-element.46.clean, bf16[34,16,128]{2,1,0:T(8,128)(2,1)S(1)} %get-tuple-element.47.other, ...), custom_call_target="tpu_custom_call" | custom-call | bytes 12582912 | tf_op jit(solution)/shard_map/time/pallas_call | solution.py:617
  42.4 1.0 %all-to-all-done.1 = f32[16,1,128]{2,1,0:T(1,128)S(1)} async-done(((f32[16,1,128]{2,1,0:T(1,128)}), f32[16,1,128]{2,1,0:T(1,128)S(1)}, u32[]{:S(2)}, u32[]{:S(2)}) %all-to-all-start.1) | async-done | bytes 8224 | tf_op jit(solution)/shard_map/all_to_all | solution.py:633
  43.4 0.6 %subtract_sqrt_fusion = (f32[2]{0:T(128)}, f32[2]{0:T(128)}) fusion(f32[128]{0:T(128)S(1)} %reduce_sum.19), kind=kLoop, calls=%fused_computation.6 | loop fusion | flops 8 | bytes 32 | tf_op jit(solution)/shard_map/sqrt | solution.py:638
  (9 shorter events, 0.1 us)
Async XLA Ops:
  0.6 10.4 %copy-start = (s32[1,2]{1,0:T(1,128)S(1)}, s32[1,2]{1,0:T(1,128)}, u32[]{:S(2)}) copy-start(s32[1,2]{1,0:T(1,128)} %param.7) | copy-start | bytes 28
  0.6 9.5 %collective-permute-start.1 = (f32[16,4096]{1,0:T(8,128)}, f32[16,4096]{1,0:T(8,128)S(1)}, u32[]{:S(2)}, u32[]{:S(2)}) collective-permute-start(f32[16,4096]{1,0:T(8,128)} %bitcast.15), channel_id=1, source_target_pairs={{0,1},{1,0},{2,3},{3,2},{4,5},{5,4},{6,7},{7,6},{8,9},{9,8},{10,11... | collective-permute-start | bytes 786440 | tf_op jit(solution)/shard_map/ppermute | solution.py:485
  5.8 5.2 %collective-permute-start = (f32[2,4,4096]{2,1,0:T(4,128)S(1)}, f32[2,4,4096]{2,1,0:T(4,128)S(1)}, u32[]{:S(2)}, u32[]{:S(2)}) collective-permute-start(f32[2,4,4096]{2,1,0:T(4,128)S(1)} %get-tuple-element.64), channel_id=1, source_target_pairs={{0,0},{2,4},{4,2},{6,8},{8,6},{10,12},{12,10},{14,16},{16,14},{18,... | collective-permute-start | bytes 393224 | tf_op jit(solution)/shard_map/ppermute | solution.py:485
  6.5 4.5 %collective-permute-start.2 = (f32[2,4,4096]{2,1,0:T(4,128)S(1)}, f32[2,4,4096]{2,1,0:T(4,128)S(1)}, u32[]{:S(2)}, u32[]{:S(2)}) collective-permute-start(f32[2,4,4096]{2,1,0:T(4,128)S(1)} %get-tuple-element.63), channel_id=1, source_target_pairs={{0,2},{2,0},{4,6},{6,4},{8,10},{10,8},{12,14},{14,12},{16,18},{18,... | collective-permute-start | bytes 393224 | tf_op jit(solution)/shard_map/ppermute | solution.py:485
  10.2 2.0 %collective-permute-start.4 = (f32[8,4096]{1,0:T(8,128)S(1)}, f32[8,4096]{1,0:T(8,128)S(1)}, u32[]{:S(2)}, u32[]{:S(2)}) collective-permute-start(f32[8,4096]{1,0:T(8,128)S(1)} %get-tuple-element.61.own_even), channel_id=1, source_target_pairs={{0,2},{2,0},{4,6},{6,4},{8,10},{10,8},{12,14},{14,12},{16,18},{18,... | collective-permute-start | bytes 393224 | tf_op jit(solution)/shard_map/ppermute | solution.py:485
  10.3 4.0 %collective-permute-start.3 = (f32[8,4096]{1,0:T(8,128)S(1)}, f32[8,4096]{1,0:T(8,128)S(1)}, u32[]{:S(2)}, u32[]{:S(2)}) collective-permute-start(f32[8,4096]{1,0:T(8,128)S(1)} %get-tuple-element.38.own_odd), channel_id=1, source_target_pairs={{0,0},{2,4},{4,2},{6,8},{8,6},{10,12},{12,10},{14,16},{16,14},{18,... | collective-permute-start | bytes 393224 | tf_op jit(solution)/shard_map/ppermute | solution.py:485
  16.5 22.9 %collective-permute-start.6 = (f32[2,16,4096]{2,1,0:T(8,128)S(1)}, f32[2,16,4096]{2,1,0:T(8,128)S(1)}, u32[]{:S(2)}, u32[]{:S(2)}) collective-permute-start(f32[2,16,4096]{2,1,0:T(8,128)S(1)} %get-tuple-element.52.inverse), channel_id=1, source_target_pairs={{0,1},{1,0},{2,3},{3,2},{4,5},{5,4},{6,7},{7,6},{8,9},{9,8},{10,11... | collective-permute-start | bytes 1572872 | tf_op jit(solution)/shard_map/ppermute | solution.py:485
  34.7 4.5 %collective-permute-start.5 = (f32[1,128]{1,0:T(1,128)S(1)}, f32[1,128]{1,0:T(1,128)S(1)}, u32[]{:S(2)}, u32[]{:S(2)}) collective-permute-start(f32[1,128]{1,0:T(1,128)S(1)} %bitcast.14), channel_id=1, source_target_pairs={{0,1},{1,0},{2,3},{3,2},{4,5},{5,4},{6,7},{7,6},{8,9},{9,8},{10,11... | collective-permute-start | bytes 1544 | tf_op jit(solution)/shard_map/ppermute | solution.py:485
  35.3 8.1 %all-to-all-start.1 = ((f32[16,1,128]{2,1,0:T(1,128)}), f32[16,1,128]{2,1,0:T(1,128)S(1)}, u32[]{:S(2)}, u32[]{:S(2)}) async-start(f32[16,1,128]{2,1,0:T(1,128)} %bitcast.6), calls=%async_computation.1 | async-start | bytes 16384 | tf_op jit(solution)/shard_map/all_to_all | solution.py:633

commit v23 on v21

--- a/solution.py
+++ b/solution.py
@@ -498,8 +498,8 @@
     if lax.axis_size(axis) != 2:
         whole = lax.psum(jnp.where(mine, shard, jnp.zeros_like(shard)), axis)
         return by_parity(odd, whole, height, 0)
-    there = by_parity(odd, paired(shard, axis, 0), height, 0)
     here = by_parity(odd, here, height, 0)
+    there = [paired(half, axis, 0) for half in here]
     return [jnp.where(mine, own, other) for own, other in zip(here, there)]
 
 
@@ -530,11 +530,11 @@
     bf16 = jnp.bfloat16
     struct = functools.partial(jax.ShapeDtypeStruct, dtype=f32)
     odd = lax.axis_index("rows") % 2 == 1
-    raw, run = lax.optimization_barrier((jnp.maximum(frames_raw, 0.0), jnp.maximum(wind_off[0], 0.0)))
+    run = lax.optimization_barrier(jnp.maximum(wind_off[0], 0.0))
+    raw = lax.optimization_barrier(jnp.maximum(frames_raw, 0.0))
     owner, offsets = lax.optimization_barrier((run_owner, jnp.clip(search_base, -8, 8)))
     own_odd, own_even = from_owner(wind_off[0], run, odd, "frames", owner[0])
     from_odd = paired(own_odd, "rows", 1)
-    from_even = paired(own_even, "rows", 0)
     frames_odd, frames_even = by_parity(odd, raw, 4, 1)
     frames_odd = paired(frames_odd, "rows", 1)
     frames_even = paired(frames_even, "rows", 0)
@@ -558,6 +558,8 @@
         cost_estimate=cost(8),
         name="smooth",
     )(raw, frames_odd, frames_even)
+    own_even, power = lax.optimization_barrier((own_even, power))
+    from_even = paired(own_even, "rows", 0)
     blocks = lax.axis_size("frames")
     def reference_scratch(height):
         return [

time: 44.3 us -> 45.9 us (1.036)
  waiting for transfers between devices: 1.11 us -> 5.86 us
  blocking collectives: 13.4 us -> 9.97 us
    ppermute x7 -> x8, waiting for transfers between devices: 0.13 us -> 4.94 us  [paired(): return lax.ppermute(value, axis, list(enumerate(partner)))]
    all_to_all x1, blocking collectives: 13.4 us -> 9.97 us  [shards(): lax.all_to_all(part, 'rows', 0, 0, axis_index_groups=order, tiled=True)]
    ppermute x7 -> x8, starting transfers between devices: 9.6 us -> 9.98 us  [paired(): return lax.ppermute(value, axis, list(enumerate(partner)))]
  transfers between devices with their start and end apart: 8 -> 9, of which waited for: 2 -> 3; matrix products, arithmetic and copies ran while one was open for 5% -> 3% of each run, Pallas kernels for 21% -> 20%
where the time goes in v23:
time: 45.9 us; the launch traced here: 45.7 us
  starting transfers between devices  14 us (31%)
  Pallas kernels  11.5 us (25%)
  blocking collectives  9.97 us (22%)
  waiting for transfers between devices  5.86 us (13%)
  other arithmetic  2.88 us (6%)
  between operations  1.44 us (3%)
    ppermute x8, starting transfers between devices, paired(): return lax.ppermute(value, axis, list(enumerate(partner)))  9.98 us
    all_to_all x1, blocking collectives, shards(): lax.all_to_all(part, 'rows', 0, 0, axis_index_groups=order, tiled=True)  9.97 us
    ppermute x8, waiting for transfers between devices, paired(): return lax.ppermute(value, axis, list(enumerate(partner)))  4.94 us
    all_to_all x1, starting transfers between devices, shards(): lax.all_to_all(part, 'rows', 0, 0, axis_index_groups=order, tiled=True)  4.03 us
    pallas_call x1, Pallas kernels, shards(): pl.pallas_call(time_kernel, out_shape=(struct((rows, columns)), struct((r...  3.06 us
    pallas_call x1, Pallas kernels, shards(): pl.pallas_call(pressure_kernel, out_shape=(struct((count, rows, columns))...  2.98 us
    pallas_call x1, Pallas kernels, shards(): pl.pallas_call(match_kernel, out_shape=(jax.ShapeDtypeStruct((tiles + 2,...  2.16 us
    pallas_call x1, Pallas kernels, shards(): pl.pallas_call(near_kernel, out_shape=(jax.ShapeDtypeStruct((tiles + 2, 2...  2.12 us
  transfers between devices with their start and end apart: 9, of which 3 were waited for; matrix products, arithmetic and copies ran while one was open for 3% of the time, Pallas kernels for 20%

profile of v23, /device:TPU:0, one launch (start us, length us, event | category | flops | bytes accessed | tf_op | source)
XLA Modules:
  0.0 45.7 jit_solution(10556761083052856027)
XLA Ops:
  0.7 1.0 %maximum_bitcast_fusion = f32[16,4096]{1,0:T(8,128)S(1)} fusion(f32[1,16,4096]{2,1,0:T(8,128)} %param.5), kind=kLoop, calls=%fused_computation | loop fusion | flops 65536 | bytes 524288 | tf_op jit(solution)/shard_map/max | solution.py:533
  1.7 3.0 %collective-permute-start.1 = (f32[8,4096]{1,0:T(8,128)S(1)}, f32[8,4096]{1,0:T(8,128)S(1)}, u32[]{:S(2)}, u32[]{:S(2)}) collective-permute-start(f32[8,4096]{1,0:T(8,128)S(1)} %get-tuple-element.64), channel_id=1, source_target_pairs={{0,1},{1,0},{2,3},{3,2},{4,5},{5,4},{6,7},{7,6},{8,9},{9,8},{10,11... | collective-permute-start | bytes 393224 | tf_op jit(solution)/shard_map/ppermute | solution.py:485
  4.7 1.1 %broadcast_maximum_fusion.frames = f32[2,16,4096]{2,1,0:T(8,128)S(1)} fusion(f32[2,16,4096]{2,1,0:T(8,128)} %param.4), kind=kLoop, calls=%fused_computation.1 | loop fusion | flops 131072 | bytes 1048576 | tf_op jit(solution)/shard_map/max | solution.py:534
  5.8 0.7 %collective-permute-start = (f32[2,4,4096]{2,1,0:T(4,128)S(1)}, f32[2,4,4096]{2,1,0:T(4,128)S(1)}, u32[]{:S(2)}, u32[]{:S(2)}) collective-permute-start(f32[2,4,4096]{2,1,0:T(4,128)S(1)} %get-tuple-element.62), channel_id=1, source_target_pairs={{0,0},{2,4},{4,2},{6,8},{8,6},{10,12},{12,10},{14,16},{16,14},{18,... | collective-permute-start | bytes 393224 | tf_op jit(solution)/shard_map/ppermute | solution.py:485
  6.5 2.9 %collective-permute-start.2 = (f32[2,4,4096]{2,1,0:T(4,128)S(1)}, f32[2,4,4096]{2,1,0:T(4,128)S(1)}, u32[]{:S(2)}, u32[]{:S(2)}) collective-permute-start(f32[2,4,4096]{2,1,0:T(4,128)S(1)} %get-tuple-element.61), channel_id=1, source_target_pairs={{0,2},{2,0},{4,6},{6,4},{8,10},{10,8},{12,14},{14,12},{16,18},{18,... | collective-permute-start | bytes 393224 | tf_op jit(solution)/shard_map/ppermute | solution.py:485
  9.4 0.5 %collective-permute-start.4 = (f32[8,4096]{1,0:T(8,128)S(1)}, f32[8,4096]{1,0:T(8,128)S(1)}, u32[]{:S(2)}, u32[]{:S(2)}) collective-permute-start(f32[8,4096]{1,0:T(8,128)S(1)} %get-tuple-element.63), channel_id=1, source_target_pairs={{0,1},{1,0},{2,3},{3,2},{4,5},{5,4},{6,7},{7,6},{8,9},{9,8},{10,11... | collective-permute-start | bytes 393224 | tf_op jit(solution)/shard_map/ppermute | solution.py:485
  10.6 0.0 collective-permute-done.1
  10.6 0.7 %collective-permute-start.3 = (f32[8,4096]{1,0:T(8,128)S(1)}, f32[8,4096]{1,0:T(8,128)S(1)}, u32[]{:S(2)}, u32[]{:S(2)}) collective-permute-start(f32[8,4096]{1,0:T(8,128)S(1)} %broadcast_select_fusion.1.own_odd), channel_id=1, source_target_pairs={{0,0},{2,4},{4,2},{6,8},{8,6},{10,12},{12,10},{14,16},{16,14},{18,... | collective-permute-start | bytes 393224 | tf_op jit(solution)/shard_map/ppermute | solution.py:485
  11.3 3.6 %collective-permute-done.4 = f32[8,4096]{1,0:T(8,128)S(1)} collective-permute-done((f32[8,4096]{1,0:T(8,128)S(1)}, f32[8,4096]{1,0:T(8,128)S(1)}, u32[]{:S(2)}, u32[]{:S(2)}) %collective-permute-start.4) | collective-permute-done | bytes 131104 | tf_op jit(solution)/shard_map/ppermute | solution.py:485
  14.9 0.0 collective-permute-done.from_odd
  14.9 1.2 %smooth.1 = (f32[2,16,4096]{2,1,0:T(8,128)S(1)}, bf16[256,4352]{1,0:T(8,128)(2,1)S(1)}, f32[16,128]{1,0:T(8,128)S(1)}, bf16[512,256]{1,0:T(8,128)(2,1)S(1)}) custom-call(f32[2,16,4096]{2,1,0:T(8,128)S(1)} %broadcast_maximum_fusion.frames, f32[2,4,4096]{2,1,0:T(4,128)S(1)} %collective-permute-done.from_odd, f32[2,4,4096]{2,1,0:T(4,128)S(1)} %collective-permute-done.2.from_even), custom_call_target="tpu_custom_call" | custom-call | bytes 8388608 | tf_op jit(solution)/shard_map/smooth/pallas_call | solution.py:542
  16.1 0.1 collective-permute-start.5
  16.2 1.3 %collective-permute-done.5.from_even = f32[8,4096]{1,0:T(8,128)S(1)} collective-permute-done((f32[8,4096]{1,0:T(8,128)S(1)}, f32[8,4096]{1,0:T(8,128)S(1)}, u32[]{:S(2)}, u32[]{:S(2)}) %collective-permute-start.5) | collective-permute-done | bytes 131104 | tf_op jit(solution)/shard_map/ppermute | solution.py:485
  17.5 2.1 %near.1 = (bf16[34,32,128]{2,1,0:T(8,128)(2,1)S(1)}, f32[128,128]{1,0:T(8,128)S(1)}, f32[8,128]{1,0:T(8,128)S(1)}) custom-call(s32[1,2]{1,0:T(1,128)S(1)} %broadcast_clamp_fusion.base, f32[8,4096]{1,0:T(8,128)S(1)} %broadcast_select_fusion.1.own_odd, f32[8,4096]{1,0:T(8,128)S(1)} %broadcast_select_fusion.own_even, ...), custom_call_target="tpu_custom_call" | custom-call | bytes 8388608 | tf_op jit(solution)/shard_map/near/pallas_call | solution.py:573
  19.7 2.2 %match.1 = (bf16[34,16,128]{2,1,0:T(8,128)(2,1)S(1)}, f32[16,128]{1,0:T(8,128)S(1)}) custom-call(s32[1,2]{1,0:T(1,128)S(1)} %broadcast_clamp_fusion.base, f32[8,4096]{1,0:T(8,128)S(1)} %broadcast_select_fusion.1.own_odd, f32[8,4096]{1,0:T(8,128)S(1)} %collective-permute-done.3.from_odd, f32[128,128]{1,0:T(8,128)S(1)} %get-tuple-element.41.near_lags, ...), custom_call_target="tpu_custom_call" | custom-call | bytes 8388608 | tf_op jit(solution)/shard_map/match/pallas_call | solution.py:587
  21.8 0.6 %collective-permute-start.7 = (f32[2,16,4096]{2,1,0:T(8,128)S(1)}, f32[2,16,4096]{2,1,0:T(8,128)S(1)}, u32[]{:S(2)}, u32[]{:S(2)}) collective-permute-start(f32[2,16,4096]{2,1,0:T(8,128)S(1)} %get-tuple-element.52.inverse), channel_id=1, source_target_pairs={{0,1},{1,0},{2,3},{3,2},{4,5},{5,4},{6,7},{7,6},{8,9},{9,8},{10,11... | collective-permute-start | bytes 1572872 | tf_op jit(solution)/shard_map/ppermute | solution.py:485
  22.4 10.0 %all_to_all.21 = f32[16,1,128]{2,1,0:T(1,128)S(1)} all-to-all(f32[16,1,128]{2,1,0:T(1,128)S(1)} %bitcast.12), channel_id=1, replica_groups={{14,16,12,18,10,20,8,22,6,24,4,26,2,28,0,30},{15,17,13,19,11,21,9,23,7,..., dimensions={0} | all-to-all | bytes 16384 | tf_op jit(solution)/shard_map/all_to_all | solution.py:601
  32.4 3.0 %pressure.1 = (f32[2,16,4096]{2,1,0:T(8,128)}, f32[2,16,4096]{2,1,0:T(8,128)S(1)}, f32[16,128]{1,0:T(8,128)}) custom-call(s32[1,2]{1,0:T(1,128)S(1)} %broadcast_clamp_fusion.base, f32[1,128]{1,0:T(1,128)S(1)} %bitcast.13, bf16[34,32,128]{2,1,0:T(8,128)(2,1)S(1)} %get-tuple-element.46.clean, bf16[34,16,128]{2,1,0:T(8,128)(2,1)S(1)} %get-tuple-element.47.other, ...), custom_call_target="tpu_custom_call" | custom-call | bytes 12582912 | tf_op jit(solution)/shard_map/pressure/pallas_call | solution.py:605
  35.4 1.6 %collective-permute-start.6 = (f32[1,128]{1,0:T(1,128)S(1)}, f32[1,128]{1,0:T(1,128)S(1)}, u32[]{:S(2)}, u32[]{:S(2)}) collective-permute-start(f32[1,128]{1,0:T(1,128)S(1)} %bitcast.14), channel_id=1, source_target_pairs={{0,1},{1,0},{2,3},{3,2},{4,5},{5,4},{6,7},{7,6},{8,9},{9,8},{10,11... | collective-permute-start | bytes 1544 | tf_op jit(solution)/shard_map/ppermute | solution.py:485
  36.9 4.0 %all-to-all-start.1 = ((f32[16,1,128]{2,1,0:T(1,128)}), f32[16,1,128]{2,1,0:T(1,128)S(1)}, u32[]{:S(2)}, u32[]{:S(2)}) async-start(f32[16,1,128]{2,1,0:T(1,128)} %bitcast.6), calls=%async_computation.1 | async-start | bytes 16384 | tf_op jit(solution)/shard_map/all_to_all | solution.py:634
  41.0 0.1 multiply_convert_fusion.base
  41.1 3.1 %time.1 = (f32[16,4096]{1,0:T(8,128)}, f32[16,4096]{1,0:T(8,128)}) custom-call(s32[1,2]{1,0:T(1,128)S(1)} %multiply_convert_fusion.base, f32[1,128]{1,0:T(1,128)S(1)} %collective-permute-done.6.totals, bf16[34,32,128]{2,1,0:T(8,128)(2,1)S(1)} %get-tuple-element.46.clean, bf16[34,16,128]{2,1,0:T(8,128)(2,1)S(1)} %get-tuple-element.47.other, ...), custom_call_target="tpu_custom_call" | custom-call | bytes 12582912 | tf_op jit(solution)/shard_map/time/pallas_call | solution.py:619
  44.1 0.9 %all-to-all-done.1 = f32[16,1,128]{2,1,0:T(1,128)S(1)} async-done(((f32[16,1,128]{2,1,0:T(1,128)}), f32[16,1,128]{2,1,0:T(1,128)S(1)}, u32[]{:S(2)}, u32[]{:S(2)}) %all-to-all-start.1) | async-done | bytes 8224 | tf_op jit(solution)/shard_map/all_to_all | solution.py:634
  45.1 0.6 %subtract_sqrt_fusion = (f32[2]{0:T(128)}, f32[2]{0:T(128)}) fusion(f32[128]{0:T(128)S(1)} %reduce_sum.19), kind=kLoop, calls=%fused_computation.8 | loop fusion | flops 8 | bytes 32 | tf_op jit(solution)/shard_map/sqrt | solution.py:639
  (13 shorter events, 0.2 us)
Async XLA Ops:
  0.6 15.6 %copy-start = (s32[1,2]{1,0:T(1,128)S(1)}, s32[1,2]{1,0:T(1,128)}, u32[]{:S(2)}) copy-start(s32[1,2]{1,0:T(1,128)} %param.7) | copy-start | bytes 28
  1.7 8.9 %collective-permute-start.1 = (f32[8,4096]{1,0:T(8,128)S(1)}, f32[8,4096]{1,0:T(8,128)S(1)}, u32[]{:S(2)}, u32[]{:S(2)}) collective-permute-start(f32[8,4096]{1,0:T(8,128)S(1)} %get-tuple-element.64), channel_id=1, source_target_pairs={{0,1},{1,0},{2,3},{3,2},{4,5},{5,4},{6,7},{7,6},{8,9},{9,8},{10,11... | collective-permute-start | bytes 393224 | tf_op jit(solution)/shard_map/ppermute | solution.py:485
  5.8 9.1 %collective-permute-start = (f32[2,4,4096]{2,1,0:T(4,128)S(1)}, f32[2,4,4096]{2,1,0:T(4,128)S(1)}, u32[]{:S(2)}, u32[]{:S(2)}) collective-permute-start(f32[2,4,4096]{2,1,0:T(4,128)S(1)} %get-tuple-element.62), channel_id=1, source_target_pairs={{0,0},{2,4},{4,2},{6,8},{8,6},{10,12},{12,10},{14,16},{16,14},{18,... | collective-permute-start | bytes 393224 | tf_op jit(solution)/shard_map/ppermute | solution.py:485
  6.5 8.4 %collective-permute-start.2 = (f32[2,4,4096]{2,1,0:T(4,128)S(1)}, f32[2,4,4096]{2,1,0:T(4,128)S(1)}, u32[]{:S(2)}, u32[]{:S(2)}) collective-permute-start(f32[2,4,4096]{2,1,0:T(4,128)S(1)} %get-tuple-element.61), channel_id=1, source_target_pairs={{0,2},{2,0},{4,6},{6,4},{8,10},{10,8},{12,14},{14,12},{16,18},{18,... | collective-permute-start | bytes 393224 | tf_op jit(solution)/shard_map/ppermute | solution.py:485
  9.4 5.5 %collective-permute-start.4 = (f32[8,4096]{1,0:T(8,128)S(1)}, f32[8,4096]{1,0:T(8,128)S(1)}, u32[]{:S(2)}, u32[]{:S(2)}) collective-permute-start(f32[8,4096]{1,0:T(8,128)S(1)} %get-tuple-element.63), channel_id=1, source_target_pairs={{0,1},{1,0},{2,3},{3,2},{4,5},{5,4},{6,7},{7,6},{8,9},{9,8},{10,11... | collective-permute-start | bytes 393224 | tf_op jit(solution)/shard_map/ppermute | solution.py:485
  10.6 9.0 %collective-permute-start.3 = (f32[8,4096]{1,0:T(8,128)S(1)}, f32[8,4096]{1,0:T(8,128)S(1)}, u32[]{:S(2)}, u32[]{:S(2)}) collective-permute-start(f32[8,4096]{1,0:T(8,128)S(1)} %broadcast_select_fusion.1.own_odd), channel_id=1, source_target_pairs={{0,0},{2,4},{4,2},{6,8},{8,6},{10,12},{12,10},{14,16},{16,14},{18,... | collective-permute-start | bytes 393224 | tf_op jit(solution)/shard_map/ppermute | solution.py:485
  16.1 1.4 %collective-permute-start.5 = (f32[8,4096]{1,0:T(8,128)S(1)}, f32[8,4096]{1,0:T(8,128)S(1)}, u32[]{:S(2)}, u32[]{:S(2)}) collective-permute-start(f32[8,4096]{1,0:T(8,128)S(1)} %broadcast_select_fusion.own_even), channel_id=1, source_target_pairs={{0,2},{2,0},{4,6},{6,4},{8,10},{10,8},{12,14},{14,12},{16,18},{18,... | collective-permute-start | bytes 393224 | tf_op jit(solution)/shard_map/ppermute | solution.py:485
  21.8 19.2 %collective-permute-start.7 = (f32[2,16,4096]{2,1,0:T(8,128)S(1)}, f32[2,16,4096]{2,1,0:T(8,128)S(1)}, u32[]{:S(2)}, u32[]{:S(2)}) collective-permute-start(f32[2,16,4096]{2,1,0:T(8,128)S(1)} %get-tuple-element.52.inverse), channel_id=1, source_target_pairs={{0,1},{1,0},{2,3},{3,2},{4,5},{5,4},{6,7},{7,6},{8,9},{9,8},{10,11... | collective-permute-start | bytes 1572872 | tf_op jit(solution)/shard_map/ppermute | solution.py:485
  35.4 5.6 %collective-permute-start.6 = (f32[1,128]{1,0:T(1,128)S(1)}, f32[1,128]{1,0:T(1,128)S(1)}, u32[]{:S(2)}, u32[]{:S(2)}) collective-permute-start(f32[1,128]{1,0:T(1,128)S(1)} %bitcast.14), channel_id=1, source_target_pairs={{0,1},{1,0},{2,3},{3,2},{4,5},{5,4},{6,7},{7,6},{8,9},{9,8},{10,11... | collective-permute-start | bytes 1544 | tf_op jit(solution)/shard_map/ppermute | solution.py:485
  36.9 8.1 %all-to-all-start.1 = ((f32[16,1,128]{2,1,0:T(1,128)}), f32[16,1,128]{2,1,0:T(1,128)S(1)}, u32[]{:S(2)}, u32[]{:S(2)}) async-start(f32[16,1,128]{2,1,0:T(1,128)} %bitcast.6), calls=%async_computation.1 | async-start | bytes 16384 | tf_op jit(solution)/shard_map/all_to_all | solution.py:634

commit v24 on v21

--- a/solution.py
+++ b/solution.py
@@ -503,9 +503,8 @@
     return [jnp.where(mine, own, other) for own, other in zip(here, there)]
 
 
-def middle_first(size):
-    order = sorted(range(size), key=lambda i: (abs(2 * i + 1 - size), i))
-    return order
+def begun_at(first, size):
+    return [[(i + first) % size for i in range(size)]]
 
 
 def total_over(value, axis):
@@ -595,8 +594,7 @@
     if blocks == 2:
         inverse_out, part = lax.optimization_barrier((inverse, part))
         other_inverse = paired(inverse_out, "frames", 0)
-    order = [middle_first(size)]
-    parts = lax.all_to_all(part, "rows", 0, 0, axis_index_groups=order, tiled=True)
+    parts = lax.all_to_all(part, "rows", 0, 0, axis_index_groups=begun_at(size // 2, size), tiled=True)
     totals = jnp.sum(parts, axis=0, keepdims=True)
     depth = -(-reach * 2 * wide // lanes) * lanes
     spread = pltpu.VMEM((depth, columns), bf16)
@@ -629,7 +627,7 @@
         total_frames = count * blocks
         time_mean = whole[0] / total_frames
         time_rms = jnp.sqrt(jnp.maximum(whole[1] / total_frames - time_mean * time_mean, 0.0))
-    sums = lax.all_to_all(part, "rows", 0, 0, axis_index_groups=order, tiled=True)
+    sums = lax.all_to_all(part, "rows", 0, 0, axis_index_groups=begun_at(size // 2 + 1, size), tiled=True)
     sums, time_mean, time_rms = lax.optimization_barrier((sums, time_mean, time_rms))
     spatial = jnp.sum(sums, axis=0)
     cell_count = rows * columns * size

time: 44.3 us -> 43.7 us (0.986)
  blocking collectives: 13.4 us -> 12.8 us
    all_to_all x1, blocking collectives: 13.4 us -> 12.8 us  [shards(): lax.all_to_all(part, 'rows', 0, 0, axis_index_groups=begun_at(size // 2,...]
  transfers between devices with their start and end apart: 8 -> 8, of which waited for: 2 -> 2; matrix products, arithmetic and copies ran while one was open for 5% -> 5% of each run, Pallas kernels for 21% -> 22%
where the time goes in v24:
time: 43.7 us; the launch traced here: 43.3 us
  starting transfers between devices  13.5 us (31%)
  blocking collectives  12.8 us (29%)
  Pallas kernels  11.5 us (26%)
  other arithmetic  2.89 us (7%)
  between operations  1.42 us (3%)
  waiting for transfers between devices  1.17 us (3%)
    all_to_all x1, blocking collectives, shards(): lax.all_to_all(part, 'rows', 0, 0, axis_index_groups=begun_at(size // 2,...  12.8 us
    ppermute x7, starting transfers between devices, paired(): return lax.ppermute(value, axis, list(enumerate(partner)))  9.61 us
    all_to_all x1, starting transfers between devices, shards(): lax.all_to_all(part, 'rows', 0, 0, axis_index_groups=begun_at(size // 2 +...  3.94 us
    pallas_call x1, Pallas kernels, shards(): pl.pallas_call(time_kernel, out_shape=(struct((rows, columns)), struct((r...  3.02 us
    pallas_call x1, Pallas kernels, shards(): pl.pallas_call(pressure_kernel, out_shape=(struct((count, rows, columns))...  3.02 us
    pallas_call x1, Pallas kernels, shards(): pl.pallas_call(match_kernel, out_shape=(jax.ShapeDtypeStruct((tiles + 2,...  2.16 us
    pallas_call x1, Pallas kernels, shards(): pl.pallas_call(near_kernel, out_shape=(jax.ShapeDtypeStruct((tiles + 2, 2...  2.13 us
    pallas_call x1, Pallas kernels, shards(): pl.pallas_call(smooth_kernel, out_shape=(struct((count, rows, columns)),...  1.17 us
  transfers between devices with their start and end apart: 8, of which 2 were waited for; matrix products, arithmetic and copies ran while one was open for 5% of the time, Pallas kernels for 22%

profile of v24, /device:TPU:0, one launch (start us, length us, event | category | flops | bytes accessed | tf_op | source)
XLA Modules:
  0.0 43.3 jit_solution(13839378997458307077)
XLA Ops:
  0.6 3.0 %collective-permute-start.1 = (f32[16,4096]{1,0:T(8,128)}, f32[16,4096]{1,0:T(8,128)S(1)}, u32[]{:S(2)}, u32[]{:S(2)}) collective-permute-start(f32[16,4096]{1,0:T(8,128)} %bitcast.15), channel_id=1, source_target_pairs={{0,1},{1,0},{2,3},{3,2},{4,5},{5,4},{6,7},{7,6},{8,9},{9,8},{10,11... | collective-permute-start | bytes 786440 | tf_op jit(solution)/shard_map/ppermute | solution.py:485
  3.7 1.0 %broadcast_maximum_fusion.1 = f32[16,4096]{1,0:T(8,128)S(1)} fusion(f32[1,16,4096]{2,1,0:T(8,128)} %param.5), kind=kLoop, calls=%fused_computation.3 | loop fusion | flops 65536 | bytes 524288 | tf_op jit(solution)/shard_map/max | solution.py:532
  4.7 1.1 %broadcast_maximum_fusion.frames = f32[2,16,4096]{2,1,0:T(8,128)S(1)} fusion(f32[2,16,4096]{2,1,0:T(8,128)} %param.4), kind=kLoop, calls=%fused_computation | loop fusion | flops 131072 | bytes 1048576 | tf_op jit(solution)/shard_map/max | solution.py:532
  5.8 0.7 %collective-permute-start = (f32[2,4,4096]{2,1,0:T(4,128)S(1)}, f32[2,4,4096]{2,1,0:T(4,128)S(1)}, u32[]{:S(2)}, u32[]{:S(2)}) collective-permute-start(f32[2,4,4096]{2,1,0:T(4,128)S(1)} %get-tuple-element.64), channel_id=1, source_target_pairs={{0,0},{2,4},{4,2},{6,8},{8,6},{10,12},{12,10},{14,16},{16,14},{18,... | collective-permute-start | bytes 393224 | tf_op jit(solution)/shard_map/ppermute | solution.py:485
  6.5 2.9 %collective-permute-start.2 = (f32[2,4,4096]{2,1,0:T(4,128)S(1)}, f32[2,4,4096]{2,1,0:T(4,128)S(1)}, u32[]{:S(2)}, u32[]{:S(2)}) collective-permute-start(f32[2,4,4096]{2,1,0:T(4,128)S(1)} %get-tuple-element.63), channel_id=1, source_target_pairs={{0,2},{2,0},{4,6},{6,4},{8,10},{10,8},{12,14},{14,12},{16,18},{18,... | collective-permute-start | bytes 393224 | tf_op jit(solution)/shard_map/ppermute | solution.py:485
  10.1 0.1 collective-permute-done.1
  10.2 0.1 collective-permute-start.4
  10.3 0.7 %collective-permute-start.3 = (f32[8,4096]{1,0:T(8,128)S(1)}, f32[8,4096]{1,0:T(8,128)S(1)}, u32[]{:S(2)}, u32[]{:S(2)}) collective-permute-start(f32[8,4096]{1,0:T(8,128)S(1)} %get-tuple-element.38.own_odd), channel_id=1, source_target_pairs={{0,0},{2,4},{4,2},{6,8},{8,6},{10,12},{12,10},{14,16},{16,14},{18,... | collective-permute-start | bytes 393224 | tf_op jit(solution)/shard_map/ppermute | solution.py:485
  11.0 0.0 collective-permute-done.from_odd
  11.0 0.0 collective-permute-done.2.from_even
  11.0 1.2 %smooth.1 = (f32[2,16,4096]{2,1,0:T(8,128)S(1)}, bf16[256,4352]{1,0:T(8,128)(2,1)S(1)}, f32[16,128]{1,0:T(8,128)S(1)}, bf16[512,256]{1,0:T(8,128)(2,1)S(1)}) custom-call(f32[2,16,4096]{2,1,0:T(8,128)S(1)} %broadcast_maximum_fusion.frames, f32[2,4,4096]{2,1,0:T(4,128)S(1)} %collective-permute-done.from_odd, f32[2,4,4096]{2,1,0:T(4,128)S(1)} %collective-permute-done.2.from_even), custom_call_target="tpu_custom_call" | custom-call | bytes 8388608 | tf_op jit(solution)/shard_map/smooth/pallas_call | solution.py:541
  12.2 0.0 collective-permute-done.4.from_even
  12.2 2.1 %near.1 = (bf16[34,32,128]{2,1,0:T(8,128)(2,1)S(1)}, f32[128,128]{1,0:T(8,128)S(1)}, f32[8,128]{1,0:T(8,128)S(1)}) custom-call(s32[1,2]{1,0:T(1,128)S(1)} %broadcast_clamp_fusion.base, f32[8,4096]{1,0:T(8,128)S(1)} %get-tuple-element.38.own_odd, f32[8,4096]{1,0:T(8,128)S(1)} %get-tuple-element.61.own_even, f32[8,4096]{1,0:T(8,128)S(1)} %collective-permute-done.4.from_even, ...), custom_call_target="tpu_custom_call" | custom-call | bytes 8388608 | tf_op jit(solution)/shard_map/near/pallas_call | solution.py:570
  14.3 0.0 collective-permute-done.3.from_odd
  14.4 2.2 %match.1 = (bf16[34,16,128]{2,1,0:T(8,128)(2,1)S(1)}, f32[16,128]{1,0:T(8,128)S(1)}) custom-call(s32[1,2]{1,0:T(1,128)S(1)} %broadcast_clamp_fusion.base, f32[8,4096]{1,0:T(8,128)S(1)} %get-tuple-element.38.own_odd, f32[8,4096]{1,0:T(8,128)S(1)} %collective-permute-done.3.from_odd, f32[128,128]{1,0:T(8,128)S(1)} %get-tuple-element.41.near_lags, ...), custom_call_target="tpu_custom_call" | custom-call | bytes 8388608 | tf_op jit(solution)/shard_map/match/pallas_call | solution.py:584
  16.5 1.8 %collective-permute-start.6 = (f32[2,16,4096]{2,1,0:T(8,128)S(1)}, f32[2,16,4096]{2,1,0:T(8,128)S(1)}, u32[]{:S(2)}, u32[]{:S(2)}) collective-permute-start(f32[2,16,4096]{2,1,0:T(8,128)S(1)} %get-tuple-element.52.inverse), channel_id=1, source_target_pairs={{0,1},{1,0},{2,3},{3,2},{4,5},{5,4},{6,7},{7,6},{8,9},{9,8},{10,11... | collective-permute-start | bytes 1572872 | tf_op jit(solution)/shard_map/ppermute | solution.py:485
  18.3 12.8 %all_to_all.21 = f32[16,1,128]{2,1,0:T(1,128)S(1)} all-to-all(f32[16,1,128]{2,1,0:T(1,128)S(1)} %bitcast.12), channel_id=1, replica_groups={{16,18,20,22,24,26,28,30,0,2,4,6,8,10,12,14},{17,19,21,23,25,27,29,31,1..., dimensions={0} | all-to-all | bytes 16384 | tf_op jit(solution)/shard_map/all_to_all | solution.py:597
  31.2 3.0 %pressure.1 = (f32[2,16,4096]{2,1,0:T(8,128)}, f32[2,16,4096]{2,1,0:T(8,128)S(1)}, f32[16,128]{1,0:T(8,128)}) custom-call(s32[1,2]{1,0:T(1,128)S(1)} %broadcast_clamp_fusion.base, f32[1,128]{1,0:T(1,128)S(1)} %bitcast.13, bf16[34,32,128]{2,1,0:T(8,128)(2,1)S(1)} %get-tuple-element.46.clean, bf16[34,16,128]{2,1,0:T(8,128)(2,1)S(1)} %get-tuple-element.47.other, ...), custom_call_target="tpu_custom_call" | custom-call | bytes 12582912 | tf_op jit(solution)/shard_map/pressure/pallas_call | solution.py:601
  34.2 0.5 %collective-permute-start.5 = (f32[1,128]{1,0:T(1,128)S(1)}, f32[1,128]{1,0:T(1,128)S(1)}, u32[]{:S(2)}, u32[]{:S(2)}) collective-permute-start(f32[1,128]{1,0:T(1,128)S(1)} %bitcast.14), channel_id=1, source_target_pairs={{0,1},{1,0},{2,3},{3,2},{4,5},{5,4},{6,7},{7,6},{8,9},{9,8},{10,11... | collective-permute-start | bytes 1544 | tf_op jit(solution)/shard_map/ppermute | solution.py:485
  34.7 3.9 %all-to-all-start.1 = ((f32[16,1,128]{2,1,0:T(1,128)}), f32[16,1,128]{2,1,0:T(1,128)S(1)}, u32[]{:S(2)}, u32[]{:S(2)}) async-start(f32[16,1,128]{2,1,0:T(1,128)} %bitcast.6), calls=%async_computation.1 | async-start | bytes 16384 | tf_op jit(solution)/shard_map/all_to_all | solution.py:630
  38.6 0.1 multiply_convert_fusion.base
  38.7 3.0 %time.1 = (f32[16,4096]{1,0:T(8,128)}, f32[16,4096]{1,0:T(8,128)}) custom-call(s32[1,2]{1,0:T(1,128)S(1)} %multiply_convert_fusion.base, f32[1,128]{1,0:T(1,128)S(1)} %collective-permute-done.5.totals, bf16[34,32,128]{2,1,0:T(8,128)(2,1)S(1)} %get-tuple-element.46.clean, bf16[34,16,128]{2,1,0:T(8,128)(2,1)S(1)} %get-tuple-element.47.other, ...), custom_call_target="tpu_custom_call" | custom-call | bytes 12582912 | tf_op jit(solution)/shard_map/time/pallas_call | solution.py:615
  41.7 1.0 %all-to-all-done.1 = f32[16,1,128]{2,1,0:T(1,128)S(1)} async-done(((f32[16,1,128]{2,1,0:T(1,128)}), f32[16,1,128]{2,1,0:T(1,128)S(1)}, u32[]{:S(2)}, u32[]{:S(2)}) %all-to-all-start.1) | async-done | bytes 8224 | tf_op jit(solution)/shard_map/all_to_all | solution.py:630
  42.7 0.6 %subtract_sqrt_fusion = (f32[2]{0:T(128)}, f32[2]{0:T(128)}) fusion(f32[128]{0:T(128)S(1)} %reduce_sum.19), kind=kLoop, calls=%fused_computation.6 | loop fusion | flops 8 | bytes 32 | tf_op jit(solution)/shard_map/sqrt | solution.py:635
  (9 shorter events, 0.1 us)
Async XLA Ops:
  0.6 10.4 %copy-start = (s32[1,2]{1,0:T(1,128)S(1)}, s32[1,2]{1,0:T(1,128)}, u32[]{:S(2)}) copy-start(s32[1,2]{1,0:T(1,128)} %param.7) | copy-start | bytes 28
  0.6 9.5 %collective-permute-start.1 = (f32[16,4096]{1,0:T(8,128)}, f32[16,4096]{1,0:T(8,128)S(1)}, u32[]{:S(2)}, u32[]{:S(2)}) collective-permute-start(f32[16,4096]{1,0:T(8,128)} %bitcast.15), channel_id=1, source_target_pairs={{0,1},{1,0},{2,3},{3,2},{4,5},{5,4},{6,7},{7,6},{8,9},{9,8},{10,11... | collective-permute-start | bytes 786440 | tf_op jit(solution)/shard_map/ppermute | solution.py:485
  5.8 5.2 %collective-permute-start = (f32[2,4,4096]{2,1,0:T(4,128)S(1)}, f32[2,4,4096]{2,1,0:T(4,128)S(1)}, u32[]{:S(2)}, u32[]{:S(2)}) collective-permute-start(f32[2,4,4096]{2,1,0:T(4,128)S(1)} %get-tuple-element.64), channel_id=1, source_target_pairs={{0,0},{2,4},{4,2},{6,8},{8,6},{10,12},{12,10},{14,16},{16,14},{18,... | collective-permute-start | bytes 393224 | tf_op jit(solution)/shard_map/ppermute | solution.py:485
  6.5 4.5 %collective-permute-start.2 = (f32[2,4,4096]{2,1,0:T(4,128)S(1)}, f32[2,4,4096]{2,1,0:T(4,128)S(1)}, u32[]{:S(2)}, u32[]{:S(2)}) collective-permute-start(f32[2,4,4096]{2,1,0:T(4,128)S(1)} %get-tuple-element.63), channel_id=1, source_target_pairs={{0,2},{2,0},{4,6},{6,4},{8,10},{10,8},{12,14},{14,12},{16,18},{18,... | collective-permute-start | bytes 393224 | tf_op jit(solution)/shard_map/ppermute | solution.py:485
  10.2 2.0 %collective-permute-start.4 = (f32[8,4096]{1,0:T(8,128)S(1)}, f32[8,4096]{1,0:T(8,128)S(1)}, u32[]{:S(2)}, u32[]{:S(2)}) collective-permute-start(f32[8,4096]{1,0:T(8,128)S(1)} %get-tuple-element.61.own_even), channel_id=1, source_target_pairs={{0,2},{2,0},{4,6},{6,4},{8,10},{10,8},{12,14},{14,12},{16,18},{18,... | collective-permute-start | bytes 393224 | tf_op jit(solution)/shard_map/ppermute | solution.py:485
  10.3 4.0 %collective-permute-start.3 = (f32[8,4096]{1,0:T(8,128)S(1)}, f32[8,4096]{1,0:T(8,128)S(1)}, u32[]{:S(2)}, u32[]{:S(2)}) collective-permute-start(f32[8,4096]{1,0:T(8,128)S(1)} %get-tuple-element.38.own_odd), channel_id=1, source_target_pairs={{0,0},{2,4},{4,2},{6,8},{8,6},{10,12},{12,10},{14,16},{16,14},{18,... | collective-permute-start | bytes 393224 | tf_op jit(solution)/shard_map/ppermute | solution.py:485
  16.5 22.2 %collective-permute-start.6 = (f32[2,16,4096]{2,1,0:T(8,128)S(1)}, f32[2,16,4096]{2,1,0:T(8,128)S(1)}, u32[]{:S(2)}, u32[]{:S(2)}) collective-permute-start(f32[2,16,4096]{2,1,0:T(8,128)S(1)} %get-tuple-element.52.inverse), channel_id=1, source_target_pairs={{0,1},{1,0},{2,3},{3,2},{4,5},{5,4},{6,7},{7,6},{8,9},{9,8},{10,11... | collective-permute-start | bytes 1572872 | tf_op jit(solution)/shard_map/ppermute | solution.py:485
  34.2 4.4 %collective-permute-start.5 = (f32[1,128]{1,0:T(1,128)S(1)}, f32[1,128]{1,0:T(1,128)S(1)}, u32[]{:S(2)}, u32[]{:S(2)}) collective-permute-start(f32[1,128]{1,0:T(1,128)S(1)} %bitcast.14), channel_id=1, source_target_pairs={{0,1},{1,0},{2,3},{3,2},{4,5},{5,4},{6,7},{7,6},{8,9},{9,8},{10,11... | collective-permute-start | bytes 1544 | tf_op jit(solution)/shard_map/ppermute | solution.py:485
  34.7 8.1 %all-to-all-start.1 = ((f32[16,1,128]{2,1,0:T(1,128)}), f32[16,1,128]{2,1,0:T(1,128)S(1)}, u32[]{:S(2)}, u32[]{:S(2)}) async-start(f32[16,1,128]{2,1,0:T(1,128)} %bitcast.6), calls=%async_computation.1 | async-start | bytes 16384 | tf_op jit(solution)/shard_map/all_to_all | solution.py:630

commit v25 on v24

--- a/solution.py
+++ b/solution.py
@@ -594,7 +594,7 @@
     if blocks == 2:
         inverse_out, part = lax.optimization_barrier((inverse, part))
         other_inverse = paired(inverse_out, "frames", 0)
-    parts = lax.all_to_all(part, "rows", 0, 0, axis_index_groups=begun_at(size // 2, size), tiled=True)
+    parts = lax.all_to_all(part, "rows", 0, 0, axis_index_groups=begun_at(size // 2 + 1, size), tiled=True)
     totals = jnp.sum(parts, axis=0, keepdims=True)
     depth = -(-reach * 2 * wide // lanes) * lanes
     spread = pltpu.VMEM((depth, columns), bf16)
@@ -627,7 +627,7 @@
         total_frames = count * blocks
         time_mean = whole[0] / total_frames
         time_rms = jnp.sqrt(jnp.maximum(whole[1] / total_frames - time_mean * time_mean, 0.0))
-    sums = lax.all_to_all(part, "rows", 0, 0, axis_index_groups=begun_at(size // 2 + 1, size), tiled=True)
+    sums = lax.all_to_all(part, "rows", 0, 0, axis_index_groups=begun_at(size // 2, size), tiled=True)
     sums, time_mean, time_rms = lax.optimization_barrier((sums, time_mean, time_rms))
     spatial = jnp.sum(sums, axis=0)
     cell_count = rows * columns * size

time: 43.7 us -> 44.2 us (1.011)
  starting transfers between devices: 13.5 us -> 14.4 us
    all_to_all x1, starting transfers between devices: 3.94 us -> 4.7 us  [shards(): lax.all_to_all(part, 'rows', 0, 0, axis_index_groups=begun_at(size // 2,...]
  transfers between devices with their start and end apart: 8 -> 8, of which waited for: 2 -> 2; matrix products, arithmetic and copies ran while one was open for 5% -> 5% of each run, Pallas kernels for 22% -> 21%
where the time goes in v25:
time: 44.2 us; the launch traced here: 43.9 us
  starting transfers between devices  14.4 us (33%)
  blocking collectives  12.6 us (29%)
  Pallas kernels  11.5 us (26%)
  other arithmetic  2.89 us (7%)
  between operations  1.42 us (3%)
  waiting for transfers between devices  1.11 us (3%)
    all_to_all x1, blocking collectives, shards(): lax.all_to_all(part, 'rows', 0, 0, axis_index_groups=begun_at(size // 2 +...  12.6 us
    ppermute x7, starting transfers between devices, paired(): return lax.ppermute(value, axis, list(enumerate(partner)))  9.7 us
    all_to_all x1, starting transfers between devices, shards(): lax.all_to_all(part, 'rows', 0, 0, axis_index_groups=begun_at(size // 2,...  4.7 us
    pallas_call x1, Pallas kernels, shards(): pl.pallas_call(time_kernel, out_shape=(struct((rows, columns)), struct((r...  3.06 us
    pallas_call x1, Pallas kernels, shards(): pl.pallas_call(pressure_kernel, out_shape=(struct((count, rows, columns))...  2.98 us
    pallas_call x1, Pallas kernels, shards(): pl.pallas_call(match_kernel, out_shape=(jax.ShapeDtypeStruct((tiles + 2,...  2.16 us
    pallas_call x1, Pallas kernels, shards(): pl.pallas_call(near_kernel, out_shape=(jax.ShapeDtypeStruct((tiles + 2, 2...  2.12 us
    pallas_call x1, Pallas kernels, shards(): pl.pallas_call(smooth_kernel, out_shape=(struct((count, rows, columns)),...  1.17 us
  transfers between devices with their start and end apart: 8, of which 2 were waited for; matrix products, arithmetic and copies ran while one was open for 5% of the time, Pallas kernels for 21%

profile of v25, /device:TPU:0, one launch (start us, length us, event | category | flops | bytes accessed | tf_op | source)
XLA Modules:
  0.0 43.9 jit_solution(1791780750061560108)
XLA Ops:
  0.6 3.0 %collective-permute-start.1 = (f32[16,4096]{1,0:T(8,128)}, f32[16,4096]{1,0:T(8,128)S(1)}, u32[]{:S(2)}, u32[]{:S(2)}) collective-permute-start(f32[16,4096]{1,0:T(8,128)} %bitcast.15), channel_id=1, source_target_pairs={{0,1},{1,0},{2,3},{3,2},{4,5},{5,4},{6,7},{7,6},{8,9},{9,8},{10,11... | collective-permute-start | bytes 786440 | tf_op jit(solution)/shard_map/ppermute | solution.py:485
  3.7 1.0 %broadcast_maximum_fusion.1 = f32[16,4096]{1,0:T(8,128)S(1)} fusion(f32[1,16,4096]{2,1,0:T(8,128)} %param.5), kind=kLoop, calls=%fused_computation.3 | loop fusion | flops 65536 | bytes 524288 | tf_op jit(solution)/shard_map/max | solution.py:532
  4.7 1.1 %broadcast_maximum_fusion.frames = f32[2,16,4096]{2,1,0:T(8,128)S(1)} fusion(f32[2,16,4096]{2,1,0:T(8,128)} %param.4), kind=kLoop, calls=%fused_computation | loop fusion | flops 131072 | bytes 1048576 | tf_op jit(solution)/shard_map/max | solution.py:532
  5.8 0.7 %collective-permute-start = (f32[2,4,4096]{2,1,0:T(4,128)S(1)}, f32[2,4,4096]{2,1,0:T(4,128)S(1)}, u32[]{:S(2)}, u32[]{:S(2)}) collective-permute-start(f32[2,4,4096]{2,1,0:T(4,128)S(1)} %get-tuple-element.64), channel_id=1, source_target_pairs={{0,0},{2,4},{4,2},{6,8},{8,6},{10,12},{12,10},{14,16},{16,14},{18,... | collective-permute-start | bytes 393224 | tf_op jit(solution)/shard_map/ppermute | solution.py:485
  6.5 2.9 %collective-permute-start.2 = (f32[2,4,4096]{2,1,0:T(4,128)S(1)}, f32[2,4,4096]{2,1,0:T(4,128)S(1)}, u32[]{:S(2)}, u32[]{:S(2)}) collective-permute-start(f32[2,4,4096]{2,1,0:T(4,128)S(1)} %get-tuple-element.63), channel_id=1, source_target_pairs={{0,2},{2,0},{4,6},{6,4},{8,10},{10,8},{12,14},{14,12},{16,18},{18,... | collective-permute-start | bytes 393224 | tf_op jit(solution)/shard_map/ppermute | solution.py:485
  10.1 0.1 collective-permute-done.1
  10.2 0.1 collective-permute-start.4
  10.3 0.7 %collective-permute-start.3 = (f32[8,4096]{1,0:T(8,128)S(1)}, f32[8,4096]{1,0:T(8,128)S(1)}, u32[]{:S(2)}, u32[]{:S(2)}) collective-permute-start(f32[8,4096]{1,0:T(8,128)S(1)} %get-tuple-element.38.own_odd), channel_id=1, source_target_pairs={{0,0},{2,4},{4,2},{6,8},{8,6},{10,12},{12,10},{14,16},{16,14},{18,... | collective-permute-start | bytes 393224 | tf_op jit(solution)/shard_map/ppermute | solution.py:485
  11.0 0.0 collective-permute-done.from_odd
  11.0 0.0 collective-permute-done.2.from_even
  11.0 1.2 %smooth.1 = (f32[2,16,4096]{2,1,0:T(8,128)S(1)}, bf16[256,4352]{1,0:T(8,128)(2,1)S(1)}, f32[16,128]{1,0:T(8,128)S(1)}, bf16[512,256]{1,0:T(8,128)(2,1)S(1)}) custom-call(f32[2,16,4096]{2,1,0:T(8,128)S(1)} %broadcast_maximum_fusion.frames, f32[2,4,4096]{2,1,0:T(4,128)S(1)} %collective-permute-done.from_odd, f32[2,4,4096]{2,1,0:T(4,128)S(1)} %collective-permute-done.2.from_even), custom_call_target="tpu_custom_call" | custom-call | bytes 8388608 | tf_op jit(solution)/shard_map/smooth/pallas_call | solution.py:541
  12.2 0.0 collective-permute-done.4.from_even
  12.2 2.1 %near.1 = (bf16[34,32,128]{2,1,0:T(8,128)(2,1)S(1)}, f32[128,128]{1,0:T(8,128)S(1)}, f32[8,128]{1,0:T(8,128)S(1)}) custom-call(s32[1,2]{1,0:T(1,128)S(1)} %broadcast_clamp_fusion.base, f32[8,4096]{1,0:T(8,128)S(1)} %get-tuple-element.38.own_odd, f32[8,4096]{1,0:T(8,128)S(1)} %get-tuple-element.61.own_even, f32[8,4096]{1,0:T(8,128)S(1)} %collective-permute-done.4.from_even, ...), custom_call_target="tpu_custom_call" | custom-call | bytes 8388608 | tf_op jit(solution)/shard_map/near/pallas_call | solution.py:570
  14.3 0.0 collective-permute-done.3.from_odd
  14.4 2.2 %match.1 = (bf16[34,16,128]{2,1,0:T(8,128)(2,1)S(1)}, f32[16,128]{1,0:T(8,128)S(1)}) custom-call(s32[1,2]{1,0:T(1,128)S(1)} %broadcast_clamp_fusion.base, f32[8,4096]{1,0:T(8,128)S(1)} %get-tuple-element.38.own_odd, f32[8,4096]{1,0:T(8,128)S(1)} %collective-permute-done.3.from_odd, f32[128,128]{1,0:T(8,128)S(1)} %get-tuple-element.41.near_lags, ...), custom_call_target="tpu_custom_call" | custom-call | bytes 8388608 | tf_op jit(solution)/shard_map/match/pallas_call | solution.py:584
  16.5 1.8 %collective-permute-start.6 = (f32[2,16,4096]{2,1,0:T(8,128)S(1)}, f32[2,16,4096]{2,1,0:T(8,128)S(1)}, u32[]{:S(2)}, u32[]{:S(2)}) collective-permute-start(f32[2,16,4096]{2,1,0:T(8,128)S(1)} %get-tuple-element.52.inverse), channel_id=1, source_target_pairs={{0,1},{1,0},{2,3},{3,2},{4,5},{5,4},{6,7},{7,6},{8,9},{9,8},{10,11... | collective-permute-start | bytes 1572872 | tf_op jit(solution)/shard_map/ppermute | solution.py:485
  18.3 12.6 %all_to_all.21 = f32[16,1,128]{2,1,0:T(1,128)S(1)} all-to-all(f32[16,1,128]{2,1,0:T(1,128)S(1)} %bitcast.12), channel_id=1, replica_groups={{18,20,22,24,26,28,30,0,2,4,6,8,10,12,14,16},{19,21,23,25,27,29,31,1,3,..., dimensions={0} | all-to-all | bytes 16384 | tf_op jit(solution)/shard_map/all_to_all | solution.py:597
  30.9 3.0 %pressure.1 = (f32[2,16,4096]{2,1,0:T(8,128)}, f32[2,16,4096]{2,1,0:T(8,128)S(1)}, f32[16,128]{1,0:T(8,128)}) custom-call(s32[1,2]{1,0:T(1,128)S(1)} %broadcast_clamp_fusion.base, f32[1,128]{1,0:T(1,128)S(1)} %bitcast.13, bf16[34,32,128]{2,1,0:T(8,128)(2,1)S(1)} %get-tuple-element.46.clean, bf16[34,16,128]{2,1,0:T(8,128)(2,1)S(1)} %get-tuple-element.47.other, ...), custom_call_target="tpu_custom_call" | custom-call | bytes 12582912 | tf_op jit(solution)/shard_map/pressure/pallas_call | solution.py:601
  33.9 0.5 %collective-permute-start.5 = (f32[1,128]{1,0:T(1,128)S(1)}, f32[1,128]{1,0:T(1,128)S(1)}, u32[]{:S(2)}, u32[]{:S(2)}) collective-permute-start(f32[1,128]{1,0:T(1,128)S(1)} %bitcast.14), channel_id=1, source_target_pairs={{0,1},{1,0},{2,3},{3,2},{4,5},{5,4},{6,7},{7,6},{8,9},{9,8},{10,11... | collective-permute-start | bytes 1544 | tf_op jit(solution)/shard_map/ppermute | solution.py:485
  34.5 4.7 %all-to-all-start.1 = ((f32[16,1,128]{2,1,0:T(1,128)}), f32[16,1,128]{2,1,0:T(1,128)S(1)}, u32[]{:S(2)}, u32[]{:S(2)}) async-start(f32[16,1,128]{2,1,0:T(1,128)} %bitcast.6), calls=%async_computation.1 | async-start | bytes 16384 | tf_op jit(solution)/shard_map/all_to_all | solution.py:630
  39.2 0.1 multiply_convert_fusion.base
  39.2 3.1 %time.1 = (f32[16,4096]{1,0:T(8,128)}, f32[16,4096]{1,0:T(8,128)}) custom-call(s32[1,2]{1,0:T(1,128)S(1)} %multiply_convert_fusion.base, f32[1,128]{1,0:T(1,128)S(1)} %collective-permute-done.5.totals, bf16[34,32,128]{2,1,0:T(8,128)(2,1)S(1)} %get-tuple-element.46.clean, bf16[34,16,128]{2,1,0:T(8,128)(2,1)S(1)} %get-tuple-element.47.other, ...), custom_call_target="tpu_custom_call" | custom-call | bytes 12582912 | tf_op jit(solution)/shard_map/time/pallas_call | solution.py:615
  42.3 1.0 %all-to-all-done.1 = f32[16,1,128]{2,1,0:T(1,128)S(1)} async-done(((f32[16,1,128]{2,1,0:T(1,128)}), f32[16,1,128]{2,1,0:T(1,128)S(1)}, u32[]{:S(2)}, u32[]{:S(2)}) %all-to-all-start.1) | async-done | bytes 8224 | tf_op jit(solution)/shard_map/all_to_all | solution.py:630
  43.3 0.6 %subtract_sqrt_fusion = (f32[2]{0:T(128)}, f32[2]{0:T(128)}) fusion(f32[128]{0:T(128)S(1)} %reduce_sum.19), kind=kLoop, calls=%fused_computation.6 | loop fusion | flops 8 | bytes 32 | tf_op jit(solution)/shard_map/sqrt | solution.py:635
  (9 shorter events, 0.1 us)
Async XLA Ops:
  0.6 10.4 %copy-start = (s32[1,2]{1,0:T(1,128)S(1)}, s32[1,2]{1,0:T(1,128)}, u32[]{:S(2)}) copy-start(s32[1,2]{1,0:T(1,128)} %param.7) | copy-start | bytes 28
  0.6 9.5 %collective-permute-start.1 = (f32[16,4096]{1,0:T(8,128)}, f32[16,4096]{1,0:T(8,128)S(1)}, u32[]{:S(2)}, u32[]{:S(2)}) collective-permute-start(f32[16,4096]{1,0:T(8,128)} %bitcast.15), channel_id=1, source_target_pairs={{0,1},{1,0},{2,3},{3,2},{4,5},{5,4},{6,7},{7,6},{8,9},{9,8},{10,11... | collective-permute-start | bytes 786440 | tf_op jit(solution)/shard_map/ppermute | solution.py:485
  5.8 5.2 %collective-permute-start = (f32[2,4,4096]{2,1,0:T(4,128)S(1)}, f32[2,4,4096]{2,1,0:T(4,128)S(1)}, u32[]{:S(2)}, u32[]{:S(2)}) collective-permute-start(f32[2,4,4096]{2,1,0:T(4,128)S(1)} %get-tuple-element.64), channel_id=1, source_target_pairs={{0,0},{2,4},{4,2},{6,8},{8,6},{10,12},{12,10},{14,16},{16,14},{18,... | collective-permute-start | bytes 393224 | tf_op jit(solution)/shard_map/ppermute | solution.py:485
  6.5 4.5 %collective-permute-start.2 = (f32[2,4,4096]{2,1,0:T(4,128)S(1)}, f32[2,4,4096]{2,1,0:T(4,128)S(1)}, u32[]{:S(2)}, u32[]{:S(2)}) collective-permute-start(f32[2,4,4096]{2,1,0:T(4,128)S(1)} %get-tuple-element.63), channel_id=1, source_target_pairs={{0,2},{2,0},{4,6},{6,4},{8,10},{10,8},{12,14},{14,12},{16,18},{18,... | collective-permute-start | bytes 393224 | tf_op jit(solution)/shard_map/ppermute | solution.py:485
  10.2 2.0 %collective-permute-start.4 = (f32[8,4096]{1,0:T(8,128)S(1)}, f32[8,4096]{1,0:T(8,128)S(1)}, u32[]{:S(2)}, u32[]{:S(2)}) collective-permute-start(f32[8,4096]{1,0:T(8,128)S(1)} %get-tuple-element.61.own_even), channel_id=1, source_target_pairs={{0,2},{2,0},{4,6},{6,4},{8,10},{10,8},{12,14},{14,12},{16,18},{18,... | collective-permute-start | bytes 393224 | tf_op jit(solution)/shard_map/ppermute | solution.py:485
  10.3 4.0 %collective-permute-start.3 = (f32[8,4096]{1,0:T(8,128)S(1)}, f32[8,4096]{1,0:T(8,128)S(1)}, u32[]{:S(2)}, u32[]{:S(2)}) collective-permute-start(f32[8,4096]{1,0:T(8,128)S(1)} %get-tuple-element.38.own_odd), channel_id=1, source_target_pairs={{0,0},{2,4},{4,2},{6,8},{8,6},{10,12},{12,10},{14,16},{16,14},{18,... | collective-permute-start | bytes 393224 | tf_op jit(solution)/shard_map/ppermute | solution.py:485
  16.5 22.7 %collective-permute-start.6 = (f32[2,16,4096]{2,1,0:T(8,128)S(1)}, f32[2,16,4096]{2,1,0:T(8,128)S(1)}, u32[]{:S(2)}, u32[]{:S(2)}) collective-permute-start(f32[2,16,4096]{2,1,0:T(8,128)S(1)} %get-tuple-element.52.inverse), channel_id=1, source_target_pairs={{0,1},{1,0},{2,3},{3,2},{4,5},{5,4},{6,7},{7,6},{8,9},{9,8},{10,11... | collective-permute-start | bytes 1572872 | tf_op jit(solution)/shard_map/ppermute | solution.py:485
  33.9 5.3 %collective-permute-start.5 = (f32[1,128]{1,0:T(1,128)S(1)}, f32[1,128]{1,0:T(1,128)S(1)}, u32[]{:S(2)}, u32[]{:S(2)}) collective-permute-start(f32[1,128]{1,0:T(1,128)S(1)} %bitcast.14), channel_id=1, source_target_pairs={{0,1},{1,0},{2,3},{3,2},{4,5},{5,4},{6,7},{7,6},{8,9},{9,8},{10,11... | collective-permute-start | bytes 1544 | tf_op jit(solution)/shard_map/ppermute | solution.py:485
  34.5 8.8 %all-to-all-start.1 = ((f32[16,1,128]{2,1,0:T(1,128)}), f32[16,1,128]{2,1,0:T(1,128)S(1)}, u32[]{:S(2)}, u32[]{:S(2)}) async-start(f32[16,1,128]{2,1,0:T(1,128)} %bitcast.6), calls=%async_computation.1 | async-start | bytes 16384 | tf_op jit(solution)/shard_map/all_to_all | solution.py:630

commit v26 on v24

--- a/solution.py
+++ b/solution.py
@@ -627,7 +627,7 @@
         total_frames = count * blocks
         time_mean = whole[0] / total_frames
         time_rms = jnp.sqrt(jnp.maximum(whole[1] / total_frames - time_mean * time_mean, 0.0))
-    sums = lax.all_to_all(part, "rows", 0, 0, axis_index_groups=begun_at(size // 2 + 1, size), tiled=True)
+    sums = lax.all_to_all(part, "rows", 0, 0, axis_index_groups=begun_at(size // 2 + 2, size), tiled=True)
     sums, time_mean, time_rms = lax.optimization_barrier((sums, time_mean, time_rms))
     spatial = jnp.sum(sums, axis=0)
     cell_count = rows * columns * size

time: 43.7 us -> 44 us (level)
  starting transfers between devices: 13.5 us -> 14.8 us
  waiting for transfers between devices: 1.17 us -> 0.21 us
    all_to_all x1, starting transfers between devices: 3.94 us -> 5.11 us  [shards(): lax.all_to_all(part, 'rows', 0, 0, axis_index_groups=begun_at(size // 2 +...]
    all_to_all x1, waiting for transfers between devices: 1.04 us -> 0.08 us  [shards(): lax.all_to_all(part, 'rows', 0, 0, axis_index_groups=begun_at(size // 2 +...]
  transfers between devices with their start and end apart: 8 -> 8, of which waited for: 2 -> 2; matrix products, arithmetic and copies ran while one was open for 5% -> 5% of each run, Pallas kernels for 22% -> 21%
where the time goes in v26:
time: 44 us; the launch traced here: 43.7 us
  starting transfers between devices  14.8 us (34%)
  blocking collectives  12.8 us (29%)
  Pallas kernels  11.5 us (26%)
  other arithmetic  2.89 us (7%)
  between operations  1.42 us (3%)
    all_to_all x1, blocking collectives, shards(): lax.all_to_all(part, 'rows', 0, 0, axis_index_groups=begun_at(size // 2,...  12.8 us
    ppermute x7, starting transfers between devices, paired(): return lax.ppermute(value, axis, list(enumerate(partner)))  9.7 us
    all_to_all x1, starting transfers between devices, shards(): lax.all_to_all(part, 'rows', 0, 0, axis_index_groups=begun_at(size // 2 +...  5.11 us
    pallas_call x1, Pallas kernels, shards(): pl.pallas_call(time_kernel, out_shape=(struct((rows, columns)), struct((r...  3.07 us
    pallas_call x1, Pallas kernels, shards(): pl.pallas_call(pressure_kernel, out_shape=(struct((count, rows, columns))...  2.98 us
    pallas_call x1, Pallas kernels, shards(): pl.pallas_call(match_kernel, out_shape=(jax.ShapeDtypeStruct((tiles + 2,...  2.16 us
    pallas_call x1, Pallas kernels, shards(): pl.pallas_call(near_kernel, out_shape=(jax.ShapeDtypeStruct((tiles + 2, 2...  2.12 us
    pallas_call x1, Pallas kernels, shards(): pl.pallas_call(smooth_kernel, out_shape=(struct((count, rows, columns)),...  1.17 us
  transfers between devices with their start and end apart: 8, of which 2 were waited for; matrix products, arithmetic and copies ran while one was open for 5% of the time, Pallas kernels for 21%

profile of v26, /device:TPU:0, one launch (start us, length us, event | category | flops | bytes accessed | tf_op | source)
XLA Modules:
  0.0 43.7 jit_solution(17805364052628510459)
XLA Ops:
  0.6 3.0 %collective-permute-start.1 = (f32[16,4096]{1,0:T(8,128)}, f32[16,4096]{1,0:T(8,128)S(1)}, u32[]{:S(2)}, u32[]{:S(2)}) collective-permute-start(f32[16,4096]{1,0:T(8,128)} %bitcast.15), channel_id=1, source_target_pairs={{0,1},{1,0},{2,3},{3,2},{4,5},{5,4},{6,7},{7,6},{8,9},{9,8},{10,11... | collective-permute-start | bytes 786440 | tf_op jit(solution)/shard_map/ppermute | solution.py:485
  3.7 1.0 %broadcast_maximum_fusion.1 = f32[16,4096]{1,0:T(8,128)S(1)} fusion(f32[1,16,4096]{2,1,0:T(8,128)} %param.5), kind=kLoop, calls=%fused_computation.3 | loop fusion | flops 65536 | bytes 524288 | tf_op jit(solution)/shard_map/max | solution.py:532
  4.7 1.1 %broadcast_maximum_fusion.frames = f32[2,16,4096]{2,1,0:T(8,128)S(1)} fusion(f32[2,16,4096]{2,1,0:T(8,128)} %param.4), kind=kLoop, calls=%fused_computation | loop fusion | flops 131072 | bytes 1048576 | tf_op jit(solution)/shard_map/max | solution.py:532
  5.8 0.7 %collective-permute-start = (f32[2,4,4096]{2,1,0:T(4,128)S(1)}, f32[2,4,4096]{2,1,0:T(4,128)S(1)}, u32[]{:S(2)}, u32[]{:S(2)}) collective-permute-start(f32[2,4,4096]{2,1,0:T(4,128)S(1)} %get-tuple-element.64), channel_id=1, source_target_pairs={{0,0},{2,4},{4,2},{6,8},{8,6},{10,12},{12,10},{14,16},{16,14},{18,... | collective-permute-start | bytes 393224 | tf_op jit(solution)/shard_map/ppermute | solution.py:485
  6.5 2.9 %collective-permute-start.2 = (f32[2,4,4096]{2,1,0:T(4,128)S(1)}, f32[2,4,4096]{2,1,0:T(4,128)S(1)}, u32[]{:S(2)}, u32[]{:S(2)}) collective-permute-start(f32[2,4,4096]{2,1,0:T(4,128)S(1)} %get-tuple-element.63), channel_id=1, source_target_pairs={{0,2},{2,0},{4,6},{6,4},{8,10},{10,8},{12,14},{14,12},{16,18},{18,... | collective-permute-start | bytes 393224 | tf_op jit(solution)/shard_map/ppermute | solution.py:485
  10.1 0.1 collective-permute-done.1
  10.2 0.1 collective-permute-start.4
  10.3 0.7 %collective-permute-start.3 = (f32[8,4096]{1,0:T(8,128)S(1)}, f32[8,4096]{1,0:T(8,128)S(1)}, u32[]{:S(2)}, u32[]{:S(2)}) collective-permute-start(f32[8,4096]{1,0:T(8,128)S(1)} %get-tuple-element.38.own_odd), channel_id=1, source_target_pairs={{0,0},{2,4},{4,2},{6,8},{8,6},{10,12},{12,10},{14,16},{16,14},{18,... | collective-permute-start | bytes 393224 | tf_op jit(solution)/shard_map/ppermute | solution.py:485
  11.0 0.0 collective-permute-done.2.from_even
  11.0 1.2 %smooth.1 = (f32[2,16,4096]{2,1,0:T(8,128)S(1)}, bf16[256,4352]{1,0:T(8,128)(2,1)S(1)}, f32[16,128]{1,0:T(8,128)S(1)}, bf16[512,256]{1,0:T(8,128)(2,1)S(1)}) custom-call(f32[2,16,4096]{2,1,0:T(8,128)S(1)} %broadcast_maximum_fusion.frames, f32[2,4,4096]{2,1,0:T(4,128)S(1)} %collective-permute-done.from_odd, f32[2,4,4096]{2,1,0:T(4,128)S(1)} %collective-permute-done.2.from_even), custom_call_target="tpu_custom_call" | custom-call | bytes 8388608 | tf_op jit(solution)/shard_map/smooth/pallas_call | solution.py:541
  12.2 2.1 %near.1 = (bf16[34,32,128]{2,1,0:T(8,128)(2,1)S(1)}, f32[128,128]{1,0:T(8,128)S(1)}, f32[8,128]{1,0:T(8,128)S(1)}) custom-call(s32[1,2]{1,0:T(1,128)S(1)} %broadcast_clamp_fusion.base, f32[8,4096]{1,0:T(8,128)S(1)} %get-tuple-element.38.own_odd, f32[8,4096]{1,0:T(8,128)S(1)} %get-tuple-element.61.own_even, f32[8,4096]{1,0:T(8,128)S(1)} %collective-permute-done.4.from_even, ...), custom_call_target="tpu_custom_call" | custom-call | bytes 8388608 | tf_op jit(solution)/shard_map/near/pallas_call | solution.py:570
  14.3 0.0 collective-permute-done.3.from_odd
  14.4 2.2 %match.1 = (bf16[34,16,128]{2,1,0:T(8,128)(2,1)S(1)}, f32[16,128]{1,0:T(8,128)S(1)}) custom-call(s32[1,2]{1,0:T(1,128)S(1)} %broadcast_clamp_fusion.base, f32[8,4096]{1,0:T(8,128)S(1)} %get-tuple-element.38.own_odd, f32[8,4096]{1,0:T(8,128)S(1)} %collective-permute-done.3.from_odd, f32[128,128]{1,0:T(8,128)S(1)} %get-tuple-element.41.near_lags, ...), custom_call_target="tpu_custom_call" | custom-call | bytes 8388608 | tf_op jit(solution)/shard_map/match/pallas_call | solution.py:584
  16.5 1.8 %collective-permute-start.6 = (f32[2,16,4096]{2,1,0:T(8,128)S(1)}, f32[2,16,4096]{2,1,0:T(8,128)S(1)}, u32[]{:S(2)}, u32[]{:S(2)}) collective-permute-start(f32[2,16,4096]{2,1,0:T(8,128)S(1)} %get-tuple-element.52.inverse), channel_id=1, source_target_pairs={{0,1},{1,0},{2,3},{3,2},{4,5},{5,4},{6,7},{7,6},{8,9},{9,8},{10,11... | collective-permute-start | bytes 1572872 | tf_op jit(solution)/shard_map/ppermute | solution.py:485
  18.3 12.8 %all_to_all.21 = f32[16,1,128]{2,1,0:T(1,128)S(1)} all-to-all(f32[16,1,128]{2,1,0:T(1,128)S(1)} %bitcast.12), channel_id=1, replica_groups={{16,18,20,22,24,26,28,30,0,2,4,6,8,10,12,14},{17,19,21,23,25,27,29,31,1..., dimensions={0} | all-to-all | bytes 16384 | tf_op jit(solution)/shard_map/all_to_all | solution.py:597
  31.2 3.0 %pressure.1 = (f32[2,16,4096]{2,1,0:T(8,128)}, f32[2,16,4096]{2,1,0:T(8,128)S(1)}, f32[16,128]{1,0:T(8,128)}) custom-call(s32[1,2]{1,0:T(1,128)S(1)} %broadcast_clamp_fusion.base, f32[1,128]{1,0:T(1,128)S(1)} %bitcast.13, bf16[34,32,128]{2,1,0:T(8,128)(2,1)S(1)} %get-tuple-element.46.clean, bf16[34,16,128]{2,1,0:T(8,128)(2,1)S(1)} %get-tuple-element.47.other, ...), custom_call_target="tpu_custom_call" | custom-call | bytes 12582912 | tf_op jit(solution)/shard_map/pressure/pallas_call | solution.py:601
  34.1 0.5 %collective-permute-start.5 = (f32[1,128]{1,0:T(1,128)S(1)}, f32[1,128]{1,0:T(1,128)S(1)}, u32[]{:S(2)}, u32[]{:S(2)}) collective-permute-start(f32[1,128]{1,0:T(1,128)S(1)} %bitcast.14), channel_id=1, source_target_pairs={{0,1},{1,0},{2,3},{3,2},{4,5},{5,4},{6,7},{7,6},{8,9},{9,8},{10,11... | collective-permute-start | bytes 1544 | tf_op jit(solution)/shard_map/ppermute | solution.py:485
  34.7 5.1 %all-to-all-start.1 = ((f32[16,1,128]{2,1,0:T(1,128)}), f32[16,1,128]{2,1,0:T(1,128)S(1)}, u32[]{:S(2)}, u32[]{:S(2)}) async-start(f32[16,1,128]{2,1,0:T(1,128)} %bitcast.6), calls=%async_computation.1 | async-start | bytes 16384 | tf_op jit(solution)/shard_map/all_to_all | solution.py:630
  39.8 0.0 collective-permute-done.5.totals
  39.8 0.1 multiply_convert_fusion.base
  39.9 0.0 collective-permute-done.6.inverse
  39.9 3.1 %time.1 = (f32[16,4096]{1,0:T(8,128)}, f32[16,4096]{1,0:T(8,128)}) custom-call(s32[1,2]{1,0:T(1,128)S(1)} %multiply_convert_fusion.base, f32[1,128]{1,0:T(1,128)S(1)} %collective-permute-done.5.totals, bf16[34,32,128]{2,1,0:T(8,128)(2,1)S(1)} %get-tuple-element.46.clean, bf16[34,16,128]{2,1,0:T(8,128)(2,1)S(1)} %get-tuple-element.47.other, ...), custom_call_target="tpu_custom_call" | custom-call | bytes 12582912 | tf_op jit(solution)/shard_map/time/pallas_call | solution.py:615
  43.0 0.1 all-to-all-done.1
  43.1 0.6 %subtract_sqrt_fusion = (f32[2]{0:T(128)}, f32[2]{0:T(128)}) fusion(f32[128]{0:T(128)S(1)} %reduce_sum.19), kind=kLoop, calls=%fused_computation.6 | loop fusion | flops 8 | bytes 32 | tf_op jit(solution)/shard_map/sqrt | solution.py:635
  (9 shorter events, 0.1 us)
Async XLA Ops:
  0.6 10.4 %copy-start = (s32[1,2]{1,0:T(1,128)S(1)}, s32[1,2]{1,0:T(1,128)}, u32[]{:S(2)}) copy-start(s32[1,2]{1,0:T(1,128)} %param.7) | copy-start | bytes 28
  0.6 9.5 %collective-permute-start.1 = (f32[16,4096]{1,0:T(8,128)}, f32[16,4096]{1,0:T(8,128)S(1)}, u32[]{:S(2)}, u32[]{:S(2)}) collective-permute-start(f32[16,4096]{1,0:T(8,128)} %bitcast.15), channel_id=1, source_target_pairs={{0,1},{1,0},{2,3},{3,2},{4,5},{5,4},{6,7},{7,6},{8,9},{9,8},{10,11... | collective-permute-start | bytes 786440 | tf_op jit(solution)/shard_map/ppermute | solution.py:485
  5.8 5.2 %collective-permute-start = (f32[2,4,4096]{2,1,0:T(4,128)S(1)}, f32[2,4,4096]{2,1,0:T(4,128)S(1)}, u32[]{:S(2)}, u32[]{:S(2)}) collective-permute-start(f32[2,4,4096]{2,1,0:T(4,128)S(1)} %get-tuple-element.64), channel_id=1, source_target_pairs={{0,0},{2,4},{4,2},{6,8},{8,6},{10,12},{12,10},{14,16},{16,14},{18,... | collective-permute-start | bytes 393224 | tf_op jit(solution)/shard_map/ppermute | solution.py:485
  6.5 4.5 %collective-permute-start.2 = (f32[2,4,4096]{2,1,0:T(4,128)S(1)}, f32[2,4,4096]{2,1,0:T(4,128)S(1)}, u32[]{:S(2)}, u32[]{:S(2)}) collective-permute-start(f32[2,4,4096]{2,1,0:T(4,128)S(1)} %get-tuple-element.63), channel_id=1, source_target_pairs={{0,2},{2,0},{4,6},{6,4},{8,10},{10,8},{12,14},{14,12},{16,18},{18,... | collective-permute-start | bytes 393224 | tf_op jit(solution)/shard_map/ppermute | solution.py:485
  10.2 2.0 %collective-permute-start.4 = (f32[8,4096]{1,0:T(8,128)S(1)}, f32[8,4096]{1,0:T(8,128)S(1)}, u32[]{:S(2)}, u32[]{:S(2)}) collective-permute-start(f32[8,4096]{1,0:T(8,128)S(1)} %get-tuple-element.61.own_even), channel_id=1, source_target_pairs={{0,2},{2,0},{4,6},{6,4},{8,10},{10,8},{12,14},{14,12},{16,18},{18,... | collective-permute-start | bytes 393224 | tf_op jit(solution)/shard_map/ppermute | solution.py:485
  10.3 4.0 %collective-permute-start.3 = (f32[8,4096]{1,0:T(8,128)S(1)}, f32[8,4096]{1,0:T(8,128)S(1)}, u32[]{:S(2)}, u32[]{:S(2)}) collective-permute-start(f32[8,4096]{1,0:T(8,128)S(1)} %get-tuple-element.38.own_odd), channel_id=1, source_target_pairs={{0,0},{2,4},{4,2},{6,8},{8,6},{10,12},{12,10},{14,16},{16,14},{18,... | collective-permute-start | bytes 393224 | tf_op jit(solution)/shard_map/ppermute | solution.py:485
  16.5 23.4 %collective-permute-start.6 = (f32[2,16,4096]{2,1,0:T(8,128)S(1)}, f32[2,16,4096]{2,1,0:T(8,128)S(1)}, u32[]{:S(2)}, u32[]{:S(2)}) collective-permute-start(f32[2,16,4096]{2,1,0:T(8,128)S(1)} %get-tuple-element.52.inverse), channel_id=1, source_target_pairs={{0,1},{1,0},{2,3},{3,2},{4,5},{5,4},{6,7},{7,6},{8,9},{9,8},{10,11... | collective-permute-start | bytes 1572872 | tf_op jit(solution)/shard_map/ppermute | solution.py:485
  34.1 5.7 %collective-permute-start.5 = (f32[1,128]{1,0:T(1,128)S(1)}, f32[1,128]{1,0:T(1,128)S(1)}, u32[]{:S(2)}, u32[]{:S(2)}) collective-permute-start(f32[1,128]{1,0:T(1,128)S(1)} %bitcast.14), channel_id=1, source_target_pairs={{0,1},{1,0},{2,3},{3,2},{4,5},{5,4},{6,7},{7,6},{8,9},{9,8},{10,11... | collective-permute-start | bytes 1544 | tf_op jit(solution)/shard_map/ppermute | solution.py:485
  34.7 8.3 %all-to-all-start.1 = ((f32[16,1,128]{2,1,0:T(1,128)}), f32[16,1,128]{2,1,0:T(1,128)S(1)}, u32[]{:S(2)}, u32[]{:S(2)}) async-start(f32[16,1,128]{2,1,0:T(1,128)} %bitcast.6), calls=%async_computation.1 | async-start | bytes 16384 | tf_op jit(solution)/shard_map/all_to_all | solution.py:630
